TPU v7x, 32 devices: a whole 2x2x4 slice. The times are simulated.
32 devices in a mesh: seq: 16 (over z, x, core), dp: 2 (over y).
Axes of the slice: x: 2, y: 2, z: 4, core: 2. Of those that a mesh axis runs over, the one named last changes fastest.
Arguments:
- queries: bfloat16 [2, 2048, 4096], P('dp', 'seq'), may hold values from -4.5 to 4.5
- context: bfloat16 [2, 2048, 1024], P('dp', 'seq'), may hold values from -4.5 to 4.5
- segment_start: int32 [2, 2048], P('dp', 'seq'), may hold values from 0 to 2047, as said below
- memory: bfloat16 [2, 16, 64, 1024], P('dp', 'seq'), may hold values from -4.5 to 4.5
- image_offset: int32 [2, 16], P('dp', 'seq'), may hold values from 0 to 128, as said below
- cross_gate: float32 [32], replicated, may hold values from -1.5 to 1.5
- out_grad: bfloat16 [2, 2048, 4096], P('dp', 'seq'), may hold values from -6 to 6
Outputs:
- query_grad: bfloat16 [2, 2048, 4096], P('dp', 'seq')
- context_grad: bfloat16 [2, 2048, 1024], P('dp', 'seq')
- memory_grad: bfloat16 [2, 16, 64, 1024], P('dp', 'seq')
- gate_grad: float32 [32], replicated
Inputs may be any that keep to these rules, and one draw needn't show every extreme that they name: `segment_start`: position of the first token of each token's segment: non-decreasing, equal to the position itself at a segment's first token; positions 0 and 2047 begin segments. `image_offset`: in each aligned block of 4 shards exactly one shard owns an image (offset below 128); every token that reads an image reads one owned at most 7 shards before its own, and that distance is reached in every draw.
All inputs are finite; a program needn't handle non-finite values.
Results may differ from a plain program's by a relative error of at most 0.012.
The roundings to bfloat16 on the way count: a program that leaves them out, or rounds other values in their place, can miss the bound.
Values may be sent and summed in bfloat16 or wider, within the bound.
No kernel may reach another device: no remote copies, remote signals or barrier semaphores. Data moves between devices by JAX's collectives and lax.ppermute only.
A program may use at most 128 MiB of HBM per device.

v0:
```python
import math

import jax
import jax.numpy as jnp
from jax import lax
from jax.sharding import PartitionSpec as P

HEAD_DIM = 128
LINK = 7
WINDOW = 64


def from_behind(shard, axis, by):
    size = lax.axis_size(axis)
    pairs = [(i, i + by) for i in range(size) if 0 <= i + by < size]
    return lax.ppermute(shard, axis, pairs)


def masked_softmax(scores, allowed):
    scores = jnp.where(allowed, scores, -1e30)
    row_top = jnp.max(scores, axis=-1, keepdims=True)
    powers = jnp.exp(scores - row_top)
    return powers / jnp.sum(powers, axis=-1, keepdims=True)


def attend(query_rows, key_part, value_part, allowed):
    score_scale = 1.0 / math.sqrt(HEAD_DIM)
    scores = (
        jnp.einsum("gqd,gkd->gqk", query_rows, key_part, preferred_element_type=jnp.float32)
        * score_scale
    )
    weights = masked_softmax(scores, allowed[None])
    narrow_weights = weights.astype(jnp.bfloat16)
    mixed = jnp.einsum(
        "gqk,gkd->gqd", narrow_weights, value_part, preferred_element_type=jnp.float32
    )
    return (weights, narrow_weights, mixed)


def attend_back(grad_mixed, query_rows, key_part, value_part, weights, narrow_weights):
    score_scale = 1.0 / math.sqrt(HEAD_DIM)
    grad_weights = jnp.einsum(
        "gqd,gkd->gqk", grad_mixed, value_part, preferred_element_type=jnp.float32
    )
    row_delta = jnp.sum(weights * grad_weights, axis=-1, keepdims=True)
    grad_scores = (weights * (grad_weights - row_delta)).astype(jnp.bfloat16)
    grad_queries = (
        jnp.einsum("gqk,gkd->gqd", grad_scores, key_part, preferred_element_type=jnp.float32)
        * score_scale
    )
    grad_keys = (
        jnp.einsum("gqk,gqd->gkd", grad_scores, query_rows, preferred_element_type=jnp.float32)
        * score_scale
    )
    grad_values = jnp.einsum(
        "gqk,gqd->gkd", narrow_weights, grad_mixed, preferred_element_type=jnp.float32
    )
    return (grad_queries, grad_keys, grad_values)


def split_pair(joined, groups):
    key_width = groups * HEAD_DIM
    key_part = joined[:, :key_width].reshape(-1, groups, HEAD_DIM).transpose(1, 0, 2)
    value_part = joined[:, key_width:].reshape(-1, groups, HEAD_DIM).transpose(1, 0, 2)
    return (key_part, value_part)


def to_rows(values, groups, repeat):
    tok_rows = values.shape[0]
    return (
        values.reshape(tok_rows, groups, repeat, HEAD_DIM)
        .transpose(1, 2, 0, 3)
        .reshape(groups, repeat * tok_rows, HEAD_DIM)
    )


def from_rows(values, tok_rows):
    groups = values.shape[0]
    repeat = values.shape[1] // tok_rows
    return (
        values.reshape(groups, repeat, tok_rows, HEAD_DIM)
        .transpose(2, 0, 1, 3)
        .reshape(tok_rows, -1)
    )


def joined_terms(key_grad, value_grad):
    key_rows = key_grad.shape[1]
    return jnp.concatenate(
        [
            key_grad.transpose(1, 0, 2).reshape(key_rows, -1),
            value_grad.transpose(1, 0, 2).reshape(key_rows, -1),
        ],
        axis=1,
    )


def on_device(queries, context, segment_start, memory, image_offset, cross_gate, out_grad):
    tok_rows = queries.shape[1]
    key_width = context.shape[2] // 2
    groups = key_width // HEAD_DIM
    repeat = cross_gate.shape[0] // groups
    image_rows = memory.shape[2]
    shard_index = lax.axis_index("seq")
    query_rows = to_rows(queries[0], groups, repeat)
    earlier = from_behind(context[0][tok_rows - WINDOW :], "seq", 1)
    joined_keys = jnp.concatenate([earlier, context[0]], axis=0)
    key_part, value_part = split_pair(joined_keys, groups)
    query_pos = shard_index * tok_rows + jnp.arange(tok_rows, dtype=jnp.int32)
    key_pos = shard_index * tok_rows - WINDOW + jnp.arange(WINDOW + tok_rows, dtype=jnp.int32)
    segment_row = segment_start[0]
    allowed = (
        (key_pos[None, :] <= query_pos[:, None])
        & (key_pos[None, :] >= query_pos[:, None] - WINDOW)
        & (key_pos[None, :] >= segment_row[:, None])
    )
    allowed = jnp.tile(allowed, (repeat, 1))
    own_image = memory[0, 0]
    own_offset = image_offset[0, 0]
    is_owner = own_offset < tok_rows
    own_flag = is_owner.astype(jnp.bfloat16).reshape(1)
    carry_image = own_image
    carry_flag = own_flag
    for link_step in range(LINK):
        before, before_flag = from_behind((carry_image, carry_flag), "seq", 1)
        carry_image = jnp.where(is_owner, own_image, before)
        carry_flag = jnp.where(is_owner, own_flag, before_flag)
    has_prev = before_flag[0] > 0
    local = jnp.arange(tok_rows, dtype=jnp.int32)
    use_own = is_owner & (local >= own_offset)
    use_prev = jnp.logical_not(use_own) & has_prev
    columns = jnp.arange(2 * image_rows, dtype=jnp.int32)
    cross_allowed = jnp.where(columns[None, :] < image_rows, use_prev[:, None], use_own[:, None])
    cross_allowed = jnp.tile(cross_allowed, (repeat, 1))
    has_image = (use_own | use_prev).astype(jnp.float32)
    image_mask = jnp.tile(has_image, repeat)[None, :, None]
    weights, narrow_weights, mixed = attend(query_rows, key_part, value_part, allowed)
    self_out = mixed.astype(jnp.bfloat16)
    joined_memory = jnp.concatenate([before, own_image], axis=0)
    memory_keys, memory_values = split_pair(joined_memory, groups)
    cross_weights, cross_narrow, cross_mixed = attend(
        self_out, memory_keys, memory_values, cross_allowed
    )
    cross_mixed = cross_mixed * image_mask
    gate_tanh = jnp.tanh(cross_gate)
    grad_out = to_rows(out_grad[0], groups, repeat).astype(jnp.float32)
    gate_part = jnp.sum(
        (grad_out * cross_mixed).reshape(groups, repeat, tok_rows, HEAD_DIM), axis=(2, 3)
    ).reshape(-1)
    gate_rows = jnp.repeat(gate_tanh.reshape(groups, repeat), tok_rows, axis=1)[:, :, None]
    grad_cross = (grad_out * gate_rows * image_mask).astype(jnp.bfloat16)
    cross_query_grad, memory_key_grad, memory_value_grad = attend_back(
        grad_cross, self_out, memory_keys, memory_values, cross_weights, cross_narrow
    )
    grad_self = (grad_out + cross_query_grad).astype(jnp.bfloat16)
    query_grad, key_grad, value_grad = attend_back(
        grad_self, query_rows, key_part, value_part, weights, narrow_weights
    )
    key_terms = joined_terms(key_grad, value_grad)
    returned = from_behind(key_terms[:WINDOW], "seq", -1)
    context_grad = (
        key_terms[WINDOW:] + jnp.pad(returned, ((tok_rows - WINDOW, 0), (0, 0)))
    ).astype(jnp.bfloat16)[None]
    image_terms = joined_terms(memory_key_grad, memory_value_grad)
    carried = image_terms[:image_rows]
    owner_weight = is_owner.astype(jnp.float32).reshape(1)
    carry_terms = carried
    for link_step in range(LINK):
        arrived = from_behind(carry_terms, "seq", -1)
        carry_terms = carried + (1.0 - owner_weight[0]) * arrived
    memory_grad = jnp.where(is_owner, image_terms[image_rows:] + arrived, 0.0).astype(jnp.bfloat16)[
        None, None
    ]
    gate_total = lax.psum(gate_part, ("seq", "dp"))
    gate_grad = (1.0 - gate_tanh * gate_tanh) * gate_total
    return (
        from_rows(query_grad, tok_rows).reshape(1, tok_rows, -1).astype(jnp.bfloat16),
        context_grad,
        memory_grad,
        gate_grad,
    )


def solution(mesh):
    placed = (
        P("dp", "seq", None),
        P("dp", "seq", None),
        P("dp", "seq"),
        P("dp", "seq", None, None),
        P("dp", "seq"),
        P(),
        P("dp", "seq", None),
    )
    return jax.shard_map(
        on_device,
        mesh=mesh,
        in_specs=placed,
        out_specs=(P("dp", "seq", None), P("dp", "seq", None), P("dp", "seq", None, None), P()),
        check_vma=False,
    )
```

profile of v0, /device:TPU:3, one launch (start us, length us, event | category | flops | bytes accessed | tf_op | source)
XLA Modules:
  0.0 247.2 jit_solution(13202380669494938537)
XLA Ops:
  1.3 4.4 %collective-permute-start.1 = (bf16[1]{0:T(256)(128)(2,1)}, bf16[1]{0:T(256)(128)(2,1)}, u32[]{:S(2)}, u32[]{:S(2)}) collective-permute-start(bf16[1]{0:T(256)(128)(2,1)} %reshape.245), channel_id=1, source_target_pairs={{0,2},{2,4},{4,6},{6,8},{8,10},{10,12},{12,14},{14,16},{16,18},{18... | collective-permute-start | bytes 14 | tf_op jit(solution)/shard_map/ppermute | solution.py:16
  5.8 1.1 copy.53
  6.8 2.1 collective-permute-start.8
  9.9 3.3 %collective-permute-start = (bf16[64,1024]{1,0:T(8,128)(2,1)S(1)}, bf16[64,1024]{1,0:T(8,128)(2,1)}, u32[]{:S(2)}, u32[]{:S(2)}) collective-permute-start(bf16[64,1024]{1,0:T(8,128)(2,1)S(1)} %slice_bitcast_fusion), channel_id=1, source_target_pairs={{0,2},{2,4},{4,6},{6,8},{8,10},{10,12},{12,14},{14,16},{16,18},{18... | collective-permute-start | bytes 393224 | tf_op jit(solution)/shard_map/ppermute | solution.py:16
  13.2 1.5 convert_bitcast_fusion
  15.6 2.7 %collective-permute-start.9 = (bf16[64,1024]{0,1:T(8,128)(2,1)}, bf16[64,1024]{0,1:T(8,128)(2,1)}, u32[]{:S(2)}, u32[]{:S(2)}) collective-permute-start(bf16[64,1024]{0,1:T(8,128)(2,1)} %broadcast_select_fusion.5), channel_id=1, source_target_pairs={{0,2},{2,4},{4,6},{6,8},{8,10},{10,12},{12,14},{14,16},{16,18},{18... | collective-permute-start | bytes 393224 | tf_op jit(solution)/shard_map/ppermute | solution.py:16
  20.2 2.0 copy.51
  22.3 1.7 reshape.255
  24.7 3.5 %collective-permute-start.2 = (bf16[1]{0:T(256)(128)(2,1)}, bf16[1]{0:T(256)(128)(2,1)}, u32[]{:S(2)}, u32[]{:S(2)}) collective-permute-start(bf16[1]{0:T(256)(128)(2,1)} %select_n.80), channel_id=1, source_target_pairs={{0,2},{2,4},{4,6},{6,8},{8,10},{10,12},{12,14},{14,16},{16,18},{18... | collective-permute-start | bytes 14 | tf_op jit(solution)/shard_map/ppermute | solution.py:16
  28.8 5.9 %collective-permute-start.3 = (bf16[1]{0:T(256)(128)(2,1)}, bf16[1]{0:T(256)(128)(2,1)}, u32[]{:S(2)}, u32[]{:S(2)}) collective-permute-start(bf16[1]{0:T(256)(128)(2,1)} %select_n.81), channel_id=1, source_target_pairs={{0,2},{2,4},{4,6},{6,8},{8,10},{10,12},{12,14},{14,16},{16,18},{18... | collective-permute-start | bytes 14 | tf_op jit(solution)/shard_map/ppermute | solution.py:16
  35.3 5.9 %collective-permute-start.4 = (bf16[1]{0:T(256)(128)(2,1)}, bf16[1]{0:T(256)(128)(2,1)}, u32[]{:S(2)}, u32[]{:S(2)}) collective-permute-start(bf16[1]{0:T(256)(128)(2,1)} %select_n.82), channel_id=1, source_target_pairs={{0,2},{2,4},{4,6},{6,8},{8,10},{10,12},{12,14},{14,16},{16,18},{18... | collective-permute-start | bytes 14 | tf_op jit(solution)/shard_map/ppermute | solution.py:16
  41.8 5.9 %collective-permute-start.5 = (bf16[1]{0:T(256)(128)(2,1)}, bf16[1]{0:T(256)(128)(2,1)}, u32[]{:S(2)}, u32[]{:S(2)}) collective-permute-start(bf16[1]{0:T(256)(128)(2,1)} %select_n.83), channel_id=1, source_target_pairs={{0,2},{2,4},{4,6},{6,8},{8,10},{10,12},{12,14},{14,16},{16,18},{18... | collective-permute-start | bytes 14 | tf_op jit(solution)/shard_map/ppermute | solution.py:16
  48.3 5.9 %collective-permute-start.6 = (bf16[1]{0:T(256)(128)(2,1)}, bf16[1]{0:T(256)(128)(2,1)}, u32[]{:S(2)}, u32[]{:S(2)}) collective-permute-start(bf16[1]{0:T(256)(128)(2,1)} %select_n.84), channel_id=1, source_target_pairs={{0,2},{2,4},{4,6},{6,8},{8,10},{10,12},{12,14},{14,16},{16,18},{18... | collective-permute-start | bytes 14 | tf_op jit(solution)/shard_map/ppermute | solution.py:16
  54.8 5.9 %collective-permute-start.7 = (bf16[1]{0:T(256)(128)(2,1)}, bf16[1]{0:T(256)(128)(2,1)}, u32[]{:S(2)}, u32[]{:S(2)}) collective-permute-start(bf16[1]{0:T(256)(128)(2,1)} %select_n.85), channel_id=1, source_target_pairs={{0,2},{2,4},{4,6},{6,8},{8,10},{10,12},{12,14},{14,16},{16,18},{18... | collective-permute-start | bytes 14 | tf_op jit(solution)/shard_map/ppermute | solution.py:16
  62.3 5.2 %collective-permute-start.10 = (bf16[64,1024]{0,1:T(8,128)(2,1)S(1)}, bf16[64,1024]{0,1:T(8,128)(2,1)S(1)}, u32[]{:S(2)}, u32[]{:S(2)}) collective-permute-start(bf16[64,1024]{0,1:T(8,128)(2,1)S(1)} %broadcast_select_fusion.4), channel_id=1, source_target_pairs={{0,2},{2,4},{4,6},{6,8},{8,10},{10,12},{12,14},{14,16},{16,18},{18... | collective-permute-start | bytes 393224 | tf_op jit(solution)/shard_map/ppermute | solution.py:16
  67.5 3.2 %collective-permute-done.10 = bf16[64,1024]{0,1:T(8,128)(2,1)S(1)} collective-permute-done((bf16[64,1024]{0,1:T(8,128)(2,1)S(1)}, bf16[64,1024]{0,1:T(8,128)(2,1)S(1)}, u32[]{:S(2)}, u32[]{:S(2)}) %collective-permute-start.10) | collective-permute-done | bytes 131104 | tf_op jit(solution)/shard_map/ppermute | solution.py:16
  70.8 5.3 %collective-permute-start.11 = (bf16[64,1024]{0,1:T(8,128)(2,1)S(1)}, bf16[64,1024]{0,1:T(8,128)(2,1)S(1)}, u32[]{:S(2)}, u32[]{:S(2)}) collective-permute-start(bf16[64,1024]{0,1:T(8,128)(2,1)S(1)} %broadcast_select_fusion.3), channel_id=1, source_target_pairs={{0,2},{2,4},{4,6},{6,8},{8,10},{10,12},{12,14},{14,16},{16,18},{18... | collective-permute-start | bytes 393224 | tf_op jit(solution)/shard_map/ppermute | solution.py:16
  76.1 3.3 %collective-permute-done.11 = bf16[64,1024]{0,1:T(8,128)(2,1)S(1)} collective-permute-done((bf16[64,1024]{0,1:T(8,128)(2,1)S(1)}, bf16[64,1024]{0,1:T(8,128)(2,1)S(1)}, u32[]{:S(2)}, u32[]{:S(2)}) %collective-permute-start.11) | collective-permute-done | bytes 131104 | tf_op jit(solution)/shard_map/ppermute | solution.py:16
  79.4 5.3 %collective-permute-start.12 = (bf16[64,1024]{0,1:T(8,128)(2,1)S(1)}, bf16[64,1024]{0,1:T(8,128)(2,1)S(1)}, u32[]{:S(2)}, u32[]{:S(2)}) collective-permute-start(bf16[64,1024]{0,1:T(8,128)(2,1)S(1)} %broadcast_select_fusion.2), channel_id=1, source_target_pairs={{0,2},{2,4},{4,6},{6,8},{8,10},{10,12},{12,14},{14,16},{16,18},{18... | collective-permute-start | bytes 393224 | tf_op jit(solution)/shard_map/ppermute | solution.py:16
  86.1 1.6 fusion.25
  88.8 5.3 %collective-permute-start.13 = (bf16[64,1024]{0,1:T(8,128)(2,1)}, bf16[64,1024]{0,1:T(8,128)(2,1)}, u32[]{:S(2)}, u32[]{:S(2)}) collective-permute-start(bf16[64,1024]{0,1:T(8,128)(2,1)} %broadcast_select_fusion.1), channel_id=1, source_target_pairs={{0,2},{2,4},{4,6},{6,8},{8,10},{10,12},{12,14},{14,16},{16,18},{18... | collective-permute-start | bytes 393224 | tf_op jit(solution)/shard_map/ppermute | solution.py:16
  94.0 3.9 %fusion.51 = (f32[4,1024]{1,0:T(4,128)S(1)}, f32[4,1024,192]{1,2,0:T(8,128)}) fusion(pred[1024,192]{0,1:T(8,128)(4,1)} %bitcast.204, bf16[4,1024,128]{2,1,0:T(8,128)(2,1)S(1)} %bitcast.192, bf16[24,4,8,128]{3,2,1,0:T(8,128)(2,1)} %get-tuple-element.16), kind=kOutput, calls=%fused_computation.103 | convolution fusion | flops 204472512 | bytes 4603904 | tf_op jit(solution)/shard_map/sub | solution.py:22
  99.0 5.0 %collective-permute-start.14 = (bf16[64,1024]{0,1:T(8,128)(2,1)S(1)}, bf16[64,1024]{0,1:T(8,128)(2,1)S(1)}, u32[]{:S(2)}, u32[]{:S(2)}) collective-permute-start(bf16[64,1024]{0,1:T(8,128)(2,1)S(1)} %broadcast_select_fusion), channel_id=1, source_target_pairs={{0,2},{2,4},{4,6},{6,8},{8,10},{10,12},{12,14},{14,16},{16,18},{18... | collective-permute-start | bytes 393224 | tf_op jit(solution)/shard_map/ppermute | solution.py:16
  103.9 3.8 %convolution_convert_fusion = bf16[4,1024,128]{2,1,0:T(8,128)(2,1)} fusion(bf16[24,4,8,128]{3,2,1,0:T(8,128)(2,1)} %get-tuple-element.17, f32[4,1024,192]{1,2,0:T(8,128)} %get-tuple-element.21, f32[4,1024]{1,0:T(4,128)S(1)} %get-tuple-element.20), kind=kOutput, calls=%fused_computation.21 | convolution fusion | flops 203423744 | bytes 4407296 | tf_op jit(solution)/shard_map/gqk,gkd->gqd/dot_general | solution.py:34
  109.6 3.5 %fusion.52 = (f32[4,1024]{1,0:T(4,128)S(1)}, f32[4,1024,128]{1,2,0:T(8,128)}) fusion(pred[1024,128]{0,1:T(8,128)(4,1)} %bitcast.205, bf16[4,1024,128]{2,1,0:T(8,128)(2,1)} %convolution_convert_fusion, bf16[128,4,128]{2,0,1:T(8,128)(2,1)S(1)} %copy.54), kind=kOutput, calls=%fused_computation.104 | convolution fusion | flops 136315008 | bytes 3424256 | tf_op jit(solution)/shard_map/sub | solution.py:22
  113.2 2.1 multiply_reduce_fusion.1
  115.4 40.3 %psum.7 = f32[32]{0:T(128)S(1)} all-reduce(f32[32]{0:T(128)S(1)} %reshape.254), channel_id=1, replica_groups=mesh['seq'=16,'dp'=2] {'seq','dp'}, use_global_device_ids=true, to_apply=%region_8.9 | all-reduce | flops 32 | bytes 256 | tf_op jit(solution)/shard_map/psum | solution.py:174
  157.8 2.2 fusion.17
  163.3 3.3 %collective-permute-start.16 = (f32[64,1024]{0,1:T(8,128)}, f32[64,1024]{0,1:T(8,128)S(1)}, u32[]{:S(2)}, u32[]{:S(2)}) collective-permute-start(f32[64,1024]{0,1:T(8,128)} %pad_maximum_fusion), channel_id=1, source_target_pairs={{2,0},{4,2},{6,4},{8,6},{10,8},{12,10},{14,12},{16,14},{18,16},{20... | collective-permute-start | bytes 786440 | tf_op jit(solution)/shard_map/ppermute | solution.py:16
  166.6 8.3 %collective-permute-done.16 = f32[64,1024]{0,1:T(8,128)S(1)} collective-permute-done((f32[64,1024]{0,1:T(8,128)}, f32[64,1024]{0,1:T(8,128)S(1)}, u32[]{:S(2)}, u32[]{:S(2)}) %collective-permute-start.16) | collective-permute-done | bytes 262176 | tf_op jit(solution)/shard_map/ppermute | solution.py:16
  175.0 2.2 collective-permute-start.17
  177.2 2.1 add_convert_fusion
  179.2 7.4 %collective-permute-done.17 = f32[64,1024]{0,1:T(8,128)S(1)} collective-permute-done((f32[64,1024]{0,1:T(8,128)S(1)}, f32[64,1024]{0,1:T(8,128)S(1)}, u32[]{:S(2)}, u32[]{:S(2)}) %collective-permute-start.17) | collective-permute-done | bytes 262176 | tf_op jit(solution)/shard_map/ppermute | solution.py:16
  186.7 2.1 collective-permute-start.18
  189.4 8.7 %collective-permute-done.18 = f32[64,1024]{0,1:T(8,128)S(1)} collective-permute-done((f32[64,1024]{0,1:T(8,128)S(1)}, f32[64,1024]{0,1:T(8,128)S(1)}, u32[]{:S(2)}, u32[]{:S(2)}) %collective-permute-start.18) | collective-permute-done | bytes 262176 | tf_op jit(solution)/shard_map/ppermute | solution.py:16
  198.1 1.9 collective-permute-start.19
  200.9 8.6 %collective-permute-done.19 = f32[64,1024]{0,1:T(8,128)S(1)} collective-permute-done((f32[64,1024]{0,1:T(8,128)S(1)}, f32[64,1024]{0,1:T(8,128)S(1)}, u32[]{:S(2)}, u32[]{:S(2)}) %collective-permute-start.19) | collective-permute-done | bytes 262176 | tf_op jit(solution)/shard_map/ppermute | solution.py:16
  209.6 1.9 collective-permute-start.20
  212.7 8.3 %collective-permute-done.20 = f32[64,1024]{0,1:T(8,128)S(1)} collective-permute-done((f32[64,1024]{0,1:T(8,128)S(1)}, f32[64,1024]{0,1:T(8,128)S(1)}, u32[]{:S(2)}, u32[]{:S(2)}) %collective-permute-start.20) | collective-permute-done | bytes 262176 | tf_op jit(solution)/shard_map/ppermute | solution.py:16
  221.1 2.1 collective-permute-start.21
  223.9 1.9 collective-permute-start.15
  225.9 6.7 %collective-permute-done.21 = f32[64,1024]{0,1:T(8,128)S(1)} collective-permute-done((f32[64,1024]{0,1:T(8,128)S(1)}, f32[64,1024]{0,1:T(8,128)S(1)}, u32[]{:S(2)}, u32[]{:S(2)}) %collective-permute-start.21) | collective-permute-done | bytes 262176 | tf_op jit(solution)/shard_map/ppermute | solution.py:16
  233.4 1.9 collective-permute-start.22
  236.1 1.2 copy.61
  237.4 1.3 convert_element_type.86
  238.6 1.7 fusion.20
  240.3 4.8 %collective-permute-done.22 = f32[64,1024]{0,1:T(8,128)} collective-permute-done((f32[64,1024]{0,1:T(8,128)}, f32[64,1024]{0,1:T(8,128)}, u32[]{:S(2)}, u32[]{:S(2)}) %collective-permute-start.22) | collective-permute-done | bytes 262176 | tf_op jit(solution)/shard_map/ppermute | solution.py:16
  245.1 1.2 fusion.21
  (99 shorter events, 21.6 us)
Async XLA Ops:
  0.6 14.1 %copy-start.15 = (s32[1,128]{1,0:T(1,128)S(1)}, s32[1,128]{1,0:T(1,128)}, u32[]{:S(2)}) copy-start(s32[1,128]{1,0:T(1,128)} %param.9) | copy-start | bytes 1540
  1.3 22.7 %collective-permute-start.1 = (bf16[1]{0:T(256)(128)(2,1)}, bf16[1]{0:T(256)(128)(2,1)}, u32[]{:S(2)}, u32[]{:S(2)}) collective-permute-start(bf16[1]{0:T(256)(128)(2,1)} %reshape.245), channel_id=1, source_target_pairs={{0,2},{2,4},{4,6},{6,8},{8,10},{10,12},{12,14},{14,16},{16,18},{18... | collective-permute-start | bytes 14 | tf_op jit(solution)/shard_map/ppermute | solution.py:16
  6.8 8.0 %collective-permute-start.8 = (bf16[64,1024]{0,1:T(8,128)(2,1)S(1)}, bf16[64,1024]{0,1:T(8,128)(2,1)S(1)}, u32[]{:S(2)}, u32[]{:S(2)}) collective-permute-start(bf16[64,1024]{0,1:T(8,128)(2,1)S(1)} %bitcast.180), channel_id=1, source_target_pairs={{0,2},{2,4},{4,6},{6,8},{8,10},{10,12},{12,14},{14,16},{16,18},{18... | collective-permute-start | bytes 393224 | tf_op jit(solution)/shard_map/ppermute | solution.py:16
  9.9 76.2 %collective-permute-start = (bf16[64,1024]{1,0:T(8,128)(2,1)S(1)}, bf16[64,1024]{1,0:T(8,128)(2,1)}, u32[]{:S(2)}, u32[]{:S(2)}) collective-permute-start(bf16[64,1024]{1,0:T(8,128)(2,1)S(1)} %slice_bitcast_fusion), channel_id=1, source_target_pairs={{0,2},{2,4},{4,6},{6,8},{8,10},{10,12},{12,14},{14,16},{16,18},{18... | collective-permute-start | bytes 393224 | tf_op jit(solution)/shard_map/ppermute | solution.py:16
  13.2 6.0 %copy-start.3 = (bf16[1,128,4096]{2,1,0:T(8,128)(2,1)S(1)}, bf16[1,128,4096]{2,1,0:T(8,128)(2,1)}, u32[]{:S(2)}) copy-start(bf16[1,128,4096]{2,1,0:T(8,128)(2,1)} %param.7) | copy-start | bytes 3145732
  15.6 45.7 %collective-permute-start.9 = (bf16[64,1024]{0,1:T(8,128)(2,1)}, bf16[64,1024]{0,1:T(8,128)(2,1)}, u32[]{:S(2)}, u32[]{:S(2)}) collective-permute-start(bf16[64,1024]{0,1:T(8,128)(2,1)} %broadcast_select_fusion.5), channel_id=1, source_target_pairs={{0,2},{2,4},{4,6},{6,8},{8,10},{10,12},{12,14},{14,16},{16,18},{18... | collective-permute-start | bytes 393224 | tf_op jit(solution)/shard_map/ppermute | solution.py:16
  24.0 136.1 %copy-start = (f32[4,1024,128]{1,2,0:T(8,128)}, f32[4,1024,128]{1,2,0:T(8,128)S(1)}, u32[]{:S(2)}) copy-start(f32[4,1024,128]{1,2,0:T(8,128)S(1)} %reshape.255) | copy-start | bytes 6291460
  24.0 62.1 %copy-start.6 = (bf16[1,128,1024]{2,1,0:T(8,128)(2,1)S(1)}, bf16[1,128,1024]{2,1,0:T(8,128)(2,1)}, u32[]{:S(2)}) copy-start(bf16[1,128,1024]{2,1,0:T(8,128)(2,1)} %param.8) | copy-start | bytes 786436
  24.7 3.5 %collective-permute-start.2 = (bf16[1]{0:T(256)(128)(2,1)}, bf16[1]{0:T(256)(128)(2,1)}, u32[]{:S(2)}, u32[]{:S(2)}) collective-permute-start(bf16[1]{0:T(256)(128)(2,1)} %select_n.80), channel_id=1, source_target_pairs={{0,2},{2,4},{4,6},{6,8},{8,10},{10,12},{12,14},{14,16},{16,18},{18... | collective-permute-start | bytes 14 | tf_op jit(solution)/shard_map/ppermute | solution.py:16
  28.8 5.9 %collective-permute-start.3 = (bf16[1]{0:T(256)(128)(2,1)}, bf16[1]{0:T(256)(128)(2,1)}, u32[]{:S(2)}, u32[]{:S(2)}) collective-permute-start(bf16[1]{0:T(256)(128)(2,1)} %select_n.81), channel_id=1, source_target_pairs={{0,2},{2,4},{4,6},{6,8},{8,10},{10,12},{12,14},{14,16},{16,18},{18... | collective-permute-start | bytes 14 | tf_op jit(solution)/shard_map/ppermute | solution.py:16
  35.3 5.9 %collective-permute-start.4 = (bf16[1]{0:T(256)(128)(2,1)}, bf16[1]{0:T(256)(128)(2,1)}, u32[]{:S(2)}, u32[]{:S(2)}) collective-permute-start(bf16[1]{0:T(256)(128)(2,1)} %select_n.82), channel_id=1, source_target_pairs={{0,2},{2,4},{4,6},{6,8},{8,10},{10,12},{12,14},{14,16},{16,18},{18... | collective-permute-start | bytes 14 | tf_op jit(solution)/shard_map/ppermute | solution.py:16
  41.8 5.9 %collective-permute-start.5 = (bf16[1]{0:T(256)(128)(2,1)}, bf16[1]{0:T(256)(128)(2,1)}, u32[]{:S(2)}, u32[]{:S(2)}) collective-permute-start(bf16[1]{0:T(256)(128)(2,1)} %select_n.83), channel_id=1, source_target_pairs={{0,2},{2,4},{4,6},{6,8},{8,10},{10,12},{12,14},{14,16},{16,18},{18... | collective-permute-start | bytes 14 | tf_op jit(solution)/shard_map/ppermute | solution.py:16
  48.3 5.9 %collective-permute-start.6 = (bf16[1]{0:T(256)(128)(2,1)}, bf16[1]{0:T(256)(128)(2,1)}, u32[]{:S(2)}, u32[]{:S(2)}) collective-permute-start(bf16[1]{0:T(256)(128)(2,1)} %select_n.84), channel_id=1, source_target_pairs={{0,2},{2,4},{4,6},{6,8},{8,10},{10,12},{12,14},{14,16},{16,18},{18... | collective-permute-start | bytes 14 | tf_op jit(solution)/shard_map/ppermute | solution.py:16
  54.8 5.9 %collective-permute-start.7 = (bf16[1]{0:T(256)(128)(2,1)}, bf16[1]{0:T(256)(128)(2,1)}, u32[]{:S(2)}, u32[]{:S(2)}) collective-permute-start(bf16[1]{0:T(256)(128)(2,1)} %select_n.85), channel_id=1, source_target_pairs={{0,2},{2,4},{4,6},{6,8},{8,10},{10,12},{12,14},{14,16},{16,18},{18... | collective-permute-start | bytes 14 | tf_op jit(solution)/shard_map/ppermute | solution.py:16
  62.3 8.5 %collective-permute-start.10 = (bf16[64,1024]{0,1:T(8,128)(2,1)S(1)}, bf16[64,1024]{0,1:T(8,128)(2,1)S(1)}, u32[]{:S(2)}, u32[]{:S(2)}) collective-permute-start(bf16[64,1024]{0,1:T(8,128)(2,1)S(1)} %broadcast_select_fusion.4), channel_id=1, source_target_pairs={{0,2},{2,4},{4,6},{6,8},{8,10},{10,12},{12,14},{14,16},{16,18},{18... | collective-permute-start | bytes 393224 | tf_op jit(solution)/shard_map/ppermute | solution.py:16
  70.8 8.6 %collective-permute-start.11 = (bf16[64,1024]{0,1:T(8,128)(2,1)S(1)}, bf16[64,1024]{0,1:T(8,128)(2,1)S(1)}, u32[]{:S(2)}, u32[]{:S(2)}) collective-permute-start(bf16[64,1024]{0,1:T(8,128)(2,1)S(1)} %broadcast_select_fusion.3), channel_id=1, source_target_pairs={{0,2},{2,4},{4,6},{6,8},{8,10},{10,12},{12,14},{14,16},{16,18},{18... | collective-permute-start | bytes 393224 | tf_op jit(solution)/shard_map/ppermute | solution.py:16
  79.4 8.6 %collective-permute-start.12 = (bf16[64,1024]{0,1:T(8,128)(2,1)S(1)}, bf16[64,1024]{0,1:T(8,128)(2,1)S(1)}, u32[]{:S(2)}, u32[]{:S(2)}) collective-permute-start(bf16[64,1024]{0,1:T(8,128)(2,1)S(1)} %broadcast_select_fusion.2), channel_id=1, source_target_pairs={{0,2},{2,4},{4,6},{6,8},{8,10},{10,12},{12,14},{14,16},{16,18},{18... | collective-permute-start | bytes 393224 | tf_op jit(solution)/shard_map/ppermute | solution.py:16
  88.8 9.2 %collective-permute-start.13 = (bf16[64,1024]{0,1:T(8,128)(2,1)}, bf16[64,1024]{0,1:T(8,128)(2,1)}, u32[]{:S(2)}, u32[]{:S(2)}) collective-permute-start(bf16[64,1024]{0,1:T(8,128)(2,1)} %broadcast_select_fusion.1), channel_id=1, source_target_pairs={{0,2},{2,4},{4,6},{6,8},{8,10},{10,12},{12,14},{14,16},{16,18},{18... | collective-permute-start | bytes 393224 | tf_op jit(solution)/shard_map/ppermute | solution.py:16
  99.0 8.8 %collective-permute-start.14 = (bf16[64,1024]{0,1:T(8,128)(2,1)S(1)}, bf16[64,1024]{0,1:T(8,128)(2,1)S(1)}, u32[]{:S(2)}, u32[]{:S(2)}) collective-permute-start(bf16[64,1024]{0,1:T(8,128)(2,1)S(1)} %broadcast_select_fusion), channel_id=1, source_target_pairs={{0,2},{2,4},{4,6},{6,8},{8,10},{10,12},{12,14},{14,16},{16,18},{18... | collective-permute-start | bytes 393224 | tf_op jit(solution)/shard_map/ppermute | solution.py:16
  109.6 3.5 %copy-start.7 = (bf16[128,512]{0,1:T(8,128)(2,1)S(1)}, bf16[128,512]{0,1:T(8,128)(2,1)}, u32[]{:S(2)}) copy-start(bf16[128,512]{0,1:T(8,128)(2,1)} %get-tuple-element.15) | copy-start | bytes 393220
  109.6 3.5 %copy-start.13 = (f32[1024]{0:T(1024)S(1)}, f32[1024]{0:T(1024)}, u32[]{:S(2)}) copy-start(f32[1024]{0:T(1024)} %broadcast_bitcast_fusion.1) | copy-start | bytes 12292
  113.1 2.1 copy-start.10
  113.2 42.6 %copy-start.16 = (f32[32]{0:T(128)S(1)}, f32[32]{0:T(128)}, u32[]{:S(2)}) copy-start(f32[32]{0:T(128)} %param.12) | copy-start | bytes 388
  157.8 2.3 copy-start.2
  157.8 2.3 copy-start.9
  157.8 2.3 copy-start.11
  157.8 2.3 copy-start.12
  157.8 2.3 copy-start.14
  160.7 1.2 copy-start.4
  163.3 11.6 %collective-permute-start.16 = (f32[64,1024]{0,1:T(8,128)}, f32[64,1024]{0,1:T(8,128)S(1)}, u32[]{:S(2)}, u32[]{:S(2)}) collective-permute-start(f32[64,1024]{0,1:T(8,128)} %pad_maximum_fusion), channel_id=1, source_target_pairs={{2,0},{4,2},{6,4},{8,6},{10,8},{12,10},{14,12},{16,14},{18,16},{20... | collective-permute-start | bytes 786440 | tf_op jit(solution)/shard_map/ppermute | solution.py:16
  174.9 13.9 %copy-start.1 = (f32[4,1024,192]{1,2,0:T(8,128)S(1)}, f32[4,1024,192]{1,2,0:T(8,128)}, u32[]{:S(2)}) copy-start(f32[4,1024,192]{1,2,0:T(8,128)} %get-tuple-element.21) | copy-start | bytes 9437188
  174.9 13.9 %copy-start.8 = (bf16[24,4,8,128]{3,2,1,0:T(8,128)(2,1)S(1)}, bf16[24,4,8,128]{3,2,1,0:T(8,128)(2,1)}, u32[]{:S(2)}) copy-start(bf16[24,4,8,128]{3,2,1,0:T(8,128)(2,1)} %get-tuple-element.17) | copy-start | bytes 589828
  175.0 11.7 %collective-permute-start.17 = (f32[64,1024]{0,1:T(8,128)S(1)}, f32[64,1024]{0,1:T(8,128)S(1)}, u32[]{:S(2)}, u32[]{:S(2)}) collective-permute-start(f32[64,1024]{0,1:T(8,128)S(1)} %multiply_add_fusion.5), channel_id=1, source_target_pairs={{2,0},{4,2},{6,4},{8,6},{10,8},{12,10},{14,12},{16,14},{18,16},{20... | collective-permute-start | bytes 786440 | tf_op jit(solution)/shard_map/ppermute | solution.py:16
  186.7 11.4 %collective-permute-start.18 = (f32[64,1024]{0,1:T(8,128)S(1)}, f32[64,1024]{0,1:T(8,128)S(1)}, u32[]{:S(2)}, u32[]{:S(2)}) collective-permute-start(f32[64,1024]{0,1:T(8,128)S(1)} %multiply_add_fusion.4), channel_id=1, source_target_pairs={{2,0},{4,2},{6,4},{8,6},{10,8},{12,10},{14,12},{16,14},{18,16},{20... | collective-permute-start | bytes 786440 | tf_op jit(solution)/shard_map/ppermute | solution.py:16
  198.1 11.4 %collective-permute-start.19 = (f32[64,1024]{0,1:T(8,128)S(1)}, f32[64,1024]{0,1:T(8,128)S(1)}, u32[]{:S(2)}, u32[]{:S(2)}) collective-permute-start(f32[64,1024]{0,1:T(8,128)S(1)} %multiply_add_fusion.3), channel_id=1, source_target_pairs={{2,0},{4,2},{6,4},{8,6},{10,8},{12,10},{14,12},{16,14},{18,16},{20... | collective-permute-start | bytes 786440 | tf_op jit(solution)/shard_map/ppermute | solution.py:16
  209.6 11.4 %collective-permute-start.20 = (f32[64,1024]{0,1:T(8,128)S(1)}, f32[64,1024]{0,1:T(8,128)S(1)}, u32[]{:S(2)}, u32[]{:S(2)}) collective-permute-start(f32[64,1024]{0,1:T(8,128)S(1)} %multiply_add_fusion.2), channel_id=1, source_target_pairs={{2,0},{4,2},{6,4},{8,6},{10,8},{12,10},{14,12},{16,14},{18,16},{20... | collective-permute-start | bytes 786440 | tf_op jit(solution)/shard_map/ppermute | solution.py:16
  221.1 14.3 %copy-start.5 = (bf16[24,4,8,128]{3,2,1,0:T(8,128)(2,1)S(1)}, bf16[24,4,8,128]{3,2,1,0:T(8,128)(2,1)}, u32[]{:S(2)}) copy-start(bf16[24,4,8,128]{3,2,1,0:T(8,128)(2,1)} %get-tuple-element.16) | copy-start | bytes 589828
  221.1 11.5 %collective-permute-start.21 = (f32[64,1024]{0,1:T(8,128)S(1)}, f32[64,1024]{0,1:T(8,128)S(1)}, u32[]{:S(2)}, u32[]{:S(2)}) collective-permute-start(f32[64,1024]{0,1:T(8,128)S(1)} %multiply_add_fusion.1), channel_id=1, source_target_pairs={{2,0},{4,2},{6,4},{8,6},{10,8},{12,10},{14,12},{16,14},{18,16},{20... | collective-permute-start | bytes 786440 | tf_op jit(solution)/shard_map/ppermute | solution.py:16
  223.9 14.7 %collective-permute-start.15 = (f32[64,1024]{1,0:T(8,128)}, f32[64,1024]{1,0:T(8,128)}, u32[]{:S(2)}, u32[]{:S(2)}) collective-permute-start(f32[64,1024]{1,0:T(8,128)} %slice.45), channel_id=1, source_target_pairs={{2,0},{4,2},{6,4},{8,6},{10,8},{12,10},{14,12},{16,14},{18,16},{20... | collective-permute-start | bytes 786440 | tf_op jit(solution)/shard_map/ppermute | solution.py:16
  233.4 11.7 %collective-permute-start.22 = (f32[64,1024]{0,1:T(8,128)}, f32[64,1024]{0,1:T(8,128)}, u32[]{:S(2)}, u32[]{:S(2)}) collective-permute-start(f32[64,1024]{0,1:T(8,128)} %multiply_add_fusion), channel_id=1, source_target_pairs={{2,0},{4,2},{6,4},{8,6},{10,8},{12,10},{14,12},{16,14},{18,16},{20... | collective-permute-start | bytes 786440 | tf_op jit(solution)/shard_map/ppermute | solution.py:16
where the time goes:
time: 248 us; the launch traced here: 247 us
  starting transfers between devices  88.6 us (36%)
  waiting for transfers between devices  59.5 us (24%)
  blocking collectives  40.3 us (16%)
  matrix products  21 us (8%)
  local copies, waits for them, and re-layouts  16.7 us (7%)
  other arithmetic  14.6 us (6%)
  between operations  6.4 us (3%)
    ppermute x23, starting transfers between devices, from_behind(): return lax.ppermute(shard, axis, pairs)  88.6 us
    ppermute x23, waiting for transfers between devices, from_behind(): return lax.ppermute(shard, axis, pairs)  59.5 us
    psum x1, blocking collectives, on_device(): gate_total = lax.psum(gate_part, ('seq', 'dp'))  40.3 us
    sub x2, matrix products, masked_softmax(): powers = jnp.exp(scores - row_top)  7.44 us
    dot_general x2, matrix products, attend(): jnp.einsum('gqk,gkd->gqd', narrow_weights, value_part, preferred_element_...  5.87 us
    unnamed x44, local copies, waits for them, and re-layouts  5.69 us
  transfers between devices with their start and end apart: 23, of which 10 were waited for; matrix products, arithmetic and copies ran while one was open for 13% of the time, Pallas kernels for 0%

commit v1 on v0

v1 whole, which is shorter than its diff:
```python
import functools
import math

import jax
import jax.numpy as jnp
from jax import lax
from jax.experimental import pallas as pl
from jax.experimental.pallas import tpu as pltpu
from jax.sharding import PartitionSpec as P

HEAD_DIM = 128
WINDOW = 64
GAP = 4
LANES = 128
SCALE = 1.0 / math.sqrt(HEAD_DIM)

VMEM = pl.BlockSpec(memory_space=pltpu.VMEM)
SMEM = pl.BlockSpec(memory_space=pltpu.SMEM)
PARAMS = pltpu.CompilerParams(vmem_limit_bytes=40 * 1024 * 1024)

NN = (((1,), (0,)), ((), ()))
NT = (((1,), (1,)), ((), ()))
TN = (((0,), (0,)), ((), ()))


def dot(a, b, dims):
    return lax.dot_general(a, b, dims, preferred_element_type=jnp.float32)


def stack(ref, first, rows, group, repeat):
    return jnp.concatenate(
        [
            ref[first : first + rows, (group * repeat + h) * HEAD_DIM : (group * repeat + h + 1) * HEAD_DIM]
            for h in range(repeat)
        ],
        axis=0,
    )


def part(ref, index):
    return ref[:, index * HEAD_DIM : (index + 1) * HEAD_DIM]


def softmax_rows(scores):
    top = jnp.max(scores, axis=0, keepdims=True)
    powers = jnp.exp(scores - top)
    return powers * (1.0 / jnp.sum(powers, axis=0, keepdims=True))


def self_mask(segment_ref, block, base):
    segment = segment_ref[0:1, block * WINDOW : (block + 1) * WINDOW]
    segment = jnp.concatenate([segment] * (LANES // WINDOW), axis=1)
    shape = (2 * WINDOW, LANES)
    key = lax.broadcasted_iota(jnp.int32, shape, 0)
    query = lax.broadcasted_iota(jnp.int32, shape, 1) % WINDOW
    key_pos = key + (base + (block - 1) * WINDOW)
    return (key >= query) & (key <= query + WINDOW) & (key_pos >= segment)


def self_weights(query_rows, keys, allowed):
    scores = dot(keys, query_rows, NT) * SCALE
    allowed = jnp.concatenate([allowed] * (scores.shape[1] // LANES), axis=1)
    return softmax_rows(jnp.where(allowed, scores, -1e30))


def joined(context_ref, halo_ref, block, index):
    own = context_ref[:, index * HEAD_DIM : (index + 1) * HEAD_DIM]
    if block == 0:
        return jnp.concatenate([part(halo_ref, index), own[:WINDOW]], axis=0)
    return own[(block - 1) * WINDOW : (block + 1) * WINDOW]


def chip_kernel(own_off, pair_off, own_ref, pair_ref, out_ref, *, tok_rows):
    is_owner = own_off[0, 0] < tok_rows
    has = is_owner | (pair_off[0, 0] < tok_rows)
    width = own_ref.shape[1]

    @pl.when(is_owner)
    def _():
        out_ref[:, :width] = own_ref[...]

    @pl.when(jnp.logical_not(is_owner))
    def _():
        out_ref[:, :width] = pair_ref[...]

    flag = jnp.where(has, 1.0, 0.0).astype(jnp.float32)
    out_ref[:, width:] = jnp.full((own_ref.shape[0], LANES), flag, jnp.float32).astype(jnp.bfloat16)


def self_kernel(query_ref, context_ref, halo_ref, segment_ref, out_ref, *, groups, repeat):
    tok_rows = query_ref.shape[0]
    base = lax.axis_index("seq") * tok_rows
    half = repeat * WINDOW
    for block in range(tok_rows // WINDOW):
        allowed = self_mask(segment_ref, block, base)
        for g in range(groups):
            rows = stack(query_ref, block * WINDOW, WINDOW, g, repeat)
            weights = self_weights(rows, joined(context_ref, halo_ref, block, g), allowed)
            values = joined(context_ref, halo_ref, block, groups + g)
            mixed = dot(values, weights.astype(jnp.bfloat16), TN)
            out_ref[g, :, block * half : (block + 1) * half] = mixed.astype(jnp.bfloat16)


def cross_kernel(
    own_off, pair_off, gate_ref, self_ref, grad_ref, own_ref, pair_ref, x_ref, z_ref, d_ref,
    grad_self_ref, to_pair_ref, to_x_ref, to_z_ref, to_d_ref, own_terms_ref, gate_out_ref, prev, *, groups, repeat
):
    tok_rows, width = grad_ref.shape[0], own_ref.shape[1]
    img = own_ref.shape[0]
    shard = lax.axis_index("seq")
    in_chip, in_block = shard % 2, shard % GAP
    off = own_off[0, 0]
    is_owner = off < tok_rows
    pair_owner = pair_off[0, 0] < tok_rows
    chip_owner = is_owner | pair_owner
    z_owner = jnp.max(z_ref[0:16, width:].astype(jnp.float32)) > 0.5
    from_pair = (in_chip == 1) & pair_owner
    from_x = (in_block >= 2) & jnp.logical_not(chip_owner)
    before = jnp.logical_not(from_pair | from_x) & (shard >= GAP)
    from_z = before & z_owner
    from_d = before & jnp.logical_not(z_owner)
    has_prev = from_pair | from_x | before

    @pl.when(from_pair)
    def _():
        prev[...] = pair_ref[...]

    @pl.when(from_x)
    def _():
        prev[...] = x_ref[:, :width]

    @pl.when(from_z)
    def _():
        prev[...] = z_ref[:, :width]

    @pl.when(jnp.logical_not(from_pair | from_x | from_z))
    def _():
        prev[...] = d_ref[:, :width]

    half = repeat * WINDOW
    rows = tok_rows * repeat
    lane = lax.broadcasted_iota(jnp.int32, (1, rows), 1)
    lane_tok = (lane // half) * WINDOW + lane % WINDOW
    own_from = jnp.where(is_owner, off, tok_rows)
    has_from = jnp.where(has_prev, 0, own_from)
    use_own = lane_tok >= own_from
    has_lane = lane_tok >= has_from
    row_tok = lax.broadcasted_iota(jnp.int32, (WINDOW, HEAD_DIM), 0)

    carried_key, carried_value = [], []
    for g in range(groups):
        keys = jnp.concatenate([part(prev, g), part(own_ref, g)], axis=0)
        values = jnp.concatenate([part(prev, groups + g), part(own_ref, groups + g)], axis=0)
        out_t = self_ref[g]
        scores = dot(keys, out_t, NN)
        weights = softmax_rows(jnp.where(use_own, scores[img:], scores[:img]) * SCALE)
        narrow = weights.astype(jnp.bfloat16)
        grad_rows, cross_rows = [], []
        for block in range(tok_rows // WINDOW):
            has_rows = row_tok + block * WINDOW >= has_from
            for h in range(repeat):
                head = g * repeat + h
                tile = grad_ref[
                    block * WINDOW : (block + 1) * WINDOW, head * HEAD_DIM : (head + 1) * HEAD_DIM
                ]
                grad_rows.append(tile)
                factor = jnp.where(has_rows, gate_ref[head], 0.0)
                cross_rows.append((tile.astype(jnp.float32) * factor).astype(jnp.bfloat16))
        grad_rows = jnp.concatenate(grad_rows, axis=0)
        cross_rows = jnp.concatenate(cross_rows, axis=0)
        plain = dot(values, grad_rows, NT)
        plain = jnp.where(use_own, plain[img:], plain[:img])
        gate_row = jnp.sum(narrow.astype(jnp.float32) * plain, axis=0, keepdims=True)
        gate_row = jnp.where(has_lane, gate_row, 0.0)
        gate_out_ref[g : g + 1, :] = gate_row[:, :half] + gate_row[:, half:]
        grad_weights = dot(values, cross_rows, NT)
        grad_weights = jnp.where(use_own, grad_weights[img:], grad_weights[:img])
        delta = jnp.sum(weights * grad_weights, axis=0, keepdims=True)
        grad_scores = weights * (grad_weights - delta)
        scores_j = jnp.concatenate(
            [jnp.where(use_own, 0.0, grad_scores), jnp.where(use_own, grad_scores, 0.0)], axis=0
        ).astype(jnp.bfloat16)
        narrow_j = jnp.concatenate(
            [jnp.where(use_own, 0.0, weights), jnp.where(use_own, weights, 0.0)], axis=0
        ).astype(jnp.bfloat16)
        grad_key = dot(scores_j, out_t, NT) * SCALE
        grad_value = dot(narrow_j, cross_rows, NN)
        grad_query = dot(scores_j, keys, TN) * SCALE
        grad_self_ref[g] = (grad_rows.astype(jnp.float32) + grad_query).astype(jnp.bfloat16)
        own_terms_ref[:, g * HEAD_DIM : (g + 1) * HEAD_DIM] = grad_key[img:]
        own_terms_ref[:, (groups + g) * HEAD_DIM : (groups + g + 1) * HEAD_DIM] = grad_value[img:]
        carried_key.append(grad_key[:img])
        carried_value.append(grad_value[:img])
    carried = jnp.concatenate(carried_key + carried_value, axis=1)
    for ref, here in ((to_pair_ref, from_pair), (to_x_ref, from_x), (to_z_ref, from_z), (to_d_ref, from_d)):
        ref[...] = (carried * jnp.where(here, 1.0, 0.0)).astype(ref.dtype)


def self_back_block(query_ref, context_ref, halo_ref, segment_ref, grad_ref, block, base, groups, repeat, put):
    half = repeat * WINDOW
    allowed = self_mask(segment_ref, block, base)
    for g in range(groups):
        rows = stack(query_ref, block * WINDOW, WINDOW, g, repeat)
        keys = joined(context_ref, halo_ref, block, g)
        values = joined(context_ref, halo_ref, block, groups + g)
        weights = self_weights(rows, keys, allowed)
        grads = grad_ref[g, block * half : (block + 1) * half, :]
        grad_weights = dot(values, grads, NT)
        delta = jnp.sum(weights * grad_weights, axis=0, keepdims=True)
        grad_scores = (weights * (grad_weights - delta)).astype(jnp.bfloat16)
        grad_query = (dot(grad_scores, keys, TN) * SCALE).astype(jnp.bfloat16)
        grad_key = dot(grad_scores, rows, NN) * SCALE
        grad_value = dot(weights.astype(jnp.bfloat16), grads, NN)
        put(g, grad_query, grad_key, grad_value)


def self_back_kernel(
    query_ref, context_ref, halo_ref, segment_ref, grad_ref, query_grad_ref, halo_out_ref, terms_ref, *, groups, repeat
):
    tok_rows = query_ref.shape[0]
    base = lax.axis_index("seq") * tok_rows
    blocks = tok_rows // WINDOW

    for block in range(blocks):

        def put(g, grad_query, grad_key, grad_value):
            for h in range(repeat):
                head = g * repeat + h
                query_grad_ref[
                    block * WINDOW : (block + 1) * WINDOW, head * HEAD_DIM : (head + 1) * HEAD_DIM
                ] = grad_query[h * WINDOW : (h + 1) * WINDOW]
            for index, grad in ((g, grad_key), (groups + g, grad_value)):
                cols = slice(index * HEAD_DIM, (index + 1) * HEAD_DIM)
                if block == 0:
                    halo_out_ref[:, cols] = grad[:WINDOW].astype(halo_out_ref.dtype)
                else:
                    before = slice((block - 1) * WINDOW, block * WINDOW)
                    terms_ref[before, cols] = terms_ref[before, cols] + grad[:WINDOW]
                terms_ref[block * WINDOW : (block + 1) * WINDOW, cols] = grad[WINDOW:]

        self_back_block(
            query_ref, context_ref, halo_ref, segment_ref, grad_ref, block, base, groups, repeat, put
        )


def chip_sum_kernel(to_pair_ref, x_ref, z_ref, d_ref, out_ref):
    f32 = jnp.float32
    out_ref[...] = (
        to_pair_ref[...].astype(f32) + x_ref[...].astype(f32) + z_ref[...].astype(f32) + d_ref[...].astype(f32)
    )


def finish_kernel(own_off, own_ref, mine_ref, pair_ref, terms_ref, halo_ref, memory_ref, context_ref, *, tok_rows):
    keep = jnp.where(own_off[0, 0] < tok_rows, 1.0, 0.0)
    memory_ref[...] = ((own_ref[...] + mine_ref[...] + pair_ref[...]) * keep).astype(memory_ref.dtype)
    size = lax.axis_size("seq")
    more = jnp.where(lax.axis_index("seq") < size - 1, 1.0, 0.0)
    first = tok_rows - WINDOW
    context_ref[:first] = terms_ref[:first].astype(context_ref.dtype)
    context_ref[first:] = (terms_ref[first:] + halo_ref[...].astype(jnp.float32) * more).astype(context_ref.dtype)


def struct(shape, dtype):
    return jax.ShapeDtypeStruct(shape, dtype)


def total(values, seq, dp):
    if seq % 16 or seq & (seq - 1) or dp != 2:
        return lax.psum(values, ("seq", "dp"))

    def swapped(value, seq_bits, dp_bits):
        pairs = [
            (s * dp + d, (s ^ seq_bits) * dp + (d ^ dp_bits)) for s in range(seq) for d in range(dp)
        ]
        return lax.ppermute(value, ("seq", "dp"), pairs)

    values = values + swapped(values, 1, 0)
    values = values + swapped(values, 2, 0) + swapped(values, 4, 0) + swapped(values, 6, 0)
    step = 8
    values = values + swapped(values, step, 0) + swapped(values, 0, 1) + swapped(values, step, 1)
    step = 16
    while step < seq:
        values = values + swapped(values, step, 0)
        step *= 2
    return values


def on_device(queries, context, segment_start, memory, image_offset, cross_gate, out_grad):
    tok_rows, model = queries.shape[1:]
    width = context.shape[2]
    groups = width // 2 // HEAD_DIM
    heads = cross_gate.shape[0]
    repeat = heads // groups
    img = memory.shape[2]
    seq, dp = lax.axis_size("seq"), lax.axis_size("dp")
    f32, bf16 = jnp.float32, jnp.bfloat16

    def send(value, where):
        return lax.ppermute(value, "seq", [(i, where(i)) for i in range(seq)])

    q, ctx, grad, own = queries[0], context[0], out_grad[0], memory[0, 0]
    pair_off = send(image_offset, lambda i: i ^ 1)
    pair = send(own, lambda i: i ^ 1)
    halo = send(ctx[tok_rows - WINDOW :], lambda i: (i + 1) % seq)
    gate_tanh = jnp.tanh(cross_gate)

    chip = pl.pallas_call(
        functools.partial(chip_kernel, tok_rows=tok_rows),
        out_shape=struct((img, width + LANES), bf16),
        in_specs=[SMEM, SMEM, VMEM, VMEM],
        out_specs=VMEM,
        compiler_params=PARAMS,
        name="chip_image",
    )(image_offset, pair_off, own, pair)
    by_x = send(chip, lambda i: i ^ 2)
    by_z = send(chip, lambda i: (i + GAP) % seq)
    by_d = send(chip, lambda i: ((i ^ 2) + GAP) % seq)

    self_out = pl.pallas_call(
        functools.partial(self_kernel, groups=groups, repeat=repeat),
        out_shape=struct((groups, HEAD_DIM, repeat * tok_rows), bf16),
        in_specs=[VMEM] * 4,
        out_specs=VMEM,
        compiler_params=PARAMS,
        cost_estimate=pl.CostEstimate(flops=2 * 10**9, bytes_accessed=3 * 10**6, transcendentals=10**6),
        name="self_forward",
    )(q, ctx, halo, segment_start)

    grad_self, to_pair, to_x, to_z, to_d, own_terms, gate_part = pl.pallas_call(
        functools.partial(cross_kernel, groups=groups, repeat=repeat),
        out_shape=[struct((groups, repeat * tok_rows, HEAD_DIM), bf16)]
        + [struct((img, width), bf16)] * 4
        + [struct((img, width), f32), struct((groups, repeat * WINDOW), f32)],
        in_specs=[SMEM] * 3 + [VMEM] * 7,
        out_specs=[VMEM] * 7,
        scratch_shapes=[pltpu.VMEM((img, width), bf16)],
        compiler_params=PARAMS,
        cost_estimate=pl.CostEstimate(flops=4 * 10**9, bytes_accessed=5 * 10**6, transcendentals=10**6),
        name="cross",
    )(image_offset, pair_off, gate_tanh, self_out, grad, own, pair, by_x, by_z, by_d)
    back_x = send(to_x, lambda i: i ^ 2)
    back_z = send(to_z, lambda i: (i - GAP) % seq)
    back_d = send(to_d, lambda i: (i - GAP) % seq ^ 2)
    gate_sum = total(gate_part, seq, dp)
    gate_sum = jnp.sum(gate_sum.reshape(heads, WINDOW), axis=1)
    gate_grad = (1.0 - gate_tanh * gate_tanh) * gate_sum

    query_grad, halo_terms, terms = pl.pallas_call(
        functools.partial(self_back_kernel, groups=groups, repeat=repeat),
        out_shape=[struct((tok_rows, model), bf16), struct((WINDOW, width), bf16), struct((tok_rows, width), f32)],
        in_specs=[VMEM] * 5,
        out_specs=[VMEM] * 3,
        compiler_params=PARAMS,
        cost_estimate=pl.CostEstimate(flops=4 * 10**9, bytes_accessed=5 * 10**6, transcendentals=10**6),
        name="self_backward",
    )(q, ctx, halo, segment_start, grad_self)
    halo_back = send(halo_terms, lambda i: (i - 1) % seq)

    mine = pl.pallas_call(
        chip_sum_kernel,
        out_shape=struct((img, width), f32),
        in_specs=[VMEM] * 4,
        out_specs=VMEM,
        compiler_params=PARAMS,
        name="chip_sum",
    )(to_pair, back_x, back_z, back_d)
    other = send(mine, lambda i: i ^ 1)
    memory_grad, context_grad = pl.pallas_call(
        functools.partial(finish_kernel, tok_rows=tok_rows),
        out_shape=[struct((img, width), bf16), struct((tok_rows, width), bf16)],
        in_specs=[SMEM] + [VMEM] * 5,
        out_specs=[VMEM] * 2,
        compiler_params=PARAMS,
        name="finish",
    )(image_offset, own_terms, mine, other, terms, halo_back)
    return (query_grad[None], context_grad[None], memory_grad[None, None], gate_grad)


def solution(mesh):
    placed = (
        P("dp", "seq", None),
        P("dp", "seq", None),
        P("dp", "seq"),
        P("dp", "seq", None, None),
        P("dp", "seq"),
        P(),
        P("dp", "seq", None),
    )
    return jax.shard_map(
        on_device,
        mesh=mesh,
        in_specs=placed,
        out_specs=(P("dp", "seq", None), P("dp", "seq", None), P("dp", "seq", None, None), P()),
        check_vma=False,
    )
```

time: 248 us -> 44.4 us (0.18)
  the two profiles are of different devices: /device:TPU:3 before, /device:TPU:1 now
where the time goes in v1:
time: 44.4 us; the launch traced here: 44.2 us
  starting transfers between devices  19.3 us (43%)
  Pallas kernels  12.2 us (27%)
  waiting for transfers between devices  7.64 us (17%)
  local copies, waits for them, and re-layouts  2.91 us (7%)
  between operations  1.41 us (3%)
  other arithmetic  0.66 us (1%)
    ppermute x11, starting transfers between devices, send(): return lax.ppermute(value, 'seq', [(i, where(i)) for i in range(seq)])  12.4 us
    ppermute x7, starting transfers between devices, swapped(): return lax.ppermute(value, ('seq', 'dp'), pairs)  6.96 us
    ppermute x11, waiting for transfers between devices, send(): return lax.ppermute(value, 'seq', [(i, where(i)) for i in range(seq)])  6.8 us
    pallas_call x1, Pallas kernels, on_device(): pl.pallas_call(functools.partial(self_back_kernel, groups=groups, repeat=...  4.27 us
    pallas_call x1, Pallas kernels, on_device(): pl.pallas_call(functools.partial(cross_kernel, groups=groups, repeat=repe...  3.89 us
    pallas_call x1, Pallas kernels, on_device(): pl.pallas_call(functools.partial(self_kernel, groups=groups, repeat=repea...  2.47 us
    unnamed x14, local copies, waits for them, and re-layouts  1.9 us
    slice x1, local copies, waits for them, and re-layouts, on_device(): halo = send(ctx[tok_rows - WINDOW:], lambda i: (i + 1) % seq)  0.93 us
  transfers between devices with their start and end apart: 18, of which 5 were waited for; matrix products, arithmetic and copies ran while one was open for 4% of the time, Pallas kernels for 17%

profile of v1, /device:TPU:1, one launch (start us, length us, event | category | flops | bytes accessed | tf_op | source)
XLA Modules:
  0.0 44.2 jit_solution(5265256113524071131)
XLA Ops:
  0.6 0.1 collective-permute-start.2
  0.8 0.9 %slice_bitcast_fusion = bf16[64,1024]{1,0:T(8,128)(2,1)S(1)} fusion(bf16[1,128,1024]{2,1,0:T(8,128)(2,1)} %param.8), kind=kLoop, calls=%fused_computation | loop fusion | bytes 262144 | tf_op jit(solution)/shard_map/slice | solution.py:304
  1.7 0.0 copy-start.1
  1.7 2.6 %collective-permute-start = (bf16[64,1024]{1,0:T(8,128)(2,1)S(1)}, bf16[64,1024]{1,0:T(8,128)(2,1)S(1)}, u32[]{:S(2)}, u32[]{:S(2)}) collective-permute-start(bf16[64,1024]{1,0:T(8,128)(2,1)S(1)} %slice_bitcast_fusion), channel_id=1, source_target_pairs={{0,2},{2,4},{4,6},{6,8},{8,10},{10,12},{12,14},{14,16},{16,18},{18... | collective-permute-start | bytes 393224 | tf_op jit(solution)/shard_map/ppermute | solution.py:299
  4.3 0.0 collective-permute-start.1
  5.0 0.6 %collective-permute-done.1.pair_off = s32[1,1]{1,0:T(1,128)} collective-permute-done((s32[1,1]{1,0:T(1,128)}, s32[1,1]{1,0:T(1,128)}, u32[]{:S(2)}, u32[]{:S(2)}) %collective-permute-start.1) | collective-permute-done | bytes 36 | tf_op jit(solution)/shard_map/ppermute | solution.py:299
  5.6 0.0 collective-permute-done.2.pair_ref
  5.6 0.7 %chip_image.1 = bf16[64,1152]{1,0:T(8,128)(2,1)S(1)} custom-call(s32[1,1]{1,0:T(1,128)S(6)} %copy.11.own_off, s32[1,1]{1,0:T(1,128)} %collective-permute-done.1.pair_off, bf16[64,1024]{1,0:T(8,128)(2,1)S(1)} %bitcast.10, bf16[64,1024]{1,0:T(8,128)(2,1)S(1)} %collective-permute-done.2.pair_ref), custom_call_target="tpu_custom_call" | custom-call | tf_op jit(solution)/shard_map/chip_image/pallas_call | solution.py:307
  6.3 2.3 %collective-permute-start.5 = (bf16[64,1152]{1,0:T(8,128)(2,1)S(1)}, bf16[64,1152]{1,0:T(8,128)(2,1)S(1)}, u32[]{:S(2)}, u32[]{:S(2)}) collective-permute-start(bf16[64,1152]{1,0:T(8,128)(2,1)S(1)} %chip_image.1), channel_id=1, source_target_pairs={{0,12},{2,14},{4,8},{6,10},{8,20},{10,22},{12,16},{14,18},{16,28},... | collective-permute-start | bytes 442376 | tf_op jit(solution)/shard_map/ppermute | solution.py:299
  8.6 1.3 %collective-permute-start.4 = (bf16[64,1152]{1,0:T(8,128)(2,1)S(1)}, bf16[64,1152]{1,0:T(8,128)(2,1)S(1)}, u32[]{:S(2)}, u32[]{:S(2)}) collective-permute-start(bf16[64,1152]{1,0:T(8,128)(2,1)S(1)} %chip_image.1), channel_id=1, source_target_pairs={{0,8},{2,10},{4,12},{6,14},{8,16},{10,18},{12,20},{14,22},{16,24},... | collective-permute-start | bytes 442376 | tf_op jit(solution)/shard_map/ppermute | solution.py:299
  9.9 0.2 collective-permute-start.3
  10.1 0.0 collective-permute-done.halo_ref
  10.1 0.7 %copy-done.5 = s32[1,128]{1,0:T(1,128)S(1)} copy-done((s32[1,128]{1,0:T(1,128)S(1)}, s32[1,128]{1,0:T(1,128)}, u32[]{:S(2)}) %copy-start.5) | copy-done | bytes 536
  10.8 1.2 %copy-done.3 = bf16[1,128,4096]{2,1,0:T(8,128)(2,1)S(1)} copy-done((bf16[1,128,4096]{2,1,0:T(8,128)(2,1)S(1)}, bf16[1,128,4096]{2,1,0:T(8,128)(2,1)}, u32[]{:S(2)}) %copy-start.3) | copy-done | bytes 1048600
  12.0 2.5 %self_forward.1.self_ref = bf16[4,128,1024]{2,1,0:T(8,128)(2,1)S(1)} custom-call(bf16[128,4096]{1,0:T(8,128)(2,1)S(1)} %bitcast.15, bf16[128,1024]{1,0:T(8,128)(2,1)S(1)} %bitcast.12, bf16[64,1024]{1,0:T(8,128)(2,1)S(1)} %collective-permute-done.halo_ref, s32[1,128]{1,0:T(1,128)S(1)} %copy-done.5), custom_call_target="tpu_custom_call" | custom-call | flops 2000000000 | bytes 3000000 | tf_op jit(solution)/shard_map/self_forward/pallas_call | solution.py:319
  14.5 0.0 collective-permute-done.5.d_ref
  14.5 3.0 %collective-permute-done.4.z_ref = bf16[64,1152]{1,0:T(8,128)(2,1)S(1)} collective-permute-done((bf16[64,1152]{1,0:T(8,128)(2,1)S(1)}, bf16[64,1152]{1,0:T(8,128)(2,1)S(1)}, u32[]{:S(2)}, u32[]{:S(2)}) %collective-permute-start.4) | collective-permute-done | bytes 147488 | tf_op jit(solution)/shard_map/ppermute | solution.py:299
  17.5 0.5 %collective-permute-done.3.x_ref = bf16[64,1152]{1,0:T(8,128)(2,1)S(1)} collective-permute-done((bf16[64,1152]{1,0:T(8,128)(2,1)S(1)}, bf16[64,1152]{1,0:T(8,128)(2,1)S(1)}, u32[]{:S(2)}, u32[]{:S(2)}) %collective-permute-start.3) | collective-permute-done | bytes 147488 | tf_op jit(solution)/shard_map/ppermute | solution.py:299
  18.0 3.9 %cross.1 = (bf16[4,1024,128]{2,1,0:T(8,128)(2,1)S(1)}, bf16[64,1024]{1,0:T(8,128)(2,1)S(1)}, bf16[64,1024]{1,0:T(8,128)(2,1)S(1)}, bf16[64,1024]{1,0:T(8,128)(2,...) custom-call(s32[1,1]{1,0:T(1,128)S(6)} %copy.11.own_off, ...), custom_call_target="tpu_custom_call" | custom-call | flops 4000000000 | bytes 5000000 | tf_op jit(solution)/shard_map/cross/pallas_call | solution.py:329
  21.9 0.7 %collective-permute-start.11 = (f32[4,512]{1,0:T(4,128)S(1)}, f32[4,512]{1,0:T(4,128)S(1)}, u32[]{:S(2)}, u32[]{:S(2)}) collective-permute-start(f32[4,512]{1,0:T(4,128)S(1)} %get-tuple-element.27), channel_id=1, source_target_pairs={{0,2},{1,3},{2,0},{3,1},{4,6},{5,7},{6,4},{7,5},{8,10},{9,11},{10,... | collective-permute-start | bytes 24584 | tf_op jit(solution)/shard_map/ppermute | solution.py:275
  22.6 0.8 %collective-permute-done.11 = f32[4,512]{1,0:T(4,128)S(1)} collective-permute-done((f32[4,512]{1,0:T(4,128)S(1)}, f32[4,512]{1,0:T(4,128)S(1)}, u32[]{:S(2)}, u32[]{:S(2)}) %collective-permute-start.11) | collective-permute-done | bytes 8224 | tf_op jit(solution)/shard_map/ppermute | solution.py:275
  23.4 0.3 collective-permute-start.14
  23.7 1.8 %collective-permute-start.13 = (f32[4,512]{1,0:T(4,128)S(1)}, f32[4,512]{1,0:T(4,128)S(1)}, u32[]{:S(2)}, u32[]{:S(2)}) collective-permute-start(f32[4,512]{1,0:T(4,128)S(1)} %add.21), channel_id=1, source_target_pairs={{0,8},{1,9},{2,10},{3,11},{4,12},{5,13},{6,14},{7,15},{8,0},{9,1},... | collective-permute-start | bytes 24584 | tf_op jit(solution)/shard_map/ppermute | solution.py:275
  25.5 0.5 %collective-permute-start.12 = (f32[4,512]{1,0:T(4,128)S(1)}, f32[4,512]{1,0:T(4,128)S(1)}, u32[]{:S(2)}, u32[]{:S(2)}) collective-permute-start(f32[4,512]{1,0:T(4,128)S(1)} %add.21), channel_id=1, source_target_pairs={{0,4},{1,5},{2,6},{3,7},{4,0},{5,1},{6,2},{7,3},{8,12},{9,13},{10,... | collective-permute-start | bytes 24584 | tf_op jit(solution)/shard_map/ppermute | solution.py:275
  26.0 0.9 %collective-permute-start.6 = (bf16[64,1024]{1,0:T(8,128)(2,1)S(1)}, bf16[64,1024]{1,0:T(8,128)(2,1)S(1)}, u32[]{:S(2)}, u32[]{:S(2)}) collective-permute-start(bf16[64,1024]{1,0:T(8,128)(2,1)S(1)} %get-tuple-element.20), channel_id=1, source_target_pairs={{0,4},{2,6},{4,0},{6,2},{8,12},{10,14},{12,8},{14,10},{16,20},{18,... | collective-permute-start | bytes 393224 | tf_op jit(solution)/shard_map/ppermute | solution.py:299
  27.0 0.8 %collective-permute-start.7 = (bf16[64,1024]{1,0:T(8,128)(2,1)S(1)}, bf16[64,1024]{1,0:T(8,128)(2,1)S(1)}, u32[]{:S(2)}, u32[]{:S(2)}) collective-permute-start(bf16[64,1024]{1,0:T(8,128)(2,1)S(1)} %get-tuple-element.21), channel_id=1, source_target_pairs={{0,24},{2,26},{4,28},{6,30},{8,0},{10,2},{12,4},{14,6},{16,8},{18,... | collective-permute-start | bytes 393224 | tf_op jit(solution)/shard_map/ppermute | solution.py:299
  27.8 0.0 collective-permute-done.14
  27.8 1.2 %collective-permute-start.8 = (bf16[64,1024]{1,0:T(8,128)(2,1)S(1)}, bf16[64,1024]{1,0:T(8,128)(2,1)S(1)}, u32[]{:S(2)}, u32[]{:S(2)}) collective-permute-start(bf16[64,1024]{1,0:T(8,128)(2,1)S(1)} %get-tuple-element.22), channel_id=1, source_target_pairs={{0,28},{2,30},{4,24},{6,26},{8,4},{10,6},{12,0},{14,2},{16,12},{18... | collective-permute-start | bytes 393224 | tf_op jit(solution)/shard_map/ppermute | solution.py:299
  28.9 0.0 collective-permute-done.13
  28.9 0.0 collective-permute-done.12
  28.9 2.0 %collective-permute-start.17 = (f32[4,512]{1,0:T(4,128)S(1)}, f32[4,512]{1,0:T(4,128)S(1)}, u32[]{:S(2)}, u32[]{:S(2)}) collective-permute-start(f32[4,512]{1,0:T(4,128)S(1)} %add_add_fusion.1), channel_id=1, source_target_pairs={{0,17},{1,16},{2,19},{3,18},{4,21},{5,20},{6,23},{7,22},{8,25},{9,... | collective-permute-start | bytes 24584 | tf_op jit(solution)/shard_map/ppermute | solution.py:275
  30.9 0.2 collective-permute-start.16
  31.1 0.0 collective-permute-done.6.x_ref
  31.1 1.4 %collective-permute-start.15 = (f32[4,512]{1,0:T(4,128)S(1)}, f32[4,512]{1,0:T(4,128)S(1)}, u32[]{:S(2)}, u32[]{:S(2)}) collective-permute-start(f32[4,512]{1,0:T(4,128)S(1)} %add_add_fusion.1), channel_id=1, source_target_pairs={{0,16},{1,17},{2,18},{3,19},{4,20},{5,21},{6,22},{7,23},{8,24},{9,... | collective-permute-start | bytes 24584 | tf_op jit(solution)/shard_map/ppermute | solution.py:275
  32.6 4.3 %self_backward.1 = (bf16[128,4096]{1,0:T(8,128)(2,1)}, bf16[64,1024]{1,0:T(8,128)(2,1)S(1)}, f32[128,1024]{1,0:T(8,128)S(1)}) custom-call(bf16[128,4096]{1,0:T(8,128)(2,1)S(1)} %bitcast.16, bf16[128,1024]{1,0:T(8,128)(2,1)S(1)} %bitcast.13, bf16[64,1024]{1,0:T(8,128)(2,1)S(1)} %collective-permute-done.halo_ref, s32[1,128]{1,0:T(1,128)S(1)} %copy-done.5, ...), custom_call_target="tpu_custom_call" | custom-call | flops 4000000000 | bytes 5000000 | tf_op jit(solution)/shard_map/self_backward/pallas_call | solution.py:348
  36.8 0.0 collective-permute-done.7.z_ref
  36.8 2.9 %collective-permute-start.10 = (bf16[64,1024]{1,0:T(8,128)(2,1)S(1)}, bf16[64,1024]{1,0:T(8,128)(2,1)S(1)}, u32[]{:S(2)}, u32[]{:S(2)}) collective-permute-start(bf16[64,1024]{1,0:T(8,128)(2,1)S(1)} %get-tuple-element.24), channel_id=1, source_target_pairs={{0,30},{2,0},{4,2},{6,4},{8,6},{10,8},{12,10},{14,12},{16,14},{18,... | collective-permute-start | bytes 393224 | tf_op jit(solution)/shard_map/ppermute | solution.py:299
  39.7 0.0 collective-permute-done.8.d_ref
  39.7 0.1 chip_sum.1.mine_ref
  39.8 0.1 collective-permute-start.9
  39.8 0.0 collective-permute-done.17
  39.9 0.0 collective-permute-done.15
  39.9 0.1 reshape.12
  40.0 0.1 reduce_sum.9
  40.1 0.5 %subtract_multiply_fusion = f32[32]{0:T(128)} fusion(f32[32]{0:T(128)S(1)} %reduce_sum.9, f32[32]{0:T(128)S(1)} %copy-done.6), kind=kLoop, calls=%fused_computation.3 | loop fusion | flops 96 | bytes 384 | tf_op jit(solution)/shard_map/mul | solution.py:346
  40.6 2.7 %collective-permute-done.10.halo_ref = bf16[64,1024]{1,0:T(8,128)(2,1)S(1)} collective-permute-done((bf16[64,1024]{1,0:T(8,128)(2,1)S(1)}, bf16[64,1024]{1,0:T(8,128)(2,1)S(1)}, u32[]{:S(2)}, u32[]{:S(2)}) %collective-permute-start.10) | collective-permute-done | bytes 131104 | tf_op jit(solution)/shard_map/ppermute | solution.py:299
  43.4 0.0 collective-permute-done.9.pair_ref
  43.4 0.8 %finish.1 = (bf16[64,1024]{1,0:T(8,128)(2,1)}, bf16[128,1024]{1,0:T(8,128)(2,1)}) custom-call(s32[1,1]{1,0:T(1,128)S(6)} %copy.11.own_off, f32[64,1024]{1,0:T(8,128)S(1)} %get-tuple-element.18.own_ref, f32[64,1024]{1,0:T(8,128)S(1)} %chip_sum.1.mine_ref, f32[64,1024]{1,0:T(8,128)S(1)} %collective-permute-done.9.pair_ref, ...), custom_call_target="tpu_custom_call" | custom-call | tf_op jit(solution)/shard_map/finish/pallas_call | solution.py:368
  (16 shorter events, 0.0 us)
Async XLA Ops:
  0.6 4.9 %copy-start = (bf16[1,1,64,1024]{3,2,1,0:T(8,128)(2,1)S(1)}, bf16[1,1,64,1024]{3,2,1,0:T(8,128)(2,1)}, u32[]{:S(2)}) copy-start(bf16[1,1,64,1024]{3,2,1,0:T(8,128)(2,1)} %param.10) | copy-start | bytes 393220
  0.6 4.9 %collective-permute-start.2 = (bf16[64,1024]{1,0:T(8,128)(2,1)}, bf16[64,1024]{1,0:T(8,128)(2,1)S(1)}, u32[]{:S(2)}, u32[]{:S(2)}) collective-permute-start(bf16[64,1024]{1,0:T(8,128)(2,1)} %bitcast.9), channel_id=1, source_target_pairs={{0,2},{2,0},{4,6},{6,4},{8,10},{10,8},{12,14},{14,12},{16,18},{18,... | collective-permute-start | bytes 393224 | tf_op jit(solution)/shard_map/ppermute | solution.py:299
  0.8 4.2 %copy-start.6 = (f32[32]{0:T(128)S(1)}, f32[32]{0:T(128)}, u32[]{:S(2)}) copy-start(f32[32]{0:T(128)} %param.12) | copy-start | bytes 388
  1.7 8.4 %copy-start.1 = (bf16[1,128,1024]{2,1,0:T(8,128)(2,1)S(1)}, bf16[1,128,1024]{2,1,0:T(8,128)(2,1)}, u32[]{:S(2)}) copy-start(bf16[1,128,1024]{2,1,0:T(8,128)(2,1)} %param.8) | copy-start | bytes 786436
  1.7 8.4 %collective-permute-start = (bf16[64,1024]{1,0:T(8,128)(2,1)S(1)}, bf16[64,1024]{1,0:T(8,128)(2,1)S(1)}, u32[]{:S(2)}, u32[]{:S(2)}) collective-permute-start(bf16[64,1024]{1,0:T(8,128)(2,1)S(1)} %slice_bitcast_fusion), channel_id=1, source_target_pairs={{0,2},{2,4},{4,6},{6,8},{8,10},{10,12},{12,14},{14,16},{16,18},{18... | collective-permute-start | bytes 393224 | tf_op jit(solution)/shard_map/ppermute | solution.py:299
  4.3 1.2 %collective-permute-start.1 = (s32[1,1]{1,0:T(1,128)}, s32[1,1]{1,0:T(1,128)}, u32[]{:S(2)}, u32[]{:S(2)}) collective-permute-start(s32[1,1]{1,0:T(1,128)} %param.11), channel_id=1, source_target_pairs={{0,2},{2,0},{4,6},{6,4},{8,10},{10,8},{12,14},{14,12},{16,18},{18,... | collective-permute-start | bytes 20 | tf_op jit(solution)/shard_map/ppermute | solution.py:299
  6.3 8.2 %collective-permute-start.5 = (bf16[64,1152]{1,0:T(8,128)(2,1)S(1)}, bf16[64,1152]{1,0:T(8,128)(2,1)S(1)}, u32[]{:S(2)}, u32[]{:S(2)}) collective-permute-start(bf16[64,1152]{1,0:T(8,128)(2,1)S(1)} %chip_image.1), channel_id=1, source_target_pairs={{0,12},{2,14},{4,8},{6,10},{8,20},{10,22},{12,16},{14,18},{16,28},... | collective-permute-start | bytes 442376 | tf_op jit(solution)/shard_map/ppermute | solution.py:299
  8.6 8.9 %collective-permute-start.4 = (bf16[64,1152]{1,0:T(8,128)(2,1)S(1)}, bf16[64,1152]{1,0:T(8,128)(2,1)S(1)}, u32[]{:S(2)}, u32[]{:S(2)}) collective-permute-start(bf16[64,1152]{1,0:T(8,128)(2,1)S(1)} %chip_image.1), channel_id=1, source_target_pairs={{0,8},{2,10},{4,12},{6,14},{8,16},{10,18},{12,20},{14,22},{16,24},... | collective-permute-start | bytes 442376 | tf_op jit(solution)/shard_map/ppermute | solution.py:299
  9.9 8.0 %collective-permute-start.3 = (bf16[64,1152]{1,0:T(8,128)(2,1)S(1)}, bf16[64,1152]{1,0:T(8,128)(2,1)S(1)}, u32[]{:S(2)}, u32[]{:S(2)}) collective-permute-start(bf16[64,1152]{1,0:T(8,128)(2,1)S(1)} %chip_image.1), channel_id=1, source_target_pairs={{0,4},{2,6},{4,0},{6,2},{8,12},{10,14},{12,8},{14,10},{16,20},{18,... | collective-permute-start | bytes 442376 | tf_op jit(solution)/shard_map/ppermute | solution.py:299
  10.1 0.7 %copy-start.5 = (s32[1,128]{1,0:T(1,128)S(1)}, s32[1,128]{1,0:T(1,128)}, u32[]{:S(2)}) copy-start(s32[1,128]{1,0:T(1,128)} %segment_ref.3) | copy-start | bytes 1540
  10.8 1.2 %copy-start.3 = (bf16[1,128,4096]{2,1,0:T(8,128)(2,1)S(1)}, bf16[1,128,4096]{2,1,0:T(8,128)(2,1)}, u32[]{:S(2)}) copy-start(bf16[1,128,4096]{2,1,0:T(8,128)(2,1)} %param.7) | copy-start | bytes 3145732
  12.0 6.0 %copy-start.2 = (bf16[1,128,4096]{2,1,0:T(8,128)(2,1)S(1)}, bf16[1,128,4096]{2,1,0:T(8,128)(2,1)}, u32[]{:S(2)}) copy-start(bf16[1,128,4096]{2,1,0:T(8,128)(2,1)} %param.13) | copy-start | bytes 3145732
  18.0 14.6 %copy-start.4 = (bf16[1,128,4096]{2,1,0:T(8,128)(2,1)S(1)}, bf16[1,128,4096]{2,1,0:T(8,128)(2,1)}, u32[]{:S(2)}) copy-start(bf16[1,128,4096]{2,1,0:T(8,128)(2,1)} %param.7) | copy-start | bytes 3145732
  21.9 1.5 %collective-permute-start.11 = (f32[4,512]{1,0:T(4,128)S(1)}, f32[4,512]{1,0:T(4,128)S(1)}, u32[]{:S(2)}, u32[]{:S(2)}) collective-permute-start(f32[4,512]{1,0:T(4,128)S(1)} %get-tuple-element.27), channel_id=1, source_target_pairs={{0,2},{1,3},{2,0},{3,1},{4,6},{5,7},{6,4},{7,5},{8,10},{9,11},{10,... | collective-permute-start | bytes 24584 | tf_op jit(solution)/shard_map/ppermute | solution.py:275
  23.4 4.4 %collective-permute-start.14 = (f32[4,512]{1,0:T(4,128)S(1)}, f32[4,512]{1,0:T(4,128)S(1)}, u32[]{:S(2)}, u32[]{:S(2)}) collective-permute-start(f32[4,512]{1,0:T(4,128)S(1)} %add.21), channel_id=1, source_target_pairs={{0,12},{1,13},{2,14},{3,15},{4,8},{5,9},{6,10},{7,11},{8,4},{9,5},... | collective-permute-start | bytes 24584 | tf_op jit(solution)/shard_map/ppermute | solution.py:275
  23.7 5.2 %collective-permute-start.13 = (f32[4,512]{1,0:T(4,128)S(1)}, f32[4,512]{1,0:T(4,128)S(1)}, u32[]{:S(2)}, u32[]{:S(2)}) collective-permute-start(f32[4,512]{1,0:T(4,128)S(1)} %add.21), channel_id=1, source_target_pairs={{0,8},{1,9},{2,10},{3,11},{4,12},{5,13},{6,14},{7,15},{8,0},{9,1},... | collective-permute-start | bytes 24584 | tf_op jit(solution)/shard_map/ppermute | solution.py:275
  25.5 3.4 %collective-permute-start.12 = (f32[4,512]{1,0:T(4,128)S(1)}, f32[4,512]{1,0:T(4,128)S(1)}, u32[]{:S(2)}, u32[]{:S(2)}) collective-permute-start(f32[4,512]{1,0:T(4,128)S(1)} %add.21), channel_id=1, source_target_pairs={{0,4},{1,5},{2,6},{3,7},{4,0},{5,1},{6,2},{7,3},{8,12},{9,13},{10,... | collective-permute-start | bytes 24584 | tf_op jit(solution)/shard_map/ppermute | solution.py:275
  26.0 5.1 %collective-permute-start.6 = (bf16[64,1024]{1,0:T(8,128)(2,1)S(1)}, bf16[64,1024]{1,0:T(8,128)(2,1)S(1)}, u32[]{:S(2)}, u32[]{:S(2)}) collective-permute-start(bf16[64,1024]{1,0:T(8,128)(2,1)S(1)} %get-tuple-element.20), channel_id=1, source_target_pairs={{0,4},{2,6},{4,0},{6,2},{8,12},{10,14},{12,8},{14,10},{16,20},{18,... | collective-permute-start | bytes 393224 | tf_op jit(solution)/shard_map/ppermute | solution.py:299
  27.0 9.8 %collective-permute-start.7 = (bf16[64,1024]{1,0:T(8,128)(2,1)S(1)}, bf16[64,1024]{1,0:T(8,128)(2,1)S(1)}, u32[]{:S(2)}, u32[]{:S(2)}) collective-permute-start(bf16[64,1024]{1,0:T(8,128)(2,1)S(1)} %get-tuple-element.21), channel_id=1, source_target_pairs={{0,24},{2,26},{4,28},{6,30},{8,0},{10,2},{12,4},{14,6},{16,8},{18,... | collective-permute-start | bytes 393224 | tf_op jit(solution)/shard_map/ppermute | solution.py:299
  27.8 11.9 %collective-permute-start.8 = (bf16[64,1024]{1,0:T(8,128)(2,1)S(1)}, bf16[64,1024]{1,0:T(8,128)(2,1)S(1)}, u32[]{:S(2)}, u32[]{:S(2)}) collective-permute-start(bf16[64,1024]{1,0:T(8,128)(2,1)S(1)} %get-tuple-element.22), channel_id=1, source_target_pairs={{0,28},{2,30},{4,24},{6,26},{8,4},{10,6},{12,0},{14,2},{16,12},{18... | collective-permute-start | bytes 393224 | tf_op jit(solution)/shard_map/ppermute | solution.py:299
  28.9 10.9 %collective-permute-start.17 = (f32[4,512]{1,0:T(4,128)S(1)}, f32[4,512]{1,0:T(4,128)S(1)}, u32[]{:S(2)}, u32[]{:S(2)}) collective-permute-start(f32[4,512]{1,0:T(4,128)S(1)} %add_add_fusion.1), channel_id=1, source_target_pairs={{0,17},{1,16},{2,19},{3,18},{4,21},{5,20},{6,23},{7,22},{8,25},{9,... | collective-permute-start | bytes 24584 | tf_op jit(solution)/shard_map/ppermute | solution.py:275
  30.9 8.9 %collective-permute-start.16 = (f32[4,512]{1,0:T(4,128)S(1)}, f32[4,512]{1,0:T(4,128)S(1)}, u32[]{:S(2)}, u32[]{:S(2)}) collective-permute-start(f32[4,512]{1,0:T(4,128)S(1)} %add_add_fusion.1), channel_id=1, source_target_pairs={{0,1},{1,0},{2,3},{3,2},{4,5},{5,4},{6,7},{7,6},{8,9},{9,8},{10,11... | collective-permute-start | bytes 24584 | tf_op jit(solution)/shard_map/ppermute | solution.py:275
  31.1 8.7 %collective-permute-start.15 = (f32[4,512]{1,0:T(4,128)S(1)}, f32[4,512]{1,0:T(4,128)S(1)}, u32[]{:S(2)}, u32[]{:S(2)}) collective-permute-start(f32[4,512]{1,0:T(4,128)S(1)} %add_add_fusion.1), channel_id=1, source_target_pairs={{0,16},{1,17},{2,18},{3,19},{4,20},{5,21},{6,22},{7,23},{8,24},{9,... | collective-permute-start | bytes 24584 | tf_op jit(solution)/shard_map/ppermute | solution.py:275
  36.8 6.5 %collective-permute-start.10 = (bf16[64,1024]{1,0:T(8,128)(2,1)S(1)}, bf16[64,1024]{1,0:T(8,128)(2,1)S(1)}, u32[]{:S(2)}, u32[]{:S(2)}) collective-permute-start(bf16[64,1024]{1,0:T(8,128)(2,1)S(1)} %get-tuple-element.24), channel_id=1, source_target_pairs={{0,30},{2,0},{4,2},{6,4},{8,6},{10,8},{12,10},{14,12},{16,14},{18,... | collective-permute-start | bytes 393224 | tf_op jit(solution)/shard_map/ppermute | solution.py:299
  39.8 3.6 %collective-permute-start.9 = (f32[64,1024]{1,0:T(8,128)S(1)}, f32[64,1024]{1,0:T(8,128)S(1)}, u32[]{:S(2)}, u32[]{:S(2)}) collective-permute-start(f32[64,1024]{1,0:T(8,128)S(1)} %chip_sum.1.mine_ref), channel_id=1, source_target_pairs={{0,2},{2,0},{4,6},{6,4},{8,10},{10,8},{12,14},{14,12},{16,18},{18,... | collective-permute-start | bytes 786440 | tf_op jit(solution)/shard_map/ppermute | solution.py:299

commit v2 on v1

v2 whole, which is shorter than its diff:
```python
import functools
import math

import jax
import jax.numpy as jnp
from jax import lax
from jax.experimental import pallas as pl
from jax.experimental.pallas import tpu as pltpu
from jax.sharding import PartitionSpec as P

HEAD_DIM = 128
WINDOW = 64
GAP = 4
LANES = 128
SCALE = 1.0 / math.sqrt(HEAD_DIM)

VMEM = pl.BlockSpec(memory_space=pltpu.VMEM)
ANY = pl.BlockSpec(memory_space=pl.ANY)
SMEM = pl.BlockSpec(memory_space=pltpu.SMEM)

NN = (((1,), (0,)), ((), ()))
NT = (((1,), (1,)), ((), ()))
TN = (((0,), (0,)), ((), ()))


def dot(a, b, dims):
    return lax.dot_general(a, b, dims, preferred_element_type=jnp.float32)


def stack(ref, first, rows, group, repeat):
    return jnp.concatenate(
        [
            ref[first : first + rows, (group * repeat + h) * HEAD_DIM : (group * repeat + h + 1) * HEAD_DIM]
            for h in range(repeat)
        ],
        axis=0,
    )


def part(ref, index):
    return ref[:, index * HEAD_DIM : (index + 1) * HEAD_DIM]


def softmax_rows(scores):
    top = jnp.max(scores, axis=0, keepdims=True)
    powers = jnp.exp(scores - top)
    return powers * (1.0 / jnp.sum(powers, axis=0, keepdims=True))


def self_mask(segment_ref, block, base):
    segment = segment_ref[0:1, block * WINDOW : (block + 1) * WINDOW]
    segment = jnp.concatenate([segment] * (LANES // WINDOW), axis=1)
    shape = (2 * WINDOW, LANES)
    key = lax.broadcasted_iota(jnp.int32, shape, 0)
    query = lax.broadcasted_iota(jnp.int32, shape, 1) % WINDOW
    key_pos = key + (base + (block - 1) * WINDOW)
    return (key >= query) & (key <= query + WINDOW) & (key_pos >= segment)


def self_weights(query_rows, keys, allowed):
    scores = dot(keys, query_rows, NT) * SCALE
    allowed = jnp.concatenate([allowed] * (scores.shape[1] // LANES), axis=1)
    return softmax_rows(jnp.where(allowed, scores, -1e30))


def joined(context_ref, halo_ref, block, index):
    own = context_ref[:, index * HEAD_DIM : (index + 1) * HEAD_DIM]
    if block == 0:
        return jnp.concatenate([part(halo_ref, index), own[:WINDOW]], axis=0)
    return own[(block - 1) * WINDOW : (block + 1) * WINDOW]


def odd_core():
    return flag(lax.axis_index("seq") % 2 == 1)


def flag(cond):
    return jnp.where(cond, 1, 0)


def choose(here, mine_ref, other_ref, out_ref, width=None):
    here = jnp.broadcast_to(here, out_ref.shape) > 0
    width = width or mine_ref.shape[1]
    mine, other = mine_ref[:, :width].astype(jnp.float32), other_ref[:, :width].astype(jnp.float32)
    out_ref[...] = jnp.where(here, mine, other).astype(out_ref.dtype)


def owner(off_ref, row, tok_rows):
    return flag(off_ref[row : row + 1, 0:1] < tok_rows)


def chip_kernel(
    off_ref, pair_off_ref, mine_ref, other_ref, tail_ref, out_ref, marked_ref, half_ref, tail_out, owner_ref, *, tok_rows
):
    off, pair_off = off_ref[0, 0], pair_off_ref[0, 0]
    width = mine_ref.shape[1]
    tail_out[...] = tail_ref[...]
    choose(flag(off < tok_rows), mine_ref, other_ref, out_ref)
    marked_ref[:, :width] = out_ref[...]
    owns = jnp.where((off < tok_rows) | (pair_off < tok_rows), 1.0, 0.0)
    marked_ref[:, width:] = jnp.full((mine_ref.shape[0], LANES), owns, jnp.float32).astype(marked_ref.dtype)
    choose(odd_core(), out_ref.at[:, width // 2 :], out_ref.at[:, : width // 2], half_ref)
    row = lax.broadcasted_iota(jnp.int32, owner_ref.shape, 0)
    owner_ref[...] = jnp.where(row == 0, off, pair_off)


def join_kernel(z_ref, x_ref, _, __, out_ref):
    out_ref[:, : z_ref.shape[1]] = z_ref[...]
    out_ref[:, z_ref.shape[1] :] = x_ref[...]


def near_kernel(chip_ref, other_ref, _, out_ref, *, step):
    choose(flag(lax.axis_index("seq") % 2 == (1 if step > 0 else 0)), chip_ref, other_ref, out_ref)


def self_kernel(query_ref, context_ref, halo_ref, segment_ref, _, out_ref, weights_ref, *, block, groups, repeat):
    tok_rows = query_ref.shape[0]
    base = lax.axis_index("seq") * tok_rows
    allowed = self_mask(segment_ref, block, base)
    for g in range(groups):
        rows = stack(query_ref, block * WINDOW, WINDOW, g, repeat)
        weights = self_weights(rows, joined(context_ref, halo_ref, block, g), allowed)
        weights_ref[g] = weights
        values = joined(context_ref, halo_ref, block, groups + g)
        out_ref[g] = dot(values, weights.astype(jnp.bfloat16), TN).astype(jnp.bfloat16)


def split(values):
    high = values.astype(jnp.bfloat16)
    rest = values - high.astype(jnp.float32)
    middle = rest.astype(jnp.bfloat16)
    low = (rest - middle.astype(jnp.float32)).astype(jnp.bfloat16)
    return jnp.concatenate([high, middle, low, jnp.zeros_like(low)], axis=0)


def unsplit(parts):
    parts = parts.astype(jnp.float32)
    rows = parts.shape[0] // 4
    return parts[:rows] + (parts[rows : 2 * rows] + parts[2 * rows : 3 * rows])


def cross_kernel(
    off_ref, gate_ref, self_0_ref, self_1_ref, grad_ref, own_ref, chip_ref, mine_ref, pair_ref,
    grad_self_ref, to_pair_ref, in_chip_ref, own_terms_ref, mask_ref, prev, *, groups, repeat
):
    tok_rows, width = grad_ref.shape[0], own_ref.shape[1]
    img = own_ref.shape[0]
    shard = lax.axis_index("seq")
    off = off_ref[0:1, 0:1]
    is_owner, pair_owner = owner(off_ref, 0, tok_rows), owner(off_ref, 1, tok_rows)
    upper, odd = flag(shard % GAP >= 2), flag(shard % 2 == 1)
    from_chip = odd * pair_owner
    from_x = upper * (1 - (is_owner | pair_owner))
    from_z = flag(shard >= GAP) * (1 - (from_chip | from_x))
    has_prev = from_chip | from_x | from_z
    marked = width + LANES
    by_mine = flag(mine_ref[0:1, width : width + 1].astype(jnp.float32) > 0.5)
    choose(by_mine, mine_ref, pair_ref, prev, width)
    for first in (0, 1):
        cols = prev.at[:, first * width // 2 : (first + 1) * width // 2]
        mine = from_x * flag(odd == first)
        choose(mine, mine_ref.at[:, marked:], cols, cols)
        choose(from_x - mine, pair_ref.at[:, marked:], cols, cols)
    choose(from_chip, chip_ref, prev, prev)

    half = repeat * WINDOW
    rows = tok_rows * repeat
    lane = lax.broadcasted_iota(jnp.int32, (1, rows), 1)
    lane_tok = (lane // half) * WINDOW + lane % WINDOW
    own_from = jnp.minimum(off, tok_rows)
    has_from = own_from * (1 - has_prev)
    from_chip, from_x, from_z = (here.astype(jnp.float32) for here in (from_chip, from_x, from_z))
    use_own = lane_tok >= own_from
    has_lane = lane_tok >= has_from
    row_tok = lax.broadcasted_iota(jnp.int32, (WINDOW, HEAD_DIM), 0)

    gate_rows = []
    for g in range(groups):
        keys = jnp.concatenate([part(prev, g), part(own_ref, g)], axis=0)
        values = jnp.concatenate([part(prev, groups + g), part(own_ref, groups + g)], axis=0)
        out_t = jnp.concatenate([self_0_ref[g], self_1_ref[g]], axis=1)
        scores = dot(keys, out_t, NN)
        weights = softmax_rows(jnp.where(use_own, scores[img:], scores[:img]) * SCALE)
        narrow = weights.astype(jnp.bfloat16)
        grad_rows, cross_rows = [], []
        for block in range(tok_rows // WINDOW):
            has_rows = row_tok + block * WINDOW >= has_from
            for h in range(repeat):
                head = g * repeat + h
                tile = grad_ref[
                    block * WINDOW : (block + 1) * WINDOW, head * HEAD_DIM : (head + 1) * HEAD_DIM
                ]
                grad_rows.append(tile)
                factor = jnp.where(has_rows, gate_ref[head : head + 1, :], 0.0)
                cross_rows.append((tile.astype(jnp.float32) * factor).astype(jnp.bfloat16))
        grad_rows = jnp.concatenate(grad_rows, axis=0)
        cross_rows = jnp.concatenate(cross_rows, axis=0)
        plain = dot(values, grad_rows, NT)
        plain = jnp.where(use_own, plain[img:], plain[:img])
        gate_row = jnp.sum(narrow.astype(jnp.float32) * plain, axis=0, keepdims=True)
        gate_row = jnp.where(has_lane, gate_row, 0.0)
        gate_row = gate_row[:, :half] + gate_row[:, half:]
        gate_rows.extend(gate_row[:, i * LANES : (i + 1) * LANES] for i in range(half // LANES))
        grad_weights = dot(values, cross_rows, NT)
        grad_weights = jnp.where(use_own, grad_weights[img:], grad_weights[:img])
        delta = jnp.sum(weights * grad_weights, axis=0, keepdims=True)
        grad_scores = weights * (grad_weights - delta)
        scores_j = jnp.concatenate(
            [jnp.where(use_own, 0.0, grad_scores), jnp.where(use_own, grad_scores, 0.0)], axis=0
        ).astype(jnp.bfloat16)
        narrow_j = jnp.concatenate(
            [jnp.where(use_own, 0.0, weights), jnp.where(use_own, weights, 0.0)], axis=0
        ).astype(jnp.bfloat16)
        grad_key = dot(scores_j, out_t, NT) * SCALE
        grad_value = dot(narrow_j, cross_rows, NN)
        grad_query = dot(scores_j, keys, TN) * SCALE
        grad_self_ref[g] = (grad_rows.astype(jnp.float32) + grad_query).astype(jnp.bfloat16)
        for index, terms in ((g, grad_key), (groups + g, grad_value)):
            cols = slice(index * HEAD_DIM, (index + 1) * HEAD_DIM)
            own_terms_ref[:, cols] = terms[img:]
            to_pair_ref[:, cols] = terms[:img] * (from_x + from_z)
            in_chip_ref[:, cols] = terms[:img] * from_chip
    gate = jnp.concatenate(gate_rows, axis=0)
    to_pair_ref[:, width:] = jnp.concatenate([gate] * (img // gate.shape[0]), axis=0)
    row = lax.broadcasted_iota(jnp.int32, mask_ref.shape, 0)
    mask_ref[...] = jnp.where(row == 0, by_mine.astype(jnp.float32) * (1.0 - from_x), from_x)


def outside_kernel(mine_ref, pair_ref, mask_ref, to_z_ref, to_x_ref, gate_ref):
    width = mine_ref.shape[1] - LANES
    total = mine_ref[...] + pair_ref[...]
    gate = total[: gate_ref.shape[0], width:]
    terms = total[:, :width]
    to_z_ref[:, :width] = (terms * mask_ref[0:1, 0:1]).astype(to_z_ref.dtype)
    to_z_ref[:, width:] = split(gate)
    odd = jnp.broadcast_to(odd_core(), (terms.shape[0], width // 2)) > 0
    half = jnp.where(odd, terms[:, width // 2 :], terms[:, : width // 2])
    to_x_ref[:, : width // 2] = (half * mask_ref[1:2, 0:1]).astype(to_x_ref.dtype)
    to_x_ref[:, width // 2 :] = split(gate)
    gate_ref[...] = gate


def chip_sum_kernel(mine_ref, x_ref, z_ref, gate_ref, halo_ref, _, out_ref, gate_out, halo_out):
    halo_out[...] = halo_ref[...]
    width = mine_ref.shape[1]
    odd = odd_core().astype(jnp.float32)
    half = width // 2
    from_x = x_ref[:, :half].astype(jnp.float32)
    out_ref[:, :half] = mine_ref[:, :half] + (from_x * (1.0 - odd) + z_ref[:, :half].astype(jnp.float32))
    out_ref[:, half:width] = mine_ref[:, half:] + (from_x * odd + z_ref[:, half:width].astype(jnp.float32))
    gate_out[...] = gate_ref[...] + unsplit(x_ref[:, half:])
    gate = unsplit(z_ref[:, width:])
    out_ref[:, width:] = jnp.concatenate([gate] * (mine_ref.shape[0] // gate.shape[0]), axis=0)


def self_back_kernel(
    query_ref, context_ref, halo_ref, weights_ref, grad_ref, _,
    query_grad_ref, key_low_ref, key_high_ref, rows_out, sems, *, block, groups, repeat
):
    copies = []
    half = repeat * WINDOW
    for g in range(groups):
        rows = stack(query_ref, block * WINDOW, WINDOW, g, repeat)
        keys = joined(context_ref, halo_ref, block, g)
        values = joined(context_ref, halo_ref, block, groups + g)
        weights = weights_ref[g]
        grads = grad_ref[g, block * half : (block + 1) * half, :]
        grad_weights = dot(values, grads, NT)
        delta = jnp.sum(weights * grad_weights, axis=0, keepdims=True)
        grad_scores = (weights * (grad_weights - delta)).astype(jnp.bfloat16)
        grad_query = (dot(grad_scores, keys, TN) * SCALE).astype(jnp.bfloat16)
        for h in range(repeat):
            head = g * repeat + h
            rows_out[:, head * HEAD_DIM : (head + 1) * HEAD_DIM] = grad_query[h * WINDOW : (h + 1) * WINDOW]
        cols = slice(g * repeat * HEAD_DIM, (g + 1) * repeat * HEAD_DIM)
        copies.append(
            pltpu.make_async_copy(
                rows_out.at[:, cols], query_grad_ref.at[block * WINDOW : (block + 1) * WINDOW, cols], sems.at[g]
            )
        )
        copies[-1].start()
        grad_key = dot(grad_scores, rows, NN) * SCALE
        grad_value = dot(weights.astype(jnp.bfloat16), grads, NN)
        for index, terms in ((g, grad_key), (groups + g, grad_value)):
            cols = slice(index * HEAD_DIM, (index + 1) * HEAD_DIM)
            key_low_ref[:, cols] = terms[:WINDOW].astype(key_low_ref.dtype)
            key_high_ref[:, cols] = terms[WINDOW:]
    for copy in copies:
        copy.wait()


def gate_kernel(chip_ref, mine_ref, pair_ref, out_ref):
    width = mine_ref.shape[1] - LANES
    rows = out_ref.shape[0]
    out_ref[...] = chip_ref[...] + (mine_ref[:rows, width:] + pair_ref[:rows, width:])


def add_kernel(one_ref, other_ref, out_ref):
    out_ref[...] = one_ref[...] + other_ref[...]


def gate_grad_kernel(one_ref, other_ref, gate_ref, out_ref):
    rows, heads = one_ref.shape[0], out_ref.shape[1]
    total = one_ref[...] + other_ref[...]
    lane = lax.broadcasted_iota(jnp.int32, total.shape, 1)
    first = jnp.sum(jnp.where(lane < WINDOW, total, 0.0), axis=1, keepdims=True)
    second = jnp.sum(jnp.where(lane < WINDOW, 0.0, total), axis=1, keepdims=True)
    row = lax.broadcasted_iota(jnp.int32, (rows, heads), 0)
    head = lax.broadcasted_iota(jnp.int32, (rows, heads), 1)
    sums = jnp.where(head == 2 * row, first, 0.0) + jnp.where(head == 2 * row + 1, second, 0.0)
    sums = jnp.sum(sums, axis=0, keepdims=True)
    tanh = gate_ref[:, :heads]
    same = lax.broadcasted_iota(jnp.int32, tanh.shape, 0) == lax.broadcasted_iota(jnp.int32, tanh.shape, 1)
    tanh = jnp.sum(jnp.where(same, tanh, 0.0), axis=0, keepdims=True)
    out_ref[...] = (1.0 - tanh * tanh) * sums


def finish_kernel(
    off_ref, own_ref, mine_ref, pair_ref, low_ref, also_ref, high_ref, halo_ref, _,
    memory_ref, context_ref, *, tok_rows
):
    width = own_ref.shape[1]
    keep = flag(off_ref[0:1, 0:1] < tok_rows).astype(jnp.float32)
    total = own_ref[...] + (mine_ref[:, :width] + pair_ref[:, :width])
    memory_ref[...] = (total * keep).astype(memory_ref.dtype)
    more = jnp.where(lax.axis_index("seq") < lax.axis_size("seq") - 1, 1.0, 0.0)
    first = tok_rows - WINDOW
    context_ref[:first] = (low_ref[...] + also_ref[...]).astype(context_ref.dtype)
    context_ref[first:] = (high_ref[...] + halo_ref[...].astype(jnp.float32) * more).astype(context_ref.dtype)


def struct(shape, dtype):
    return jax.ShapeDtypeStruct(shape, dtype)


def call(
    name, kernel, out_shape, in_specs, scratch=(), out_specs=None, aliases=None, flops=10**6, moved=10**6
):
    return pl.pallas_call(
        kernel,
        out_shape=out_shape,
        in_specs=in_specs,
        out_specs=[VMEM] * len(out_shape) if out_specs is None else out_specs,
        scratch_shapes=scratch,
        input_output_aliases=aliases or {},
        compiler_params=pltpu.CompilerParams(vmem_limit_bytes=40 * 2**20),
        cost_estimate=pl.CostEstimate(flops=flops, bytes_accessed=moved, transcendentals=0),
        name=name,
    )


def on_device(queries, context, segment_start, memory, image_offset, cross_gate, out_grad):
    tok_rows, model = queries.shape[1:]
    width = context.shape[2]
    groups = width // 2 // HEAD_DIM
    heads = cross_gate.shape[0]
    repeat = heads // groups
    img = memory.shape[2]
    half = repeat * WINDOW
    seq, dp = lax.axis_size("seq"), lax.axis_size("dp")
    f32, bf16 = jnp.float32, jnp.bfloat16

    swaps = seq == 4 * GAP and dp == 2

    def send(value, where):
        return lax.ppermute(value, "seq", [(i, where(i)) for i in range(seq)])

    def send_all(value, where):
        pairs = [(s, d, *where(s, d)) for s in range(seq) for d in range(dp)]
        return lax.ppermute(value, ("seq", "dp"), [(s * dp + d, t * dp + e) for s, d, t, e in pairs])

    def send_near(value, step):
        if not swaps:
            return (send(value, lambda i: (i + step) % seq),)
        off_chip = lambda s, d: (s, d ^ 1) if s in (0, seq - 1) else (((s + 1) ^ 1) - 1, d)
        return send(value, lambda i: i ^ 1), send_all(value, off_chip)

    def merge(name, arrived, step, after):
        if len(arrived) == 1:
            return arrived[0]
        return call(name, functools.partial(near_kernel, step=step), [window], [VMEM] * 2 + [ANY])(*arrived, after)[0]

    def send_z(value, step):
        return send(value, lambda i: ((i if i % 2 == 0 else i ^ 2) + step * GAP) % seq)

    q, ctx, grad = queries[0], context[0], out_grad[0]
    gate_tanh = jnp.tanh(cross_gate)
    gate_rows = jnp.broadcast_to(gate_tanh[:, None], (heads, LANES))
    image = struct((img, width), bf16)
    window = struct((WINDOW, width), bf16)
    own = memory[0, 0]
    pair = send(own, lambda i: i ^ 1)
    pair_off = send(image_offset, lambda i: i ^ 1)
    tail = ctx[tok_rows - WINDOW :]
    chip, marked, chip_half, tail, off = call(
        "chip_image",
        functools.partial(chip_kernel, tok_rows=tok_rows),
        [image, struct((img, width + LANES), bf16), struct((img, width // 2), bf16), window, struct((8, LANES), jnp.int32)],
        [SMEM] * 2 + [VMEM] * 3,
    )(image_offset, pair_off, own, pair, tail)
    by_z = send_z(marked, 1)
    by_x = send(chip_half, lambda i: i ^ 2)
    halo = merge("halo", send_near(tail, 1), 1, chip)
    self_out, kept = [None, None], [None, None]

    def self_forward(block, after):
        self_out[block], kept[block] = call(
            f"self_forward_{block}",
            functools.partial(self_kernel, block=block, groups=groups, repeat=repeat),
            [struct((groups, HEAD_DIM, half), bf16), struct((groups, 2 * WINDOW, half), f32)],
            [VMEM] * 4 + [ANY],
            flops=10**6,
            moved=10**5,
        )(q, ctx, tail if block else halo, segment_start, after)

    self_forward(1, chip)
    arrived = call("arrived", join_kernel, [struct((img, width + LANES + width // 2), bf16)], [VMEM] * 2 + [ANY] * 2)(
        by_z, by_x, self_out[1], halo
    )[0]

    by_pair = send(arrived, lambda i: i ^ 1)
    self_forward(0, arrived)

    gate_shape = struct((heads * WINDOW // LANES, LANES), f32)
    grad_self, to_pair, in_chip, own_terms, masks = call(
        "cross",
        functools.partial(cross_kernel, groups=groups, repeat=repeat),
        [
            struct((groups, repeat * tok_rows, HEAD_DIM), bf16),
            struct((img, width + LANES), f32),
            struct((img, width), f32),
            struct((img, width), f32),
            struct((8, LANES), f32),
        ],
        [VMEM] * 9,
        scratch=[pltpu.VMEM((img, width), bf16)],
    )(off, gate_rows, *self_out, grad, own, chip, arrived, by_pair)
    from_pair = send(to_pair, lambda i: i ^ 1)
    to_z, to_x, gate_chip = call(
        "outside",
        outside_kernel,
        [struct((img, width + LANES), bf16), struct((img, width // 2 + LANES), bf16), gate_shape],
        [VMEM] * 3,
    )(to_pair, from_pair, masks)
    from_z = send_z(to_z, -1)
    from_x = send(to_x, lambda i: i ^ 2)

    def self_backward(block, after):
        return call(
            f"self_backward_{block}",
            functools.partial(self_back_kernel, block=block, groups=groups, repeat=repeat),
            [
                struct((tok_rows, model), bf16),
                struct((WINDOW, width), f32 if block else bf16),
                struct((WINDOW, width), f32),
            ],
            [VMEM] * 5 + [ANY],
            scratch=[pltpu.VMEM((WINDOW, model), bf16), pltpu.SemaphoreType.DMA((groups,))],
            out_specs=[ANY, VMEM, VMEM],
            aliases={5: 0} if block else None,
            flops=10**6,
            moved=10**5,
        )(q, ctx, tail if block else halo, kept[block], grad_self, after)

    query_grad, halo_terms, low = self_backward(0, to_z)
    query_grad, also, high = self_backward(1, query_grad)
    mine, gate_near, halo_terms = call(
        "chip_sum",
        chip_sum_kernel,
        [struct((img, width + LANES), f32), gate_shape, window],
        [VMEM] * 5 + [ANY],
    )(in_chip, from_x, from_z, gate_chip, halo_terms, high)
    other = send(mine, lambda i: i ^ 1)
    halo_back = merge("halo_back", send_near(halo_terms, -1), -1, mine)
    gate_sum = call("gate_sum", gate_kernel, [gate_shape], [VMEM] * 3)(gate_near, mine, other)[0]
    memory_grad, context_grad = call(
        "finish",
        functools.partial(finish_kernel, tok_rows=tok_rows),
        [image, struct((tok_rows, width), bf16)],
        [VMEM] * 8 + [ANY],
    )(off, own_terms, mine, other, low, also, high, halo_back, gate_sum)

    if not swaps:
        gate_total = lax.psum(to_pair[: gate_shape.shape[0], width:], ("seq", "dp"))
        gate_grad = (1.0 - gate_tanh * gate_tanh) * jnp.sum(gate_total.reshape(heads, WINDOW), axis=1)
        return (query_grad[None], context_grad[None], memory_grad[None, None], gate_grad)
    gate_sum = call("gate_docs", add_kernel, [gate_shape], [VMEM] * 2)(
        gate_sum, send_all(gate_sum, lambda s, d: (s, d ^ 1))
    )[0]
    gate_grad = call("gate_grad", gate_grad_kernel, [struct((1, heads), f32)], [VMEM] * 3)(
        gate_sum, send_all(gate_sum, lambda s, d: (s ^ 2 * GAP, d)), gate_rows
    )[0].reshape(heads)
    return (query_grad[None], context_grad[None], memory_grad[None, None], gate_grad)


def solution(mesh):
    placed = (
        P("dp", "seq", None),
        P("dp", "seq", None),
        P("dp", "seq"),
        P("dp", "seq", None, None),
        P("dp", "seq"),
        P(),
        P("dp", "seq", None),
    )
    return jax.shard_map(
        on_device,
        mesh=mesh,
        in_specs=placed,
        out_specs=(P("dp", "seq", None), P("dp", "seq", None), P("dp", "seq", None, None), P()),
        check_vma=False,
    )
```

time: 44.4 us -> 40.6 us (0.914)
  the two profiles are of different devices: /device:TPU:1 before, /device:TPU:0 now
where the time goes in v2:
time: 40.6 us; the launch traced here: 40.4 us
  starting transfers between devices  14.8 us (36%)
  Pallas kernels  11.9 us (29%)
  waiting for transfers between devices  8.69 us (21%)
  local copies, waits for them, and re-layouts  3.47 us (9%)
  between operations  1.47 us (4%)
    ppermute x11, starting transfers between devices, send(): return lax.ppermute(value, 'seq', [(i, where(i)) for i in range(seq)])  9.5 us
    ppermute x4, starting transfers between devices, send_all(): lax.ppermute(value, ('seq', 'dp'), [(s * dp + d, t * dp + e) for s, d, t,...  5.33 us
    ppermute x4, waiting for transfers between devices, send_all(): lax.ppermute(value, ('seq', 'dp'), [(s * dp + d, t * dp + e) for s, d, t,...  5.09 us
    pallas_call x2, Pallas kernels, self_backward(): call(f'self_backward_{block}', functools.partial(self_back_kernel, block=...  4.21 us
    ppermute x11, waiting for transfers between devices, send(): return lax.ppermute(value, 'seq', [(i, where(i)) for i in range(seq)])  3.6 us
    pallas_call x2, Pallas kernels, self_forward(): call(f'self_forward_{block}', functools.partial(self_kernel, block=block,...  2.69 us
    pallas_call x1, Pallas kernels, on_device(): call('cross', functools.partial(cross_kernel, groups=groups, repeat=repea...  2.54 us
    unnamed x14, local copies, waits for them, and re-layouts  2.44 us
  transfers between devices with their start and end apart: 15, of which 5 were waited for; matrix products, arithmetic and copies ran while one was open for 2% of the time, Pallas kernels for 19%

profile of v2, /device:TPU:0, one launch (start us, length us, event | category | flops | bytes accessed | tf_op | source)
XLA Modules:
  0.0 40.4 jit_solution(16965805204220299684)
XLA Ops:
  0.6 0.5 %collective-permute-start = (s32[1,1]{1,0:T(1,128)}, s32[1,1]{1,0:T(1,128)}, u32[]{:S(2)}, u32[]{:S(2)}) collective-permute-start(s32[1,1]{1,0:T(1,128)} %param.11), channel_id=1, source_target_pairs={{0,2},{2,0},{4,6},{6,4},{8,10},{10,8},{12,14},{14,12},{16,18},{18,... | collective-permute-start | bytes 20 | tf_op jit(solution)/shard_map/ppermute | solution.py:366
  1.1 0.1 collective-permute-start.1
  1.9 1.0 %slice_bitcast_fusion.tail_ref = bf16[64,1024]{1,0:T(8,128)(2,1)S(1)} fusion(bf16[1,128,1024]{2,1,0:T(8,128)(2,1)} %param.8), kind=kLoop, calls=%fused_computation | loop fusion | bytes 262144 | tf_op jit(solution)/shard_map/slice | solution.py:394
  2.8 0.0 copy-start.2
  2.9 0.0 collective-permute-done.pair_off_ref
  2.9 0.0 collective-permute-done.1.other_ref
  2.9 0.7 %chip_image.1 = (bf16[64,1024]{1,0:T(8,128)(2,1)S(1)}, bf16[64,1152]{1,0:T(8,128)(2,1)S(1)}, bf16[64,512]{1,0:T(8,128)(2,1)S(1)}, bf16[64,1024]{1,0:T(8,128)(2,1)S(1)}, s32[8,128]{1,0:T(8,128)S(1)}) custom-call(s32[1,1]{1,0:T(1,128)S(6)} %copy.13.off_ref, s32[1,1]{1,0:T(1,128)} %collective-permute-done.pair_off_ref, bf16[64,1024]{1,0:T(8,128)(2,1)S(1)} %bitcast.20, ...), custom_call_target="tpu_custom_call" | custom-call | flops 1000000 | bytes 1000000 | tf_op jit(solution)/shard_map/chip_image/pallas_call | solution.py:395
  3.6 3.1 %collective-permute-start.4 = (bf16[64,1152]{1,0:T(8,128)(2,1)S(1)}, bf16[64,1152]{1,0:T(8,128)(2,1)S(1)}, u32[]{:S(2)}, u32[]{:S(2)}) collective-permute-start(bf16[64,1152]{1,0:T(8,128)(2,1)S(1)} %get-tuple-element.36), channel_id=1, source_target_pairs={{0,8},{2,14},{4,12},{6,10},{8,16},{10,22},{12,20},{14,18},{16,24},... | collective-permute-start | bytes 442376 | tf_op jit(solution)/shard_map/ppermute | solution.py:366
  6.7 1.5 %collective-permute-start.3 = (bf16[64,1024]{1,0:T(8,128)(2,1)S(1)}, bf16[64,1024]{1,0:T(8,128)(2,1)S(1)}, u32[]{:S(2)}, u32[]{:S(2)}) collective-permute-start(bf16[64,1024]{1,0:T(8,128)(2,1)S(1)} %get-tuple-element.32.halo_ref), channel_id=1, source_target_pairs={{0,1},{1,0},{2,4},{3,5},{4,2},{5,3},{6,8},{7,9},{8,6},{9,7},{10,12... | collective-permute-start | bytes 393224 | tf_op jit(solution)/shard_map/ppermute | solution.py:370
  8.2 0.1 collective-permute-start.2
  8.3 1.5 %collective-permute-start.5 = (bf16[64,512]{1,0:T(8,128)(2,1)S(1)}, bf16[64,512]{1,0:T(8,128)(2,1)S(1)}, u32[]{:S(2)}, u32[]{:S(2)}) collective-permute-start(bf16[64,512]{1,0:T(8,128)(2,1)S(1)} %get-tuple-element.37), channel_id=1, source_target_pairs={{0,4},{2,6},{4,0},{6,2},{8,12},{10,14},{12,8},{14,10},{16,20},{18,... | collective-permute-start | bytes 196616 | tf_op jit(solution)/shard_map/ppermute | solution.py:366
  9.8 0.7 %copy-done.5 = s32[1,128]{1,0:T(1,128)S(1)} copy-done((s32[1,128]{1,0:T(1,128)S(1)}, s32[1,128]{1,0:T(1,128)}, u32[]{:S(2)}) %copy-start.5) | copy-done | bytes 536
  10.5 1.2 %copy-done = bf16[1,128,4096]{2,1,0:T(8,128)(2,1)S(1)} copy-done((bf16[1,128,4096]{2,1,0:T(8,128)(2,1)S(1)}, bf16[1,128,4096]{2,1,0:T(8,128)(2,1)}, u32[]{:S(2)}) %copy-start) | copy-done | bytes 1048600
  11.7 1.3 %self_forward_1.1 = (bf16[4,128,512]{2,1,0:T(8,128)(2,1)S(1)}, f32[4,128,512]{2,1,0:T(8,128)S(1)}) custom-call(bf16[128,4096]{1,0:T(8,128)(2,1)S(1)} %bitcast.10, bf16[128,1024]{1,0:T(8,128)(2,1)S(1)} %bitcast.14, bf16[64,1024]{1,0:T(8,128)(2,1)S(1)} %get-tuple-element.32.halo_ref, s32[1,128]{1,0:T(1,128)S(1)} %copy-done.5, ...), custom_call_target="tpu_custom_call" | custom-call | flops 1000000 | bytes 100000 | tf_op jit(solution)/shard_map/self_forward_1/pallas_call | solution.py:407
  13.1 0.0 copy-start.1
  13.1 0.0 collective-permute-done.3.other_ref
  13.1 0.0 collective-permute-done.2.chip_ref
  13.1 1.8 %collective-permute-done.5.x_ref = bf16[64,512]{1,0:T(8,128)(2,1)S(1)} collective-permute-done((bf16[64,512]{1,0:T(8,128)(2,1)S(1)}, bf16[64,512]{1,0:T(8,128)(2,1)S(1)}, u32[]{:S(2)}, u32[]{:S(2)}) %collective-permute-start.5) | collective-permute-done | bytes 65568 | tf_op jit(solution)/shard_map/ppermute | solution.py:366
  14.9 0.0 collective-permute-done.4.z_ref
  15.0 0.0 copy-start.3
  15.0 0.1 collective-permute-start.6
  15.1 0.5 %copy-done.6 = f32[32]{0:T(128)S(1)} copy-done((f32[32]{0:T(128)S(1)}, f32[32]{0:T(128)}, u32[]{:S(2)}) %copy-start.6) | copy-done | bytes 152
  15.6 1.3 %self_forward_0.1 = (bf16[4,128,512]{2,1,0:T(8,128)(2,1)S(1)}, f32[4,128,512]{2,1,0:T(8,128)S(1)}) custom-call(bf16[128,4096]{1,0:T(8,128)(2,1)S(1)} %bitcast.11, bf16[128,1024]{1,0:T(8,128)(2,1)S(1)} %bitcast.15, bf16[64,1024]{1,0:T(8,128)(2,1)S(1)} %halo.1.__.halo_ref, s32[1,128]{1,0:T(1,128)S(1)} %copy-done.5, bf16[64,1664]{1,0:T(8,128)(2,1)S(1)} %arrived.1._.mine_ref), custom_call_target="tpu_custom_call" | custom-call | flops 1000000 | bytes 100000 | tf_op jit(solution)/shard_map/self_forward_0/pallas_call | solution.py:407
  17.0 0.0 collective-permute-done.6.pair_ref
  17.0 0.1 broadcast_in_dim.15.gate_ref
  17.0 2.5 %cross.1 = (bf16[4,1024,128]{2,1,0:T(8,128)(2,1)S(1)}, f32[64,1152]{1,0:T(8,128)S(1)}, f32[64,1024]{1,0:T(8,128)S(1)}, f32[64,1024]{1,0:T(8,128)S(1)}, f32[8,128]{1,0:T(8,128)S(1)}) custom-call(s32[8,128]{1,0:T(8,128)S(1)} %get-tuple-element.35.off_ref, f32[32,128]{1,0:T(8,128)S(1)} %broadcast_in_dim.15.gate_ref, ...), custom_call_target="tpu_custom_call" | custom-call | flops 1000000 | bytes 1000000 | tf_op jit(solution)/shard_map/cross/pallas_call | solution.py:425
  19.6 0.1 collective-permute-start.7
  19.7 1.6 %collective-permute-done.7.pair_ref = f32[64,1152]{1,0:T(8,128)S(1)} collective-permute-done((f32[64,1152]{1,0:T(8,128)S(1)}, f32[64,1152]{1,0:T(8,128)S(1)}, u32[]{:S(2)}, u32[]{:S(2)}) %collective-permute-start.7) | collective-permute-done | bytes 294944 | tf_op jit(solution)/shard_map/ppermute | solution.py:366
  21.2 0.1 outside.1
  21.3 3.2 %collective-permute-start.9 = (bf16[64,1152]{1,0:T(8,128)(2,1)S(1)}, bf16[64,1152]{1,0:T(8,128)(2,1)S(1)}, u32[]{:S(2)}, u32[]{:S(2)}) collective-permute-start(bf16[64,1152]{1,0:T(8,128)(2,1)S(1)} %get-tuple-element.44._), channel_id=1, source_target_pairs={{0,24},{2,30},{4,28},{6,26},{8,0},{10,6},{12,4},{14,2},{16,8},{18,... | collective-permute-start | bytes 442376 | tf_op jit(solution)/shard_map/ppermute | solution.py:366
  24.5 0.0 collective-permute-start.8
  24.5 2.1 %self_backward_0.1 = (bf16[128,4096]{1,0:T(8,128)(2,1)}, bf16[64,1024]{1,0:T(8,128)(2,1)S(1)}, f32[64,1024]{1,0:T(8,128)S(1)}) custom-call(bf16[128,4096]{1,0:T(8,128)(2,1)S(1)} %bitcast.12, bf16[128,1024]{1,0:T(8,128)(2,1)S(1)} %bitcast.16, bf16[64,1024]{1,0:T(8,128)(2,1)S(1)} %halo.1.__.halo_ref, f32[4,128,512]{2,1,0:T(8,128)S(1)} %get-tuple-element.41.weights_ref, ...), custom_call_target="tpu_custom_call" | custom-call | flops 1000000 | bytes 100000 | tf_op jit(solution)/shard_map/self_backward_0/pallas_call | solution.py:449
  26.6 2.1 %self_backward_1.1 = (bf16[128,4096]{1,0:T(8,128)(2,1)}, f32[64,1024]{1,0:T(8,128)S(1)}, f32[64,1024]{1,0:T(8,128)S(1)}) custom-call(bf16[128,4096]{1,0:T(8,128)(2,1)S(1)} %bitcast.13, bf16[128,1024]{1,0:T(8,128)(2,1)S(1)} %bitcast.17, bf16[64,1024]{1,0:T(8,128)(2,1)S(1)} %get-tuple-element.32.halo_ref, ...), custom_call_target="tpu_custom_call", output_to_operand_aliasing={{0}: (5, {})} | custom-call | flops 1000000 | bytes 100000 | tf_op jit(solution)/shard_map/self_backward_1/pallas_call | solution.py:449
  28.7 0.2 collective-permute-done.8.x_ref
  28.9 0.0 collective-permute-done.9.z_ref
  29.0 0.1 chip_sum.1
  29.0 0.9 %collective-permute-start.10 = (f32[64,1152]{1,0:T(8,128)S(1)}, f32[64,1152]{1,0:T(8,128)S(1)}, u32[]{:S(2)}, u32[]{:S(2)}) collective-permute-start(f32[64,1152]{1,0:T(8,128)S(1)} %get-tuple-element.53._.mine_ref), channel_id=1, source_target_pairs={{0,2},{2,0},{4,6},{6,4},{8,10},{10,8},{12,14},{14,12},{16,18},{18,... | collective-permute-start | bytes 884744 | tf_op jit(solution)/shard_map/ppermute | solution.py:366
  29.9 1.5 %collective-permute-start.12 = (bf16[64,1024]{1,0:T(8,128)(2,1)S(1)}, bf16[64,1024]{1,0:T(8,128)(2,1)S(1)}, u32[]{:S(2)}, u32[]{:S(2)}) collective-permute-start(bf16[64,1024]{1,0:T(8,128)(2,1)S(1)} %get-tuple-element.56), channel_id=1, source_target_pairs={{0,1},{1,0},{2,4},{3,5},{4,2},{5,3},{6,8},{7,9},{8,6},{9,7},{10,12... | collective-permute-start | bytes 393224 | tf_op jit(solution)/shard_map/ppermute | solution.py:370
  31.5 0.0 collective-permute-start.11
  31.5 0.0 collective-permute-done.10.pair_ref
  31.5 1.2 %collective-permute-start.13 = (f32[16,128]{1,0:T(8,128)S(1)}, f32[16,128]{1,0:T(8,128)S(1)}, u32[]{:S(2)}, u32[]{:S(2)}) collective-permute-start(f32[16,128]{1,0:T(8,128)S(1)} %gate_sum.1._.one_ref), channel_id=1, source_target_pairs={{0,1},{1,0},{2,3},{3,2},{4,5},{5,4},{6,7},{7,6},{8,9},{9,8},{10,11... | collective-permute-start | bytes 24584 | tf_op jit(solution)/shard_map/ppermute | solution.py:370
  32.7 2.5 %collective-permute-done.13.other_ref = f32[16,128]{1,0:T(8,128)S(1)} collective-permute-done((f32[16,128]{1,0:T(8,128)S(1)}, f32[16,128]{1,0:T(8,128)S(1)}, u32[]{:S(2)}, u32[]{:S(2)}) %collective-permute-start.13) | collective-permute-done | bytes 8224 | tf_op jit(solution)/shard_map/ppermute | solution.py:370
  35.2 1.1 %collective-permute-start.14 = (f32[16,128]{1,0:T(8,128)S(1)}, f32[16,128]{1,0:T(8,128)S(1)}, u32[]{:S(2)}, u32[]{:S(2)}) collective-permute-start(f32[16,128]{1,0:T(8,128)S(1)} %gate_docs.1.one_ref), channel_id=1, source_target_pairs={{0,16},{1,17},{2,18},{3,19},{4,20},{5,21},{6,22},{7,23},{8,24},{9,... | collective-permute-start | bytes 24584 | tf_op jit(solution)/shard_map/ppermute | solution.py:370
  36.3 0.0 collective-permute-done.12.other_ref
  36.3 0.0 collective-permute-done.11.chip_ref
  36.3 0.8 %finish.1 = (bf16[64,1024]{1,0:T(8,128)(2,1)}, bf16[128,1024]{1,0:T(8,128)(2,1)}) custom-call(s32[8,128]{1,0:T(8,128)S(1)} %get-tuple-element.35.off_ref, f32[64,1024]{1,0:T(8,128)S(1)} %get-tuple-element.47.own_ref, f32[64,1152]{1,0:T(8,128)S(1)} %get-tuple-element.53._.mine_ref, f32[64,1152]{1,0:T(8,128)S(1)} %collective-permute-done.10.pair_ref, ...), custom_call_target="tpu_custom_call" | custom-call | flops 1000000 | bytes 1000000 | tf_op jit(solution)/shard_map/finish/pallas_call | solution.py:476
  37.2 2.6 %collective-permute-done.14.other_ref = f32[16,128]{1,0:T(8,128)S(1)} collective-permute-done((f32[16,128]{1,0:T(8,128)S(1)}, f32[16,128]{1,0:T(8,128)S(1)}, u32[]{:S(2)}, u32[]{:S(2)}) %collective-permute-start.14) | collective-permute-done | bytes 8224 | tf_op jit(solution)/shard_map/ppermute | solution.py:370
  39.8 0.6 %gate_grad.1 = f32[1,32]{1,0:T(1,128)} custom-call(f32[16,128]{1,0:T(8,128)S(1)} %gate_docs.1.one_ref, f32[16,128]{1,0:T(8,128)S(1)} %collective-permute-done.14.other_ref, f32[32,128]{1,0:T(8,128)S(1)} %broadcast_in_dim.15.gate_ref), custom_call_target="tpu_custom_call" | custom-call | flops 1000000 | bytes 1000000 | tf_op jit(solution)/shard_map/gate_grad/pallas_call | solution.py:490
  (14 shorter events, 0.1 us)
Async XLA Ops:
  0.6 2.2 %collective-permute-start = (s32[1,1]{1,0:T(1,128)}, s32[1,1]{1,0:T(1,128)}, u32[]{:S(2)}, u32[]{:S(2)}) collective-permute-start(s32[1,1]{1,0:T(1,128)} %param.11), channel_id=1, source_target_pairs={{0,2},{2,0},{4,6},{6,4},{8,10},{10,8},{12,14},{14,12},{16,18},{18,... | collective-permute-start | bytes 20 | tf_op jit(solution)/shard_map/ppermute | solution.py:366
  1.1 1.7 %collective-permute-start.1 = (bf16[64,1024]{1,0:T(8,128)(2,1)}, bf16[64,1024]{1,0:T(8,128)(2,1)S(1)}, u32[]{:S(2)}, u32[]{:S(2)}) collective-permute-start(bf16[64,1024]{1,0:T(8,128)(2,1)} %bitcast.19), channel_id=1, source_target_pairs={{0,2},{2,0},{4,6},{6,4},{8,10},{10,8},{12,14},{14,12},{16,18},{18,... | collective-permute-start | bytes 393224 | tf_op jit(solution)/shard_map/ppermute | solution.py:366
  1.9 1.0 %copy-start.4 = (bf16[1,1,64,1024]{3,2,1,0:T(8,128)(2,1)S(1)}, bf16[1,1,64,1024]{3,2,1,0:T(8,128)(2,1)}, u32[]{:S(2)}) copy-start(bf16[1,1,64,1024]{3,2,1,0:T(8,128)(2,1)} %param.10) | copy-start | bytes 393220
  2.8 7.0 %copy-start.2 = (bf16[1,128,1024]{2,1,0:T(8,128)(2,1)S(1)}, bf16[1,128,1024]{2,1,0:T(8,128)(2,1)}, u32[]{:S(2)}) copy-start(bf16[1,128,1024]{2,1,0:T(8,128)(2,1)} %param.8) | copy-start | bytes 786436
  3.6 11.3 %collective-permute-start.4 = (bf16[64,1152]{1,0:T(8,128)(2,1)S(1)}, bf16[64,1152]{1,0:T(8,128)(2,1)S(1)}, u32[]{:S(2)}, u32[]{:S(2)}) collective-permute-start(bf16[64,1152]{1,0:T(8,128)(2,1)S(1)} %get-tuple-element.36), channel_id=1, source_target_pairs={{0,8},{2,14},{4,12},{6,10},{8,16},{10,22},{12,20},{14,18},{16,24},... | collective-permute-start | bytes 442376 | tf_op jit(solution)/shard_map/ppermute | solution.py:366
  6.7 6.4 %collective-permute-start.3 = (bf16[64,1024]{1,0:T(8,128)(2,1)S(1)}, bf16[64,1024]{1,0:T(8,128)(2,1)S(1)}, u32[]{:S(2)}, u32[]{:S(2)}) collective-permute-start(bf16[64,1024]{1,0:T(8,128)(2,1)S(1)} %get-tuple-element.32.halo_ref), channel_id=1, source_target_pairs={{0,1},{1,0},{2,4},{3,5},{4,2},{5,3},{6,8},{7,9},{8,6},{9,7},{10,12... | collective-permute-start | bytes 393224 | tf_op jit(solution)/shard_map/ppermute | solution.py:370
  8.2 4.9 %collective-permute-start.2 = (bf16[64,1024]{1,0:T(8,128)(2,1)S(1)}, bf16[64,1024]{1,0:T(8,128)(2,1)S(1)}, u32[]{:S(2)}, u32[]{:S(2)}) collective-permute-start(bf16[64,1024]{1,0:T(8,128)(2,1)S(1)} %get-tuple-element.32.halo_ref), channel_id=1, source_target_pairs={{0,2},{2,0},{4,6},{6,4},{8,10},{10,8},{12,14},{14,12},{16,18},{18,... | collective-permute-start | bytes 393224 | tf_op jit(solution)/shard_map/ppermute | solution.py:366
  8.3 6.7 %collective-permute-start.5 = (bf16[64,512]{1,0:T(8,128)(2,1)S(1)}, bf16[64,512]{1,0:T(8,128)(2,1)S(1)}, u32[]{:S(2)}, u32[]{:S(2)}) collective-permute-start(bf16[64,512]{1,0:T(8,128)(2,1)S(1)} %get-tuple-element.37), channel_id=1, source_target_pairs={{0,4},{2,6},{4,0},{6,2},{8,12},{10,14},{12,8},{14,10},{16,20},{18,... | collective-permute-start | bytes 196616 | tf_op jit(solution)/shard_map/ppermute | solution.py:366
  9.8 0.7 %copy-start.5 = (s32[1,128]{1,0:T(1,128)S(1)}, s32[1,128]{1,0:T(1,128)}, u32[]{:S(2)}) copy-start(s32[1,128]{1,0:T(1,128)} %segment_ref.3) | copy-start | bytes 1540
  10.5 1.2 %copy-start = (bf16[1,128,4096]{2,1,0:T(8,128)(2,1)S(1)}, bf16[1,128,4096]{2,1,0:T(8,128)(2,1)}, u32[]{:S(2)}) copy-start(bf16[1,128,4096]{2,1,0:T(8,128)(2,1)} %param.7) | copy-start | bytes 3145732
  13.1 2.6 %copy-start.1 = (bf16[1,128,4096]{2,1,0:T(8,128)(2,1)S(1)}, bf16[1,128,4096]{2,1,0:T(8,128)(2,1)}, u32[]{:S(2)}) copy-start(bf16[1,128,4096]{2,1,0:T(8,128)(2,1)} %param.7) | copy-start | bytes 3145732
  14.9 0.7 %copy-start.6 = (f32[32]{0:T(128)S(1)}, f32[32]{0:T(128)}, u32[]{:S(2)}) copy-start(f32[32]{0:T(128)} %param.12) | copy-start | bytes 388
  15.0 2.1 %copy-start.3 = (bf16[1,128,4096]{2,1,0:T(8,128)(2,1)S(1)}, bf16[1,128,4096]{2,1,0:T(8,128)(2,1)}, u32[]{:S(2)}) copy-start(bf16[1,128,4096]{2,1,0:T(8,128)(2,1)} %param.13) | copy-start | bytes 3145732
  15.0 2.0 %collective-permute-start.6 = (bf16[64,1664]{1,0:T(8,128)(2,1)S(1)}, bf16[64,1664]{1,0:T(8,128)(2,1)S(1)}, u32[]{:S(2)}, u32[]{:S(2)}) collective-permute-start(bf16[64,1664]{1,0:T(8,128)(2,1)S(1)} %arrived.1._.mine_ref), channel_id=1, source_target_pairs={{0,2},{2,0},{4,6},{6,4},{8,10},{10,8},{12,14},{14,12},{16,18},{18,... | collective-permute-start | bytes 638984 | tf_op jit(solution)/shard_map/ppermute | solution.py:366
  19.6 1.6 %collective-permute-start.7 = (f32[64,1152]{1,0:T(8,128)S(1)}, f32[64,1152]{1,0:T(8,128)S(1)}, u32[]{:S(2)}, u32[]{:S(2)}) collective-permute-start(f32[64,1152]{1,0:T(8,128)S(1)} %get-tuple-element.42.mine_ref), channel_id=1, source_target_pairs={{0,2},{2,0},{4,6},{6,4},{8,10},{10,8},{12,14},{14,12},{16,18},{18,... | collective-permute-start | bytes 884744 | tf_op jit(solution)/shard_map/ppermute | solution.py:366
  21.3 7.6 %collective-permute-start.9 = (bf16[64,1152]{1,0:T(8,128)(2,1)S(1)}, bf16[64,1152]{1,0:T(8,128)(2,1)S(1)}, u32[]{:S(2)}, u32[]{:S(2)}) collective-permute-start(bf16[64,1152]{1,0:T(8,128)(2,1)S(1)} %get-tuple-element.44._), channel_id=1, source_target_pairs={{0,24},{2,30},{4,28},{6,26},{8,0},{10,6},{12,4},{14,2},{16,8},{18,... | collective-permute-start | bytes 442376 | tf_op jit(solution)/shard_map/ppermute | solution.py:366
  24.5 4.4 %collective-permute-start.8 = (bf16[64,640]{1,0:T(8,128)(2,1)S(1)}, bf16[64,640]{1,0:T(8,128)(2,1)S(1)}, u32[]{:S(2)}, u32[]{:S(2)}) collective-permute-start(bf16[64,640]{1,0:T(8,128)(2,1)S(1)} %get-tuple-element.49), channel_id=1, source_target_pairs={{0,4},{2,6},{4,0},{6,2},{8,12},{10,14},{12,8},{14,10},{16,20},{18,... | collective-permute-start | bytes 245768 | tf_op jit(solution)/shard_map/ppermute | solution.py:366
  29.0 2.4 %collective-permute-start.10 = (f32[64,1152]{1,0:T(8,128)S(1)}, f32[64,1152]{1,0:T(8,128)S(1)}, u32[]{:S(2)}, u32[]{:S(2)}) collective-permute-start(f32[64,1152]{1,0:T(8,128)S(1)} %get-tuple-element.53._.mine_ref), channel_id=1, source_target_pairs={{0,2},{2,0},{4,6},{6,4},{8,10},{10,8},{12,14},{14,12},{16,18},{18,... | collective-permute-start | bytes 884744 | tf_op jit(solution)/shard_map/ppermute | solution.py:366
  29.9 6.3 %collective-permute-start.12 = (bf16[64,1024]{1,0:T(8,128)(2,1)S(1)}, bf16[64,1024]{1,0:T(8,128)(2,1)S(1)}, u32[]{:S(2)}, u32[]{:S(2)}) collective-permute-start(bf16[64,1024]{1,0:T(8,128)(2,1)S(1)} %get-tuple-element.56), channel_id=1, source_target_pairs={{0,1},{1,0},{2,4},{3,5},{4,2},{5,3},{6,8},{7,9},{8,6},{9,7},{10,12... | collective-permute-start | bytes 393224 | tf_op jit(solution)/shard_map/ppermute | solution.py:370
  31.5 4.8 %collective-permute-start.11 = (bf16[64,1024]{1,0:T(8,128)(2,1)S(1)}, bf16[64,1024]{1,0:T(8,128)(2,1)S(1)}, u32[]{:S(2)}, u32[]{:S(2)}) collective-permute-start(bf16[64,1024]{1,0:T(8,128)(2,1)S(1)} %get-tuple-element.56), channel_id=1, source_target_pairs={{0,2},{2,0},{4,6},{6,4},{8,10},{10,8},{12,14},{14,12},{16,18},{18,... | collective-permute-start | bytes 393224 | tf_op jit(solution)/shard_map/ppermute | solution.py:366
  31.5 3.7 %collective-permute-start.13 = (f32[16,128]{1,0:T(8,128)S(1)}, f32[16,128]{1,0:T(8,128)S(1)}, u32[]{:S(2)}, u32[]{:S(2)}) collective-permute-start(f32[16,128]{1,0:T(8,128)S(1)} %gate_sum.1._.one_ref), channel_id=1, source_target_pairs={{0,1},{1,0},{2,3},{3,2},{4,5},{5,4},{6,7},{7,6},{8,9},{9,8},{10,11... | collective-permute-start | bytes 24584 | tf_op jit(solution)/shard_map/ppermute | solution.py:370
  35.2 4.5 %collective-permute-start.14 = (f32[16,128]{1,0:T(8,128)S(1)}, f32[16,128]{1,0:T(8,128)S(1)}, u32[]{:S(2)}, u32[]{:S(2)}) collective-permute-start(f32[16,128]{1,0:T(8,128)S(1)} %gate_docs.1.one_ref), channel_id=1, source_target_pairs={{0,16},{1,17},{2,18},{3,19},{4,20},{5,21},{6,22},{7,23},{8,24},{9,... | collective-permute-start | bytes 24584 | tf_op jit(solution)/shard_map/ppermute | solution.py:370

commit v3 on v2

--- a/solution.py
+++ b/solution.py
@@ -226,7 +226,7 @@
     mask_ref[...] = jnp.where(row == 0, by_mine.astype(jnp.float32) * (1.0 - from_x), from_x)
 
 
-def outside_kernel(mine_ref, pair_ref, mask_ref, to_z_ref, to_x_ref, gate_ref):
+def outside_kernel(mine_ref, pair_ref, mask_ref, _, to_z_ref, to_x_ref, gate_ref):
     width = mine_ref.shape[1] - LANES
     total = mine_ref[...] + pair_ref[...]
     gate = total[: gate_ref.shape[0], width:]
@@ -240,7 +240,8 @@
     gate_ref[...] = gate
 
 
-def chip_sum_kernel(mine_ref, x_ref, z_ref, gate_ref, halo_ref, _, out_ref, gate_out, halo_out):
+def chip_sum_kernel(mine_ref, x_ref, z_ref, gate_ref, *refs):
+    *gates, halo_ref, _, out_ref, gate_out, halo_out = refs
     halo_out[...] = halo_ref[...]
     width = mine_ref.shape[1]
     odd = odd_core().astype(jnp.float32)
@@ -250,13 +251,15 @@
     out_ref[:, half:width] = mine_ref[:, half:] + (from_x * odd + z_ref[:, half:width].astype(jnp.float32))
     gate_out[...] = gate_ref[...] + unsplit(x_ref[:, half:])
     gate = unsplit(z_ref[:, width:])
+    for ref in gates:
+        gate = gate + ref[...]
     out_ref[:, width:] = jnp.concatenate([gate] * (mine_ref.shape[0] // gate.shape[0]), axis=0)
 
 
 def self_back_kernel(
-    query_ref, context_ref, halo_ref, weights_ref, grad_ref, _,
-    query_grad_ref, key_low_ref, key_high_ref, rows_out, sems, *, block, groups, repeat
+    query_ref, context_ref, halo_ref, weights_ref, grad_ref, *refs, block, groups, repeat
 ):
+    query_grad_ref, key_low_ref, key_high_ref, rows_out, sems = refs[-5:]
     copies = []
     half = repeat * WINDOW
     for g in range(groups):
@@ -295,10 +298,6 @@
     out_ref[...] = chip_ref[...] + (mine_ref[:rows, width:] + pair_ref[:rows, width:])
 
 
-def add_kernel(one_ref, other_ref, out_ref):
-    out_ref[...] = one_ref[...] + other_ref[...]
-
-
 def gate_grad_kernel(one_ref, other_ref, gate_ref, out_ref):
     rows, heads = one_ref.shape[0], out_ref.shape[1]
     total = one_ref[...] + other_ref[...]
@@ -436,16 +435,8 @@
         scratch=[pltpu.VMEM((img, width), bf16)],
     )(off, gate_rows, *self_out, grad, own, chip, arrived, by_pair)
     from_pair = send(to_pair, lambda i: i ^ 1)
-    to_z, to_x, gate_chip = call(
-        "outside",
-        outside_kernel,
-        [struct((img, width + LANES), bf16), struct((img, width // 2 + LANES), bf16), gate_shape],
-        [VMEM] * 3,
-    )(to_pair, from_pair, masks)
-    from_z = send_z(to_z, -1)
-    from_x = send(to_x, lambda i: i ^ 2)
-
-    def self_backward(block, after):
+
+    def self_backward(block, after, late=None):
         return call(
             f"self_backward_{block}",
             functools.partial(self_back_kernel, block=block, groups=groups, repeat=repeat),
@@ -454,41 +445,49 @@
                 struct((WINDOW, width), f32 if block else bf16),
                 struct((WINDOW, width), f32),
             ],
-            [VMEM] * 5 + [ANY],
+            [VMEM] * 5 + [ANY] * (1 if late is None else 2),
             scratch=[pltpu.VMEM((WINDOW, model), bf16), pltpu.SemaphoreType.DMA((groups,))],
             out_specs=[ANY, VMEM, VMEM],
             aliases={5: 0} if block else None,
             flops=10**6,
             moved=10**5,
-        )(q, ctx, tail if block else halo, kept[block], grad_self, after)
-
-    query_grad, halo_terms, low = self_backward(0, to_z)
-    query_grad, also, high = self_backward(1, query_grad)
-    mine, gate_near, halo_terms = call(
+        )(q, ctx, tail if block else halo, kept[block], grad_self, after, *([] if late is None else [late]))
+
+    query_grad, halo_terms, low = self_backward(0, to_pair)
+    to_z, to_x, gate = call(
+        "outside",
+        outside_kernel,
+        [struct((img, width + LANES), bf16), struct((img, width // 2 + LANES), bf16), gate_shape],
+        [VMEM] * 3 + [ANY],
+    )(to_pair, from_pair, masks, halo_terms)
+    from_z = send_z(to_z, -1)
+    from_x = send(to_x, lambda i: i ^ 2)
+    gates = []
+    if swaps:
+        gates = [send_z(gate, 1), send_z(gate, 2)]
+    query_grad, also, high = self_backward(1, query_grad, to_z)
+    mine, gate, halo_terms = call(
         "chip_sum",
         chip_sum_kernel,
         [struct((img, width + LANES), f32), gate_shape, window],
-        [VMEM] * 5 + [ANY],
-    )(in_chip, from_x, from_z, gate_chip, halo_terms, high)
+        [VMEM] * (5 + len(gates)) + [ANY],
+    )(in_chip, from_x, from_z, gate, *gates, halo_terms, high)
     other = send(mine, lambda i: i ^ 1)
     halo_back = merge("halo_back", send_near(halo_terms, -1), -1, mine)
-    gate_sum = call("gate_sum", gate_kernel, [gate_shape], [VMEM] * 3)(gate_near, mine, other)[0]
+    gate = call("gate_sum", gate_kernel, [gate_shape], [VMEM] * 3)(gate, mine, other)[0]
     memory_grad, context_grad = call(
         "finish",
         functools.partial(finish_kernel, tok_rows=tok_rows),
         [image, struct((tok_rows, width), bf16)],
         [VMEM] * 8 + [ANY],
-    )(off, own_terms, mine, other, low, also, high, halo_back, gate_sum)
+    )(off, own_terms, mine, other, low, also, high, halo_back, gate)
 
     if not swaps:
         gate_total = lax.psum(to_pair[: gate_shape.shape[0], width:], ("seq", "dp"))
         gate_grad = (1.0 - gate_tanh * gate_tanh) * jnp.sum(gate_total.reshape(heads, WINDOW), axis=1)
         return (query_grad[None], context_grad[None], memory_grad[None, None], gate_grad)
-    gate_sum = call("gate_docs", add_kernel, [gate_shape], [VMEM] * 2)(
-        gate_sum, send_all(gate_sum, lambda s, d: (s, d ^ 1))
-    )[0]
     gate_grad = call("gate_grad", gate_grad_kernel, [struct((1, heads), f32)], [VMEM] * 3)(
-        gate_sum, send_all(gate_sum, lambda s, d: (s ^ 2 * GAP, d)), gate_rows
+        gate, send_all(gate, lambda s, d: (s, d ^ 1)), gate_rows
     )[0].reshape(heads)
     return (query_grad[None], context_grad[None], memory_grad[None, None], gate_grad)
 

time: 40.6 us -> 39 us (0.961)
  waiting for transfers between devices: 8.69 us -> 5.73 us
  starting transfers between devices: 14.8 us -> 16.1 us
    ppermute x4 -> x3, waiting for transfers between devices: 5.09 us -> 2.14 us  [send_all(): lax.ppermute(value, ('seq', 'dp'), [(s * dp + d, t * dp + e) for s, d, t,...]
    ppermute x11 -> x13, starting transfers between devices: 9.5 us -> 11.7 us  [send(): return lax.ppermute(value, 'seq', [(i, where(i)) for i in range(seq)])]
    ppermute x4 -> x3, starting transfers between devices: 5.33 us -> 4.42 us  [send_all(): lax.ppermute(value, ('seq', 'dp'), [(s * dp + d, t * dp + e) for s, d, t,...]
    ppermute x11 -> x13, waiting for transfers between devices: 3.6 us -> 3.59 us  [send(): return lax.ppermute(value, 'seq', [(i, where(i)) for i in range(seq)])]
  transfers between devices with their start and end apart: 15 -> 16, of which waited for: 5 -> 3; matrix products, arithmetic and copies ran while one was open for 2% -> 2% of each run, Pallas kernels for 19% -> 20%
where the time goes in v3:
time: 39 us; the launch traced here: 38.8 us
  starting transfers between devices  16.1 us (41%)
  Pallas kernels  12 us (31%)
  waiting for transfers between devices  5.73 us (15%)
  local copies, waits for them, and re-layouts  3.47 us (9%)
  between operations  1.49 us (4%)
    ppermute x13, starting transfers between devices, send(): return lax.ppermute(value, 'seq', [(i, where(i)) for i in range(seq)])  11.7 us
    ppermute x3, starting transfers between devices, send_all(): lax.ppermute(value, ('seq', 'dp'), [(s * dp + d, t * dp + e) for s, d, t,...  4.42 us
    pallas_call x2, Pallas kernels, self_backward(): call(f'self_backward_{block}', functools.partial(self_back_kernel, block=...  4.21 us
    ppermute x13, waiting for transfers between devices, send(): return lax.ppermute(value, 'seq', [(i, where(i)) for i in range(seq)])  3.59 us
    pallas_call x2, Pallas kernels, self_forward(): call(f'self_forward_{block}', functools.partial(self_kernel, block=block,...  2.7 us
    pallas_call x1, Pallas kernels, on_device(): call('cross', functools.partial(cross_kernel, groups=groups, repeat=repea...  2.56 us
    unnamed x14, local copies, waits for them, and re-layouts  2.44 us
    ppermute x3, waiting for transfers between devices, send_all(): lax.ppermute(value, ('seq', 'dp'), [(s * dp + d, t * dp + e) for s, d, t,...  2.14 us
  transfers between devices with their start and end apart: 16, of which 3 were waited for; matrix products, arithmetic and copies ran while one was open for 2% of the time, Pallas kernels for 20%

profile of v3, /device:TPU:0, one launch (start us, length us, event | category | flops | bytes accessed | tf_op | source)
XLA Modules:
  0.0 38.8 jit_solution(8953017412367838857)
XLA Ops:
  0.6 0.5 %collective-permute-start = (s32[1,1]{1,0:T(1,128)}, s32[1,1]{1,0:T(1,128)}, u32[]{:S(2)}, u32[]{:S(2)}) collective-permute-start(s32[1,1]{1,0:T(1,128)} %param.11), channel_id=1, source_target_pairs={{0,2},{2,0},{4,6},{6,4},{8,10},{10,8},{12,14},{14,12},{16,18},{18,... | collective-permute-start | bytes 20 | tf_op jit(solution)/shard_map/ppermute | solution.py:365
  1.1 0.1 collective-permute-start.1
  1.9 1.0 %slice_bitcast_fusion.tail_ref = bf16[64,1024]{1,0:T(8,128)(2,1)S(1)} fusion(bf16[1,128,1024]{2,1,0:T(8,128)(2,1)} %param.8), kind=kLoop, calls=%fused_computation | loop fusion | bytes 262144 | tf_op jit(solution)/shard_map/slice | solution.py:393
  2.8 0.0 copy-start.2
  2.9 0.0 collective-permute-done.pair_off_ref
  2.9 0.0 collective-permute-done.1.other_ref
  2.9 0.8 %chip_image.1 = (bf16[64,1024]{1,0:T(8,128)(2,1)S(1)}, bf16[64,1152]{1,0:T(8,128)(2,1)S(1)}, bf16[64,512]{1,0:T(8,128)(2,1)S(1)}, bf16[64,1024]{1,0:T(8,128)(2,1)S(1)}, s32[8,128]{1,0:T(8,128)S(1)}) custom-call(s32[1,1]{1,0:T(1,128)S(6)} %copy.13.off_ref, s32[1,1]{1,0:T(1,128)} %collective-permute-done.pair_off_ref, bf16[64,1024]{1,0:T(8,128)(2,1)S(1)} %bitcast.20, ...), custom_call_target="tpu_custom_call" | custom-call | flops 1000000 | bytes 1000000 | tf_op jit(solution)/shard_map/chip_image/pallas_call | solution.py:394
  3.7 3.1 %collective-permute-start.4 = (bf16[64,1152]{1,0:T(8,128)(2,1)S(1)}, bf16[64,1152]{1,0:T(8,128)(2,1)S(1)}, u32[]{:S(2)}, u32[]{:S(2)}) collective-permute-start(bf16[64,1152]{1,0:T(8,128)(2,1)S(1)} %get-tuple-element.36), channel_id=1, source_target_pairs={{0,8},{2,14},{4,12},{6,10},{8,16},{10,22},{12,20},{14,18},{16,24},... | collective-permute-start | bytes 442376 | tf_op jit(solution)/shard_map/ppermute | solution.py:365
  6.7 1.5 %collective-permute-start.3 = (bf16[64,1024]{1,0:T(8,128)(2,1)S(1)}, bf16[64,1024]{1,0:T(8,128)(2,1)S(1)}, u32[]{:S(2)}, u32[]{:S(2)}) collective-permute-start(bf16[64,1024]{1,0:T(8,128)(2,1)S(1)} %get-tuple-element.32.halo_ref), channel_id=1, source_target_pairs={{0,1},{1,0},{2,4},{3,5},{4,2},{5,3},{6,8},{7,9},{8,6},{9,7},{10,12... | collective-permute-start | bytes 393224 | tf_op jit(solution)/shard_map/ppermute | solution.py:369
  8.3 0.1 collective-permute-start.2
  8.4 1.5 %collective-permute-start.5 = (bf16[64,512]{1,0:T(8,128)(2,1)S(1)}, bf16[64,512]{1,0:T(8,128)(2,1)S(1)}, u32[]{:S(2)}, u32[]{:S(2)}) collective-permute-start(bf16[64,512]{1,0:T(8,128)(2,1)S(1)} %get-tuple-element.37), channel_id=1, source_target_pairs={{0,4},{2,6},{4,0},{6,2},{8,12},{10,14},{12,8},{14,10},{16,20},{18,... | collective-permute-start | bytes 196616 | tf_op jit(solution)/shard_map/ppermute | solution.py:365
  9.9 0.7 %copy-done.5 = s32[1,128]{1,0:T(1,128)S(1)} copy-done((s32[1,128]{1,0:T(1,128)S(1)}, s32[1,128]{1,0:T(1,128)}, u32[]{:S(2)}) %copy-start.5) | copy-done | bytes 536
  10.6 1.2 %copy-done = bf16[1,128,4096]{2,1,0:T(8,128)(2,1)S(1)} copy-done((bf16[1,128,4096]{2,1,0:T(8,128)(2,1)S(1)}, bf16[1,128,4096]{2,1,0:T(8,128)(2,1)}, u32[]{:S(2)}) %copy-start) | copy-done | bytes 1048600
  11.8 1.3 %self_forward_1.1 = (bf16[4,128,512]{2,1,0:T(8,128)(2,1)S(1)}, f32[4,128,512]{2,1,0:T(8,128)S(1)}) custom-call(bf16[128,4096]{1,0:T(8,128)(2,1)S(1)} %bitcast.10, bf16[128,1024]{1,0:T(8,128)(2,1)S(1)} %bitcast.14, bf16[64,1024]{1,0:T(8,128)(2,1)S(1)} %get-tuple-element.32.halo_ref, s32[1,128]{1,0:T(1,128)S(1)} %copy-done.5, ...), custom_call_target="tpu_custom_call" | custom-call | flops 1000000 | bytes 100000 | tf_op jit(solution)/shard_map/self_forward_1/pallas_call | solution.py:406
  13.1 0.0 copy-start.1
  13.1 0.0 collective-permute-done.3.other_ref
  13.2 0.0 collective-permute-done.2.chip_ref
  13.2 1.8 %collective-permute-done.5.x_ref = bf16[64,512]{1,0:T(8,128)(2,1)S(1)} collective-permute-done((bf16[64,512]{1,0:T(8,128)(2,1)S(1)}, bf16[64,512]{1,0:T(8,128)(2,1)S(1)}, u32[]{:S(2)}, u32[]{:S(2)}) %collective-permute-start.5) | collective-permute-done | bytes 65568 | tf_op jit(solution)/shard_map/ppermute | solution.py:365
  15.0 0.0 collective-permute-done.4.z_ref
  15.0 0.0 copy-start.3
  15.1 0.1 collective-permute-start.6
  15.1 0.5 %copy-done.6 = f32[32]{0:T(128)S(1)} copy-done((f32[32]{0:T(128)S(1)}, f32[32]{0:T(128)}, u32[]{:S(2)}) %copy-start.6) | copy-done | bytes 152
  15.7 1.4 %self_forward_0.1 = (bf16[4,128,512]{2,1,0:T(8,128)(2,1)S(1)}, f32[4,128,512]{2,1,0:T(8,128)S(1)}) custom-call(bf16[128,4096]{1,0:T(8,128)(2,1)S(1)} %bitcast.11, bf16[128,1024]{1,0:T(8,128)(2,1)S(1)} %bitcast.15, bf16[64,1024]{1,0:T(8,128)(2,1)S(1)} %halo.1.__.halo_ref, s32[1,128]{1,0:T(1,128)S(1)} %copy-done.5, bf16[64,1664]{1,0:T(8,128)(2,1)S(1)} %arrived.1._.mine_ref), custom_call_target="tpu_custom_call" | custom-call | flops 1000000 | bytes 100000 | tf_op jit(solution)/shard_map/self_forward_0/pallas_call | solution.py:406
  17.0 0.0 collective-permute-done.6.pair_ref
  17.1 0.1 broadcast_in_dim.15.gate_ref
  17.1 2.6 %cross.1 = (bf16[4,1024,128]{2,1,0:T(8,128)(2,1)S(1)}, f32[64,1152]{1,0:T(8,128)S(1)}, f32[64,1024]{1,0:T(8,128)S(1)}, f32[64,1024]{1,0:T(8,128)S(1)}, f32[8,128]{1,0:T(8,128)S(1)}) custom-call(s32[8,128]{1,0:T(8,128)S(1)} %get-tuple-element.35.off_ref, f32[32,128]{1,0:T(8,128)S(1)} %broadcast_in_dim.15.gate_ref, ...), custom_call_target="tpu_custom_call" | custom-call | flops 1000000 | bytes 1000000 | tf_op jit(solution)/shard_map/cross/pallas_call | solution.py:424
  19.7 0.1 collective-permute-start.7
  19.8 2.1 %self_backward_0.1 = (bf16[128,4096]{1,0:T(8,128)(2,1)}, bf16[64,1024]{1,0:T(8,128)(2,1)S(1)}, f32[64,1024]{1,0:T(8,128)S(1)}) custom-call(bf16[128,4096]{1,0:T(8,128)(2,1)S(1)} %bitcast.12, bf16[128,1024]{1,0:T(8,128)(2,1)S(1)} %bitcast.16, bf16[64,1024]{1,0:T(8,128)(2,1)S(1)} %halo.1.__.halo_ref, f32[4,128,512]{2,1,0:T(8,128)S(1)} %get-tuple-element.41.weights_ref, ...), custom_call_target="tpu_custom_call" | custom-call | flops 1000000 | bytes 100000 | tf_op jit(solution)/shard_map/self_backward_0/pallas_call | solution.py:440
  21.9 0.0 collective-permute-done.7.pair_ref
  21.9 0.1 outside.1
  22.0 3.2 %collective-permute-start.9 = (bf16[64,1152]{1,0:T(8,128)(2,1)S(1)}, bf16[64,1152]{1,0:T(8,128)(2,1)S(1)}, u32[]{:S(2)}, u32[]{:S(2)}) collective-permute-start(bf16[64,1152]{1,0:T(8,128)(2,1)S(1)} %get-tuple-element.46.refs_1_), channel_id=1, source_target_pairs={{0,24},{2,30},{4,28},{6,26},{8,0},{10,6},{12,4},{14,2},{16,8},{18,... | collective-permute-start | bytes 442376 | tf_op jit(solution)/shard_map/ppermute | solution.py:365
  25.2 0.0 collective-permute-start.8
  25.2 1.3 %collective-permute-start.11 = (f32[16,128]{1,0:T(8,128)S(1)}, f32[16,128]{1,0:T(8,128)S(1)}, u32[]{:S(2)}, u32[]{:S(2)}) collective-permute-start(f32[16,128]{1,0:T(8,128)S(1)} %get-tuple-element.51.gate_ref), channel_id=1, source_target_pairs={{0,16},{2,22},{4,20},{6,18},{8,24},{10,30},{12,28},{14,26},{16,0},... | collective-permute-start | bytes 24584 | tf_op jit(solution)/shard_map/ppermute | solution.py:365
  26.4 1.6 %collective-permute-start.10 = (f32[16,128]{1,0:T(8,128)S(1)}, f32[16,128]{1,0:T(8,128)S(1)}, u32[]{:S(2)}, u32[]{:S(2)}) collective-permute-start(f32[16,128]{1,0:T(8,128)S(1)} %get-tuple-element.51.gate_ref), channel_id=1, source_target_pairs={{0,8},{2,14},{4,12},{6,10},{8,16},{10,22},{12,20},{14,18},{16,24},... | collective-permute-start | bytes 24584 | tf_op jit(solution)/shard_map/ppermute | solution.py:365
  28.0 2.1 %self_backward_1.1 = (bf16[128,4096]{1,0:T(8,128)(2,1)}, f32[64,1024]{1,0:T(8,128)S(1)}, f32[64,1024]{1,0:T(8,128)S(1)}) custom-call(bf16[128,4096]{1,0:T(8,128)(2,1)S(1)} %bitcast.13, bf16[128,1024]{1,0:T(8,128)(2,1)S(1)} %bitcast.17, bf16[64,1024]{1,0:T(8,128)(2,1)S(1)} %get-tuple-element.32.halo_ref, ...), custom_call_target="tpu_custom_call", output_to_operand_aliasing={{0}: (5, {})} | custom-call | flops 1000000 | bytes 100000 | tf_op jit(solution)/shard_map/self_backward_1/pallas_call | solution.py:440
  30.1 1.8 %collective-permute-done.10.refs_0_ = f32[16,128]{1,0:T(8,128)S(1)} collective-permute-done((f32[16,128]{1,0:T(8,128)S(1)}, f32[16,128]{1,0:T(8,128)S(1)}, u32[]{:S(2)}, u32[]{:S(2)}) %collective-permute-start.10) | collective-permute-done | bytes 8224 | tf_op jit(solution)/shard_map/ppermute | solution.py:365
  31.9 0.0 collective-permute-done.8.x_ref
  31.9 0.0 collective-permute-done.9.z_ref
  31.9 0.1 chip_sum.1
  32.0 0.3 collective-permute-start.12
  32.2 1.5 %collective-permute-start.14 = (bf16[64,1024]{1,0:T(8,128)(2,1)S(1)}, bf16[64,1024]{1,0:T(8,128)(2,1)S(1)}, u32[]{:S(2)}, u32[]{:S(2)}) collective-permute-start(bf16[64,1024]{1,0:T(8,128)(2,1)S(1)} %get-tuple-element.56), channel_id=1, source_target_pairs={{0,1},{1,0},{2,4},{3,5},{4,2},{5,3},{6,8},{7,9},{8,6},{9,7},{10,12... | collective-permute-start | bytes 393224 | tf_op jit(solution)/shard_map/ppermute | solution.py:369
  33.7 0.0 collective-permute-start.13
  33.7 0.0 collective-permute-done.12.pair_ref
  33.8 1.4 %collective-permute-start.15 = (f32[16,128]{1,0:T(8,128)S(1)}, f32[16,128]{1,0:T(8,128)S(1)}, u32[]{:S(2)}, u32[]{:S(2)}) collective-permute-start(f32[16,128]{1,0:T(8,128)S(1)} %gate_sum.1._.one_ref), channel_id=1, source_target_pairs={{0,1},{1,0},{2,3},{3,2},{4,5},{5,4},{6,7},{7,6},{8,9},{9,8},{10,11... | collective-permute-start | bytes 24584 | tf_op jit(solution)/shard_map/ppermute | solution.py:369
  35.1 2.1 %collective-permute-done.14.other_ref = bf16[64,1024]{1,0:T(8,128)(2,1)S(1)} collective-permute-done((bf16[64,1024]{1,0:T(8,128)(2,1)S(1)}, bf16[64,1024]{1,0:T(8,128)(2,1)S(1)}, u32[]{:S(2)}, u32[]{:S(2)}) %collective-permute-start.14) | collective-permute-done | bytes 131104 | tf_op jit(solution)/shard_map/ppermute | solution.py:369
  37.3 0.8 %finish.1 = (bf16[64,1024]{1,0:T(8,128)(2,1)}, bf16[128,1024]{1,0:T(8,128)(2,1)}) custom-call(s32[8,128]{1,0:T(8,128)S(1)} %get-tuple-element.35.off_ref, f32[64,1024]{1,0:T(8,128)S(1)} %get-tuple-element.48.own_ref, f32[64,1152]{1,0:T(8,128)S(1)} %get-tuple-element.53._.mine_ref, f32[64,1152]{1,0:T(8,128)S(1)} %collective-permute-done.12.pair_ref, ...), custom_call_target="tpu_custom_call" | custom-call | flops 1000000 | bytes 1000000 | tf_op jit(solution)/shard_map/finish/pallas_call | solution.py:478
  38.2 0.0 collective-permute-done.15.other_ref
  38.2 0.6 %gate_grad.1 = f32[1,32]{1,0:T(1,128)} custom-call(f32[16,128]{1,0:T(8,128)S(1)} %gate_sum.1._.one_ref, f32[16,128]{1,0:T(8,128)S(1)} %collective-permute-done.15.other_ref, f32[32,128]{1,0:T(8,128)S(1)} %broadcast_in_dim.15.gate_ref), custom_call_target="tpu_custom_call" | custom-call | flops 1000000 | bytes 1000000 | tf_op jit(solution)/shard_map/gate_grad/pallas_call | solution.py:489
  (15 shorter events, 0.1 us)
Async XLA Ops:
  0.6 2.2 %collective-permute-start = (s32[1,1]{1,0:T(1,128)}, s32[1,1]{1,0:T(1,128)}, u32[]{:S(2)}, u32[]{:S(2)}) collective-permute-start(s32[1,1]{1,0:T(1,128)} %param.11), channel_id=1, source_target_pairs={{0,2},{2,0},{4,6},{6,4},{8,10},{10,8},{12,14},{14,12},{16,18},{18,... | collective-permute-start | bytes 20 | tf_op jit(solution)/shard_map/ppermute | solution.py:365
  1.1 1.7 %collective-permute-start.1 = (bf16[64,1024]{1,0:T(8,128)(2,1)}, bf16[64,1024]{1,0:T(8,128)(2,1)S(1)}, u32[]{:S(2)}, u32[]{:S(2)}) collective-permute-start(bf16[64,1024]{1,0:T(8,128)(2,1)} %bitcast.19), channel_id=1, source_target_pairs={{0,2},{2,0},{4,6},{6,4},{8,10},{10,8},{12,14},{14,12},{16,18},{18,... | collective-permute-start | bytes 393224 | tf_op jit(solution)/shard_map/ppermute | solution.py:365
  1.9 1.0 %copy-start.4 = (bf16[1,1,64,1024]{3,2,1,0:T(8,128)(2,1)S(1)}, bf16[1,1,64,1024]{3,2,1,0:T(8,128)(2,1)}, u32[]{:S(2)}) copy-start(bf16[1,1,64,1024]{3,2,1,0:T(8,128)(2,1)} %param.10) | copy-start | bytes 393220
  2.8 7.1 %copy-start.2 = (bf16[1,128,1024]{2,1,0:T(8,128)(2,1)S(1)}, bf16[1,128,1024]{2,1,0:T(8,128)(2,1)}, u32[]{:S(2)}) copy-start(bf16[1,128,1024]{2,1,0:T(8,128)(2,1)} %param.8) | copy-start | bytes 786436
  3.7 11.3 %collective-permute-start.4 = (bf16[64,1152]{1,0:T(8,128)(2,1)S(1)}, bf16[64,1152]{1,0:T(8,128)(2,1)S(1)}, u32[]{:S(2)}, u32[]{:S(2)}) collective-permute-start(bf16[64,1152]{1,0:T(8,128)(2,1)S(1)} %get-tuple-element.36), channel_id=1, source_target_pairs={{0,8},{2,14},{4,12},{6,10},{8,16},{10,22},{12,20},{14,18},{16,24},... | collective-permute-start | bytes 442376 | tf_op jit(solution)/shard_map/ppermute | solution.py:365
  6.7 6.4 %collective-permute-start.3 = (bf16[64,1024]{1,0:T(8,128)(2,1)S(1)}, bf16[64,1024]{1,0:T(8,128)(2,1)S(1)}, u32[]{:S(2)}, u32[]{:S(2)}) collective-permute-start(bf16[64,1024]{1,0:T(8,128)(2,1)S(1)} %get-tuple-element.32.halo_ref), channel_id=1, source_target_pairs={{0,1},{1,0},{2,4},{3,5},{4,2},{5,3},{6,8},{7,9},{8,6},{9,7},{10,12... | collective-permute-start | bytes 393224 | tf_op jit(solution)/shard_map/ppermute | solution.py:369
  8.3 4.9 %collective-permute-start.2 = (bf16[64,1024]{1,0:T(8,128)(2,1)S(1)}, bf16[64,1024]{1,0:T(8,128)(2,1)S(1)}, u32[]{:S(2)}, u32[]{:S(2)}) collective-permute-start(bf16[64,1024]{1,0:T(8,128)(2,1)S(1)} %get-tuple-element.32.halo_ref), channel_id=1, source_target_pairs={{0,2},{2,0},{4,6},{6,4},{8,10},{10,8},{12,14},{14,12},{16,18},{18,... | collective-permute-start | bytes 393224 | tf_op jit(solution)/shard_map/ppermute | solution.py:365
  8.4 6.7 %collective-permute-start.5 = (bf16[64,512]{1,0:T(8,128)(2,1)S(1)}, bf16[64,512]{1,0:T(8,128)(2,1)S(1)}, u32[]{:S(2)}, u32[]{:S(2)}) collective-permute-start(bf16[64,512]{1,0:T(8,128)(2,1)S(1)} %get-tuple-element.37), channel_id=1, source_target_pairs={{0,4},{2,6},{4,0},{6,2},{8,12},{10,14},{12,8},{14,10},{16,20},{18,... | collective-permute-start | bytes 196616 | tf_op jit(solution)/shard_map/ppermute | solution.py:365
  9.9 0.7 %copy-start.5 = (s32[1,128]{1,0:T(1,128)S(1)}, s32[1,128]{1,0:T(1,128)}, u32[]{:S(2)}) copy-start(s32[1,128]{1,0:T(1,128)} %segment_ref.3) | copy-start | bytes 1540
  10.6 1.2 %copy-start = (bf16[1,128,4096]{2,1,0:T(8,128)(2,1)S(1)}, bf16[1,128,4096]{2,1,0:T(8,128)(2,1)}, u32[]{:S(2)}) copy-start(bf16[1,128,4096]{2,1,0:T(8,128)(2,1)} %param.7) | copy-start | bytes 3145732
  13.1 2.6 %copy-start.1 = (bf16[1,128,4096]{2,1,0:T(8,128)(2,1)S(1)}, bf16[1,128,4096]{2,1,0:T(8,128)(2,1)}, u32[]{:S(2)}) copy-start(bf16[1,128,4096]{2,1,0:T(8,128)(2,1)} %param.7) | copy-start | bytes 3145732
  15.0 0.7 %copy-start.6 = (f32[32]{0:T(128)S(1)}, f32[32]{0:T(128)}, u32[]{:S(2)}) copy-start(f32[32]{0:T(128)} %param.12) | copy-start | bytes 388
  15.0 2.1 %copy-start.3 = (bf16[1,128,4096]{2,1,0:T(8,128)(2,1)S(1)}, bf16[1,128,4096]{2,1,0:T(8,128)(2,1)}, u32[]{:S(2)}) copy-start(bf16[1,128,4096]{2,1,0:T(8,128)(2,1)} %param.13) | copy-start | bytes 3145732
  15.1 2.0 %collective-permute-start.6 = (bf16[64,1664]{1,0:T(8,128)(2,1)S(1)}, bf16[64,1664]{1,0:T(8,128)(2,1)S(1)}, u32[]{:S(2)}, u32[]{:S(2)}) collective-permute-start(bf16[64,1664]{1,0:T(8,128)(2,1)S(1)} %arrived.1._.mine_ref), channel_id=1, source_target_pairs={{0,2},{2,0},{4,6},{6,4},{8,10},{10,8},{12,14},{14,12},{16,18},{18,... | collective-permute-start | bytes 638984 | tf_op jit(solution)/shard_map/ppermute | solution.py:365
  19.7 2.2 %collective-permute-start.7 = (f32[64,1152]{1,0:T(8,128)S(1)}, f32[64,1152]{1,0:T(8,128)S(1)}, u32[]{:S(2)}, u32[]{:S(2)}) collective-permute-start(f32[64,1152]{1,0:T(8,128)S(1)} %get-tuple-element.42.refs_0_.mine_ref), channel_id=1, source_target_pairs={{0,2},{2,0},{4,6},{6,4},{8,10},{10,8},{12,14},{14,12},{16,18},{18,... | collective-permute-start | bytes 884744 | tf_op jit(solution)/shard_map/ppermute | solution.py:365
  22.0 9.9 %collective-permute-start.9 = (bf16[64,1152]{1,0:T(8,128)(2,1)S(1)}, bf16[64,1152]{1,0:T(8,128)(2,1)S(1)}, u32[]{:S(2)}, u32[]{:S(2)}) collective-permute-start(bf16[64,1152]{1,0:T(8,128)(2,1)S(1)} %get-tuple-element.46.refs_1_), channel_id=1, source_target_pairs={{0,24},{2,30},{4,28},{6,26},{8,0},{10,6},{12,4},{14,2},{16,8},{18,... | collective-permute-start | bytes 442376 | tf_op jit(solution)/shard_map/ppermute | solution.py:365
  25.2 6.7 %collective-permute-start.8 = (bf16[64,640]{1,0:T(8,128)(2,1)S(1)}, bf16[64,640]{1,0:T(8,128)(2,1)S(1)}, u32[]{:S(2)}, u32[]{:S(2)}) collective-permute-start(bf16[64,640]{1,0:T(8,128)(2,1)S(1)} %get-tuple-element.50), channel_id=1, source_target_pairs={{0,4},{2,6},{4,0},{6,2},{8,12},{10,14},{12,8},{14,10},{16,20},{18,... | collective-permute-start | bytes 245768 | tf_op jit(solution)/shard_map/ppermute | solution.py:365
  25.2 4.9 %collective-permute-start.11 = (f32[16,128]{1,0:T(8,128)S(1)}, f32[16,128]{1,0:T(8,128)S(1)}, u32[]{:S(2)}, u32[]{:S(2)}) collective-permute-start(f32[16,128]{1,0:T(8,128)S(1)} %get-tuple-element.51.gate_ref), channel_id=1, source_target_pairs={{0,16},{2,22},{4,20},{6,18},{8,24},{10,30},{12,28},{14,26},{16,0},... | collective-permute-start | bytes 24584 | tf_op jit(solution)/shard_map/ppermute | solution.py:365
  26.4 5.4 %collective-permute-start.10 = (f32[16,128]{1,0:T(8,128)S(1)}, f32[16,128]{1,0:T(8,128)S(1)}, u32[]{:S(2)}, u32[]{:S(2)}) collective-permute-start(f32[16,128]{1,0:T(8,128)S(1)} %get-tuple-element.51.gate_ref), channel_id=1, source_target_pairs={{0,8},{2,14},{4,12},{6,10},{8,16},{10,22},{12,20},{14,18},{16,24},... | collective-permute-start | bytes 24584 | tf_op jit(solution)/shard_map/ppermute | solution.py:365
  32.0 1.8 %collective-permute-start.12 = (f32[64,1152]{1,0:T(8,128)S(1)}, f32[64,1152]{1,0:T(8,128)S(1)}, u32[]{:S(2)}, u32[]{:S(2)}) collective-permute-start(f32[64,1152]{1,0:T(8,128)S(1)} %get-tuple-element.53._.mine_ref), channel_id=1, source_target_pairs={{0,2},{2,0},{4,6},{6,4},{8,10},{10,8},{12,14},{14,12},{16,18},{18,... | collective-permute-start | bytes 884744 | tf_op jit(solution)/shard_map/ppermute | solution.py:365
  32.2 5.1 %collective-permute-start.14 = (bf16[64,1024]{1,0:T(8,128)(2,1)S(1)}, bf16[64,1024]{1,0:T(8,128)(2,1)S(1)}, u32[]{:S(2)}, u32[]{:S(2)}) collective-permute-start(bf16[64,1024]{1,0:T(8,128)(2,1)S(1)} %get-tuple-element.56), channel_id=1, source_target_pairs={{0,1},{1,0},{2,4},{3,5},{4,2},{5,3},{6,8},{7,9},{8,6},{9,7},{10,12... | collective-permute-start | bytes 393224 | tf_op jit(solution)/shard_map/ppermute | solution.py:369
  33.7 3.5 %collective-permute-start.13 = (bf16[64,1024]{1,0:T(8,128)(2,1)S(1)}, bf16[64,1024]{1,0:T(8,128)(2,1)S(1)}, u32[]{:S(2)}, u32[]{:S(2)}) collective-permute-start(bf16[64,1024]{1,0:T(8,128)(2,1)S(1)} %get-tuple-element.56), channel_id=1, source_target_pairs={{0,2},{2,0},{4,6},{6,4},{8,10},{10,8},{12,14},{14,12},{16,18},{18,... | collective-permute-start | bytes 393224 | tf_op jit(solution)/shard_map/ppermute | solution.py:365
  33.8 4.4 %collective-permute-start.15 = (f32[16,128]{1,0:T(8,128)S(1)}, f32[16,128]{1,0:T(8,128)S(1)}, u32[]{:S(2)}, u32[]{:S(2)}) collective-permute-start(f32[16,128]{1,0:T(8,128)S(1)} %gate_sum.1._.one_ref), channel_id=1, source_target_pairs={{0,1},{1,0},{2,3},{3,2},{4,5},{5,4},{6,7},{7,6},{8,9},{9,8},{10,11... | collective-permute-start | bytes 24584 | tf_op jit(solution)/shard_map/ppermute | solution.py:369

commit v4 on v3

--- a/solution.py
+++ b/solution.py
@@ -12,6 +12,8 @@
 WINDOW = 64
 GAP = 4
 LANES = 128
+MORE = 16
+MARKS = 384
 SCALE = 1.0 / math.sqrt(HEAD_DIM)
 
 VMEM = pl.BlockSpec(memory_space=pltpu.VMEM)
@@ -85,23 +87,21 @@
     out_ref[...] = jnp.where(here, mine, other).astype(out_ref.dtype)
 
 
-def owner(off_ref, row, tok_rows):
-    return flag(off_ref[row : row + 1, 0:1] < tok_rows)
-
-
-def chip_kernel(
-    off_ref, pair_off_ref, mine_ref, other_ref, tail_ref, out_ref, marked_ref, half_ref, tail_out, owner_ref, *, tok_rows
-):
-    off, pair_off = off_ref[0, 0], pair_off_ref[0, 0]
-    width = mine_ref.shape[1]
-    tail_out[...] = tail_ref[...]
-    choose(flag(off < tok_rows), mine_ref, other_ref, out_ref)
+def owner(owner_ref, row):
+    return flag(owner_ref[row : row + 1, 0:1] > 0.5)
+
+
+def chip_kernel(mine_ref, other_ref, out_ref, marked_ref, half_ref, owner_ref):
+    width = out_ref.shape[1]
+    mine, other = mine_ref[0:1, width : width + 1], other_ref[0:1, width : width + 1]
+    mine, other = mine.astype(jnp.float32), other.astype(jnp.float32)
+    choose(flag(mine > 0.5), mine_ref, other_ref, out_ref, width)
     marked_ref[:, :width] = out_ref[...]
-    owns = jnp.where((off < tok_rows) | (pair_off < tok_rows), 1.0, 0.0)
-    marked_ref[:, width:] = jnp.full((mine_ref.shape[0], LANES), owns, jnp.float32).astype(marked_ref.dtype)
+    owns = jnp.maximum(mine, other)
+    marked_ref[:, width:] = jnp.broadcast_to(owns, (out_ref.shape[0], LANES)).astype(marked_ref.dtype)
     choose(odd_core(), out_ref.at[:, width // 2 :], out_ref.at[:, : width // 2], half_ref)
     row = lax.broadcasted_iota(jnp.int32, owner_ref.shape, 0)
-    owner_ref[...] = jnp.where(row == 0, off, pair_off)
+    owner_ref[...] = jnp.where(row == 0, mine, other)
 
 
 def join_kernel(z_ref, x_ref, _, __, out_ref):
@@ -110,7 +110,8 @@
 
 
 def near_kernel(chip_ref, other_ref, _, out_ref, *, step):
-    choose(flag(lax.axis_index("seq") % 2 == (1 if step > 0 else 0)), chip_ref, other_ref, out_ref)
+    first = chip_ref.shape[0] - out_ref.shape[0]
+    choose(flag(lax.axis_index("seq") % 2 == (1 if step > 0 else 0)), chip_ref.at[first:], other_ref.at[first:], out_ref)
 
 
 def self_kernel(query_ref, context_ref, halo_ref, segment_ref, _, out_ref, weights_ref, *, block, groups, repeat):
@@ -140,14 +141,14 @@
 
 
 def cross_kernel(
-    off_ref, gate_ref, self_0_ref, self_1_ref, grad_ref, own_ref, chip_ref, mine_ref, pair_ref,
-    grad_self_ref, to_pair_ref, in_chip_ref, own_terms_ref, mask_ref, prev, *, groups, repeat
+    off_ref, owner_ref, gate_ref, self_0_ref, self_1_ref, grad_ref, own_ref, chip_ref, mine_ref, pair_ref,
+    scores_ref, to_pair_ref, in_chip_ref, own_terms_ref, mask_ref, prev, *, groups, repeat
 ):
-    tok_rows, width = grad_ref.shape[0], own_ref.shape[1]
+    tok_rows, width = grad_ref.shape[0], chip_ref.shape[1]
     img = own_ref.shape[0]
     shard = lax.axis_index("seq")
     off = off_ref[0:1, 0:1]
-    is_owner, pair_owner = owner(off_ref, 0, tok_rows), owner(off_ref, 1, tok_rows)
+    is_owner, pair_owner = owner(owner_ref, 0), owner(owner_ref, 1)
     upper, odd = flag(shard % GAP >= 2), flag(shard % 2 == 1)
     from_chip = odd * pair_owner
     from_x = upper * (1 - (is_owner | pair_owner))
@@ -213,8 +214,7 @@
         ).astype(jnp.bfloat16)
         grad_key = dot(scores_j, out_t, NT) * SCALE
         grad_value = dot(narrow_j, cross_rows, NN)
-        grad_query = dot(scores_j, keys, TN) * SCALE
-        grad_self_ref[g] = (grad_rows.astype(jnp.float32) + grad_query).astype(jnp.bfloat16)
+        scores_ref[g] = scores_j
         for index, terms in ((g, grad_key), (groups + g, grad_value)):
             cols = slice(index * HEAD_DIM, (index + 1) * HEAD_DIM)
             own_terms_ref[:, cols] = terms[img:]
@@ -224,6 +224,16 @@
     to_pair_ref[:, width:] = jnp.concatenate([gate] * (img // gate.shape[0]), axis=0)
     row = lax.broadcasted_iota(jnp.int32, mask_ref.shape, 0)
     mask_ref[...] = jnp.where(row == 0, by_mine.astype(jnp.float32) * (1.0 - from_x), from_x)
+
+
+def cross_query_kernel(scores_ref, grad_ref, own_ref, prev, _, grad_self_ref, *, groups, repeat):
+    for g in range(groups):
+        keys = jnp.concatenate([part(prev, g), part(own_ref, g)], axis=0)
+        grad_query = dot(scores_ref[g], keys, TN) * SCALE
+        for block in range(grad_ref.shape[0] // WINDOW):
+            rows = slice(block * repeat * WINDOW, (block + 1) * repeat * WINDOW)
+            grad_rows = stack(grad_ref, block * WINDOW, WINDOW, g, repeat).astype(jnp.float32)
+            grad_self_ref[g, rows, :] = (grad_rows + grad_query[rows]).astype(jnp.bfloat16)
 
 
 def outside_kernel(mine_ref, pair_ref, mask_ref, _, to_z_ref, to_x_ref, gate_ref):
@@ -241,8 +251,7 @@
 
 
 def chip_sum_kernel(mine_ref, x_ref, z_ref, gate_ref, *refs):
-    *gates, halo_ref, _, out_ref, gate_out, halo_out = refs
-    halo_out[...] = halo_ref[...]
+    *gates, _, out_ref, gate_out = refs
     width = mine_ref.shape[1]
     odd = odd_core().astype(jnp.float32)
     half = width // 2
@@ -298,9 +307,8 @@
     out_ref[...] = chip_ref[...] + (mine_ref[:rows, width:] + pair_ref[:rows, width:])
 
 
-def gate_grad_kernel(one_ref, other_ref, gate_ref, out_ref):
-    rows, heads = one_ref.shape[0], out_ref.shape[1]
-    total = one_ref[...] + other_ref[...]
+def gate_grad(total, gate_ref):
+    rows, heads = total.shape[0], gate_ref.shape[0]
     lane = lax.broadcasted_iota(jnp.int32, total.shape, 1)
     first = jnp.sum(jnp.where(lane < WINDOW, total, 0.0), axis=1, keepdims=True)
     second = jnp.sum(jnp.where(lane < WINDOW, 0.0, total), axis=1, keepdims=True)
@@ -311,21 +319,25 @@
     tanh = gate_ref[:, :heads]
     same = lax.broadcasted_iota(jnp.int32, tanh.shape, 0) == lax.broadcasted_iota(jnp.int32, tanh.shape, 1)
     tanh = jnp.sum(jnp.where(same, tanh, 0.0), axis=0, keepdims=True)
-    out_ref[...] = (1.0 - tanh * tanh) * sums
+    return (1.0 - tanh * tanh) * sums
 
 
 def finish_kernel(
-    off_ref, own_ref, mine_ref, pair_ref, low_ref, also_ref, high_ref, halo_ref, _,
-    memory_ref, context_ref, *, tok_rows
+    owner_ref, own_ref, mine_ref, pair_ref, low_ref, also_ref, high_ref, halo_ref, gate_ref, *refs, tok_rows
 ):
+    *far_refs, tanh_ref, memory_ref, context_ref, gate_out = refs
     width = own_ref.shape[1]
-    keep = flag(off_ref[0:1, 0:1] < tok_rows).astype(jnp.float32)
+    keep = owner(owner_ref, 0).astype(jnp.float32)
     total = own_ref[...] + (mine_ref[:, :width] + pair_ref[:, :width])
     memory_ref[...] = (total * keep).astype(memory_ref.dtype)
     more = jnp.where(lax.axis_index("seq") < lax.axis_size("seq") - 1, 1.0, 0.0)
     first = tok_rows - WINDOW
     context_ref[:first] = (low_ref[...] + also_ref[...]).astype(context_ref.dtype)
     context_ref[first:] = (high_ref[...] + halo_ref[...].astype(jnp.float32) * more).astype(context_ref.dtype)
+    gate = gate_ref[...]
+    for ref in far_refs:
+        gate = gate + ref[...]
+    gate_out[...] = gate_grad(gate, tanh_ref)
 
 
 def struct(shape, dtype):
@@ -333,7 +345,7 @@
 
 
 def call(
-    name, kernel, out_shape, in_specs, scratch=(), out_specs=None, aliases=None, flops=10**6, moved=10**6
+    name, kernel, out_shape, in_specs, scratch=(), out_specs=None, aliases=None, flops=1000, moved=1000
 ):
     return pl.pallas_call(
         kernel,
@@ -376,11 +388,15 @@
 
     def merge(name, arrived, step, after):
         if len(arrived) == 1:
-            return arrived[0]
+            return arrived[0][arrived[0].shape[0] - WINDOW :]
         return call(name, functools.partial(near_kernel, step=step), [window], [VMEM] * 2 + [ANY])(*arrived, after)[0]
 
-    def send_z(value, step):
-        return send(value, lambda i: ((i if i % 2 == 0 else i ^ 2) + step * GAP) % seq)
+    def send_z(value, step, straight=False):
+        def where(i):
+            wraps = not 0 <= i + step * GAP < seq
+            return ((i if i % 2 == 0 or (straight and wraps) else i ^ 2) + step * GAP) % seq
+
+        return send(value, where)
 
     q, ctx, grad = queries[0], context[0], out_grad[0]
     gate_tanh = jnp.tanh(cross_gate)
@@ -388,18 +404,20 @@
     image = struct((img, width), bf16)
     window = struct((WINDOW, width), bf16)
     own = memory[0, 0]
+    is_owner = (image_offset < tok_rows).astype(bf16)
+    own = jnp.concatenate([own, jnp.broadcast_to(is_owner, (img, MARKS))], axis=1)
     pair = send(own, lambda i: i ^ 1)
-    pair_off = send(image_offset, lambda i: i ^ 1)
-    tail = ctx[tok_rows - WINDOW :]
-    chip, marked, chip_half, tail, off = call(
+    tail = ctx[tok_rows - WINDOW - MORE :]
+    halos = send_near(tail, 1)
+    chip, marked, chip_half, owners = call(
         "chip_image",
-        functools.partial(chip_kernel, tok_rows=tok_rows),
-        [image, struct((img, width + LANES), bf16), struct((img, width // 2), bf16), window, struct((8, LANES), jnp.int32)],
-        [SMEM] * 2 + [VMEM] * 3,
-    )(image_offset, pair_off, own, pair, tail)
-    by_z = send_z(marked, 1)
+        chip_kernel,
+        [image, struct((img, width + LANES), bf16), struct((img, width // 2), bf16), struct((8, LANES), f32)],
+        [VMEM] * 2,
+    )(own, pair)
+    off = jnp.broadcast_to(image_offset, (8, LANES))
+    by_z = send_z(marked, 1, True)
     by_x = send(chip_half, lambda i: i ^ 2)
-    halo = merge("halo", send_near(tail, 1), 1, chip)
     self_out, kept = [None, None], [None, None]
 
     def self_forward(block, after):
@@ -413,6 +431,7 @@
         )(q, ctx, tail if block else halo, segment_start, after)
 
     self_forward(1, chip)
+    halo = merge("halo", halos, 1, self_out[1])
     arrived = call("arrived", join_kernel, [struct((img, width + LANES + width // 2), bf16)], [VMEM] * 2 + [ANY] * 2)(
         by_z, by_x, self_out[1], halo
     )[0]
@@ -421,20 +440,26 @@
     self_forward(0, arrived)
 
     gate_shape = struct((heads * WINDOW // LANES, LANES), f32)
-    grad_self, to_pair, in_chip, own_terms, masks = call(
+    scores, to_pair, in_chip, own_terms, masks, prev = call(
         "cross",
         functools.partial(cross_kernel, groups=groups, repeat=repeat),
         [
-            struct((groups, repeat * tok_rows, HEAD_DIM), bf16),
+            struct((groups, 2 * img, repeat * tok_rows), bf16),
             struct((img, width + LANES), f32),
             struct((img, width), f32),
             struct((img, width), f32),
             struct((8, LANES), f32),
+            image,
         ],
-        [VMEM] * 9,
-        scratch=[pltpu.VMEM((img, width), bf16)],
-    )(off, gate_rows, *self_out, grad, own, chip, arrived, by_pair)
+        [VMEM] * 10,
+    )(off, owners, gate_rows, *self_out, grad, own, chip, arrived, by_pair)
     from_pair = send(to_pair, lambda i: i ^ 1)
+    grad_self = call(
+        "cross_query",
+        functools.partial(cross_query_kernel, groups=groups, repeat=repeat),
+        [struct((groups, repeat * tok_rows, HEAD_DIM), bf16)],
+        [VMEM] * 4 + [ANY],
+    )(scores, grad, own, prev, to_pair)[0]
 
     def self_backward(block, after, late=None):
         return call(
@@ -453,43 +478,41 @@
             moved=10**5,
         )(q, ctx, tail if block else halo, kept[block], grad_self, after, *([] if late is None else [late]))
 
-    query_grad, halo_terms, low = self_backward(0, to_pair)
     to_z, to_x, gate = call(
         "outside",
         outside_kernel,
         [struct((img, width + LANES), bf16), struct((img, width // 2 + LANES), bf16), gate_shape],
         [VMEM] * 3 + [ANY],
-    )(to_pair, from_pair, masks, halo_terms)
+    )(to_pair, from_pair, masks, grad_self)
     from_z = send_z(to_z, -1)
     from_x = send(to_x, lambda i: i ^ 2)
     gates = []
     if swaps:
         gates = [send_z(gate, 1), send_z(gate, 2)]
-    query_grad, also, high = self_backward(1, query_grad, to_z)
-    mine, gate, halo_terms = call(
+    query_grad, halo_terms, low = self_backward(0, to_z)
+    mine, gate = call(
         "chip_sum",
         chip_sum_kernel,
-        [struct((img, width + LANES), f32), gate_shape, window],
-        [VMEM] * (5 + len(gates)) + [ANY],
-    )(in_chip, from_x, from_z, gate, *gates, halo_terms, high)
+        [struct((img, width + LANES), f32), gate_shape],
+        [VMEM] * (4 + len(gates)) + [ANY],
+    )(in_chip, from_x, from_z, gate, *gates, low)
     other = send(mine, lambda i: i ^ 1)
-    halo_back = merge("halo_back", send_near(halo_terms, -1), -1, mine)
+    halo_back = send_near(halo_terms, -1)
+    query_grad, also, high = self_backward(1, query_grad, mine)
+    halo_back = merge("halo_back", halo_back, -1, high)
     gate = call("gate_sum", gate_kernel, [gate_shape], [VMEM] * 3)(gate, mine, other)[0]
-    memory_grad, context_grad = call(
+    if swaps:
+        far = [send_all(gate, lambda s, d: (s, d ^ 1))]
+    else:
+        gate = lax.psum(to_pair[: gate_shape.shape[0], width:], ("seq", "dp"))
+        far = []
+    memory_grad, context_grad, cross_gate_grad = call(
         "finish",
         functools.partial(finish_kernel, tok_rows=tok_rows),
-        [image, struct((tok_rows, width), bf16)],
-        [VMEM] * 8 + [ANY],
-    )(off, own_terms, mine, other, low, also, high, halo_back, gate)
-
-    if not swaps:
-        gate_total = lax.psum(to_pair[: gate_shape.shape[0], width:], ("seq", "dp"))
-        gate_grad = (1.0 - gate_tanh * gate_tanh) * jnp.sum(gate_total.reshape(heads, WINDOW), axis=1)
-        return (query_grad[None], context_grad[None], memory_grad[None, None], gate_grad)
-    gate_grad = call("gate_grad", gate_grad_kernel, [struct((1, heads), f32)], [VMEM] * 3)(
-        gate, send_all(gate, lambda s, d: (s, d ^ 1)), gate_rows
-    )[0].reshape(heads)
-    return (query_grad[None], context_grad[None], memory_grad[None, None], gate_grad)
+        [image, struct((tok_rows, width), bf16), struct((1, heads), f32)],
+        [VMEM] * (10 + len(far)),
+    )(owners, own_terms, mine, other, low, also, high, halo_back, gate, *far, gate_rows)
+    return (query_grad[None], context_grad[None], memory_grad[None, None], cross_gate_grad.reshape(heads))
 
 
 def solution(mesh):

time: 39 us -> 36.2 us (0.928)
  starting transfers between devices: 16.1 us -> 14.9 us
  Pallas kernels: 12 us -> 10.8 us
  local copies, waits for them, and re-layouts: 3.47 us -> 2.91 us
    ppermute x13 -> x12, starting transfers between devices: 11.7 us -> 9.56 us  [send(): return lax.ppermute(value, 'seq', [(i, where(i)) for i in range(seq)])]
    ppermute x13 -> x12, waiting for transfers between devices: 3.59 us -> 5.58 us  [send(): return lax.ppermute(value, 'seq', [(i, where(i)) for i in range(seq)])]
    ppermute x3, waiting for transfers between devices: 2.14 us -> 0.34 us  [send_all(): lax.ppermute(value, ('seq', 'dp'), [(s * dp + d, t * dp + e) for s, d, t,...]
    slice x1, local copies, waits for them, and re-layouts: 0.95 us -> 0.01 us  [on_device(): tail = ctx[tok_rows - WINDOW - MORE:]]
    concatenate x0 -> x1, local copies, waits for them, and re-layouts: none -> 0.92 us  [on_device(): jnp.concatenate([own, jnp.broadcast_to(is_owner, (img, MARKS))], axis=1)]
    ppermute x3, starting transfers between devices: 4.42 us -> 5.34 us  [send_all(): lax.ppermute(value, ('seq', 'dp'), [(s * dp + d, t * dp + e) for s, d, t,...]
    pallas_call x2, Pallas kernels: 1.4 us -> 0.6 us  [the longest x1 0.51 us: on_device(): call('cross_query', functools.partial(cross_query_kernel, groups=groups,...]
    unnamed x14 -> x12, local copies, waits for them, and re-layouts: 2.44 us -> 1.9 us
  transfers between devices with their start and end apart: 16 -> 15, of which waited for: 3 -> 7; matrix products, arithmetic and copies ran while one was open for 2% -> 0% of each run, Pallas kernels for 20% -> 21%
where the time goes in v4:
time: 36.2 us; the launch traced here: 36 us
  starting transfers between devices  14.9 us (41%)
  Pallas kernels  10.8 us (30%)
  waiting for transfers between devices  5.92 us (16%)
  local copies, waits for them, and re-layouts  2.91 us (8%)
  between operations  1.51 us (4%)
    ppermute x12, starting transfers between devices, send(): return lax.ppermute(value, 'seq', [(i, where(i)) for i in range(seq)])  9.56 us
    ppermute x12, waiting for transfers between devices, send(): return lax.ppermute(value, 'seq', [(i, where(i)) for i in range(seq)])  5.58 us
    ppermute x3, starting transfers between devices, send_all(): lax.ppermute(value, ('seq', 'dp'), [(s * dp + d, t * dp + e) for s, d, t,...  5.34 us
    pallas_call x2, Pallas kernels, self_backward(): call(f'self_backward_{block}', functools.partial(self_back_kernel, block=...  4.19 us
    pallas_call x2, Pallas kernels, self_forward(): call(f'self_forward_{block}', functools.partial(self_kernel, block=block,...  2.71 us
    pallas_call x1, Pallas kernels, on_device(): call('cross', functools.partial(cross_kernel, groups=groups, repeat=repea...  2.14 us
    unnamed x12, local copies, waits for them, and re-layouts  1.9 us
    concatenate x1, local copies, waits for them, and re-layouts, on_device(): jnp.concatenate([own, jnp.broadcast_to(is_owner, (img, MARKS))], axis=1)  0.92 us
  transfers between devices with their start and end apart: 15, of which 7 were waited for; matrix products, arithmetic and copies ran while one was open for 0% of the time, Pallas kernels for 21%

profile of v4, /device:TPU:0, one launch (start us, length us, event | category | flops | bytes accessed | tf_op | source)
XLA Modules:
  0.0 36.0 jit_solution(11610753505024963178)
XLA Ops:
  0.6 0.0 copy-start.2
  1.3 0.9 %concatenate.3.mine_ref.own_ref = bf16[64,1408]{1,0:T(8,128)(2,1)S(1)} pad(bf16[64,1024]{1,0:T(8,128)(2,1)} %bitcast.24, bf16[]{:T(256)} %bitcast.4), padding=0_0x0_384 | pad | bytes 311298 | tf_op jit(solution)/shard_map/concatenate | solution.py:408
  2.3 0.5 %collective-permute-start = (bf16[64,1408]{1,0:T(8,128)(2,1)S(1)}, bf16[64,1408]{1,0:T(8,128)(2,1)S(1)}, u32[]{:S(2)}, u32[]{:S(2)}) collective-permute-start(bf16[64,1408]{1,0:T(8,128)(2,1)S(1)} %concatenate.3.mine_ref.own_ref), channel_id=1, source_target_pairs={{0,2},{2,0},{4,6},{6,4},{8,10},{10,8},{12,14},{14,12},{16,18},{18,... | collective-permute-start | bytes 540680 | tf_op jit(solution)/shard_map/ppermute | solution.py:377
  2.8 2.6 %collective-permute-start.2 = (bf16[80,1024]{1,0:T(8,128)(2,1)S(1)}, bf16[80,1024]{1,0:T(8,128)(2,1)S(1)}, u32[]{:S(2)}, u32[]{:S(2)}) collective-permute-start(bf16[80,1024]{1,0:T(8,128)(2,1)S(1)} %slice_bitcast_fusion.halo_ref), channel_id=1, source_target_pairs={{0,1},{1,0},{2,4},{3,5},{4,2},{5,3},{6,8},{7,9},{8,6},{9,7},{10,12... | collective-permute-start | bytes 491528 | tf_op jit(solution)/shard_map/ppermute | solution.py:381
  5.4 0.1 collective-permute-start.1
  5.5 0.0 collective-permute-done.other_ref
  5.5 0.1 chip_image.1
  5.6 1.6 %collective-permute-start.3 = (bf16[64,1152]{1,0:T(8,128)(2,1)S(1)}, bf16[64,1152]{1,0:T(8,128)(2,1)S(1)}, u32[]{:S(2)}, u32[]{:S(2)}) collective-permute-start(bf16[64,1152]{1,0:T(8,128)(2,1)S(1)} %get-tuple-element.36), channel_id=1, source_target_pairs={{0,8},{2,14},{4,12},{6,10},{8,16},{10,22},{12,20},{14,18},{16,24},... | collective-permute-start | bytes 442376 | tf_op jit(solution)/shard_map/ppermute | solution.py:377
  7.2 1.5 %collective-permute-start.4 = (bf16[64,512]{1,0:T(8,128)(2,1)S(1)}, bf16[64,512]{1,0:T(8,128)(2,1)S(1)}, u32[]{:S(2)}, u32[]{:S(2)}) collective-permute-start(bf16[64,512]{1,0:T(8,128)(2,1)S(1)} %get-tuple-element.37), channel_id=1, source_target_pairs={{0,4},{2,6},{4,0},{6,2},{8,12},{10,14},{12,8},{14,10},{16,20},{18,... | collective-permute-start | bytes 196616 | tf_op jit(solution)/shard_map/ppermute | solution.py:377
  8.8 0.7 %copy-done.4 = s32[1,128]{1,0:T(1,128)S(1)} copy-done((s32[1,128]{1,0:T(1,128)S(1)}, s32[1,128]{1,0:T(1,128)}, u32[]{:S(2)}) %copy-start.4) | copy-done | bytes 536
  9.4 1.2 %copy-done = bf16[1,128,4096]{2,1,0:T(8,128)(2,1)S(1)} copy-done((bf16[1,128,4096]{2,1,0:T(8,128)(2,1)S(1)}, bf16[1,128,4096]{2,1,0:T(8,128)(2,1)}, u32[]{:S(2)}) %copy-start) | copy-done | bytes 1048600
  10.6 1.4 %self_forward_1.1 = (bf16[4,128,512]{2,1,0:T(8,128)(2,1)S(1)}, f32[4,128,512]{2,1,0:T(8,128)S(1)}) custom-call(bf16[128,4096]{1,0:T(8,128)(2,1)S(1)} %bitcast.13, bf16[128,1024]{1,0:T(8,128)(2,1)S(1)} %bitcast.17, bf16[80,1024]{1,0:T(8,128)(2,1)S(1)} %slice_bitcast_fusion.halo_ref, s32[1,128]{1,0:T(1,128)S(1)} %copy-done.4, ...), custom_call_target="tpu_custom_call" | custom-call | flops 1000000 | bytes 100000 | tf_op jit(solution)/shard_map/self_forward_1/pallas_call | solution.py:424
  12.0 0.0 copy-start.1
  12.0 0.0 collective-permute-done.2.other_ref
  12.0 0.0 collective-permute-done.1.chip_ref
  12.1 0.0 copy-start.5
  12.1 0.0 collective-permute-done.4.x_ref
  12.1 3.3 %collective-permute-done.3.z_ref = bf16[64,1152]{1,0:T(8,128)(2,1)S(1)} collective-permute-done((bf16[64,1152]{1,0:T(8,128)(2,1)S(1)}, bf16[64,1152]{1,0:T(8,128)(2,1)S(1)}, u32[]{:S(2)}, u32[]{:S(2)}) %collective-permute-start.3) | collective-permute-done | bytes 147488 | tf_op jit(solution)/shard_map/ppermute | solution.py:377
  15.4 0.0 copy-start.3
  15.4 0.1 collective-permute-start.5
  15.5 1.4 %self_forward_0.1 = (bf16[4,128,512]{2,1,0:T(8,128)(2,1)S(1)}, f32[4,128,512]{2,1,0:T(8,128)S(1)}) custom-call(bf16[128,4096]{1,0:T(8,128)(2,1)S(1)} %bitcast.14, bf16[128,1024]{1,0:T(8,128)(2,1)S(1)} %bitcast.18, bf16[64,1024]{1,0:T(8,128)(2,1)S(1)} %halo.1.__.halo_ref, s32[1,128]{1,0:T(1,128)S(1)} %copy-done.4, bf16[64,1664]{1,0:T(8,128)(2,1)S(1)} %arrived.1._.mine_ref), custom_call_target="tpu_custom_call" | custom-call | flops 1000000 | bytes 100000 | tf_op jit(solution)/shard_map/self_forward_0/pallas_call | solution.py:424
  16.9 0.1 collective-permute-done.5.pair_ref
  17.0 0.1 broadcast_in_dim.34.gate_ref.refs_1_
  17.0 2.1 %cross.1 = (bf16[4,128,1024]{2,1,0:T(8,128)(2,1)S(1)}, f32[64,1152]{1,0:T(8,128)S(1)}, f32[64,1024]{1,0:T(8,128)S(1)}, f32[64,1024]{1,0:T(8,128)S(1)}, f32[8,128...) custom-call(s32[8,128]{1,0:T(8,128)S(1)} %broadcast_in_dim.33.off_ref, f32[8,128]{1,0:T(8,128)S(1)} %get-tuple-element.34.owner_ref, ...), custom_call_target="tpu_custom_call" | custom-call | flops 1000 | bytes 1000 | tf_op jit(solution)/shard_map/cross/pallas_call | solution.py:443
  19.2 0.5 %collective-permute-start.6 = (f32[64,1152]{1,0:T(8,128)S(1)}, f32[64,1152]{1,0:T(8,128)S(1)}, u32[]{:S(2)}, u32[]{:S(2)}) collective-permute-start(f32[64,1152]{1,0:T(8,128)S(1)} %get-tuple-element.41._.mine_ref), channel_id=1, source_target_pairs={{0,2},{2,0},{4,6},{6,4},{8,10},{10,8},{12,14},{14,12},{16,18},{18,... | collective-permute-start | bytes 884744 | tf_op jit(solution)/shard_map/ppermute | solution.py:377
  19.7 0.5 %cross_query.1._.grad_ref = bf16[4,1024,128]{2,1,0:T(8,128)(2,1)S(1)} custom-call(bf16[4,128,1024]{2,1,0:T(8,128)(2,1)S(1)} %get-tuple-element.39.scores_ref, bf16[128,4096]{1,0:T(8,128)(2,1)S(1)} %bitcast.22, bf16[64,1408]{1,0:T(8,128)(2,1)S(1)} %concatenate.3.mine_ref.own_ref, bf16[64,1024]{1,0:T(8,128)(2,1)S(1)} %get-tuple-element.40.prev, ...), custom_call_target="tpu_custom_call" | custom-call | flops 1000 | bytes 1000 | tf_op jit(solution)/shard_map/cross_query/pallas_call | solution.py:457
  20.2 0.7 %collective-permute-done.6.pair_ref = f32[64,1152]{1,0:T(8,128)S(1)} collective-permute-done((f32[64,1152]{1,0:T(8,128)S(1)}, f32[64,1152]{1,0:T(8,128)S(1)}, u32[]{:S(2)}, u32[]{:S(2)}) %collective-permute-start.6) | collective-permute-done | bytes 294944 | tf_op jit(solution)/shard_map/ppermute | solution.py:377
  20.9 0.1 outside.1
  21.0 2.3 %collective-permute-start.8 = (bf16[64,1152]{1,0:T(8,128)(2,1)S(1)}, bf16[64,1152]{1,0:T(8,128)(2,1)S(1)}, u32[]{:S(2)}, u32[]{:S(2)}) collective-permute-start(bf16[64,1152]{1,0:T(8,128)(2,1)S(1)} %get-tuple-element.44.refs_0_), channel_id=1, source_target_pairs={{0,24},{2,30},{4,28},{6,26},{8,0},{10,6},{12,4},{14,2},{16,8},{18,... | collective-permute-start | bytes 442376 | tf_op jit(solution)/shard_map/ppermute | solution.py:377
  23.3 0.0 collective-permute-start.7
  23.3 0.2 collective-permute-start.10
  23.5 1.8 %collective-permute-start.9 = (f32[16,128]{1,0:T(8,128)S(1)}, f32[16,128]{1,0:T(8,128)S(1)}, u32[]{:S(2)}, u32[]{:S(2)}) collective-permute-start(f32[16,128]{1,0:T(8,128)S(1)} %get-tuple-element.48.gate_ref), channel_id=1, source_target_pairs={{0,8},{2,14},{4,12},{6,10},{8,16},{10,22},{12,20},{14,18},{16,24},... | collective-permute-start | bytes 24584 | tf_op jit(solution)/shard_map/ppermute | solution.py:377
  25.3 2.1 %self_backward_0.1 = (bf16[128,4096]{1,0:T(8,128)(2,1)}, bf16[64,1024]{1,0:T(8,128)(2,1)S(1)}, f32[64,1024]{1,0:T(8,128)S(1)}) custom-call(bf16[128,4096]{1,0:T(8,128)(2,1)S(1)} %bitcast.15, bf16[128,1024]{1,0:T(8,128)(2,1)S(1)} %bitcast.19, bf16[64,1024]{1,0:T(8,128)(2,1)S(1)} %halo.1.__.halo_ref, f32[4,128,512]{2,1,0:T(8,128)S(1)} %get-tuple-element.42.weights_ref, ...), custom_call_target="tpu_custom_call" | custom-call | flops 1000000 | bytes 100000 | tf_op jit(solution)/shard_map/self_backward_0/pallas_call | solution.py:465
  27.4 0.5 %collective-permute-done.10.refs_1_ = f32[16,128]{1,0:T(8,128)S(1)} collective-permute-done((f32[16,128]{1,0:T(8,128)S(1)}, f32[16,128]{1,0:T(8,128)S(1)}, u32[]{:S(2)}, u32[]{:S(2)}) %collective-permute-start.10) | collective-permute-done | bytes 8224 | tf_op jit(solution)/shard_map/ppermute | solution.py:377
  27.9 1.1 %collective-permute-done.9.refs_0_ = f32[16,128]{1,0:T(8,128)S(1)} collective-permute-done((f32[16,128]{1,0:T(8,128)S(1)}, f32[16,128]{1,0:T(8,128)S(1)}, u32[]{:S(2)}, u32[]{:S(2)}) %collective-permute-start.9) | collective-permute-done | bytes 8224 | tf_op jit(solution)/shard_map/ppermute | solution.py:377
  29.0 0.0 collective-permute-done.7.x_ref
  29.0 0.0 collective-permute-done.8.z_ref
  29.0 0.1 chip_sum.1
  29.0 0.9 %collective-permute-start.11 = (f32[64,1152]{1,0:T(8,128)S(1)}, f32[64,1152]{1,0:T(8,128)S(1)}, u32[]{:S(2)}, u32[]{:S(2)}) collective-permute-start(f32[64,1152]{1,0:T(8,128)S(1)} %get-tuple-element.50.refs_1_.mine_ref), channel_id=1, source_target_pairs={{0,2},{2,0},{4,6},{6,4},{8,10},{10,8},{12,14},{14,12},{16,18},{18,... | collective-permute-start | bytes 884744 | tf_op jit(solution)/shard_map/ppermute | solution.py:377
  29.9 1.5 %collective-permute-start.13 = (bf16[64,1024]{1,0:T(8,128)(2,1)S(1)}, bf16[64,1024]{1,0:T(8,128)(2,1)S(1)}, u32[]{:S(2)}, u32[]{:S(2)}) collective-permute-start(bf16[64,1024]{1,0:T(8,128)(2,1)S(1)} %get-tuple-element.55), channel_id=1, source_target_pairs={{0,1},{1,0},{2,4},{3,5},{4,2},{5,3},{6,8},{7,9},{8,6},{9,7},{10,12... | collective-permute-start | bytes 393224 | tf_op jit(solution)/shard_map/ppermute | solution.py:381
  31.4 0.0 collective-permute-start.12
  31.4 0.0 collective-permute-done.11.pair_ref
  31.4 1.2 %collective-permute-start.14 = (f32[16,128]{1,0:T(8,128)S(1)}, f32[16,128]{1,0:T(8,128)S(1)}, u32[]{:S(2)}, u32[]{:S(2)}) collective-permute-start(f32[16,128]{1,0:T(8,128)S(1)} %gate_sum.1.gate_ref), channel_id=1, source_target_pairs={{0,1},{1,0},{2,3},{3,2},{4,5},{5,4},{6,7},{7,6},{8,9},{9,8},{10,11... | collective-permute-start | bytes 24584 | tf_op jit(solution)/shard_map/ppermute | solution.py:381
  32.7 2.1 %self_backward_1.1 = (bf16[128,4096]{1,0:T(8,128)(2,1)}, f32[64,1024]{1,0:T(8,128)S(1)}, f32[64,1024]{1,0:T(8,128)S(1)}) custom-call(bf16[128,4096]{1,0:T(8,128)(2,1)S(1)} %bitcast.16, bf16[128,1024]{1,0:T(8,128)(2,1)S(1)} %bitcast.20, bf16[80,1024]{1,0:T(8,128)(2,1)S(1)} %slice_bitcast_fusion.halo_ref, ...), custom_call_target="tpu_custom_call", output_to_operand_aliasing={{0}: (5, {})} | custom-call | flops 1000000 | bytes 100000 | tf_op jit(solution)/shard_map/self_backward_1/pallas_call | solution.py:465
  34.8 0.2 collective-permute-done.13.other_ref
  35.0 0.0 collective-permute-done.12.chip_ref
  35.0 0.1 collective-permute-done.14.refs_0_
  35.2 0.8 %finish.1 = (bf16[64,1024]{1,0:T(8,128)(2,1)}, bf16[128,1024]{1,0:T(8,128)(2,1)}, f32[1,32]{1,0:T(1,128)}) custom-call(f32[8,128]{1,0:T(8,128)S(1)} %get-tuple-element.34.owner_ref, f32[64,1024]{1,0:T(8,128)S(1)} %get-tuple-element.52.own_ref, f32[64,1152]{1,0:T(8,128)S(1)} %get-tuple-element.50.refs_1_.mine_ref, ...), custom_call_target="tpu_custom_call" | custom-call | flops 1000 | bytes 1000 | tf_op jit(solution)/shard_map/finish/pallas_call | solution.py:509
  (13 shorter events, 0.1 us)
Async XLA Ops:
  0.6 2.2 %copy-start.2 = (bf16[1,128,1024]{2,1,0:T(8,128)(2,1)S(1)}, bf16[1,128,1024]{2,1,0:T(8,128)(2,1)}, u32[]{:S(2)}) copy-start(bf16[1,128,1024]{2,1,0:T(8,128)(2,1)} %param.8) | copy-start | bytes 786436
  2.3 3.2 %collective-permute-start = (bf16[64,1408]{1,0:T(8,128)(2,1)S(1)}, bf16[64,1408]{1,0:T(8,128)(2,1)S(1)}, u32[]{:S(2)}, u32[]{:S(2)}) collective-permute-start(bf16[64,1408]{1,0:T(8,128)(2,1)S(1)} %concatenate.3.mine_ref.own_ref), channel_id=1, source_target_pairs={{0,2},{2,0},{4,6},{6,4},{8,10},{10,8},{12,14},{14,12},{16,18},{18,... | collective-permute-start | bytes 540680 | tf_op jit(solution)/shard_map/ppermute | solution.py:377
  2.8 9.2 %collective-permute-start.2 = (bf16[80,1024]{1,0:T(8,128)(2,1)S(1)}, bf16[80,1024]{1,0:T(8,128)(2,1)S(1)}, u32[]{:S(2)}, u32[]{:S(2)}) collective-permute-start(bf16[80,1024]{1,0:T(8,128)(2,1)S(1)} %slice_bitcast_fusion.halo_ref), channel_id=1, source_target_pairs={{0,1},{1,0},{2,4},{3,5},{4,2},{5,3},{6,8},{7,9},{8,6},{9,7},{10,12... | collective-permute-start | bytes 491528 | tf_op jit(solution)/shard_map/ppermute | solution.py:381
  5.4 6.6 %collective-permute-start.1 = (bf16[80,1024]{1,0:T(8,128)(2,1)S(1)}, bf16[80,1024]{1,0:T(8,128)(2,1)S(1)}, u32[]{:S(2)}, u32[]{:S(2)}) collective-permute-start(bf16[80,1024]{1,0:T(8,128)(2,1)S(1)} %slice_bitcast_fusion.halo_ref), channel_id=1, source_target_pairs={{0,2},{2,0},{4,6},{6,4},{8,10},{10,8},{12,14},{14,12},{16,18},{18,... | collective-permute-start | bytes 491528 | tf_op jit(solution)/shard_map/ppermute | solution.py:377
  5.6 9.8 %collective-permute-start.3 = (bf16[64,1152]{1,0:T(8,128)(2,1)S(1)}, bf16[64,1152]{1,0:T(8,128)(2,1)S(1)}, u32[]{:S(2)}, u32[]{:S(2)}) collective-permute-start(bf16[64,1152]{1,0:T(8,128)(2,1)S(1)} %get-tuple-element.36), channel_id=1, source_target_pairs={{0,8},{2,14},{4,12},{6,10},{8,16},{10,22},{12,20},{14,18},{16,24},... | collective-permute-start | bytes 442376 | tf_op jit(solution)/shard_map/ppermute | solution.py:377
  7.2 4.9 %collective-permute-start.4 = (bf16[64,512]{1,0:T(8,128)(2,1)S(1)}, bf16[64,512]{1,0:T(8,128)(2,1)S(1)}, u32[]{:S(2)}, u32[]{:S(2)}) collective-permute-start(bf16[64,512]{1,0:T(8,128)(2,1)S(1)} %get-tuple-element.37), channel_id=1, source_target_pairs={{0,4},{2,6},{4,0},{6,2},{8,12},{10,14},{12,8},{14,10},{16,20},{18,... | collective-permute-start | bytes 196616 | tf_op jit(solution)/shard_map/ppermute | solution.py:377
  8.8 0.7 %copy-start.4 = (s32[1,128]{1,0:T(1,128)S(1)}, s32[1,128]{1,0:T(1,128)}, u32[]{:S(2)}) copy-start(s32[1,128]{1,0:T(1,128)} %segment_ref.3) | copy-start | bytes 1540
  9.4 1.2 %copy-start = (bf16[1,128,4096]{2,1,0:T(8,128)(2,1)S(1)}, bf16[1,128,4096]{2,1,0:T(8,128)(2,1)}, u32[]{:S(2)}) copy-start(bf16[1,128,4096]{2,1,0:T(8,128)(2,1)} %param.7) | copy-start | bytes 3145732
  12.0 3.5 %copy-start.1 = (bf16[1,128,4096]{2,1,0:T(8,128)(2,1)S(1)}, bf16[1,128,4096]{2,1,0:T(8,128)(2,1)}, u32[]{:S(2)}) copy-start(bf16[1,128,4096]{2,1,0:T(8,128)(2,1)} %param.7) | copy-start | bytes 3145732
  12.1 3.4 %copy-start.5 = (f32[32]{0:T(128)S(1)}, f32[32]{0:T(128)}, u32[]{:S(2)}) copy-start(f32[32]{0:T(128)} %param.12) | copy-start | bytes 388
  15.4 1.6 %copy-start.3 = (bf16[1,128,4096]{2,1,0:T(8,128)(2,1)S(1)}, bf16[1,128,4096]{2,1,0:T(8,128)(2,1)}, u32[]{:S(2)}) copy-start(bf16[1,128,4096]{2,1,0:T(8,128)(2,1)} %param.13) | copy-start | bytes 3145732
  15.4 1.5 %collective-permute-start.5 = (bf16[64,1664]{1,0:T(8,128)(2,1)S(1)}, bf16[64,1664]{1,0:T(8,128)(2,1)S(1)}, u32[]{:S(2)}, u32[]{:S(2)}) collective-permute-start(bf16[64,1664]{1,0:T(8,128)(2,1)S(1)} %arrived.1._.mine_ref), channel_id=1, source_target_pairs={{0,2},{2,0},{4,6},{6,4},{8,10},{10,8},{12,14},{14,12},{16,18},{18,... | collective-permute-start | bytes 638984 | tf_op jit(solution)/shard_map/ppermute | solution.py:377
  19.2 1.7 %collective-permute-start.6 = (f32[64,1152]{1,0:T(8,128)S(1)}, f32[64,1152]{1,0:T(8,128)S(1)}, u32[]{:S(2)}, u32[]{:S(2)}) collective-permute-start(f32[64,1152]{1,0:T(8,128)S(1)} %get-tuple-element.41._.mine_ref), channel_id=1, source_target_pairs={{0,2},{2,0},{4,6},{6,4},{8,10},{10,8},{12,14},{14,12},{16,18},{18,... | collective-permute-start | bytes 884744 | tf_op jit(solution)/shard_map/ppermute | solution.py:377
  21.0 8.0 %collective-permute-start.8 = (bf16[64,1152]{1,0:T(8,128)(2,1)S(1)}, bf16[64,1152]{1,0:T(8,128)(2,1)S(1)}, u32[]{:S(2)}, u32[]{:S(2)}) collective-permute-start(bf16[64,1152]{1,0:T(8,128)(2,1)S(1)} %get-tuple-element.44.refs_0_), channel_id=1, source_target_pairs={{0,24},{2,30},{4,28},{6,26},{8,0},{10,6},{12,4},{14,2},{16,8},{18,... | collective-permute-start | bytes 442376 | tf_op jit(solution)/shard_map/ppermute | solution.py:377
  23.3 5.7 %collective-permute-start.7 = (bf16[64,640]{1,0:T(8,128)(2,1)S(1)}, bf16[64,640]{1,0:T(8,128)(2,1)S(1)}, u32[]{:S(2)}, u32[]{:S(2)}) collective-permute-start(bf16[64,640]{1,0:T(8,128)(2,1)S(1)} %get-tuple-element.47), channel_id=1, source_target_pairs={{0,4},{2,6},{4,0},{6,2},{8,12},{10,14},{12,8},{14,10},{16,20},{18,... | collective-permute-start | bytes 245768 | tf_op jit(solution)/shard_map/ppermute | solution.py:377
  23.3 4.6 %collective-permute-start.10 = (f32[16,128]{1,0:T(8,128)S(1)}, f32[16,128]{1,0:T(8,128)S(1)}, u32[]{:S(2)}, u32[]{:S(2)}) collective-permute-start(f32[16,128]{1,0:T(8,128)S(1)} %get-tuple-element.48.gate_ref), channel_id=1, source_target_pairs={{0,16},{2,22},{4,20},{6,18},{8,24},{10,30},{12,28},{14,26},{16,0},... | collective-permute-start | bytes 24584 | tf_op jit(solution)/shard_map/ppermute | solution.py:377
  23.5 5.4 %collective-permute-start.9 = (f32[16,128]{1,0:T(8,128)S(1)}, f32[16,128]{1,0:T(8,128)S(1)}, u32[]{:S(2)}, u32[]{:S(2)}) collective-permute-start(f32[16,128]{1,0:T(8,128)S(1)} %get-tuple-element.48.gate_ref), channel_id=1, source_target_pairs={{0,8},{2,14},{4,12},{6,10},{8,16},{10,22},{12,20},{14,18},{16,24},... | collective-permute-start | bytes 24584 | tf_op jit(solution)/shard_map/ppermute | solution.py:377
  29.0 2.4 %collective-permute-start.11 = (f32[64,1152]{1,0:T(8,128)S(1)}, f32[64,1152]{1,0:T(8,128)S(1)}, u32[]{:S(2)}, u32[]{:S(2)}) collective-permute-start(f32[64,1152]{1,0:T(8,128)S(1)} %get-tuple-element.50.refs_1_.mine_ref), channel_id=1, source_target_pairs={{0,2},{2,0},{4,6},{6,4},{8,10},{10,8},{12,14},{14,12},{16,18},{18,... | collective-permute-start | bytes 884744 | tf_op jit(solution)/shard_map/ppermute | solution.py:377
  29.9 5.1 %collective-permute-start.13 = (bf16[64,1024]{1,0:T(8,128)(2,1)S(1)}, bf16[64,1024]{1,0:T(8,128)(2,1)S(1)}, u32[]{:S(2)}, u32[]{:S(2)}) collective-permute-start(bf16[64,1024]{1,0:T(8,128)(2,1)S(1)} %get-tuple-element.55), channel_id=1, source_target_pairs={{0,1},{1,0},{2,4},{3,5},{4,2},{5,3},{6,8},{7,9},{8,6},{9,7},{10,12... | collective-permute-start | bytes 393224 | tf_op jit(solution)/shard_map/ppermute | solution.py:381
  31.4 3.5 %collective-permute-start.12 = (bf16[64,1024]{1,0:T(8,128)(2,1)S(1)}, bf16[64,1024]{1,0:T(8,128)(2,1)S(1)}, u32[]{:S(2)}, u32[]{:S(2)}) collective-permute-start(bf16[64,1024]{1,0:T(8,128)(2,1)S(1)} %get-tuple-element.55), channel_id=1, source_target_pairs={{0,2},{2,0},{4,6},{6,4},{8,10},{10,8},{12,14},{14,12},{16,18},{18,... | collective-permute-start | bytes 393224 | tf_op jit(solution)/shard_map/ppermute | solution.py:377
  31.4 3.7 %collective-permute-start.14 = (f32[16,128]{1,0:T(8,128)S(1)}, f32[16,128]{1,0:T(8,128)S(1)}, u32[]{:S(2)}, u32[]{:S(2)}) collective-permute-start(f32[16,128]{1,0:T(8,128)S(1)} %gate_sum.1.gate_ref), channel_id=1, source_target_pairs={{0,1},{1,0},{2,3},{3,2},{4,5},{5,4},{6,7},{7,6},{8,9},{9,8},{10,11... | collective-permute-start | bytes 24584 | tf_op jit(solution)/shard_map/ppermute | solution.py:381

commit v5 on v4

--- a/solution.py
+++ b/solution.py
@@ -59,10 +59,9 @@
     return (key >= query) & (key <= query + WINDOW) & (key_pos >= segment)
 
 
-def self_weights(query_rows, keys, allowed):
-    scores = dot(keys, query_rows, NT) * SCALE
+def self_weights(scores, allowed):
     allowed = jnp.concatenate([allowed] * (scores.shape[1] // LANES), axis=1)
-    return softmax_rows(jnp.where(allowed, scores, -1e30))
+    return softmax_rows(jnp.where(allowed, scores * SCALE, -1e30))
 
 
 def joined(context_ref, halo_ref, block, index):
@@ -118,12 +117,15 @@
     tok_rows = query_ref.shape[0]
     base = lax.axis_index("seq") * tok_rows
     allowed = self_mask(segment_ref, block, base)
+    scores = [
+        dot(joined(context_ref, halo_ref, block, g), stack(query_ref, block * WINDOW, WINDOW, g, repeat), NT)
+        for g in range(groups)
+    ]
+    weights = [self_weights(scores[g], allowed) for g in range(groups)]
     for g in range(groups):
-        rows = stack(query_ref, block * WINDOW, WINDOW, g, repeat)
-        weights = self_weights(rows, joined(context_ref, halo_ref, block, g), allowed)
-        weights_ref[g] = weights
+        weights_ref[g] = weights[g]
         values = joined(context_ref, halo_ref, block, groups + g)
-        out_ref[g] = dot(values, weights.astype(jnp.bfloat16), TN).astype(jnp.bfloat16)
+        out_ref[g] = dot(values, weights[g].astype(jnp.bfloat16), TN).astype(jnp.bfloat16)
 
 
 def split(values):
@@ -142,7 +144,7 @@
 
 def cross_kernel(
     off_ref, owner_ref, gate_ref, self_0_ref, self_1_ref, grad_ref, own_ref, chip_ref, mine_ref, pair_ref,
-    scores_ref, to_pair_ref, in_chip_ref, own_terms_ref, mask_ref, prev, *, groups, repeat
+    scores_ref, to_pair_ref, in_chip_ref, own_terms_ref, mask_ref, prev, *, groups, repeat, step=2
 ):
     tok_rows, width = grad_ref.shape[0], chip_ref.shape[1]
     img = own_ref.shape[0]
@@ -175,51 +177,56 @@
     has_lane = lane_tok >= has_from
     row_tok = lax.broadcasted_iota(jnp.int32, (WINDOW, HEAD_DIM), 0)
 
+    def pick(joint):
+        return jnp.where(use_own, joint[img:], joint[:img])
+
+    def join(values):
+        zero = jnp.zeros_like(values)
+        both = [jnp.where(use_own, zero, values), jnp.where(use_own, values, zero)]
+        return jnp.concatenate(both, axis=0).astype(jnp.bfloat16)
+
+    blocks = range(tok_rows // WINDOW)
     gate_rows = []
-    for g in range(groups):
-        keys = jnp.concatenate([part(prev, g), part(own_ref, g)], axis=0)
-        values = jnp.concatenate([part(prev, groups + g), part(own_ref, groups + g)], axis=0)
-        out_t = jnp.concatenate([self_0_ref[g], self_1_ref[g]], axis=1)
-        scores = dot(keys, out_t, NN)
-        weights = softmax_rows(jnp.where(use_own, scores[img:], scores[:img]) * SCALE)
-        narrow = weights.astype(jnp.bfloat16)
-        grad_rows, cross_rows = [], []
-        for block in range(tok_rows // WINDOW):
-            has_rows = row_tok + block * WINDOW >= has_from
-            for h in range(repeat):
-                head = g * repeat + h
-                tile = grad_ref[
-                    block * WINDOW : (block + 1) * WINDOW, head * HEAD_DIM : (head + 1) * HEAD_DIM
+    for first in range(0, groups, step):
+        every = range(first, first + step)
+        keys = {g: jnp.concatenate([part(prev, g), part(own_ref, g)], axis=0) for g in every}
+        values = {g: jnp.concatenate([part(prev, groups + g), part(own_ref, groups + g)], axis=0) for g in every}
+        out_t = {g: jnp.concatenate([self_0_ref[g], self_1_ref[g]], axis=1) for g in every}
+        scores = {g: dot(keys[g], out_t[g], NN) for g in every}
+        plain, cross_rows, grad_weights = {}, {}, {}
+        for g in every:
+            tiles = [stack(grad_ref, block * WINDOW, WINDOW, g, repeat) for block in blocks]
+            plain[g] = dot(values[g], jnp.concatenate(tiles, axis=0), NT)
+            scaled = []
+            for block in blocks:
+                has_rows = row_tok + block * WINDOW >= has_from
+                factors = [
+                    jnp.where(has_rows, gate_ref[g * repeat + h : g * repeat + h + 1, :], 0.0) for h in range(repeat)
                 ]
-                grad_rows.append(tile)
-                factor = jnp.where(has_rows, gate_ref[head : head + 1, :], 0.0)
-                cross_rows.append((tile.astype(jnp.float32) * factor).astype(jnp.bfloat16))
-        grad_rows = jnp.concatenate(grad_rows, axis=0)
-        cross_rows = jnp.concatenate(cross_rows, axis=0)
-        plain = dot(values, grad_rows, NT)
-        plain = jnp.where(use_own, plain[img:], plain[:img])
-        gate_row = jnp.sum(narrow.astype(jnp.float32) * plain, axis=0, keepdims=True)
-        gate_row = jnp.where(has_lane, gate_row, 0.0)
-        gate_row = gate_row[:, :half] + gate_row[:, half:]
-        gate_rows.extend(gate_row[:, i * LANES : (i + 1) * LANES] for i in range(half // LANES))
-        grad_weights = dot(values, cross_rows, NT)
-        grad_weights = jnp.where(use_own, grad_weights[img:], grad_weights[:img])
-        delta = jnp.sum(weights * grad_weights, axis=0, keepdims=True)
-        grad_scores = weights * (grad_weights - delta)
-        scores_j = jnp.concatenate(
-            [jnp.where(use_own, 0.0, grad_scores), jnp.where(use_own, grad_scores, 0.0)], axis=0
-        ).astype(jnp.bfloat16)
-        narrow_j = jnp.concatenate(
-            [jnp.where(use_own, 0.0, weights), jnp.where(use_own, weights, 0.0)], axis=0
-        ).astype(jnp.bfloat16)
-        grad_key = dot(scores_j, out_t, NT) * SCALE
-        grad_value = dot(narrow_j, cross_rows, NN)
-        scores_ref[g] = scores_j
-        for index, terms in ((g, grad_key), (groups + g, grad_value)):
-            cols = slice(index * HEAD_DIM, (index + 1) * HEAD_DIM)
-            own_terms_ref[:, cols] = terms[img:]
-            to_pair_ref[:, cols] = terms[:img] * (from_x + from_z)
-            in_chip_ref[:, cols] = terms[:img] * from_chip
+                scaled.append(
+                    (tiles[block].astype(jnp.float32) * jnp.concatenate(factors, axis=0)).astype(jnp.bfloat16)
+                )
+            cross_rows[g] = jnp.concatenate(scaled, axis=0)
+            grad_weights[g] = dot(values[g], cross_rows[g], NT)
+        weights = {g: softmax_rows(pick(scores[g]) * SCALE) for g in every}
+        score_terms = {}
+        for g in every:
+            gate_row = jnp.sum(weights[g].astype(jnp.bfloat16).astype(jnp.float32) * pick(plain[g]), axis=0, keepdims=True)
+            gate_row = jnp.where(has_lane, gate_row, 0.0)
+            gate_row = gate_row[:, :half] + gate_row[:, half:]
+            gate_rows.extend(gate_row[:, i * LANES : (i + 1) * LANES] for i in range(half // LANES))
+            weight_terms = pick(grad_weights[g])
+            delta = jnp.sum(weights[g] * weight_terms, axis=0, keepdims=True)
+            score_terms[g] = join(weights[g] * (weight_terms - delta))
+            scores_ref[g] = score_terms[g]
+        for g in every:
+            grad_key = dot(score_terms[g], out_t[g], NT) * SCALE
+            grad_value = dot(join(weights[g]), cross_rows[g], NN)
+            for index, terms in ((g, grad_key), (groups + g, grad_value)):
+                cols = slice(index * HEAD_DIM, (index + 1) * HEAD_DIM)
+                own_terms_ref[:, cols] = terms[img:]
+                to_pair_ref[:, cols] = terms[:img] * (from_x + from_z)
+                in_chip_ref[:, cols] = terms[:img] * from_chip
     gate = jnp.concatenate(gate_rows, axis=0)
     to_pair_ref[:, width:] = jnp.concatenate([gate] * (img // gate.shape[0]), axis=0)
     row = lax.broadcasted_iota(jnp.int32, mask_ref.shape, 0)
@@ -251,36 +258,40 @@
 
 
 def chip_sum_kernel(mine_ref, x_ref, z_ref, gate_ref, *refs):
-    *gates, _, out_ref, gate_out = refs
+    *gates, _, out_ref, gate_out, to_pair_ref = refs
     width = mine_ref.shape[1]
     odd = odd_core().astype(jnp.float32)
     half = width // 2
     from_x = x_ref[:, :half].astype(jnp.float32)
-    out_ref[:, :half] = mine_ref[:, :half] + (from_x * (1.0 - odd) + z_ref[:, :half].astype(jnp.float32))
-    out_ref[:, half:width] = mine_ref[:, half:] + (from_x * odd + z_ref[:, half:width].astype(jnp.float32))
-    gate_out[...] = gate_ref[...] + unsplit(x_ref[:, half:])
+    first = mine_ref[:, :half] + (from_x * (1.0 - odd) + z_ref[:, :half].astype(jnp.float32))
+    second = mine_ref[:, half:] + (from_x * odd + z_ref[:, half:width].astype(jnp.float32))
+    for cols, terms in ((slice(0, half), first), (slice(half, width), second)):
+        out_ref[:, cols] = terms
+        to_pair_ref[:, cols] = terms.astype(to_pair_ref.dtype)
     gate = unsplit(z_ref[:, width:])
     for ref in gates:
         gate = gate + ref[...]
-    out_ref[:, width:] = jnp.concatenate([gate] * (mine_ref.shape[0] // gate.shape[0]), axis=0)
+    gate_out[...] = gate_ref[...] + unsplit(x_ref[:, half:]) + gate
+    to_pair_ref[:, width:] = split(gate)
 
 
 def self_back_kernel(
     query_ref, context_ref, halo_ref, weights_ref, grad_ref, *refs, block, groups, repeat
 ):
     query_grad_ref, key_low_ref, key_high_ref, rows_out, sems = refs[-5:]
+    half = repeat * WINDOW
+    every = range(groups)
+    rows = [stack(query_ref, block * WINDOW, WINDOW, g, repeat) for g in every]
+    keys = [joined(context_ref, halo_ref, block, g) for g in every]
+    grads = [grad_ref[g, block * half : (block + 1) * half, :] for g in every]
+    grad_weights = [dot(joined(context_ref, halo_ref, block, groups + g), grads[g], NT) for g in every]
+    grad_scores = []
+    for g in every:
+        delta = jnp.sum(weights_ref[g] * grad_weights[g], axis=0, keepdims=True)
+        grad_scores.append((weights_ref[g] * (grad_weights[g] - delta)).astype(jnp.bfloat16))
     copies = []
-    half = repeat * WINDOW
-    for g in range(groups):
-        rows = stack(query_ref, block * WINDOW, WINDOW, g, repeat)
-        keys = joined(context_ref, halo_ref, block, g)
-        values = joined(context_ref, halo_ref, block, groups + g)
-        weights = weights_ref[g]
-        grads = grad_ref[g, block * half : (block + 1) * half, :]
-        grad_weights = dot(values, grads, NT)
-        delta = jnp.sum(weights * grad_weights, axis=0, keepdims=True)
-        grad_scores = (weights * (grad_weights - delta)).astype(jnp.bfloat16)
-        grad_query = (dot(grad_scores, keys, TN) * SCALE).astype(jnp.bfloat16)
+    for g in every:
+        grad_query = (dot(grad_scores[g], keys[g], TN) * SCALE).astype(jnp.bfloat16)
         for h in range(repeat):
             head = g * repeat + h
             rows_out[:, head * HEAD_DIM : (head + 1) * HEAD_DIM] = grad_query[h * WINDOW : (h + 1) * WINDOW]
@@ -291,20 +302,19 @@
             )
         )
         copies[-1].start()
-        grad_key = dot(grad_scores, rows, NN) * SCALE
-        grad_value = dot(weights.astype(jnp.bfloat16), grads, NN)
+    for g in every:
+        grad_key = dot(grad_scores[g], rows[g], NN) * SCALE
+        grad_value = dot(weights_ref[g].astype(jnp.bfloat16), grads[g], NN)
         for index, terms in ((g, grad_key), (groups + g, grad_value)):
             cols = slice(index * HEAD_DIM, (index + 1) * HEAD_DIM)
-            key_low_ref[:, cols] = terms[:WINDOW].astype(key_low_ref.dtype)
+            key_low_ref[key_low_ref.shape[0] - WINDOW :, cols] = terms[:WINDOW].astype(key_low_ref.dtype)
             key_high_ref[:, cols] = terms[WINDOW:]
     for copy in copies:
         copy.wait()
 
 
-def gate_kernel(chip_ref, mine_ref, pair_ref, out_ref):
-    width = mine_ref.shape[1] - LANES
-    rows = out_ref.shape[0]
-    out_ref[...] = chip_ref[...] + (mine_ref[:rows, width:] + pair_ref[:rows, width:])
+def gate_kernel(mine_ref, pair_ref, out_ref):
+    out_ref[...] = mine_ref[...] + unsplit(pair_ref[:, pair_ref.shape[1] - LANES :])
 
 
 def gate_grad(total, gate_ref):
@@ -326,9 +336,9 @@
     owner_ref, own_ref, mine_ref, pair_ref, low_ref, also_ref, high_ref, halo_ref, gate_ref, *refs, tok_rows
 ):
     *far_refs, tanh_ref, memory_ref, context_ref, gate_out = refs
-    width = own_ref.shape[1]
+    width = mine_ref.shape[1]
     keep = owner(owner_ref, 0).astype(jnp.float32)
-    total = own_ref[...] + (mine_ref[:, :width] + pair_ref[:, :width])
+    total = own_ref[...] + (mine_ref[...] + pair_ref[:, :width].astype(jnp.float32))
     memory_ref[...] = (total * keep).astype(memory_ref.dtype)
     more = jnp.where(lax.axis_index("seq") < lax.axis_size("seq") - 1, 1.0, 0.0)
     first = tok_rows - WINDOW
@@ -467,7 +477,7 @@
             functools.partial(self_back_kernel, block=block, groups=groups, repeat=repeat),
             [
                 struct((tok_rows, model), bf16),
-                struct((WINDOW, width), f32 if block else bf16),
+                struct((WINDOW, width), f32) if block else struct((WINDOW + MORE, width), bf16),
                 struct((WINDOW, width), f32),
             ],
             [VMEM] * 5 + [ANY] * (1 if late is None else 2),
@@ -490,17 +500,17 @@
     if swaps:
         gates = [send_z(gate, 1), send_z(gate, 2)]
     query_grad, halo_terms, low = self_backward(0, to_z)
-    mine, gate = call(
+    mine, gate, to_chip = call(
         "chip_sum",
         chip_sum_kernel,
-        [struct((img, width + LANES), f32), gate_shape],
+        [struct((img, width), f32), gate_shape, struct((img, width + LANES), bf16)],
         [VMEM] * (4 + len(gates)) + [ANY],
     )(in_chip, from_x, from_z, gate, *gates, low)
-    other = send(mine, lambda i: i ^ 1)
+    other = send(to_chip, lambda i: i ^ 1)
     halo_back = send_near(halo_terms, -1)
     query_grad, also, high = self_backward(1, query_grad, mine)
     halo_back = merge("halo_back", halo_back, -1, high)
-    gate = call("gate_sum", gate_kernel, [gate_shape], [VMEM] * 3)(gate, mine, other)[0]
+    gate = call("gate_sum", gate_kernel, [gate_shape], [VMEM] * 2)(gate, other)[0]
     if swaps:
         far = [send_all(gate, lambda s, d: (s, d ^ 1))]
     else:

time: 36.2 us -> 35.4 us (0.978)
  Pallas kernels: 10.8 us -> 8.4 us
  waiting for transfers between devices: 5.92 us -> 7.38 us
    pallas_call x2, Pallas kernels: 4.19 us -> 2.9 us  [self_backward(): call(f'self_backward_{block}', functools.partial(self_back_kernel, block=...]
    ppermute x12, waiting for transfers between devices: 5.58 us -> 6.77 us  [send(): return lax.ppermute(value, 'seq', [(i, where(i)) for i in range(seq)])]
    pallas_call x2, Pallas kernels: 2.71 us -> 1.54 us  [self_forward(): call(f'self_forward_{block}', functools.partial(self_kernel, block=block,...]
    ppermute x3, starting transfers between devices: 5.34 us -> 5.72 us  [send_all(): lax.ppermute(value, ('seq', 'dp'), [(s * dp + d, t * dp + e) for s, d, t,...]
  transfers between devices with their start and end apart: 15 -> 15, of which waited for: 7 -> 7; matrix products, arithmetic and copies ran while one was open for 0% -> 0% of each run, Pallas kernels for 21% -> 15%
where the time goes in v5:
time: 35.4 us; the launch traced here: 35.2 us
  starting transfers between devices  15 us (42%)
  Pallas kernels  8.4 us (24%)
  waiting for transfers between devices  7.38 us (21%)
  local copies, waits for them, and re-layouts  2.91 us (8%)
  between operations  1.52 us (4%)
    ppermute x12, starting transfers between devices, send(): return lax.ppermute(value, 'seq', [(i, where(i)) for i in range(seq)])  9.29 us
    ppermute x12, waiting for transfers between devices, send(): return lax.ppermute(value, 'seq', [(i, where(i)) for i in range(seq)])  6.77 us
    ppermute x3, starting transfers between devices, send_all(): lax.ppermute(value, ('seq', 'dp'), [(s * dp + d, t * dp + e) for s, d, t,...  5.72 us
    pallas_call x2, Pallas kernels, self_backward(): call(f'self_backward_{block}', functools.partial(self_back_kernel, block=...  2.9 us
    pallas_call x1, Pallas kernels, on_device(): call('cross', functools.partial(cross_kernel, groups=groups, repeat=repea...  2.17 us
    unnamed x12, local copies, waits for them, and re-layouts  1.9 us
    pallas_call x2, Pallas kernels, self_forward(): call(f'self_forward_{block}', functools.partial(self_kernel, block=block,...  1.54 us
    concatenate x1, local copies, waits for them, and re-layouts, on_device(): jnp.concatenate([own, jnp.broadcast_to(is_owner, (img, MARKS))], axis=1)  0.92 us
  transfers between devices with their start and end apart: 15, of which 7 were waited for; matrix products, arithmetic and copies ran while one was open for 0% of the time, Pallas kernels for 15%

profile of v5, /device:TPU:0, one launch (start us, length us, event | category | flops | bytes accessed | tf_op | source)
XLA Modules:
  0.0 35.2 jit_solution(16863836351683616391)
XLA Ops:
  1.3 0.9 %concatenate.3.mine_ref.own_ref = bf16[64,1408]{1,0:T(8,128)(2,1)S(1)} pad(bf16[64,1024]{1,0:T(8,128)(2,1)} %bitcast.24, bf16[]{:T(256)} %bitcast.4), padding=0_0x0_384 | pad | bytes 311298 | tf_op jit(solution)/shard_map/concatenate | solution.py:418
  2.3 0.5 %collective-permute-start = (bf16[64,1408]{1,0:T(8,128)(2,1)S(1)}, bf16[64,1408]{1,0:T(8,128)(2,1)S(1)}, u32[]{:S(2)}, u32[]{:S(2)}) collective-permute-start(bf16[64,1408]{1,0:T(8,128)(2,1)S(1)} %concatenate.3.mine_ref.own_ref), channel_id=1, source_target_pairs={{0,2},{2,0},{4,6},{6,4},{8,10},{10,8},{12,14},{14,12},{16,18},{18,... | collective-permute-start | bytes 540680 | tf_op jit(solution)/shard_map/ppermute | solution.py:387
  2.8 2.6 %collective-permute-start.2 = (bf16[80,1024]{1,0:T(8,128)(2,1)S(1)}, bf16[80,1024]{1,0:T(8,128)(2,1)S(1)}, u32[]{:S(2)}, u32[]{:S(2)}) collective-permute-start(bf16[80,1024]{1,0:T(8,128)(2,1)S(1)} %slice_bitcast_fusion.halo_ref), channel_id=1, source_target_pairs={{0,1},{1,0},{2,4},{3,5},{4,2},{5,3},{6,8},{7,9},{8,6},{9,7},{10,12... | collective-permute-start | bytes 491528 | tf_op jit(solution)/shard_map/ppermute | solution.py:391
  5.4 0.1 collective-permute-start.1
  5.5 0.0 collective-permute-done.other_ref
  5.5 0.1 chip_image.1
  5.6 1.6 %collective-permute-start.3 = (bf16[64,1152]{1,0:T(8,128)(2,1)S(1)}, bf16[64,1152]{1,0:T(8,128)(2,1)S(1)}, u32[]{:S(2)}, u32[]{:S(2)}) collective-permute-start(bf16[64,1152]{1,0:T(8,128)(2,1)S(1)} %get-tuple-element.37), channel_id=1, source_target_pairs={{0,8},{2,14},{4,12},{6,10},{8,16},{10,22},{12,20},{14,18},{16,24},... | collective-permute-start | bytes 442376 | tf_op jit(solution)/shard_map/ppermute | solution.py:387
  7.2 1.5 %collective-permute-start.4 = (bf16[64,512]{1,0:T(8,128)(2,1)S(1)}, bf16[64,512]{1,0:T(8,128)(2,1)S(1)}, u32[]{:S(2)}, u32[]{:S(2)}) collective-permute-start(bf16[64,512]{1,0:T(8,128)(2,1)S(1)} %get-tuple-element.38), channel_id=1, source_target_pairs={{0,4},{2,6},{4,0},{6,2},{8,12},{10,14},{12,8},{14,10},{16,20},{18,... | collective-permute-start | bytes 196616 | tf_op jit(solution)/shard_map/ppermute | solution.py:387
  8.8 0.7 %copy-done.4 = s32[1,128]{1,0:T(1,128)S(1)} copy-done((s32[1,128]{1,0:T(1,128)S(1)}, s32[1,128]{1,0:T(1,128)}, u32[]{:S(2)}) %copy-start.4) | copy-done | bytes 536
  9.4 1.2 %copy-done = bf16[1,128,4096]{2,1,0:T(8,128)(2,1)S(1)} copy-done((bf16[1,128,4096]{2,1,0:T(8,128)(2,1)S(1)}, bf16[1,128,4096]{2,1,0:T(8,128)(2,1)}, u32[]{:S(2)}) %copy-start) | copy-done | bytes 1048600
  10.6 0.8 %self_forward_1.1 = (bf16[4,128,512]{2,1,0:T(8,128)(2,1)S(1)}, f32[4,128,512]{2,1,0:T(8,128)S(1)}) custom-call(bf16[128,4096]{1,0:T(8,128)(2,1)S(1)} %bitcast.13, bf16[128,1024]{1,0:T(8,128)(2,1)S(1)} %bitcast.17, bf16[80,1024]{1,0:T(8,128)(2,1)S(1)} %slice_bitcast_fusion.halo_ref, s32[1,128]{1,0:T(1,128)S(1)} %copy-done.4, ...), custom_call_target="tpu_custom_call" | custom-call | flops 1000000 | bytes 100000 | tf_op jit(solution)/shard_map/self_forward_1/pallas_call | solution.py:434
  11.4 0.0 copy-start.1
  11.4 0.0 collective-permute-done.2.other_ref
  11.4 0.0 collective-permute-done.1.chip_ref
  11.5 0.0 copy-start.5
  11.5 0.4 %collective-permute-done.4.x_ref = bf16[64,512]{1,0:T(8,128)(2,1)S(1)} collective-permute-done((bf16[64,512]{1,0:T(8,128)(2,1)S(1)}, bf16[64,512]{1,0:T(8,128)(2,1)S(1)}, u32[]{:S(2)}, u32[]{:S(2)}) %collective-permute-start.4) | collective-permute-done | bytes 65568 | tf_op jit(solution)/shard_map/ppermute | solution.py:387
  11.9 3.5 %collective-permute-done.3.z_ref = bf16[64,1152]{1,0:T(8,128)(2,1)S(1)} collective-permute-done((bf16[64,1152]{1,0:T(8,128)(2,1)S(1)}, bf16[64,1152]{1,0:T(8,128)(2,1)S(1)}, u32[]{:S(2)}, u32[]{:S(2)}) %collective-permute-start.3) | collective-permute-done | bytes 147488 | tf_op jit(solution)/shard_map/ppermute | solution.py:387
  15.4 0.0 copy-start.3
  15.4 0.1 collective-permute-start.5
  15.5 0.8 %self_forward_0.1 = (bf16[4,128,512]{2,1,0:T(8,128)(2,1)S(1)}, f32[4,128,512]{2,1,0:T(8,128)S(1)}) custom-call(bf16[128,4096]{1,0:T(8,128)(2,1)S(1)} %bitcast.14, bf16[128,1024]{1,0:T(8,128)(2,1)S(1)} %bitcast.18, bf16[64,1024]{1,0:T(8,128)(2,1)S(1)} %halo.1.__.halo_ref, s32[1,128]{1,0:T(1,128)S(1)} %copy-done.4, bf16[64,1664]{1,0:T(8,128)(2,1)S(1)} %arrived.1._.mine_ref), custom_call_target="tpu_custom_call" | custom-call | flops 1000000 | bytes 100000 | tf_op jit(solution)/shard_map/self_forward_0/pallas_call | solution.py:434
  16.3 0.6 %collective-permute-done.5.pair_ref = bf16[64,1664]{1,0:T(8,128)(2,1)S(1)} collective-permute-done((bf16[64,1664]{1,0:T(8,128)(2,1)S(1)}, bf16[64,1664]{1,0:T(8,128)(2,1)S(1)}, u32[]{:S(2)}, u32[]{:S(2)}) %collective-permute-start.5) | collective-permute-done | bytes 213024 | tf_op jit(solution)/shard_map/ppermute | solution.py:387
  17.0 0.1 broadcast_in_dim.34.gate_ref.refs_1_
  17.0 0.0 copy-done.3
  17.0 2.2 %cross.1 = (bf16[4,128,1024]{2,1,0:T(8,128)(2,1)S(1)}, f32[64,1152]{1,0:T(8,128)S(1)}, f32[64,1024]{1,0:T(8,128)S(1)}, f32[64,1024]{1,0:T(8,128)S(1)}, f32[8,128...) custom-call(s32[8,128]{1,0:T(8,128)S(1)} %broadcast_in_dim.33.off_ref, f32[8,128]{1,0:T(8,128)S(1)} %get-tuple-element.35.owner_ref, ...), custom_call_target="tpu_custom_call" | custom-call | flops 1000 | bytes 1000 | tf_op jit(solution)/shard_map/cross/pallas_call | solution.py:453
  19.2 0.2 collective-permute-start.6
  19.4 0.5 %cross_query.1._.grad_ref = bf16[4,1024,128]{2,1,0:T(8,128)(2,1)S(1)} custom-call(bf16[4,128,1024]{2,1,0:T(8,128)(2,1)S(1)} %get-tuple-element.40.scores_ref, bf16[128,4096]{1,0:T(8,128)(2,1)S(1)} %bitcast.22, bf16[64,1408]{1,0:T(8,128)(2,1)S(1)} %concatenate.3.mine_ref.own_ref, bf16[64,1024]{1,0:T(8,128)(2,1)S(1)} %get-tuple-element.41.prev, ...), custom_call_target="tpu_custom_call" | custom-call | flops 1000 | bytes 1000 | tf_op jit(solution)/shard_map/cross_query/pallas_call | solution.py:467
  19.9 0.9 %collective-permute-done.6.pair_ref = f32[64,1152]{1,0:T(8,128)S(1)} collective-permute-done((f32[64,1152]{1,0:T(8,128)S(1)}, f32[64,1152]{1,0:T(8,128)S(1)}, u32[]{:S(2)}, u32[]{:S(2)}) %collective-permute-start.6) | collective-permute-done | bytes 294944 | tf_op jit(solution)/shard_map/ppermute | solution.py:387
  20.8 0.1 outside.1
  21.0 2.3 %collective-permute-start.8 = (bf16[64,1152]{1,0:T(8,128)(2,1)S(1)}, bf16[64,1152]{1,0:T(8,128)(2,1)S(1)}, u32[]{:S(2)}, u32[]{:S(2)}) collective-permute-start(bf16[64,1152]{1,0:T(8,128)(2,1)S(1)} %get-tuple-element.45.refs_0_), channel_id=1, source_target_pairs={{0,24},{2,30},{4,28},{6,26},{8,0},{10,6},{12,4},{14,2},{16,8},{18,... | collective-permute-start | bytes 442376 | tf_op jit(solution)/shard_map/ppermute | solution.py:387
  23.3 0.0 collective-permute-start.7
  23.3 0.2 collective-permute-start.10
  23.5 1.8 %collective-permute-start.9 = (f32[16,128]{1,0:T(8,128)S(1)}, f32[16,128]{1,0:T(8,128)S(1)}, u32[]{:S(2)}, u32[]{:S(2)}) collective-permute-start(f32[16,128]{1,0:T(8,128)S(1)} %get-tuple-element.49.gate_ref), channel_id=1, source_target_pairs={{0,8},{2,14},{4,12},{6,10},{8,16},{10,22},{12,20},{14,18},{16,24},... | collective-permute-start | bytes 24584 | tf_op jit(solution)/shard_map/ppermute | solution.py:387
  25.3 1.5 %self_backward_0.1 = (bf16[128,4096]{1,0:T(8,128)(2,1)}, bf16[80,1024]{1,0:T(8,128)(2,1)S(1)}, f32[64,1024]{1,0:T(8,128)S(1)}) custom-call(bf16[128,4096]{1,0:T(8,128)(2,1)S(1)} %bitcast.15, bf16[128,1024]{1,0:T(8,128)(2,1)S(1)} %bitcast.19, bf16[64,1024]{1,0:T(8,128)(2,1)S(1)} %halo.1.__.halo_ref, f32[4,128,512]{2,1,0:T(8,128)S(1)} %get-tuple-element.43.weights_ref, ...), custom_call_target="tpu_custom_call" | custom-call | flops 1000000 | bytes 100000 | tf_op jit(solution)/shard_map/self_backward_0/pallas_call | solution.py:475
  26.8 1.6 %collective-permute-start.13 = (bf16[80,1024]{1,0:T(8,128)(2,1)S(1)}, bf16[80,1024]{1,0:T(8,128)(2,1)S(1)}, u32[]{:S(2)}, u32[]{:S(2)}) collective-permute-start(bf16[80,1024]{1,0:T(8,128)(2,1)S(1)} %get-tuple-element.57), channel_id=1, source_target_pairs={{0,1},{1,0},{2,4},{3,5},{4,2},{5,3},{6,8},{7,9},{8,6},{9,7},{10,12... | collective-permute-start | bytes 491528 | tf_op jit(solution)/shard_map/ppermute | solution.py:391
  28.3 0.0 collective-permute-done.10.refs_1_
  28.3 0.3 collective-permute-start.12
  28.6 0.3 collective-permute-done.9.refs_0_
  28.9 0.0 collective-permute-done.7.x_ref
  28.9 0.0 collective-permute-done.8.z_ref
  28.9 0.1 chip_sum.1
  29.0 0.6 %collective-permute-start.11 = (bf16[64,1152]{1,0:T(8,128)(2,1)S(1)}, bf16[64,1152]{1,0:T(8,128)(2,1)S(1)}, u32[]{:S(2)}, u32[]{:S(2)}) collective-permute-start(bf16[64,1152]{1,0:T(8,128)(2,1)S(1)} %get-tuple-element.54), channel_id=1, source_target_pairs={{0,2},{2,0},{4,6},{6,4},{8,10},{10,8},{12,14},{14,12},{16,18},{18,... | collective-permute-start | bytes 442376 | tf_op jit(solution)/shard_map/ppermute | solution.py:387
  29.7 1.0 %collective-permute-done.11.pair_ref = bf16[64,1152]{1,0:T(8,128)(2,1)S(1)} collective-permute-done((bf16[64,1152]{1,0:T(8,128)(2,1)S(1)}, bf16[64,1152]{1,0:T(8,128)(2,1)S(1)}, u32[]{:S(2)}, u32[]{:S(2)}) %collective-permute-start.11) | collective-permute-done | bytes 147488 | tf_op jit(solution)/shard_map/ppermute | solution.py:387
  30.7 1.5 %collective-permute-start.14 = (f32[16,128]{1,0:T(8,128)S(1)}, f32[16,128]{1,0:T(8,128)S(1)}, u32[]{:S(2)}, u32[]{:S(2)}) collective-permute-start(f32[16,128]{1,0:T(8,128)S(1)} %gate_sum.1.gate_ref), channel_id=1, source_target_pairs={{0,1},{1,0},{2,3},{3,2},{4,5},{5,4},{6,7},{7,6},{8,9},{9,8},{10,11... | collective-permute-start | bytes 24584 | tf_op jit(solution)/shard_map/ppermute | solution.py:391
  32.2 1.4 %self_backward_1.1 = (bf16[128,4096]{1,0:T(8,128)(2,1)}, f32[64,1024]{1,0:T(8,128)S(1)}, f32[64,1024]{1,0:T(8,128)S(1)}) custom-call(bf16[128,4096]{1,0:T(8,128)(2,1)S(1)} %bitcast.16, bf16[128,1024]{1,0:T(8,128)(2,1)S(1)} %bitcast.20, bf16[80,1024]{1,0:T(8,128)(2,1)S(1)} %slice_bitcast_fusion.halo_ref, ...), custom_call_target="tpu_custom_call", output_to_operand_aliasing={{0}: (5, {})} | custom-call | flops 1000000 | bytes 100000 | tf_op jit(solution)/shard_map/self_backward_1/pallas_call | solution.py:475
  33.7 0.0 collective-permute-done.13.other_ref
  33.7 0.0 collective-permute-done.12.chip_ref
  33.7 0.6 %collective-permute-done.14.refs_0_ = f32[16,128]{1,0:T(8,128)S(1)} collective-permute-done((f32[16,128]{1,0:T(8,128)S(1)}, f32[16,128]{1,0:T(8,128)S(1)}, u32[]{:S(2)}, u32[]{:S(2)}) %collective-permute-start.14) | collective-permute-done | bytes 8224 | tf_op jit(solution)/shard_map/ppermute | solution.py:391
  34.3 0.9 %finish.1 = (bf16[64,1024]{1,0:T(8,128)(2,1)}, bf16[128,1024]{1,0:T(8,128)(2,1)}, f32[1,32]{1,0:T(1,128)}) custom-call(f32[8,128]{1,0:T(8,128)S(1)} %get-tuple-element.35.owner_ref, f32[64,1024]{1,0:T(8,128)S(1)} %get-tuple-element.53.own_ref, f32[64,1024]{1,0:T(8,128)S(1)} %get-tuple-element.51.refs_1_.mine_ref, ...), custom_call_target="tpu_custom_call" | custom-call | flops 1000 | bytes 1000 | tf_op jit(solution)/shard_map/finish/pallas_call | solution.py:519
  (13 shorter events, 0.1 us)
Async XLA Ops:
  0.6 2.2 %copy-start.2 = (bf16[1,128,1024]{2,1,0:T(8,128)(2,1)S(1)}, bf16[1,128,1024]{2,1,0:T(8,128)(2,1)}, u32[]{:S(2)}) copy-start(bf16[1,128,1024]{2,1,0:T(8,128)(2,1)} %param.8) | copy-start | bytes 786436
  2.3 3.2 %collective-permute-start = (bf16[64,1408]{1,0:T(8,128)(2,1)S(1)}, bf16[64,1408]{1,0:T(8,128)(2,1)S(1)}, u32[]{:S(2)}, u32[]{:S(2)}) collective-permute-start(bf16[64,1408]{1,0:T(8,128)(2,1)S(1)} %concatenate.3.mine_ref.own_ref), channel_id=1, source_target_pairs={{0,2},{2,0},{4,6},{6,4},{8,10},{10,8},{12,14},{14,12},{16,18},{18,... | collective-permute-start | bytes 540680 | tf_op jit(solution)/shard_map/ppermute | solution.py:387
  2.8 8.6 %collective-permute-start.2 = (bf16[80,1024]{1,0:T(8,128)(2,1)S(1)}, bf16[80,1024]{1,0:T(8,128)(2,1)S(1)}, u32[]{:S(2)}, u32[]{:S(2)}) collective-permute-start(bf16[80,1024]{1,0:T(8,128)(2,1)S(1)} %slice_bitcast_fusion.halo_ref), channel_id=1, source_target_pairs={{0,1},{1,0},{2,4},{3,5},{4,2},{5,3},{6,8},{7,9},{8,6},{9,7},{10,12... | collective-permute-start | bytes 491528 | tf_op jit(solution)/shard_map/ppermute | solution.py:391
  5.4 6.0 %collective-permute-start.1 = (bf16[80,1024]{1,0:T(8,128)(2,1)S(1)}, bf16[80,1024]{1,0:T(8,128)(2,1)S(1)}, u32[]{:S(2)}, u32[]{:S(2)}) collective-permute-start(bf16[80,1024]{1,0:T(8,128)(2,1)S(1)} %slice_bitcast_fusion.halo_ref), channel_id=1, source_target_pairs={{0,2},{2,0},{4,6},{6,4},{8,10},{10,8},{12,14},{14,12},{16,18},{18,... | collective-permute-start | bytes 491528 | tf_op jit(solution)/shard_map/ppermute | solution.py:387
  5.6 9.8 %collective-permute-start.3 = (bf16[64,1152]{1,0:T(8,128)(2,1)S(1)}, bf16[64,1152]{1,0:T(8,128)(2,1)S(1)}, u32[]{:S(2)}, u32[]{:S(2)}) collective-permute-start(bf16[64,1152]{1,0:T(8,128)(2,1)S(1)} %get-tuple-element.37), channel_id=1, source_target_pairs={{0,8},{2,14},{4,12},{6,10},{8,16},{10,22},{12,20},{14,18},{16,24},... | collective-permute-start | bytes 442376 | tf_op jit(solution)/shard_map/ppermute | solution.py:387
  7.2 4.7 %collective-permute-start.4 = (bf16[64,512]{1,0:T(8,128)(2,1)S(1)}, bf16[64,512]{1,0:T(8,128)(2,1)S(1)}, u32[]{:S(2)}, u32[]{:S(2)}) collective-permute-start(bf16[64,512]{1,0:T(8,128)(2,1)S(1)} %get-tuple-element.38), channel_id=1, source_target_pairs={{0,4},{2,6},{4,0},{6,2},{8,12},{10,14},{12,8},{14,10},{16,20},{18,... | collective-permute-start | bytes 196616 | tf_op jit(solution)/shard_map/ppermute | solution.py:387
  8.8 0.7 %copy-start.4 = (s32[1,128]{1,0:T(1,128)S(1)}, s32[1,128]{1,0:T(1,128)}, u32[]{:S(2)}) copy-start(s32[1,128]{1,0:T(1,128)} %segment_ref.3) | copy-start | bytes 1540
  9.4 1.2 %copy-start = (bf16[1,128,4096]{2,1,0:T(8,128)(2,1)S(1)}, bf16[1,128,4096]{2,1,0:T(8,128)(2,1)}, u32[]{:S(2)}) copy-start(bf16[1,128,4096]{2,1,0:T(8,128)(2,1)} %param.7) | copy-start | bytes 3145732
  11.4 4.1 %copy-start.1 = (bf16[1,128,4096]{2,1,0:T(8,128)(2,1)S(1)}, bf16[1,128,4096]{2,1,0:T(8,128)(2,1)}, u32[]{:S(2)}) copy-start(bf16[1,128,4096]{2,1,0:T(8,128)(2,1)} %param.7) | copy-start | bytes 3145732
  11.5 4.0 %copy-start.5 = (f32[32]{0:T(128)S(1)}, f32[32]{0:T(128)}, u32[]{:S(2)}) copy-start(f32[32]{0:T(128)} %param.12) | copy-start | bytes 388
  15.4 1.6 %copy-start.3 = (bf16[1,128,4096]{2,1,0:T(8,128)(2,1)S(1)}, bf16[1,128,4096]{2,1,0:T(8,128)(2,1)}, u32[]{:S(2)}) copy-start(bf16[1,128,4096]{2,1,0:T(8,128)(2,1)} %param.13) | copy-start | bytes 3145732
  15.4 1.5 %collective-permute-start.5 = (bf16[64,1664]{1,0:T(8,128)(2,1)S(1)}, bf16[64,1664]{1,0:T(8,128)(2,1)S(1)}, u32[]{:S(2)}, u32[]{:S(2)}) collective-permute-start(bf16[64,1664]{1,0:T(8,128)(2,1)S(1)} %arrived.1._.mine_ref), channel_id=1, source_target_pairs={{0,2},{2,0},{4,6},{6,4},{8,10},{10,8},{12,14},{14,12},{16,18},{18,... | collective-permute-start | bytes 638984 | tf_op jit(solution)/shard_map/ppermute | solution.py:387
  19.2 1.6 %collective-permute-start.6 = (f32[64,1152]{1,0:T(8,128)S(1)}, f32[64,1152]{1,0:T(8,128)S(1)}, u32[]{:S(2)}, u32[]{:S(2)}) collective-permute-start(f32[64,1152]{1,0:T(8,128)S(1)} %get-tuple-element.42._.mine_ref), channel_id=1, source_target_pairs={{0,2},{2,0},{4,6},{6,4},{8,10},{10,8},{12,14},{14,12},{16,18},{18,... | collective-permute-start | bytes 884744 | tf_op jit(solution)/shard_map/ppermute | solution.py:387
  21.0 8.0 %collective-permute-start.8 = (bf16[64,1152]{1,0:T(8,128)(2,1)S(1)}, bf16[64,1152]{1,0:T(8,128)(2,1)S(1)}, u32[]{:S(2)}, u32[]{:S(2)}) collective-permute-start(bf16[64,1152]{1,0:T(8,128)(2,1)S(1)} %get-tuple-element.45.refs_0_), channel_id=1, source_target_pairs={{0,24},{2,30},{4,28},{6,26},{8,0},{10,6},{12,4},{14,2},{16,8},{18,... | collective-permute-start | bytes 442376 | tf_op jit(solution)/shard_map/ppermute | solution.py:387
  23.3 5.7 %collective-permute-start.7 = (bf16[64,640]{1,0:T(8,128)(2,1)S(1)}, bf16[64,640]{1,0:T(8,128)(2,1)S(1)}, u32[]{:S(2)}, u32[]{:S(2)}) collective-permute-start(bf16[64,640]{1,0:T(8,128)(2,1)S(1)} %get-tuple-element.48), channel_id=1, source_target_pairs={{0,4},{2,6},{4,0},{6,2},{8,12},{10,14},{12,8},{14,10},{16,20},{18,... | collective-permute-start | bytes 245768 | tf_op jit(solution)/shard_map/ppermute | solution.py:387
  23.3 5.1 %collective-permute-start.10 = (f32[16,128]{1,0:T(8,128)S(1)}, f32[16,128]{1,0:T(8,128)S(1)}, u32[]{:S(2)}, u32[]{:S(2)}) collective-permute-start(f32[16,128]{1,0:T(8,128)S(1)} %get-tuple-element.49.gate_ref), channel_id=1, source_target_pairs={{0,16},{2,22},{4,20},{6,18},{8,24},{10,30},{12,28},{14,26},{16,0},... | collective-permute-start | bytes 24584 | tf_op jit(solution)/shard_map/ppermute | solution.py:387
  23.5 5.4 %collective-permute-start.9 = (f32[16,128]{1,0:T(8,128)S(1)}, f32[16,128]{1,0:T(8,128)S(1)}, u32[]{:S(2)}, u32[]{:S(2)}) collective-permute-start(f32[16,128]{1,0:T(8,128)S(1)} %get-tuple-element.49.gate_ref), channel_id=1, source_target_pairs={{0,8},{2,14},{4,12},{6,10},{8,16},{10,22},{12,20},{14,18},{16,24},... | collective-permute-start | bytes 24584 | tf_op jit(solution)/shard_map/ppermute | solution.py:387
  26.8 6.9 %collective-permute-start.13 = (bf16[80,1024]{1,0:T(8,128)(2,1)S(1)}, bf16[80,1024]{1,0:T(8,128)(2,1)S(1)}, u32[]{:S(2)}, u32[]{:S(2)}) collective-permute-start(bf16[80,1024]{1,0:T(8,128)(2,1)S(1)} %get-tuple-element.57), channel_id=1, source_target_pairs={{0,1},{1,0},{2,4},{3,5},{4,2},{5,3},{6,8},{7,9},{8,6},{9,7},{10,12... | collective-permute-start | bytes 491528 | tf_op jit(solution)/shard_map/ppermute | solution.py:391
  28.3 5.3 %collective-permute-start.12 = (bf16[80,1024]{1,0:T(8,128)(2,1)S(1)}, bf16[80,1024]{1,0:T(8,128)(2,1)S(1)}, u32[]{:S(2)}, u32[]{:S(2)}) collective-permute-start(bf16[80,1024]{1,0:T(8,128)(2,1)S(1)} %get-tuple-element.57), channel_id=1, source_target_pairs={{0,2},{2,0},{4,6},{6,4},{8,10},{10,8},{12,14},{14,12},{16,18},{18,... | collective-permute-start | bytes 491528 | tf_op jit(solution)/shard_map/ppermute | solution.py:387
  29.0 1.6 %collective-permute-start.11 = (bf16[64,1152]{1,0:T(8,128)(2,1)S(1)}, bf16[64,1152]{1,0:T(8,128)(2,1)S(1)}, u32[]{:S(2)}, u32[]{:S(2)}) collective-permute-start(bf16[64,1152]{1,0:T(8,128)(2,1)S(1)} %get-tuple-element.54), channel_id=1, source_target_pairs={{0,2},{2,0},{4,6},{6,4},{8,10},{10,8},{12,14},{14,12},{16,18},{18,... | collective-permute-start | bytes 442376 | tf_op jit(solution)/shard_map/ppermute | solution.py:387
  30.7 3.7 %collective-permute-start.14 = (f32[16,128]{1,0:T(8,128)S(1)}, f32[16,128]{1,0:T(8,128)S(1)}, u32[]{:S(2)}, u32[]{:S(2)}) collective-permute-start(f32[16,128]{1,0:T(8,128)S(1)} %gate_sum.1.gate_ref), channel_id=1, source_target_pairs={{0,1},{1,0},{2,3},{3,2},{4,5},{5,4},{6,7},{7,6},{8,9},{9,8},{10,11... | collective-permute-start | bytes 24584 | tf_op jit(solution)/shard_map/ppermute | solution.py:391

commit v6 on v5

--- a/solution.py
+++ b/solution.py
@@ -12,6 +12,7 @@
 WINDOW = 64
 GAP = 4
 LANES = 128
+WIDE = 2
 MORE = 16
 MARKS = 384
 SCALE = 1.0 / math.sqrt(HEAD_DIM)
@@ -144,7 +145,7 @@
 
 def cross_kernel(
     off_ref, owner_ref, gate_ref, self_0_ref, self_1_ref, grad_ref, own_ref, chip_ref, mine_ref, pair_ref,
-    scores_ref, to_pair_ref, in_chip_ref, own_terms_ref, mask_ref, prev, *, groups, repeat, step=2
+    scores_ref, to_pair_ref, to_x_ref, in_chip_ref, own_terms_ref, mask_ref, prev, *, groups, repeat, step=2
 ):
     tok_rows, width = grad_ref.shape[0], chip_ref.shape[1]
     img = own_ref.shape[0]
@@ -225,10 +226,12 @@
             for index, terms in ((g, grad_key), (groups + g, grad_value)):
                 cols = slice(index * HEAD_DIM, (index + 1) * HEAD_DIM)
                 own_terms_ref[:, cols] = terms[img:]
-                to_pair_ref[:, cols] = terms[:img] * (from_x + from_z)
+                to_pair_ref[:, cols] = terms[:img] * from_z
+                to_x_ref[:, cols] = (terms[:img] * from_x).astype(to_x_ref.dtype)
                 in_chip_ref[:, cols] = terms[:img] * from_chip
     gate = jnp.concatenate(gate_rows, axis=0)
     to_pair_ref[:, width:] = jnp.concatenate([gate] * (img // gate.shape[0]), axis=0)
+    to_x_ref[:, width:] = jnp.concatenate([split(gate)] * (to_x_ref.shape[1] // LANES - width // LANES), axis=1)
     row = lax.broadcasted_iota(jnp.int32, mask_ref.shape, 0)
     mask_ref[...] = jnp.where(row == 0, by_mine.astype(jnp.float32) * (1.0 - from_x), from_x)
 
@@ -243,35 +246,25 @@
             grad_self_ref[g, rows, :] = (grad_rows + grad_query[rows]).astype(jnp.bfloat16)
 
 
-def outside_kernel(mine_ref, pair_ref, mask_ref, _, to_z_ref, to_x_ref, gate_ref):
+def outside_kernel(mine_ref, pair_ref, mask_ref, _, to_z_ref, gate_ref):
     width = mine_ref.shape[1] - LANES
     total = mine_ref[...] + pair_ref[...]
     gate = total[: gate_ref.shape[0], width:]
-    terms = total[:, :width]
-    to_z_ref[:, :width] = (terms * mask_ref[0:1, 0:1]).astype(to_z_ref.dtype)
+    to_z_ref[:, :width] = (total[:, :width] * mask_ref[0:1, 0:1]).astype(to_z_ref.dtype)
     to_z_ref[:, width:] = split(gate)
-    odd = jnp.broadcast_to(odd_core(), (terms.shape[0], width // 2)) > 0
-    half = jnp.where(odd, terms[:, width // 2 :], terms[:, : width // 2])
-    to_x_ref[:, : width // 2] = (half * mask_ref[1:2, 0:1]).astype(to_x_ref.dtype)
-    to_x_ref[:, width // 2 :] = split(gate)
     gate_ref[...] = gate
 
 
 def chip_sum_kernel(mine_ref, x_ref, z_ref, gate_ref, *refs):
     *gates, _, out_ref, gate_out, to_pair_ref = refs
     width = mine_ref.shape[1]
-    odd = odd_core().astype(jnp.float32)
-    half = width // 2
-    from_x = x_ref[:, :half].astype(jnp.float32)
-    first = mine_ref[:, :half] + (from_x * (1.0 - odd) + z_ref[:, :half].astype(jnp.float32))
-    second = mine_ref[:, half:] + (from_x * odd + z_ref[:, half:width].astype(jnp.float32))
-    for cols, terms in ((slice(0, half), first), (slice(half, width), second)):
-        out_ref[:, cols] = terms
-        to_pair_ref[:, cols] = terms.astype(to_pair_ref.dtype)
-    gate = unsplit(z_ref[:, width:])
+    terms = mine_ref[...] + (x_ref[:, :width].astype(jnp.float32) + z_ref[:, :width].astype(jnp.float32))
+    out_ref[...] = terms
+    to_pair_ref[:, :width] = terms.astype(to_pair_ref.dtype)
+    gate = unsplit(z_ref[:, width:]) + unsplit(x_ref[:, width : width + LANES])
     for ref in gates:
         gate = gate + ref[...]
-    gate_out[...] = gate_ref[...] + unsplit(x_ref[:, half:]) + gate
+    gate_out[...] = gate_ref[...] + gate
     to_pair_ref[:, width:] = split(gate)
 
 
@@ -450,12 +443,13 @@
     self_forward(0, arrived)
 
     gate_shape = struct((heads * WINDOW // LANES, LANES), f32)
-    scores, to_pair, in_chip, own_terms, masks, prev = call(
+    scores, to_pair, to_x, in_chip, own_terms, masks, prev = call(
         "cross",
         functools.partial(cross_kernel, groups=groups, repeat=repeat),
         [
             struct((groups, 2 * img, repeat * tok_rows), bf16),
             struct((img, width + LANES), f32),
+            struct((img, width + WIDE * LANES), bf16),
             struct((img, width), f32),
             struct((img, width), f32),
             struct((8, LANES), f32),
@@ -464,6 +458,7 @@
         [VMEM] * 10,
     )(off, owners, gate_rows, *self_out, grad, own, chip, arrived, by_pair)
     from_pair = send(to_pair, lambda i: i ^ 1)
+    from_x = send(to_x, lambda i: i ^ 2)
     grad_self = call(
         "cross_query",
         functools.partial(cross_query_kernel, groups=groups, repeat=repeat),
@@ -488,14 +483,13 @@
             moved=10**5,
         )(q, ctx, tail if block else halo, kept[block], grad_self, after, *([] if late is None else [late]))
 
-    to_z, to_x, gate = call(
+    to_z, gate = call(
         "outside",
         outside_kernel,
-        [struct((img, width + LANES), bf16), struct((img, width // 2 + LANES), bf16), gate_shape],
+        [struct((img, width + LANES), bf16), gate_shape],
         [VMEM] * 3 + [ANY],
     )(to_pair, from_pair, masks, grad_self)
     from_z = send_z(to_z, -1)
-    from_x = send(to_x, lambda i: i ^ 2)
     gates = []
     if swaps:
         gates = [send_z(gate, 1), send_z(gate, 2)]

time: 35.4 us -> 34.9 us (0.986)
  starting transfers between devices: 15 us -> 13.4 us
  waiting for transfers between devices: 7.38 us -> 8.55 us
    ppermute x12, starting transfers between devices: 9.29 us -> 7.68 us  [send(): return lax.ppermute(value, 'seq', [(i, where(i)) for i in range(seq)])]
    ppermute x12, waiting for transfers between devices: 6.77 us -> 7.95 us  [send(): return lax.ppermute(value, 'seq', [(i, where(i)) for i in range(seq)])]
  transfers between devices with their start and end apart: 15 -> 15, of which waited for: 7 -> 8; matrix products, arithmetic and copies ran while one was open for 0% -> 0% of each run, Pallas kernels for 15% -> 15%
where the time goes in v6:
time: 34.9 us; the launch traced here: 34.7 us
  starting transfers between devices  13.4 us (38%)
  waiting for transfers between devices  8.55 us (24%)
  Pallas kernels  8.35 us (24%)
  local copies, waits for them, and re-layouts  2.91 us (8%)
  between operations  1.52 us (4%)
    ppermute x12, waiting for transfers between devices, send(): return lax.ppermute(value, 'seq', [(i, where(i)) for i in range(seq)])  7.95 us
    ppermute x12, starting transfers between devices, send(): return lax.ppermute(value, 'seq', [(i, where(i)) for i in range(seq)])  7.68 us
    ppermute x3, starting transfers between devices, send_all(): lax.ppermute(value, ('seq', 'dp'), [(s * dp + d, t * dp + e) for s, d, t,...  5.71 us
    pallas_call x2, Pallas kernels, self_backward(): call(f'self_backward_{block}', functools.partial(self_back_kernel, block=...  2.91 us
    pallas_call x1, Pallas kernels, on_device(): call('cross', functools.partial(cross_kernel, groups=groups, repeat=repea...  2.14 us
    unnamed x12, local copies, waits for them, and re-layouts  1.9 us
    pallas_call x2, Pallas kernels, self_forward(): call(f'self_forward_{block}', functools.partial(self_kernel, block=block,...  1.54 us
    concatenate x1, local copies, waits for them, and re-layouts, on_device(): jnp.concatenate([own, jnp.broadcast_to(is_owner, (img, MARKS))], axis=1)  0.92 us
  transfers between devices with their start and end apart: 15, of which 8 were waited for; matrix products, arithmetic and copies ran while one was open for 0% of the time, Pallas kernels for 15%

profile of v6, /device:TPU:0, one launch (start us, length us, event | category | flops | bytes accessed | tf_op | source)
XLA Modules:
  0.0 34.7 jit_solution(11016099246470407410)
XLA Ops:
  0.6 0.0 copy-start.2
  1.3 0.9 %concatenate.3.mine_ref.own_ref = bf16[64,1408]{1,0:T(8,128)(2,1)S(1)} pad(bf16[64,1024]{1,0:T(8,128)(2,1)} %bitcast.24, bf16[]{:T(256)} %bitcast.4), padding=0_0x0_384 | pad | bytes 311298 | tf_op jit(solution)/shard_map/concatenate | solution.py:411
  2.3 0.5 %collective-permute-start = (bf16[64,1408]{1,0:T(8,128)(2,1)S(1)}, bf16[64,1408]{1,0:T(8,128)(2,1)S(1)}, u32[]{:S(2)}, u32[]{:S(2)}) collective-permute-start(bf16[64,1408]{1,0:T(8,128)(2,1)S(1)} %concatenate.3.mine_ref.own_ref), channel_id=1, source_target_pairs={{0,2},{2,0},{4,6},{6,4},{8,10},{10,8},{12,14},{14,12},{16,18},{18,... | collective-permute-start | bytes 540680 | tf_op jit(solution)/shard_map/ppermute | solution.py:380
  2.8 2.6 %collective-permute-start.2 = (bf16[80,1024]{1,0:T(8,128)(2,1)S(1)}, bf16[80,1024]{1,0:T(8,128)(2,1)S(1)}, u32[]{:S(2)}, u32[]{:S(2)}) collective-permute-start(bf16[80,1024]{1,0:T(8,128)(2,1)S(1)} %slice_bitcast_fusion.halo_ref), channel_id=1, source_target_pairs={{0,1},{1,0},{2,4},{3,5},{4,2},{5,3},{6,8},{7,9},{8,6},{9,7},{10,12... | collective-permute-start | bytes 491528 | tf_op jit(solution)/shard_map/ppermute | solution.py:384
  5.4 0.1 collective-permute-start.1
  5.5 0.0 collective-permute-done.other_ref
  5.5 0.1 chip_image.1
  5.6 1.6 %collective-permute-start.3 = (bf16[64,1152]{1,0:T(8,128)(2,1)S(1)}, bf16[64,1152]{1,0:T(8,128)(2,1)S(1)}, u32[]{:S(2)}, u32[]{:S(2)}) collective-permute-start(bf16[64,1152]{1,0:T(8,128)(2,1)S(1)} %get-tuple-element.37), channel_id=1, source_target_pairs={{0,8},{2,14},{4,12},{6,10},{8,16},{10,22},{12,20},{14,18},{16,24},... | collective-permute-start | bytes 442376 | tf_op jit(solution)/shard_map/ppermute | solution.py:380
  7.2 1.5 %collective-permute-start.4 = (bf16[64,512]{1,0:T(8,128)(2,1)S(1)}, bf16[64,512]{1,0:T(8,128)(2,1)S(1)}, u32[]{:S(2)}, u32[]{:S(2)}) collective-permute-start(bf16[64,512]{1,0:T(8,128)(2,1)S(1)} %get-tuple-element.38), channel_id=1, source_target_pairs={{0,4},{2,6},{4,0},{6,2},{8,12},{10,14},{12,8},{14,10},{16,20},{18,... | collective-permute-start | bytes 196616 | tf_op jit(solution)/shard_map/ppermute | solution.py:380
  8.8 0.7 %copy-done.4 = s32[1,128]{1,0:T(1,128)S(1)} copy-done((s32[1,128]{1,0:T(1,128)S(1)}, s32[1,128]{1,0:T(1,128)}, u32[]{:S(2)}) %copy-start.4) | copy-done | bytes 536
  9.4 1.2 %copy-done = bf16[1,128,4096]{2,1,0:T(8,128)(2,1)S(1)} copy-done((bf16[1,128,4096]{2,1,0:T(8,128)(2,1)S(1)}, bf16[1,128,4096]{2,1,0:T(8,128)(2,1)}, u32[]{:S(2)}) %copy-start) | copy-done | bytes 1048600
  10.6 0.8 %self_forward_1.1 = (bf16[4,128,512]{2,1,0:T(8,128)(2,1)S(1)}, f32[4,128,512]{2,1,0:T(8,128)S(1)}) custom-call(bf16[128,4096]{1,0:T(8,128)(2,1)S(1)} %bitcast.13, bf16[128,1024]{1,0:T(8,128)(2,1)S(1)} %bitcast.17, bf16[80,1024]{1,0:T(8,128)(2,1)S(1)} %slice_bitcast_fusion.halo_ref, s32[1,128]{1,0:T(1,128)S(1)} %copy-done.4, ...), custom_call_target="tpu_custom_call" | custom-call | flops 1000000 | bytes 100000 | tf_op jit(solution)/shard_map/self_forward_1/pallas_call | solution.py:427
  11.4 0.0 copy-start.1
  11.4 0.0 collective-permute-done.2.other_ref
  11.4 0.0 collective-permute-done.1.chip_ref
  11.5 0.0 copy-start.5
  11.5 0.4 %collective-permute-done.4.x_ref = bf16[64,512]{1,0:T(8,128)(2,1)S(1)} collective-permute-done((bf16[64,512]{1,0:T(8,128)(2,1)S(1)}, bf16[64,512]{1,0:T(8,128)(2,1)S(1)}, u32[]{:S(2)}, u32[]{:S(2)}) %collective-permute-start.4) | collective-permute-done | bytes 65568 | tf_op jit(solution)/shard_map/ppermute | solution.py:380
  11.9 3.5 %collective-permute-done.3.z_ref = bf16[64,1152]{1,0:T(8,128)(2,1)S(1)} collective-permute-done((bf16[64,1152]{1,0:T(8,128)(2,1)S(1)}, bf16[64,1152]{1,0:T(8,128)(2,1)S(1)}, u32[]{:S(2)}, u32[]{:S(2)}) %collective-permute-start.3) | collective-permute-done | bytes 147488 | tf_op jit(solution)/shard_map/ppermute | solution.py:380
  15.4 0.0 copy-start.3
  15.4 0.1 collective-permute-start.5
  15.5 0.8 %self_forward_0.1 = (bf16[4,128,512]{2,1,0:T(8,128)(2,1)S(1)}, f32[4,128,512]{2,1,0:T(8,128)S(1)}) custom-call(bf16[128,4096]{1,0:T(8,128)(2,1)S(1)} %bitcast.14, bf16[128,1024]{1,0:T(8,128)(2,1)S(1)} %bitcast.18, bf16[64,1024]{1,0:T(8,128)(2,1)S(1)} %halo.1.__.halo_ref, s32[1,128]{1,0:T(1,128)S(1)} %copy-done.4, bf16[64,1664]{1,0:T(8,128)(2,1)S(1)} %arrived.1._.mine_ref), custom_call_target="tpu_custom_call" | custom-call | flops 1000000 | bytes 100000 | tf_op jit(solution)/shard_map/self_forward_0/pallas_call | solution.py:427
  16.3 0.6 %collective-permute-done.5.pair_ref = bf16[64,1664]{1,0:T(8,128)(2,1)S(1)} collective-permute-done((bf16[64,1664]{1,0:T(8,128)(2,1)S(1)}, bf16[64,1664]{1,0:T(8,128)(2,1)S(1)}, u32[]{:S(2)}, u32[]{:S(2)}) %collective-permute-start.5) | collective-permute-done | bytes 213024 | tf_op jit(solution)/shard_map/ppermute | solution.py:380
  17.0 0.1 broadcast_in_dim.34.gate_ref.refs_1_
  17.0 2.1 %cross.1 = (bf16[4,128,1024]{2,1,0:T(8,128)(2,1)S(1)}, f32[64,1152]{1,0:T(8,128)S(1)}, bf16[64,1280]{1,0:T(8,128)(2,1)S(1)}, f32[64,1024]{1,0:T(8,128)S(1)}, f32...) custom-call(s32[8,128]{1,0:T(8,128)S(1)} %broadcast_in_dim.33.off_ref, ...), custom_call_target="tpu_custom_call" | custom-call | flops 1000 | bytes 1000 | tf_op jit(solution)/shard_map/cross/pallas_call | solution.py:446
  19.2 0.2 collective-permute-start.6
  19.4 0.0 collective-permute-start.7
  19.4 0.5 %cross_query.1._.grad_ref = bf16[4,1024,128]{2,1,0:T(8,128)(2,1)S(1)} custom-call(bf16[4,128,1024]{2,1,0:T(8,128)(2,1)S(1)} %get-tuple-element.40.scores_ref, bf16[128,4096]{1,0:T(8,128)(2,1)S(1)} %bitcast.22, bf16[64,1408]{1,0:T(8,128)(2,1)S(1)} %concatenate.3.mine_ref.own_ref, bf16[64,1024]{1,0:T(8,128)(2,1)S(1)} %get-tuple-element.41.prev, ...), custom_call_target="tpu_custom_call" | custom-call | flops 1000 | bytes 1000 | tf_op jit(solution)/shard_map/cross_query/pallas_call | solution.py:462
  19.9 0.9 %collective-permute-done.6.pair_ref = f32[64,1152]{1,0:T(8,128)S(1)} collective-permute-done((f32[64,1152]{1,0:T(8,128)S(1)}, f32[64,1152]{1,0:T(8,128)S(1)}, u32[]{:S(2)}, u32[]{:S(2)}) %collective-permute-start.6) | collective-permute-done | bytes 294944 | tf_op jit(solution)/shard_map/ppermute | solution.py:380
  20.8 0.1 outside.1
  20.9 2.3 %collective-permute-start.8 = (bf16[64,1152]{1,0:T(8,128)(2,1)S(1)}, bf16[64,1152]{1,0:T(8,128)(2,1)S(1)}, u32[]{:S(2)}, u32[]{:S(2)}) collective-permute-start(bf16[64,1152]{1,0:T(8,128)(2,1)S(1)} %get-tuple-element.45.refs_0_), channel_id=1, source_target_pairs={{0,24},{2,30},{4,28},{6,26},{8,0},{10,6},{12,4},{14,2},{16,8},{18,... | collective-permute-start | bytes 442376 | tf_op jit(solution)/shard_map/ppermute | solution.py:380
  23.2 0.0 collective-permute-start.10
  23.2 1.1 %collective-permute-start.9 = (f32[16,128]{1,0:T(8,128)S(1)}, f32[16,128]{1,0:T(8,128)S(1)}, u32[]{:S(2)}, u32[]{:S(2)}) collective-permute-start(f32[16,128]{1,0:T(8,128)S(1)} %get-tuple-element.49.gate_ref), channel_id=1, source_target_pairs={{0,8},{2,14},{4,12},{6,10},{8,16},{10,22},{12,20},{14,18},{16,24},... | collective-permute-start | bytes 24584 | tf_op jit(solution)/shard_map/ppermute | solution.py:380
  24.4 1.5 %self_backward_0.1 = (bf16[128,4096]{1,0:T(8,128)(2,1)}, bf16[80,1024]{1,0:T(8,128)(2,1)S(1)}, f32[64,1024]{1,0:T(8,128)S(1)}) custom-call(bf16[128,4096]{1,0:T(8,128)(2,1)S(1)} %bitcast.15, bf16[128,1024]{1,0:T(8,128)(2,1)S(1)} %bitcast.19, bf16[64,1024]{1,0:T(8,128)(2,1)S(1)} %halo.1.__.halo_ref, f32[4,128,512]{2,1,0:T(8,128)S(1)} %get-tuple-element.43.weights_ref, ...), custom_call_target="tpu_custom_call" | custom-call | flops 1000000 | bytes 100000 | tf_op jit(solution)/shard_map/self_backward_0/pallas_call | solution.py:470
  25.8 1.6 %collective-permute-start.13 = (bf16[80,1024]{1,0:T(8,128)(2,1)S(1)}, bf16[80,1024]{1,0:T(8,128)(2,1)S(1)}, u32[]{:S(2)}, u32[]{:S(2)}) collective-permute-start(bf16[80,1024]{1,0:T(8,128)(2,1)S(1)} %get-tuple-element.57), channel_id=1, source_target_pairs={{0,1},{1,0},{2,4},{3,5},{4,2},{5,3},{6,8},{7,9},{8,6},{9,7},{10,12... | collective-permute-start | bytes 491528 | tf_op jit(solution)/shard_map/ppermute | solution.py:384
  27.4 0.0 collective-permute-done.7.x_ref
  27.4 0.0 collective-permute-start.12
  27.4 0.4 %collective-permute-done.10.refs_1_ = f32[16,128]{1,0:T(8,128)S(1)} collective-permute-done((f32[16,128]{1,0:T(8,128)S(1)}, f32[16,128]{1,0:T(8,128)S(1)}, u32[]{:S(2)}, u32[]{:S(2)}) %collective-permute-start.10) | collective-permute-done | bytes 8224 | tf_op jit(solution)/shard_map/ppermute | solution.py:380
  27.9 0.8 %collective-permute-done.9.refs_0_ = f32[16,128]{1,0:T(8,128)S(1)} collective-permute-done((f32[16,128]{1,0:T(8,128)S(1)}, f32[16,128]{1,0:T(8,128)S(1)}, u32[]{:S(2)}, u32[]{:S(2)}) %collective-permute-start.9) | collective-permute-done | bytes 8224 | tf_op jit(solution)/shard_map/ppermute | solution.py:380
  28.7 0.0 collective-permute-done.8.z_ref
  28.7 0.1 chip_sum.1
  28.7 0.2 collective-permute-start.11
  28.9 1.3 %collective-permute-done.11.pair_ref = bf16[64,1152]{1,0:T(8,128)(2,1)S(1)} collective-permute-done((bf16[64,1152]{1,0:T(8,128)(2,1)S(1)}, bf16[64,1152]{1,0:T(8,128)(2,1)S(1)}, u32[]{:S(2)}, u32[]{:S(2)}) %collective-permute-start.11) | collective-permute-done | bytes 147488 | tf_op jit(solution)/shard_map/ppermute | solution.py:380
  30.2 1.5 %collective-permute-start.14 = (f32[16,128]{1,0:T(8,128)S(1)}, f32[16,128]{1,0:T(8,128)S(1)}, u32[]{:S(2)}, u32[]{:S(2)}) collective-permute-start(f32[16,128]{1,0:T(8,128)S(1)} %gate_sum.1.gate_ref), channel_id=1, source_target_pairs={{0,1},{1,0},{2,3},{3,2},{4,5},{5,4},{6,7},{7,6},{8,9},{9,8},{10,11... | collective-permute-start | bytes 24584 | tf_op jit(solution)/shard_map/ppermute | solution.py:384
  31.7 1.5 %self_backward_1.1 = (bf16[128,4096]{1,0:T(8,128)(2,1)}, f32[64,1024]{1,0:T(8,128)S(1)}, f32[64,1024]{1,0:T(8,128)S(1)}) custom-call(bf16[128,4096]{1,0:T(8,128)(2,1)S(1)} %bitcast.16, bf16[128,1024]{1,0:T(8,128)(2,1)S(1)} %bitcast.20, bf16[80,1024]{1,0:T(8,128)(2,1)S(1)} %slice_bitcast_fusion.halo_ref, ...), custom_call_target="tpu_custom_call", output_to_operand_aliasing={{0}: (5, {})} | custom-call | flops 1000000 | bytes 100000 | tf_op jit(solution)/shard_map/self_backward_1/pallas_call | solution.py:470
  33.2 0.0 collective-permute-done.13.other_ref
  33.2 0.0 collective-permute-done.12.chip_ref
  33.2 0.6 %collective-permute-done.14.refs_0_ = f32[16,128]{1,0:T(8,128)S(1)} collective-permute-done((f32[16,128]{1,0:T(8,128)S(1)}, f32[16,128]{1,0:T(8,128)S(1)}, u32[]{:S(2)}, u32[]{:S(2)}) %collective-permute-start.14) | collective-permute-done | bytes 8224 | tf_op jit(solution)/shard_map/ppermute | solution.py:384
  33.8 0.9 %finish.1 = (bf16[64,1024]{1,0:T(8,128)(2,1)}, bf16[128,1024]{1,0:T(8,128)(2,1)}, f32[1,32]{1,0:T(1,128)}) custom-call(f32[8,128]{1,0:T(8,128)S(1)} %get-tuple-element.35.owner_ref, f32[64,1024]{1,0:T(8,128)S(1)} %get-tuple-element.53.own_ref, f32[64,1024]{1,0:T(8,128)S(1)} %get-tuple-element.51.refs_1_.mine_ref, ...), custom_call_target="tpu_custom_call" | custom-call | flops 1000 | bytes 1000 | tf_op jit(solution)/shard_map/finish/pallas_call | solution.py:513
  (13 shorter events, 0.1 us)
Async XLA Ops:
  0.6 2.2 %copy-start.2 = (bf16[1,128,1024]{2,1,0:T(8,128)(2,1)S(1)}, bf16[1,128,1024]{2,1,0:T(8,128)(2,1)}, u32[]{:S(2)}) copy-start(bf16[1,128,1024]{2,1,0:T(8,128)(2,1)} %param.8) | copy-start | bytes 786436
  2.3 3.2 %collective-permute-start = (bf16[64,1408]{1,0:T(8,128)(2,1)S(1)}, bf16[64,1408]{1,0:T(8,128)(2,1)S(1)}, u32[]{:S(2)}, u32[]{:S(2)}) collective-permute-start(bf16[64,1408]{1,0:T(8,128)(2,1)S(1)} %concatenate.3.mine_ref.own_ref), channel_id=1, source_target_pairs={{0,2},{2,0},{4,6},{6,4},{8,10},{10,8},{12,14},{14,12},{16,18},{18,... | collective-permute-start | bytes 540680 | tf_op jit(solution)/shard_map/ppermute | solution.py:380
  2.8 8.6 %collective-permute-start.2 = (bf16[80,1024]{1,0:T(8,128)(2,1)S(1)}, bf16[80,1024]{1,0:T(8,128)(2,1)S(1)}, u32[]{:S(2)}, u32[]{:S(2)}) collective-permute-start(bf16[80,1024]{1,0:T(8,128)(2,1)S(1)} %slice_bitcast_fusion.halo_ref), channel_id=1, source_target_pairs={{0,1},{1,0},{2,4},{3,5},{4,2},{5,3},{6,8},{7,9},{8,6},{9,7},{10,12... | collective-permute-start | bytes 491528 | tf_op jit(solution)/shard_map/ppermute | solution.py:384
  5.4 6.0 %collective-permute-start.1 = (bf16[80,1024]{1,0:T(8,128)(2,1)S(1)}, bf16[80,1024]{1,0:T(8,128)(2,1)S(1)}, u32[]{:S(2)}, u32[]{:S(2)}) collective-permute-start(bf16[80,1024]{1,0:T(8,128)(2,1)S(1)} %slice_bitcast_fusion.halo_ref), channel_id=1, source_target_pairs={{0,2},{2,0},{4,6},{6,4},{8,10},{10,8},{12,14},{14,12},{16,18},{18,... | collective-permute-start | bytes 491528 | tf_op jit(solution)/shard_map/ppermute | solution.py:380
  5.6 9.8 %collective-permute-start.3 = (bf16[64,1152]{1,0:T(8,128)(2,1)S(1)}, bf16[64,1152]{1,0:T(8,128)(2,1)S(1)}, u32[]{:S(2)}, u32[]{:S(2)}) collective-permute-start(bf16[64,1152]{1,0:T(8,128)(2,1)S(1)} %get-tuple-element.37), channel_id=1, source_target_pairs={{0,8},{2,14},{4,12},{6,10},{8,16},{10,22},{12,20},{14,18},{16,24},... | collective-permute-start | bytes 442376 | tf_op jit(solution)/shard_map/ppermute | solution.py:380
  7.2 4.7 %collective-permute-start.4 = (bf16[64,512]{1,0:T(8,128)(2,1)S(1)}, bf16[64,512]{1,0:T(8,128)(2,1)S(1)}, u32[]{:S(2)}, u32[]{:S(2)}) collective-permute-start(bf16[64,512]{1,0:T(8,128)(2,1)S(1)} %get-tuple-element.38), channel_id=1, source_target_pairs={{0,4},{2,6},{4,0},{6,2},{8,12},{10,14},{12,8},{14,10},{16,20},{18,... | collective-permute-start | bytes 196616 | tf_op jit(solution)/shard_map/ppermute | solution.py:380
  8.8 0.7 %copy-start.4 = (s32[1,128]{1,0:T(1,128)S(1)}, s32[1,128]{1,0:T(1,128)}, u32[]{:S(2)}) copy-start(s32[1,128]{1,0:T(1,128)} %segment_ref.3) | copy-start | bytes 1540
  9.4 1.2 %copy-start = (bf16[1,128,4096]{2,1,0:T(8,128)(2,1)S(1)}, bf16[1,128,4096]{2,1,0:T(8,128)(2,1)}, u32[]{:S(2)}) copy-start(bf16[1,128,4096]{2,1,0:T(8,128)(2,1)} %param.7) | copy-start | bytes 3145732
  11.4 4.1 %copy-start.1 = (bf16[1,128,4096]{2,1,0:T(8,128)(2,1)S(1)}, bf16[1,128,4096]{2,1,0:T(8,128)(2,1)}, u32[]{:S(2)}) copy-start(bf16[1,128,4096]{2,1,0:T(8,128)(2,1)} %param.7) | copy-start | bytes 3145732
  11.5 4.0 %copy-start.5 = (f32[32]{0:T(128)S(1)}, f32[32]{0:T(128)}, u32[]{:S(2)}) copy-start(f32[32]{0:T(128)} %param.12) | copy-start | bytes 388
  15.4 1.6 %copy-start.3 = (bf16[1,128,4096]{2,1,0:T(8,128)(2,1)S(1)}, bf16[1,128,4096]{2,1,0:T(8,128)(2,1)}, u32[]{:S(2)}) copy-start(bf16[1,128,4096]{2,1,0:T(8,128)(2,1)} %param.13) | copy-start | bytes 3145732
  15.4 1.5 %collective-permute-start.5 = (bf16[64,1664]{1,0:T(8,128)(2,1)S(1)}, bf16[64,1664]{1,0:T(8,128)(2,1)S(1)}, u32[]{:S(2)}, u32[]{:S(2)}) collective-permute-start(bf16[64,1664]{1,0:T(8,128)(2,1)S(1)} %arrived.1._.mine_ref), channel_id=1, source_target_pairs={{0,2},{2,0},{4,6},{6,4},{8,10},{10,8},{12,14},{14,12},{16,18},{18,... | collective-permute-start | bytes 638984 | tf_op jit(solution)/shard_map/ppermute | solution.py:380
  19.2 1.6 %collective-permute-start.6 = (f32[64,1152]{1,0:T(8,128)S(1)}, f32[64,1152]{1,0:T(8,128)S(1)}, u32[]{:S(2)}, u32[]{:S(2)}) collective-permute-start(f32[64,1152]{1,0:T(8,128)S(1)} %get-tuple-element.42._.mine_ref), channel_id=1, source_target_pairs={{0,2},{2,0},{4,6},{6,4},{8,10},{10,8},{12,14},{14,12},{16,18},{18,... | collective-permute-start | bytes 884744 | tf_op jit(solution)/shard_map/ppermute | solution.py:380
  19.4 8.1 %collective-permute-start.7 = (bf16[64,1280]{1,0:T(8,128)(2,1)S(1)}, bf16[64,1280]{1,0:T(8,128)(2,1)S(1)}, u32[]{:S(2)}, u32[]{:S(2)}) collective-permute-start(bf16[64,1280]{1,0:T(8,128)(2,1)S(1)} %get-tuple-element.48), channel_id=1, source_target_pairs={{0,4},{2,6},{4,0},{6,2},{8,12},{10,14},{12,8},{14,10},{16,20},{18,... | collective-permute-start | bytes 491528 | tf_op jit(solution)/shard_map/ppermute | solution.py:380
  20.9 7.8 %collective-permute-start.8 = (bf16[64,1152]{1,0:T(8,128)(2,1)S(1)}, bf16[64,1152]{1,0:T(8,128)(2,1)S(1)}, u32[]{:S(2)}, u32[]{:S(2)}) collective-permute-start(bf16[64,1152]{1,0:T(8,128)(2,1)S(1)} %get-tuple-element.45.refs_0_), channel_id=1, source_target_pairs={{0,24},{2,30},{4,28},{6,26},{8,0},{10,6},{12,4},{14,2},{16,8},{18,... | collective-permute-start | bytes 442376 | tf_op jit(solution)/shard_map/ppermute | solution.py:380
  23.2 4.6 %collective-permute-start.10 = (f32[16,128]{1,0:T(8,128)S(1)}, f32[16,128]{1,0:T(8,128)S(1)}, u32[]{:S(2)}, u32[]{:S(2)}) collective-permute-start(f32[16,128]{1,0:T(8,128)S(1)} %get-tuple-element.49.gate_ref), channel_id=1, source_target_pairs={{0,16},{2,22},{4,20},{6,18},{8,24},{10,30},{12,28},{14,26},{16,0},... | collective-permute-start | bytes 24584 | tf_op jit(solution)/shard_map/ppermute | solution.py:380
  23.2 5.4 %collective-permute-start.9 = (f32[16,128]{1,0:T(8,128)S(1)}, f32[16,128]{1,0:T(8,128)S(1)}, u32[]{:S(2)}, u32[]{:S(2)}) collective-permute-start(f32[16,128]{1,0:T(8,128)S(1)} %get-tuple-element.49.gate_ref), channel_id=1, source_target_pairs={{0,8},{2,14},{4,12},{6,10},{8,16},{10,22},{12,20},{14,18},{16,24},... | collective-permute-start | bytes 24584 | tf_op jit(solution)/shard_map/ppermute | solution.py:380
  25.8 7.3 %collective-permute-start.13 = (bf16[80,1024]{1,0:T(8,128)(2,1)S(1)}, bf16[80,1024]{1,0:T(8,128)(2,1)S(1)}, u32[]{:S(2)}, u32[]{:S(2)}) collective-permute-start(bf16[80,1024]{1,0:T(8,128)(2,1)S(1)} %get-tuple-element.57), channel_id=1, source_target_pairs={{0,1},{1,0},{2,4},{3,5},{4,2},{5,3},{6,8},{7,9},{8,6},{9,7},{10,12... | collective-permute-start | bytes 491528 | tf_op jit(solution)/shard_map/ppermute | solution.py:384
  27.4 5.8 %collective-permute-start.12 = (bf16[80,1024]{1,0:T(8,128)(2,1)S(1)}, bf16[80,1024]{1,0:T(8,128)(2,1)S(1)}, u32[]{:S(2)}, u32[]{:S(2)}) collective-permute-start(bf16[80,1024]{1,0:T(8,128)(2,1)S(1)} %get-tuple-element.57), channel_id=1, source_target_pairs={{0,2},{2,0},{4,6},{6,4},{8,10},{10,8},{12,14},{14,12},{16,18},{18,... | collective-permute-start | bytes 491528 | tf_op jit(solution)/shard_map/ppermute | solution.py:380
  28.7 1.4 %collective-permute-start.11 = (bf16[64,1152]{1,0:T(8,128)(2,1)S(1)}, bf16[64,1152]{1,0:T(8,128)(2,1)S(1)}, u32[]{:S(2)}, u32[]{:S(2)}) collective-permute-start(bf16[64,1152]{1,0:T(8,128)(2,1)S(1)} %get-tuple-element.54), channel_id=1, source_target_pairs={{0,2},{2,0},{4,6},{6,4},{8,10},{10,8},{12,14},{14,12},{16,18},{18,... | collective-permute-start | bytes 442376 | tf_op jit(solution)/shard_map/ppermute | solution.py:380
  30.2 3.7 %collective-permute-start.14 = (f32[16,128]{1,0:T(8,128)S(1)}, f32[16,128]{1,0:T(8,128)S(1)}, u32[]{:S(2)}, u32[]{:S(2)}) collective-permute-start(f32[16,128]{1,0:T(8,128)S(1)} %gate_sum.1.gate_ref), channel_id=1, source_target_pairs={{0,1},{1,0},{2,3},{3,2},{4,5},{5,4},{6,7},{7,6},{8,9},{9,8},{10,11... | collective-permute-start | bytes 24584 | tf_op jit(solution)/shard_map/ppermute | solution.py:384

commit v7 on v6

--- a/solution.py
+++ b/solution.py
@@ -91,10 +91,13 @@
     return flag(owner_ref[row : row + 1, 0:1] > 0.5)
 
 
+def read_mark(ref, first):
+    return ref[0:16, first : first + LANES].astype(jnp.float32)[0:1, 0:1]
+
+
 def chip_kernel(mine_ref, other_ref, out_ref, marked_ref, half_ref, owner_ref):
     width = out_ref.shape[1]
-    mine, other = mine_ref[0:1, width : width + 1], other_ref[0:1, width : width + 1]
-    mine, other = mine.astype(jnp.float32), other.astype(jnp.float32)
+    mine, other = read_mark(mine_ref, width), read_mark(other_ref, width)
     choose(flag(mine > 0.5), mine_ref, other_ref, out_ref, width)
     marked_ref[:, :width] = out_ref[...]
     owns = jnp.maximum(mine, other)
@@ -158,7 +161,7 @@
     from_z = flag(shard >= GAP) * (1 - (from_chip | from_x))
     has_prev = from_chip | from_x | from_z
     marked = width + LANES
-    by_mine = flag(mine_ref[0:1, width : width + 1].astype(jnp.float32) > 0.5)
+    by_mine = flag(read_mark(mine_ref, width) > 0.5)
     choose(by_mine, mine_ref, pair_ref, prev, width)
     for first in (0, 1):
         cols = prev.at[:, first * width // 2 : (first + 1) * width // 2]

time: 34.9 us -> 34.9 us (level)
  no operation moved by 1% of the time
where the time goes in v7:
time: 34.9 us; the launch traced here: 34.7 us
  starting transfers between devices  13.4 us (38%)
  waiting for transfers between devices  8.56 us (25%)
  Pallas kernels  8.35 us (24%)
  local copies, waits for them, and re-layouts  2.91 us (8%)
  between operations  1.52 us (4%)
    ppermute x12, waiting for transfers between devices, send(): return lax.ppermute(value, 'seq', [(i, where(i)) for i in range(seq)])  7.96 us
    ppermute x12, starting transfers between devices, send(): return lax.ppermute(value, 'seq', [(i, where(i)) for i in range(seq)])  7.67 us
    ppermute x3, starting transfers between devices, send_all(): lax.ppermute(value, ('seq', 'dp'), [(s * dp + d, t * dp + e) for s, d, t,...  5.71 us
    pallas_call x2, Pallas kernels, self_backward(): call(f'self_backward_{block}', functools.partial(self_back_kernel, block=...  2.91 us
    pallas_call x1, Pallas kernels, on_device(): call('cross', functools.partial(cross_kernel, groups=groups, repeat=repea...  2.14 us
    unnamed x12, local copies, waits for them, and re-layouts  1.9 us
    pallas_call x2, Pallas kernels, self_forward(): call(f'self_forward_{block}', functools.partial(self_kernel, block=block,...  1.54 us
    concatenate x1, local copies, waits for them, and re-layouts, on_device(): jnp.concatenate([own, jnp.broadcast_to(is_owner, (img, MARKS))], axis=1)  0.92 us
  transfers between devices with their start and end apart: 15, of which 8 were waited for; matrix products, arithmetic and copies ran while one was open for 0% of the time, Pallas kernels for 15%

profile of v7, /device:TPU:0, one launch (start us, length us, event | category | flops | bytes accessed | tf_op | source)
XLA Modules:
  0.0 34.7 jit_solution(376772141702350731)
XLA Ops:
  0.6 0.0 copy-start.2
  1.3 0.9 %concatenate.3.mine_ref.own_ref = bf16[64,1408]{1,0:T(8,128)(2,1)S(1)} pad(bf16[64,1024]{1,0:T(8,128)(2,1)} %bitcast.24, bf16[]{:T(256)} %bitcast.4), padding=0_0x0_384 | pad | bytes 311298 | tf_op jit(solution)/shard_map/concatenate | solution.py:414
  2.3 0.5 %collective-permute-start = (bf16[64,1408]{1,0:T(8,128)(2,1)S(1)}, bf16[64,1408]{1,0:T(8,128)(2,1)S(1)}, u32[]{:S(2)}, u32[]{:S(2)}) collective-permute-start(bf16[64,1408]{1,0:T(8,128)(2,1)S(1)} %concatenate.3.mine_ref.own_ref), channel_id=1, source_target_pairs={{0,2},{2,0},{4,6},{6,4},{8,10},{10,8},{12,14},{14,12},{16,18},{18,... | collective-permute-start | bytes 540680 | tf_op jit(solution)/shard_map/ppermute | solution.py:383
  2.8 2.6 %collective-permute-start.2 = (bf16[80,1024]{1,0:T(8,128)(2,1)S(1)}, bf16[80,1024]{1,0:T(8,128)(2,1)S(1)}, u32[]{:S(2)}, u32[]{:S(2)}) collective-permute-start(bf16[80,1024]{1,0:T(8,128)(2,1)S(1)} %slice_bitcast_fusion.halo_ref), channel_id=1, source_target_pairs={{0,1},{1,0},{2,4},{3,5},{4,2},{5,3},{6,8},{7,9},{8,6},{9,7},{10,12... | collective-permute-start | bytes 491528 | tf_op jit(solution)/shard_map/ppermute | solution.py:387
  5.4 0.1 collective-permute-start.1
  5.5 0.0 collective-permute-done.other_ref
  5.5 0.1 chip_image.1
  5.6 1.6 %collective-permute-start.3 = (bf16[64,1152]{1,0:T(8,128)(2,1)S(1)}, bf16[64,1152]{1,0:T(8,128)(2,1)S(1)}, u32[]{:S(2)}, u32[]{:S(2)}) collective-permute-start(bf16[64,1152]{1,0:T(8,128)(2,1)S(1)} %get-tuple-element.37), channel_id=1, source_target_pairs={{0,8},{2,14},{4,12},{6,10},{8,16},{10,22},{12,20},{14,18},{16,24},... | collective-permute-start | bytes 442376 | tf_op jit(solution)/shard_map/ppermute | solution.py:383
  7.2 1.5 %collective-permute-start.4 = (bf16[64,512]{1,0:T(8,128)(2,1)S(1)}, bf16[64,512]{1,0:T(8,128)(2,1)S(1)}, u32[]{:S(2)}, u32[]{:S(2)}) collective-permute-start(bf16[64,512]{1,0:T(8,128)(2,1)S(1)} %get-tuple-element.38), channel_id=1, source_target_pairs={{0,4},{2,6},{4,0},{6,2},{8,12},{10,14},{12,8},{14,10},{16,20},{18,... | collective-permute-start | bytes 196616 | tf_op jit(solution)/shard_map/ppermute | solution.py:383
  8.8 0.7 %copy-done.4 = s32[1,128]{1,0:T(1,128)S(1)} copy-done((s32[1,128]{1,0:T(1,128)S(1)}, s32[1,128]{1,0:T(1,128)}, u32[]{:S(2)}) %copy-start.4) | copy-done | bytes 536
  9.4 1.2 %copy-done = bf16[1,128,4096]{2,1,0:T(8,128)(2,1)S(1)} copy-done((bf16[1,128,4096]{2,1,0:T(8,128)(2,1)S(1)}, bf16[1,128,4096]{2,1,0:T(8,128)(2,1)}, u32[]{:S(2)}) %copy-start) | copy-done | bytes 1048600
  10.6 0.8 %self_forward_1.1 = (bf16[4,128,512]{2,1,0:T(8,128)(2,1)S(1)}, f32[4,128,512]{2,1,0:T(8,128)S(1)}) custom-call(bf16[128,4096]{1,0:T(8,128)(2,1)S(1)} %bitcast.13, bf16[128,1024]{1,0:T(8,128)(2,1)S(1)} %bitcast.17, bf16[80,1024]{1,0:T(8,128)(2,1)S(1)} %slice_bitcast_fusion.halo_ref, s32[1,128]{1,0:T(1,128)S(1)} %copy-done.4, ...), custom_call_target="tpu_custom_call" | custom-call | flops 1000000 | bytes 100000 | tf_op jit(solution)/shard_map/self_forward_1/pallas_call | solution.py:430
  11.4 0.0 copy-start.1
  11.4 0.0 collective-permute-done.2.other_ref
  11.4 0.0 collective-permute-done.1.chip_ref
  11.5 0.0 copy-start.5
  11.5 0.4 %collective-permute-done.4.x_ref = bf16[64,512]{1,0:T(8,128)(2,1)S(1)} collective-permute-done((bf16[64,512]{1,0:T(8,128)(2,1)S(1)}, bf16[64,512]{1,0:T(8,128)(2,1)S(1)}, u32[]{:S(2)}, u32[]{:S(2)}) %collective-permute-start.4) | collective-permute-done | bytes 65568 | tf_op jit(solution)/shard_map/ppermute | solution.py:383
  11.9 3.5 %collective-permute-done.3.z_ref = bf16[64,1152]{1,0:T(8,128)(2,1)S(1)} collective-permute-done((bf16[64,1152]{1,0:T(8,128)(2,1)S(1)}, bf16[64,1152]{1,0:T(8,128)(2,1)S(1)}, u32[]{:S(2)}, u32[]{:S(2)}) %collective-permute-start.3) | collective-permute-done | bytes 147488 | tf_op jit(solution)/shard_map/ppermute | solution.py:383
  15.4 0.0 copy-start.3
  15.4 0.1 collective-permute-start.5
  15.5 0.8 %self_forward_0.1 = (bf16[4,128,512]{2,1,0:T(8,128)(2,1)S(1)}, f32[4,128,512]{2,1,0:T(8,128)S(1)}) custom-call(bf16[128,4096]{1,0:T(8,128)(2,1)S(1)} %bitcast.14, bf16[128,1024]{1,0:T(8,128)(2,1)S(1)} %bitcast.18, bf16[64,1024]{1,0:T(8,128)(2,1)S(1)} %halo.1.__.halo_ref, s32[1,128]{1,0:T(1,128)S(1)} %copy-done.4, bf16[64,1664]{1,0:T(8,128)(2,1)S(1)} %arrived.1._.mine_ref), custom_call_target="tpu_custom_call" | custom-call | flops 1000000 | bytes 100000 | tf_op jit(solution)/shard_map/self_forward_0/pallas_call | solution.py:430
  16.3 0.6 %collective-permute-done.5.pair_ref = bf16[64,1664]{1,0:T(8,128)(2,1)S(1)} collective-permute-done((bf16[64,1664]{1,0:T(8,128)(2,1)S(1)}, bf16[64,1664]{1,0:T(8,128)(2,1)S(1)}, u32[]{:S(2)}, u32[]{:S(2)}) %collective-permute-start.5) | collective-permute-done | bytes 213024 | tf_op jit(solution)/shard_map/ppermute | solution.py:383
  17.0 0.1 broadcast_in_dim.34.gate_ref.refs_1_
  17.0 2.1 %cross.1 = (bf16[4,128,1024]{2,1,0:T(8,128)(2,1)S(1)}, f32[64,1152]{1,0:T(8,128)S(1)}, bf16[64,1280]{1,0:T(8,128)(2,1)S(1)}, f32[64,1024]{1,0:T(8,128)S(1)}, f32...) custom-call(s32[8,128]{1,0:T(8,128)S(1)} %broadcast_in_dim.33.off_ref, ...), custom_call_target="tpu_custom_call" | custom-call | flops 1000 | bytes 1000 | tf_op jit(solution)/shard_map/cross/pallas_call | solution.py:449
  19.2 0.2 collective-permute-start.6
  19.4 0.0 collective-permute-start.7
  19.4 0.5 %cross_query.1._.grad_ref = bf16[4,1024,128]{2,1,0:T(8,128)(2,1)S(1)} custom-call(bf16[4,128,1024]{2,1,0:T(8,128)(2,1)S(1)} %get-tuple-element.40.scores_ref, bf16[128,4096]{1,0:T(8,128)(2,1)S(1)} %bitcast.22, bf16[64,1408]{1,0:T(8,128)(2,1)S(1)} %concatenate.3.mine_ref.own_ref, bf16[64,1024]{1,0:T(8,128)(2,1)S(1)} %get-tuple-element.41.prev, ...), custom_call_target="tpu_custom_call" | custom-call | flops 1000 | bytes 1000 | tf_op jit(solution)/shard_map/cross_query/pallas_call | solution.py:465
  19.9 0.9 %collective-permute-done.6.pair_ref = f32[64,1152]{1,0:T(8,128)S(1)} collective-permute-done((f32[64,1152]{1,0:T(8,128)S(1)}, f32[64,1152]{1,0:T(8,128)S(1)}, u32[]{:S(2)}, u32[]{:S(2)}) %collective-permute-start.6) | collective-permute-done | bytes 294944 | tf_op jit(solution)/shard_map/ppermute | solution.py:383
  20.8 0.1 outside.1
  20.9 2.3 %collective-permute-start.8 = (bf16[64,1152]{1,0:T(8,128)(2,1)S(1)}, bf16[64,1152]{1,0:T(8,128)(2,1)S(1)}, u32[]{:S(2)}, u32[]{:S(2)}) collective-permute-start(bf16[64,1152]{1,0:T(8,128)(2,1)S(1)} %get-tuple-element.45.refs_0_), channel_id=1, source_target_pairs={{0,24},{2,30},{4,28},{6,26},{8,0},{10,6},{12,4},{14,2},{16,8},{18,... | collective-permute-start | bytes 442376 | tf_op jit(solution)/shard_map/ppermute | solution.py:383
  23.2 0.0 collective-permute-start.10
  23.2 1.1 %collective-permute-start.9 = (f32[16,128]{1,0:T(8,128)S(1)}, f32[16,128]{1,0:T(8,128)S(1)}, u32[]{:S(2)}, u32[]{:S(2)}) collective-permute-start(f32[16,128]{1,0:T(8,128)S(1)} %get-tuple-element.49.gate_ref), channel_id=1, source_target_pairs={{0,8},{2,14},{4,12},{6,10},{8,16},{10,22},{12,20},{14,18},{16,24},... | collective-permute-start | bytes 24584 | tf_op jit(solution)/shard_map/ppermute | solution.py:383
  24.3 1.5 %self_backward_0.1 = (bf16[128,4096]{1,0:T(8,128)(2,1)}, bf16[80,1024]{1,0:T(8,128)(2,1)S(1)}, f32[64,1024]{1,0:T(8,128)S(1)}) custom-call(bf16[128,4096]{1,0:T(8,128)(2,1)S(1)} %bitcast.15, bf16[128,1024]{1,0:T(8,128)(2,1)S(1)} %bitcast.19, bf16[64,1024]{1,0:T(8,128)(2,1)S(1)} %halo.1.__.halo_ref, f32[4,128,512]{2,1,0:T(8,128)S(1)} %get-tuple-element.43.weights_ref, ...), custom_call_target="tpu_custom_call" | custom-call | flops 1000000 | bytes 100000 | tf_op jit(solution)/shard_map/self_backward_0/pallas_call | solution.py:473
  25.8 1.6 %collective-permute-start.13 = (bf16[80,1024]{1,0:T(8,128)(2,1)S(1)}, bf16[80,1024]{1,0:T(8,128)(2,1)S(1)}, u32[]{:S(2)}, u32[]{:S(2)}) collective-permute-start(bf16[80,1024]{1,0:T(8,128)(2,1)S(1)} %get-tuple-element.57), channel_id=1, source_target_pairs={{0,1},{1,0},{2,4},{3,5},{4,2},{5,3},{6,8},{7,9},{8,6},{9,7},{10,12... | collective-permute-start | bytes 491528 | tf_op jit(solution)/shard_map/ppermute | solution.py:387
  27.4 0.0 collective-permute-done.7.x_ref
  27.4 0.0 collective-permute-start.12
  27.4 0.4 %collective-permute-done.10.refs_1_ = f32[16,128]{1,0:T(8,128)S(1)} collective-permute-done((f32[16,128]{1,0:T(8,128)S(1)}, f32[16,128]{1,0:T(8,128)S(1)}, u32[]{:S(2)}, u32[]{:S(2)}) %collective-permute-start.10) | collective-permute-done | bytes 8224 | tf_op jit(solution)/shard_map/ppermute | solution.py:383
  27.8 0.8 %collective-permute-done.9.refs_0_ = f32[16,128]{1,0:T(8,128)S(1)} collective-permute-done((f32[16,128]{1,0:T(8,128)S(1)}, f32[16,128]{1,0:T(8,128)S(1)}, u32[]{:S(2)}, u32[]{:S(2)}) %collective-permute-start.9) | collective-permute-done | bytes 8224 | tf_op jit(solution)/shard_map/ppermute | solution.py:383
  28.7 0.0 collective-permute-done.8.z_ref
  28.7 0.1 chip_sum.1
  28.7 0.2 collective-permute-start.11
  28.9 1.3 %collective-permute-done.11.pair_ref = bf16[64,1152]{1,0:T(8,128)(2,1)S(1)} collective-permute-done((bf16[64,1152]{1,0:T(8,128)(2,1)S(1)}, bf16[64,1152]{1,0:T(8,128)(2,1)S(1)}, u32[]{:S(2)}, u32[]{:S(2)}) %collective-permute-start.11) | collective-permute-done | bytes 147488 | tf_op jit(solution)/shard_map/ppermute | solution.py:383
  30.2 1.5 %collective-permute-start.14 = (f32[16,128]{1,0:T(8,128)S(1)}, f32[16,128]{1,0:T(8,128)S(1)}, u32[]{:S(2)}, u32[]{:S(2)}) collective-permute-start(f32[16,128]{1,0:T(8,128)S(1)} %gate_sum.1.gate_ref), channel_id=1, source_target_pairs={{0,1},{1,0},{2,3},{3,2},{4,5},{5,4},{6,7},{7,6},{8,9},{9,8},{10,11... | collective-permute-start | bytes 24584 | tf_op jit(solution)/shard_map/ppermute | solution.py:387
  31.7 1.5 %self_backward_1.1 = (bf16[128,4096]{1,0:T(8,128)(2,1)}, f32[64,1024]{1,0:T(8,128)S(1)}, f32[64,1024]{1,0:T(8,128)S(1)}) custom-call(bf16[128,4096]{1,0:T(8,128)(2,1)S(1)} %bitcast.16, bf16[128,1024]{1,0:T(8,128)(2,1)S(1)} %bitcast.20, bf16[80,1024]{1,0:T(8,128)(2,1)S(1)} %slice_bitcast_fusion.halo_ref, ...), custom_call_target="tpu_custom_call", output_to_operand_aliasing={{0}: (5, {})} | custom-call | flops 1000000 | bytes 100000 | tf_op jit(solution)/shard_map/self_backward_1/pallas_call | solution.py:473
  33.2 0.0 collective-permute-done.13.other_ref
  33.2 0.0 collective-permute-done.12.chip_ref
  33.2 0.6 %collective-permute-done.14.refs_0_ = f32[16,128]{1,0:T(8,128)S(1)} collective-permute-done((f32[16,128]{1,0:T(8,128)S(1)}, f32[16,128]{1,0:T(8,128)S(1)}, u32[]{:S(2)}, u32[]{:S(2)}) %collective-permute-start.14) | collective-permute-done | bytes 8224 | tf_op jit(solution)/shard_map/ppermute | solution.py:387
  33.8 0.9 %finish.1 = (bf16[64,1024]{1,0:T(8,128)(2,1)}, bf16[128,1024]{1,0:T(8,128)(2,1)}, f32[1,32]{1,0:T(1,128)}) custom-call(f32[8,128]{1,0:T(8,128)S(1)} %get-tuple-element.35.owner_ref, f32[64,1024]{1,0:T(8,128)S(1)} %get-tuple-element.53.own_ref, f32[64,1024]{1,0:T(8,128)S(1)} %get-tuple-element.51.refs_1_.mine_ref, ...), custom_call_target="tpu_custom_call" | custom-call | flops 1000 | bytes 1000 | tf_op jit(solution)/shard_map/finish/pallas_call | solution.py:516
  (13 shorter events, 0.1 us)
Async XLA Ops:
  0.6 2.2 %copy-start.2 = (bf16[1,128,1024]{2,1,0:T(8,128)(2,1)S(1)}, bf16[1,128,1024]{2,1,0:T(8,128)(2,1)}, u32[]{:S(2)}) copy-start(bf16[1,128,1024]{2,1,0:T(8,128)(2,1)} %param.8) | copy-start | bytes 786436
  2.3 3.2 %collective-permute-start = (bf16[64,1408]{1,0:T(8,128)(2,1)S(1)}, bf16[64,1408]{1,0:T(8,128)(2,1)S(1)}, u32[]{:S(2)}, u32[]{:S(2)}) collective-permute-start(bf16[64,1408]{1,0:T(8,128)(2,1)S(1)} %concatenate.3.mine_ref.own_ref), channel_id=1, source_target_pairs={{0,2},{2,0},{4,6},{6,4},{8,10},{10,8},{12,14},{14,12},{16,18},{18,... | collective-permute-start | bytes 540680 | tf_op jit(solution)/shard_map/ppermute | solution.py:383
  2.8 8.6 %collective-permute-start.2 = (bf16[80,1024]{1,0:T(8,128)(2,1)S(1)}, bf16[80,1024]{1,0:T(8,128)(2,1)S(1)}, u32[]{:S(2)}, u32[]{:S(2)}) collective-permute-start(bf16[80,1024]{1,0:T(8,128)(2,1)S(1)} %slice_bitcast_fusion.halo_ref), channel_id=1, source_target_pairs={{0,1},{1,0},{2,4},{3,5},{4,2},{5,3},{6,8},{7,9},{8,6},{9,7},{10,12... | collective-permute-start | bytes 491528 | tf_op jit(solution)/shard_map/ppermute | solution.py:387
  5.4 6.0 %collective-permute-start.1 = (bf16[80,1024]{1,0:T(8,128)(2,1)S(1)}, bf16[80,1024]{1,0:T(8,128)(2,1)S(1)}, u32[]{:S(2)}, u32[]{:S(2)}) collective-permute-start(bf16[80,1024]{1,0:T(8,128)(2,1)S(1)} %slice_bitcast_fusion.halo_ref), channel_id=1, source_target_pairs={{0,2},{2,0},{4,6},{6,4},{8,10},{10,8},{12,14},{14,12},{16,18},{18,... | collective-permute-start | bytes 491528 | tf_op jit(solution)/shard_map/ppermute | solution.py:383
  5.6 9.8 %collective-permute-start.3 = (bf16[64,1152]{1,0:T(8,128)(2,1)S(1)}, bf16[64,1152]{1,0:T(8,128)(2,1)S(1)}, u32[]{:S(2)}, u32[]{:S(2)}) collective-permute-start(bf16[64,1152]{1,0:T(8,128)(2,1)S(1)} %get-tuple-element.37), channel_id=1, source_target_pairs={{0,8},{2,14},{4,12},{6,10},{8,16},{10,22},{12,20},{14,18},{16,24},... | collective-permute-start | bytes 442376 | tf_op jit(solution)/shard_map/ppermute | solution.py:383
  7.2 4.7 %collective-permute-start.4 = (bf16[64,512]{1,0:T(8,128)(2,1)S(1)}, bf16[64,512]{1,0:T(8,128)(2,1)S(1)}, u32[]{:S(2)}, u32[]{:S(2)}) collective-permute-start(bf16[64,512]{1,0:T(8,128)(2,1)S(1)} %get-tuple-element.38), channel_id=1, source_target_pairs={{0,4},{2,6},{4,0},{6,2},{8,12},{10,14},{12,8},{14,10},{16,20},{18,... | collective-permute-start | bytes 196616 | tf_op jit(solution)/shard_map/ppermute | solution.py:383
  8.8 0.7 %copy-start.4 = (s32[1,128]{1,0:T(1,128)S(1)}, s32[1,128]{1,0:T(1,128)}, u32[]{:S(2)}) copy-start(s32[1,128]{1,0:T(1,128)} %segment_ref.3) | copy-start | bytes 1540
  9.4 1.2 %copy-start = (bf16[1,128,4096]{2,1,0:T(8,128)(2,1)S(1)}, bf16[1,128,4096]{2,1,0:T(8,128)(2,1)}, u32[]{:S(2)}) copy-start(bf16[1,128,4096]{2,1,0:T(8,128)(2,1)} %param.7) | copy-start | bytes 3145732
  11.4 4.1 %copy-start.1 = (bf16[1,128,4096]{2,1,0:T(8,128)(2,1)S(1)}, bf16[1,128,4096]{2,1,0:T(8,128)(2,1)}, u32[]{:S(2)}) copy-start(bf16[1,128,4096]{2,1,0:T(8,128)(2,1)} %param.7) | copy-start | bytes 3145732
  11.5 4.0 %copy-start.5 = (f32[32]{0:T(128)S(1)}, f32[32]{0:T(128)}, u32[]{:S(2)}) copy-start(f32[32]{0:T(128)} %param.12) | copy-start | bytes 388
  15.4 1.6 %copy-start.3 = (bf16[1,128,4096]{2,1,0:T(8,128)(2,1)S(1)}, bf16[1,128,4096]{2,1,0:T(8,128)(2,1)}, u32[]{:S(2)}) copy-start(bf16[1,128,4096]{2,1,0:T(8,128)(2,1)} %param.13) | copy-start | bytes 3145732
  15.4 1.5 %collective-permute-start.5 = (bf16[64,1664]{1,0:T(8,128)(2,1)S(1)}, bf16[64,1664]{1,0:T(8,128)(2,1)S(1)}, u32[]{:S(2)}, u32[]{:S(2)}) collective-permute-start(bf16[64,1664]{1,0:T(8,128)(2,1)S(1)} %arrived.1._.mine_ref), channel_id=1, source_target_pairs={{0,2},{2,0},{4,6},{6,4},{8,10},{10,8},{12,14},{14,12},{16,18},{18,... | collective-permute-start | bytes 638984 | tf_op jit(solution)/shard_map/ppermute | solution.py:383
  19.2 1.6 %collective-permute-start.6 = (f32[64,1152]{1,0:T(8,128)S(1)}, f32[64,1152]{1,0:T(8,128)S(1)}, u32[]{:S(2)}, u32[]{:S(2)}) collective-permute-start(f32[64,1152]{1,0:T(8,128)S(1)} %get-tuple-element.42._.mine_ref), channel_id=1, source_target_pairs={{0,2},{2,0},{4,6},{6,4},{8,10},{10,8},{12,14},{14,12},{16,18},{18,... | collective-permute-start | bytes 884744 | tf_op jit(solution)/shard_map/ppermute | solution.py:383
  19.4 8.1 %collective-permute-start.7 = (bf16[64,1280]{1,0:T(8,128)(2,1)S(1)}, bf16[64,1280]{1,0:T(8,128)(2,1)S(1)}, u32[]{:S(2)}, u32[]{:S(2)}) collective-permute-start(bf16[64,1280]{1,0:T(8,128)(2,1)S(1)} %get-tuple-element.48), channel_id=1, source_target_pairs={{0,4},{2,6},{4,0},{6,2},{8,12},{10,14},{12,8},{14,10},{16,20},{18,... | collective-permute-start | bytes 491528 | tf_op jit(solution)/shard_map/ppermute | solution.py:383
  20.9 7.8 %collective-permute-start.8 = (bf16[64,1152]{1,0:T(8,128)(2,1)S(1)}, bf16[64,1152]{1,0:T(8,128)(2,1)S(1)}, u32[]{:S(2)}, u32[]{:S(2)}) collective-permute-start(bf16[64,1152]{1,0:T(8,128)(2,1)S(1)} %get-tuple-element.45.refs_0_), channel_id=1, source_target_pairs={{0,24},{2,30},{4,28},{6,26},{8,0},{10,6},{12,4},{14,2},{16,8},{18,... | collective-permute-start | bytes 442376 | tf_op jit(solution)/shard_map/ppermute | solution.py:383
  23.2 4.6 %collective-permute-start.10 = (f32[16,128]{1,0:T(8,128)S(1)}, f32[16,128]{1,0:T(8,128)S(1)}, u32[]{:S(2)}, u32[]{:S(2)}) collective-permute-start(f32[16,128]{1,0:T(8,128)S(1)} %get-tuple-element.49.gate_ref), channel_id=1, source_target_pairs={{0,16},{2,22},{4,20},{6,18},{8,24},{10,30},{12,28},{14,26},{16,0},... | collective-permute-start | bytes 24584 | tf_op jit(solution)/shard_map/ppermute | solution.py:383
  23.2 5.4 %collective-permute-start.9 = (f32[16,128]{1,0:T(8,128)S(1)}, f32[16,128]{1,0:T(8,128)S(1)}, u32[]{:S(2)}, u32[]{:S(2)}) collective-permute-start(f32[16,128]{1,0:T(8,128)S(1)} %get-tuple-element.49.gate_ref), channel_id=1, source_target_pairs={{0,8},{2,14},{4,12},{6,10},{8,16},{10,22},{12,20},{14,18},{16,24},... | collective-permute-start | bytes 24584 | tf_op jit(solution)/shard_map/ppermute | solution.py:383
  25.8 7.4 %collective-permute-start.13 = (bf16[80,1024]{1,0:T(8,128)(2,1)S(1)}, bf16[80,1024]{1,0:T(8,128)(2,1)S(1)}, u32[]{:S(2)}, u32[]{:S(2)}) collective-permute-start(bf16[80,1024]{1,0:T(8,128)(2,1)S(1)} %get-tuple-element.57), channel_id=1, source_target_pairs={{0,1},{1,0},{2,4},{3,5},{4,2},{5,3},{6,8},{7,9},{8,6},{9,7},{10,12... | collective-permute-start | bytes 491528 | tf_op jit(solution)/shard_map/ppermute | solution.py:387
  27.4 5.8 %collective-permute-start.12 = (bf16[80,1024]{1,0:T(8,128)(2,1)S(1)}, bf16[80,1024]{1,0:T(8,128)(2,1)S(1)}, u32[]{:S(2)}, u32[]{:S(2)}) collective-permute-start(bf16[80,1024]{1,0:T(8,128)(2,1)S(1)} %get-tuple-element.57), channel_id=1, source_target_pairs={{0,2},{2,0},{4,6},{6,4},{8,10},{10,8},{12,14},{14,12},{16,18},{18,... | collective-permute-start | bytes 491528 | tf_op jit(solution)/shard_map/ppermute | solution.py:383
  28.7 1.4 %collective-permute-start.11 = (bf16[64,1152]{1,0:T(8,128)(2,1)S(1)}, bf16[64,1152]{1,0:T(8,128)(2,1)S(1)}, u32[]{:S(2)}, u32[]{:S(2)}) collective-permute-start(bf16[64,1152]{1,0:T(8,128)(2,1)S(1)} %get-tuple-element.54), channel_id=1, source_target_pairs={{0,2},{2,0},{4,6},{6,4},{8,10},{10,8},{12,14},{14,12},{16,18},{18,... | collective-permute-start | bytes 442376 | tf_op jit(solution)/shard_map/ppermute | solution.py:383
  30.2 3.7 %collective-permute-start.14 = (f32[16,128]{1,0:T(8,128)S(1)}, f32[16,128]{1,0:T(8,128)S(1)}, u32[]{:S(2)}, u32[]{:S(2)}) collective-permute-start(f32[16,128]{1,0:T(8,128)S(1)} %gate_sum.1.gate_ref), channel_id=1, source_target_pairs={{0,1},{1,0},{2,3},{3,2},{4,5},{5,4},{6,7},{7,6},{8,9},{9,8},{10,11... | collective-permute-start | bytes 24584 | tf_op jit(solution)/shard_map/ppermute | solution.py:387

commit v8 on v7

--- a/solution.py
+++ b/solution.py
@@ -12,7 +12,7 @@
 WINDOW = 64
 GAP = 4
 LANES = 128
-WIDE = 2
+WIDE = 1
 MORE = 16
 MARKS = 384
 SCALE = 1.0 / math.sqrt(HEAD_DIM)

time: 34.9 us -> 34.9 us (level)
  no operation moved by 1% of the time
where the time goes in v8:
time: 34.9 us; the launch traced here: 34.7 us
  starting transfers between devices  13.4 us (38%)
  waiting for transfers between devices  8.56 us (25%)
  Pallas kernels  8.34 us (24%)
  local copies, waits for them, and re-layouts  2.91 us (8%)
  between operations  1.52 us (4%)
    ppermute x12, waiting for transfers between devices, send(): return lax.ppermute(value, 'seq', [(i, where(i)) for i in range(seq)])  7.96 us
    ppermute x12, starting transfers between devices, send(): return lax.ppermute(value, 'seq', [(i, where(i)) for i in range(seq)])  7.67 us
    ppermute x3, starting transfers between devices, send_all(): lax.ppermute(value, ('seq', 'dp'), [(s * dp + d, t * dp + e) for s, d, t,...  5.71 us
    pallas_call x2, Pallas kernels, self_backward(): call(f'self_backward_{block}', functools.partial(self_back_kernel, block=...  2.91 us
    pallas_call x1, Pallas kernels, on_device(): call('cross', functools.partial(cross_kernel, groups=groups, repeat=repea...  2.13 us
    unnamed x12, local copies, waits for them, and re-layouts  1.9 us
    pallas_call x2, Pallas kernels, self_forward(): call(f'self_forward_{block}', functools.partial(self_kernel, block=block,...  1.54 us
    concatenate x1, local copies, waits for them, and re-layouts, on_device(): jnp.concatenate([own, jnp.broadcast_to(is_owner, (img, MARKS))], axis=1)  0.92 us
  transfers between devices with their start and end apart: 15, of which 8 were waited for; matrix products, arithmetic and copies ran while one was open for 0% of the time, Pallas kernels for 15%

profile of v8, /device:TPU:0, one launch (start us, length us, event | category | flops | bytes accessed | tf_op | source)
XLA Modules:
  0.0 34.7 jit_solution(4170756777456146738)
XLA Ops:
  0.6 0.0 copy-start.2
  1.3 0.9 %concatenate.3.mine_ref.own_ref = bf16[64,1408]{1,0:T(8,128)(2,1)S(1)} pad(bf16[64,1024]{1,0:T(8,128)(2,1)} %bitcast.24, bf16[]{:T(256)} %bitcast.4), padding=0_0x0_384 | pad | bytes 311298 | tf_op jit(solution)/shard_map/concatenate | solution.py:414
  2.3 0.5 %collective-permute-start = (bf16[64,1408]{1,0:T(8,128)(2,1)S(1)}, bf16[64,1408]{1,0:T(8,128)(2,1)S(1)}, u32[]{:S(2)}, u32[]{:S(2)}) collective-permute-start(bf16[64,1408]{1,0:T(8,128)(2,1)S(1)} %concatenate.3.mine_ref.own_ref), channel_id=1, source_target_pairs={{0,2},{2,0},{4,6},{6,4},{8,10},{10,8},{12,14},{14,12},{16,18},{18,... | collective-permute-start | bytes 540680 | tf_op jit(solution)/shard_map/ppermute | solution.py:383
  2.8 2.6 %collective-permute-start.2 = (bf16[80,1024]{1,0:T(8,128)(2,1)S(1)}, bf16[80,1024]{1,0:T(8,128)(2,1)S(1)}, u32[]{:S(2)}, u32[]{:S(2)}) collective-permute-start(bf16[80,1024]{1,0:T(8,128)(2,1)S(1)} %slice_bitcast_fusion.halo_ref), channel_id=1, source_target_pairs={{0,1},{1,0},{2,4},{3,5},{4,2},{5,3},{6,8},{7,9},{8,6},{9,7},{10,12... | collective-permute-start | bytes 491528 | tf_op jit(solution)/shard_map/ppermute | solution.py:387
  5.4 0.1 collective-permute-start.1
  5.5 0.0 collective-permute-done.other_ref
  5.5 0.1 chip_image.1
  5.6 1.6 %collective-permute-start.3 = (bf16[64,1152]{1,0:T(8,128)(2,1)S(1)}, bf16[64,1152]{1,0:T(8,128)(2,1)S(1)}, u32[]{:S(2)}, u32[]{:S(2)}) collective-permute-start(bf16[64,1152]{1,0:T(8,128)(2,1)S(1)} %get-tuple-element.37), channel_id=1, source_target_pairs={{0,8},{2,14},{4,12},{6,10},{8,16},{10,22},{12,20},{14,18},{16,24},... | collective-permute-start | bytes 442376 | tf_op jit(solution)/shard_map/ppermute | solution.py:383
  7.2 1.5 %collective-permute-start.4 = (bf16[64,512]{1,0:T(8,128)(2,1)S(1)}, bf16[64,512]{1,0:T(8,128)(2,1)S(1)}, u32[]{:S(2)}, u32[]{:S(2)}) collective-permute-start(bf16[64,512]{1,0:T(8,128)(2,1)S(1)} %get-tuple-element.38), channel_id=1, source_target_pairs={{0,4},{2,6},{4,0},{6,2},{8,12},{10,14},{12,8},{14,10},{16,20},{18,... | collective-permute-start | bytes 196616 | tf_op jit(solution)/shard_map/ppermute | solution.py:383
  8.8 0.7 %copy-done.4 = s32[1,128]{1,0:T(1,128)S(1)} copy-done((s32[1,128]{1,0:T(1,128)S(1)}, s32[1,128]{1,0:T(1,128)}, u32[]{:S(2)}) %copy-start.4) | copy-done | bytes 536
  9.4 1.2 %copy-done = bf16[1,128,4096]{2,1,0:T(8,128)(2,1)S(1)} copy-done((bf16[1,128,4096]{2,1,0:T(8,128)(2,1)S(1)}, bf16[1,128,4096]{2,1,0:T(8,128)(2,1)}, u32[]{:S(2)}) %copy-start) | copy-done | bytes 1048600
  10.6 0.8 %self_forward_1.1 = (bf16[4,128,512]{2,1,0:T(8,128)(2,1)S(1)}, f32[4,128,512]{2,1,0:T(8,128)S(1)}) custom-call(bf16[128,4096]{1,0:T(8,128)(2,1)S(1)} %bitcast.13, bf16[128,1024]{1,0:T(8,128)(2,1)S(1)} %bitcast.17, bf16[80,1024]{1,0:T(8,128)(2,1)S(1)} %slice_bitcast_fusion.halo_ref, s32[1,128]{1,0:T(1,128)S(1)} %copy-done.4, ...), custom_call_target="tpu_custom_call" | custom-call | flops 1000000 | bytes 100000 | tf_op jit(solution)/shard_map/self_forward_1/pallas_call | solution.py:430
  11.4 0.0 copy-start.1
  11.4 0.0 collective-permute-done.2.other_ref
  11.4 0.0 collective-permute-done.1.chip_ref
  11.5 0.0 copy-start.5
  11.5 0.4 %collective-permute-done.4.x_ref = bf16[64,512]{1,0:T(8,128)(2,1)S(1)} collective-permute-done((bf16[64,512]{1,0:T(8,128)(2,1)S(1)}, bf16[64,512]{1,0:T(8,128)(2,1)S(1)}, u32[]{:S(2)}, u32[]{:S(2)}) %collective-permute-start.4) | collective-permute-done | bytes 65568 | tf_op jit(solution)/shard_map/ppermute | solution.py:383
  11.9 3.5 %collective-permute-done.3.z_ref = bf16[64,1152]{1,0:T(8,128)(2,1)S(1)} collective-permute-done((bf16[64,1152]{1,0:T(8,128)(2,1)S(1)}, bf16[64,1152]{1,0:T(8,128)(2,1)S(1)}, u32[]{:S(2)}, u32[]{:S(2)}) %collective-permute-start.3) | collective-permute-done | bytes 147488 | tf_op jit(solution)/shard_map/ppermute | solution.py:383
  15.4 0.0 copy-start.3
  15.4 0.1 collective-permute-start.5
  15.5 0.8 %self_forward_0.1 = (bf16[4,128,512]{2,1,0:T(8,128)(2,1)S(1)}, f32[4,128,512]{2,1,0:T(8,128)S(1)}) custom-call(bf16[128,4096]{1,0:T(8,128)(2,1)S(1)} %bitcast.14, bf16[128,1024]{1,0:T(8,128)(2,1)S(1)} %bitcast.18, bf16[64,1024]{1,0:T(8,128)(2,1)S(1)} %halo.1.__.halo_ref, s32[1,128]{1,0:T(1,128)S(1)} %copy-done.4, bf16[64,1664]{1,0:T(8,128)(2,1)S(1)} %arrived.1._.mine_ref), custom_call_target="tpu_custom_call" | custom-call | flops 1000000 | bytes 100000 | tf_op jit(solution)/shard_map/self_forward_0/pallas_call | solution.py:430
  16.3 0.6 %collective-permute-done.5.pair_ref = bf16[64,1664]{1,0:T(8,128)(2,1)S(1)} collective-permute-done((bf16[64,1664]{1,0:T(8,128)(2,1)S(1)}, bf16[64,1664]{1,0:T(8,128)(2,1)S(1)}, u32[]{:S(2)}, u32[]{:S(2)}) %collective-permute-start.5) | collective-permute-done | bytes 213024 | tf_op jit(solution)/shard_map/ppermute | solution.py:383
  17.0 0.1 broadcast_in_dim.34.gate_ref.refs_1_
  17.0 2.1 %cross.1 = (bf16[4,128,1024]{2,1,0:T(8,128)(2,1)S(1)}, f32[64,1152]{1,0:T(8,128)S(1)}, bf16[64,1152]{1,0:T(8,128)(2,1)S(1)}, f32[64,1024]{1,0:T(8,128)S(1)}, f32...) custom-call(s32[8,128]{1,0:T(8,128)S(1)} %broadcast_in_dim.33.off_ref, ...), custom_call_target="tpu_custom_call" | custom-call | flops 1000 | bytes 1000 | tf_op jit(solution)/shard_map/cross/pallas_call | solution.py:449
  19.2 0.2 collective-permute-start.6
  19.4 0.0 collective-permute-start.7
  19.4 0.5 %cross_query.1._.grad_ref = bf16[4,1024,128]{2,1,0:T(8,128)(2,1)S(1)} custom-call(bf16[4,128,1024]{2,1,0:T(8,128)(2,1)S(1)} %get-tuple-element.40.scores_ref, bf16[128,4096]{1,0:T(8,128)(2,1)S(1)} %bitcast.22, bf16[64,1408]{1,0:T(8,128)(2,1)S(1)} %concatenate.3.mine_ref.own_ref, bf16[64,1024]{1,0:T(8,128)(2,1)S(1)} %get-tuple-element.41.prev, ...), custom_call_target="tpu_custom_call" | custom-call | flops 1000 | bytes 1000 | tf_op jit(solution)/shard_map/cross_query/pallas_call | solution.py:465
  19.9 0.9 %collective-permute-done.6.pair_ref = f32[64,1152]{1,0:T(8,128)S(1)} collective-permute-done((f32[64,1152]{1,0:T(8,128)S(1)}, f32[64,1152]{1,0:T(8,128)S(1)}, u32[]{:S(2)}, u32[]{:S(2)}) %collective-permute-start.6) | collective-permute-done | bytes 294944 | tf_op jit(solution)/shard_map/ppermute | solution.py:383
  20.8 0.1 outside.1
  20.9 2.3 %collective-permute-start.8 = (bf16[64,1152]{1,0:T(8,128)(2,1)S(1)}, bf16[64,1152]{1,0:T(8,128)(2,1)S(1)}, u32[]{:S(2)}, u32[]{:S(2)}) collective-permute-start(bf16[64,1152]{1,0:T(8,128)(2,1)S(1)} %get-tuple-element.45.refs_0_), channel_id=1, source_target_pairs={{0,24},{2,30},{4,28},{6,26},{8,0},{10,6},{12,4},{14,2},{16,8},{18,... | collective-permute-start | bytes 442376 | tf_op jit(solution)/shard_map/ppermute | solution.py:383
  23.2 0.0 collective-permute-start.10
  23.2 1.1 %collective-permute-start.9 = (f32[16,128]{1,0:T(8,128)S(1)}, f32[16,128]{1,0:T(8,128)S(1)}, u32[]{:S(2)}, u32[]{:S(2)}) collective-permute-start(f32[16,128]{1,0:T(8,128)S(1)} %get-tuple-element.49.gate_ref), channel_id=1, source_target_pairs={{0,8},{2,14},{4,12},{6,10},{8,16},{10,22},{12,20},{14,18},{16,24},... | collective-permute-start | bytes 24584 | tf_op jit(solution)/shard_map/ppermute | solution.py:383
  24.3 1.5 %self_backward_0.1 = (bf16[128,4096]{1,0:T(8,128)(2,1)}, bf16[80,1024]{1,0:T(8,128)(2,1)S(1)}, f32[64,1024]{1,0:T(8,128)S(1)}) custom-call(bf16[128,4096]{1,0:T(8,128)(2,1)S(1)} %bitcast.15, bf16[128,1024]{1,0:T(8,128)(2,1)S(1)} %bitcast.19, bf16[64,1024]{1,0:T(8,128)(2,1)S(1)} %halo.1.__.halo_ref, f32[4,128,512]{2,1,0:T(8,128)S(1)} %get-tuple-element.43.weights_ref, ...), custom_call_target="tpu_custom_call" | custom-call | flops 1000000 | bytes 100000 | tf_op jit(solution)/shard_map/self_backward_0/pallas_call | solution.py:473
  25.8 1.6 %collective-permute-start.13 = (bf16[80,1024]{1,0:T(8,128)(2,1)S(1)}, bf16[80,1024]{1,0:T(8,128)(2,1)S(1)}, u32[]{:S(2)}, u32[]{:S(2)}) collective-permute-start(bf16[80,1024]{1,0:T(8,128)(2,1)S(1)} %get-tuple-element.57), channel_id=1, source_target_pairs={{0,1},{1,0},{2,4},{3,5},{4,2},{5,3},{6,8},{7,9},{8,6},{9,7},{10,12... | collective-permute-start | bytes 491528 | tf_op jit(solution)/shard_map/ppermute | solution.py:387
  27.4 0.0 collective-permute-done.7.x_ref
  27.4 0.0 collective-permute-start.12
  27.4 0.4 %collective-permute-done.10.refs_1_ = f32[16,128]{1,0:T(8,128)S(1)} collective-permute-done((f32[16,128]{1,0:T(8,128)S(1)}, f32[16,128]{1,0:T(8,128)S(1)}, u32[]{:S(2)}, u32[]{:S(2)}) %collective-permute-start.10) | collective-permute-done | bytes 8224 | tf_op jit(solution)/shard_map/ppermute | solution.py:383
  27.9 0.8 %collective-permute-done.9.refs_0_ = f32[16,128]{1,0:T(8,128)S(1)} collective-permute-done((f32[16,128]{1,0:T(8,128)S(1)}, f32[16,128]{1,0:T(8,128)S(1)}, u32[]{:S(2)}, u32[]{:S(2)}) %collective-permute-start.9) | collective-permute-done | bytes 8224 | tf_op jit(solution)/shard_map/ppermute | solution.py:383
  28.7 0.0 collective-permute-done.8.z_ref
  28.7 0.1 chip_sum.1
  28.7 0.2 collective-permute-start.11
  28.9 1.3 %collective-permute-done.11.pair_ref = bf16[64,1152]{1,0:T(8,128)(2,1)S(1)} collective-permute-done((bf16[64,1152]{1,0:T(8,128)(2,1)S(1)}, bf16[64,1152]{1,0:T(8,128)(2,1)S(1)}, u32[]{:S(2)}, u32[]{:S(2)}) %collective-permute-start.11) | collective-permute-done | bytes 147488 | tf_op jit(solution)/shard_map/ppermute | solution.py:383
  30.2 1.5 %collective-permute-start.14 = (f32[16,128]{1,0:T(8,128)S(1)}, f32[16,128]{1,0:T(8,128)S(1)}, u32[]{:S(2)}, u32[]{:S(2)}) collective-permute-start(f32[16,128]{1,0:T(8,128)S(1)} %gate_sum.1.gate_ref), channel_id=1, source_target_pairs={{0,1},{1,0},{2,3},{3,2},{4,5},{5,4},{6,7},{7,6},{8,9},{9,8},{10,11... | collective-permute-start | bytes 24584 | tf_op jit(solution)/shard_map/ppermute | solution.py:387
  31.7 1.5 %self_backward_1.1 = (bf16[128,4096]{1,0:T(8,128)(2,1)}, f32[64,1024]{1,0:T(8,128)S(1)}, f32[64,1024]{1,0:T(8,128)S(1)}) custom-call(bf16[128,4096]{1,0:T(8,128)(2,1)S(1)} %bitcast.16, bf16[128,1024]{1,0:T(8,128)(2,1)S(1)} %bitcast.20, bf16[80,1024]{1,0:T(8,128)(2,1)S(1)} %slice_bitcast_fusion.halo_ref, ...), custom_call_target="tpu_custom_call", output_to_operand_aliasing={{0}: (5, {})} | custom-call | flops 1000000 | bytes 100000 | tf_op jit(solution)/shard_map/self_backward_1/pallas_call | solution.py:473
  33.2 0.0 collective-permute-done.13.other_ref
  33.2 0.0 collective-permute-done.12.chip_ref
  33.2 0.6 %collective-permute-done.14.refs_0_ = f32[16,128]{1,0:T(8,128)S(1)} collective-permute-done((f32[16,128]{1,0:T(8,128)S(1)}, f32[16,128]{1,0:T(8,128)S(1)}, u32[]{:S(2)}, u32[]{:S(2)}) %collective-permute-start.14) | collective-permute-done | bytes 8224 | tf_op jit(solution)/shard_map/ppermute | solution.py:387
  33.8 0.9 %finish.1 = (bf16[64,1024]{1,0:T(8,128)(2,1)}, bf16[128,1024]{1,0:T(8,128)(2,1)}, f32[1,32]{1,0:T(1,128)}) custom-call(f32[8,128]{1,0:T(8,128)S(1)} %get-tuple-element.35.owner_ref, f32[64,1024]{1,0:T(8,128)S(1)} %get-tuple-element.53.own_ref, f32[64,1024]{1,0:T(8,128)S(1)} %get-tuple-element.51.refs_1_.mine_ref, ...), custom_call_target="tpu_custom_call" | custom-call | flops 1000 | bytes 1000 | tf_op jit(solution)/shard_map/finish/pallas_call | solution.py:516
  (13 shorter events, 0.1 us)
Async XLA Ops:
  0.6 2.2 %copy-start.2 = (bf16[1,128,1024]{2,1,0:T(8,128)(2,1)S(1)}, bf16[1,128,1024]{2,1,0:T(8,128)(2,1)}, u32[]{:S(2)}) copy-start(bf16[1,128,1024]{2,1,0:T(8,128)(2,1)} %param.8) | copy-start | bytes 786436
  2.3 3.2 %collective-permute-start = (bf16[64,1408]{1,0:T(8,128)(2,1)S(1)}, bf16[64,1408]{1,0:T(8,128)(2,1)S(1)}, u32[]{:S(2)}, u32[]{:S(2)}) collective-permute-start(bf16[64,1408]{1,0:T(8,128)(2,1)S(1)} %concatenate.3.mine_ref.own_ref), channel_id=1, source_target_pairs={{0,2},{2,0},{4,6},{6,4},{8,10},{10,8},{12,14},{14,12},{16,18},{18,... | collective-permute-start | bytes 540680 | tf_op jit(solution)/shard_map/ppermute | solution.py:383
  2.8 8.6 %collective-permute-start.2 = (bf16[80,1024]{1,0:T(8,128)(2,1)S(1)}, bf16[80,1024]{1,0:T(8,128)(2,1)S(1)}, u32[]{:S(2)}, u32[]{:S(2)}) collective-permute-start(bf16[80,1024]{1,0:T(8,128)(2,1)S(1)} %slice_bitcast_fusion.halo_ref), channel_id=1, source_target_pairs={{0,1},{1,0},{2,4},{3,5},{4,2},{5,3},{6,8},{7,9},{8,6},{9,7},{10,12... | collective-permute-start | bytes 491528 | tf_op jit(solution)/shard_map/ppermute | solution.py:387
  5.4 6.0 %collective-permute-start.1 = (bf16[80,1024]{1,0:T(8,128)(2,1)S(1)}, bf16[80,1024]{1,0:T(8,128)(2,1)S(1)}, u32[]{:S(2)}, u32[]{:S(2)}) collective-permute-start(bf16[80,1024]{1,0:T(8,128)(2,1)S(1)} %slice_bitcast_fusion.halo_ref), channel_id=1, source_target_pairs={{0,2},{2,0},{4,6},{6,4},{8,10},{10,8},{12,14},{14,12},{16,18},{18,... | collective-permute-start | bytes 491528 | tf_op jit(solution)/shard_map/ppermute | solution.py:383
  5.6 9.8 %collective-permute-start.3 = (bf16[64,1152]{1,0:T(8,128)(2,1)S(1)}, bf16[64,1152]{1,0:T(8,128)(2,1)S(1)}, u32[]{:S(2)}, u32[]{:S(2)}) collective-permute-start(bf16[64,1152]{1,0:T(8,128)(2,1)S(1)} %get-tuple-element.37), channel_id=1, source_target_pairs={{0,8},{2,14},{4,12},{6,10},{8,16},{10,22},{12,20},{14,18},{16,24},... | collective-permute-start | bytes 442376 | tf_op jit(solution)/shard_map/ppermute | solution.py:383
  7.2 4.7 %collective-permute-start.4 = (bf16[64,512]{1,0:T(8,128)(2,1)S(1)}, bf16[64,512]{1,0:T(8,128)(2,1)S(1)}, u32[]{:S(2)}, u32[]{:S(2)}) collective-permute-start(bf16[64,512]{1,0:T(8,128)(2,1)S(1)} %get-tuple-element.38), channel_id=1, source_target_pairs={{0,4},{2,6},{4,0},{6,2},{8,12},{10,14},{12,8},{14,10},{16,20},{18,... | collective-permute-start | bytes 196616 | tf_op jit(solution)/shard_map/ppermute | solution.py:383
  8.8 0.7 %copy-start.4 = (s32[1,128]{1,0:T(1,128)S(1)}, s32[1,128]{1,0:T(1,128)}, u32[]{:S(2)}) copy-start(s32[1,128]{1,0:T(1,128)} %segment_ref.3) | copy-start | bytes 1540
  9.4 1.2 %copy-start = (bf16[1,128,4096]{2,1,0:T(8,128)(2,1)S(1)}, bf16[1,128,4096]{2,1,0:T(8,128)(2,1)}, u32[]{:S(2)}) copy-start(bf16[1,128,4096]{2,1,0:T(8,128)(2,1)} %param.7) | copy-start | bytes 3145732
  11.4 4.1 %copy-start.1 = (bf16[1,128,4096]{2,1,0:T(8,128)(2,1)S(1)}, bf16[1,128,4096]{2,1,0:T(8,128)(2,1)}, u32[]{:S(2)}) copy-start(bf16[1,128,4096]{2,1,0:T(8,128)(2,1)} %param.7) | copy-start | bytes 3145732
  11.5 4.0 %copy-start.5 = (f32[32]{0:T(128)S(1)}, f32[32]{0:T(128)}, u32[]{:S(2)}) copy-start(f32[32]{0:T(128)} %param.12) | copy-start | bytes 388
  15.4 1.6 %copy-start.3 = (bf16[1,128,4096]{2,1,0:T(8,128)(2,1)S(1)}, bf16[1,128,4096]{2,1,0:T(8,128)(2,1)}, u32[]{:S(2)}) copy-start(bf16[1,128,4096]{2,1,0:T(8,128)(2,1)} %param.13) | copy-start | bytes 3145732
  15.4 1.5 %collective-permute-start.5 = (bf16[64,1664]{1,0:T(8,128)(2,1)S(1)}, bf16[64,1664]{1,0:T(8,128)(2,1)S(1)}, u32[]{:S(2)}, u32[]{:S(2)}) collective-permute-start(bf16[64,1664]{1,0:T(8,128)(2,1)S(1)} %arrived.1._.mine_ref), channel_id=1, source_target_pairs={{0,2},{2,0},{4,6},{6,4},{8,10},{10,8},{12,14},{14,12},{16,18},{18,... | collective-permute-start | bytes 638984 | tf_op jit(solution)/shard_map/ppermute | solution.py:383
  19.2 1.6 %collective-permute-start.6 = (f32[64,1152]{1,0:T(8,128)S(1)}, f32[64,1152]{1,0:T(8,128)S(1)}, u32[]{:S(2)}, u32[]{:S(2)}) collective-permute-start(f32[64,1152]{1,0:T(8,128)S(1)} %get-tuple-element.42._.mine_ref), channel_id=1, source_target_pairs={{0,2},{2,0},{4,6},{6,4},{8,10},{10,8},{12,14},{14,12},{16,18},{18,... | collective-permute-start | bytes 884744 | tf_op jit(solution)/shard_map/ppermute | solution.py:383
  19.4 8.0 %collective-permute-start.7 = (bf16[64,1152]{1,0:T(8,128)(2,1)S(1)}, bf16[64,1152]{1,0:T(8,128)(2,1)S(1)}, u32[]{:S(2)}, u32[]{:S(2)}) collective-permute-start(bf16[64,1152]{1,0:T(8,128)(2,1)S(1)} %get-tuple-element.48), channel_id=1, source_target_pairs={{0,4},{2,6},{4,0},{6,2},{8,12},{10,14},{12,8},{14,10},{16,20},{18,... | collective-permute-start | bytes 442376 | tf_op jit(solution)/shard_map/ppermute | solution.py:383
  20.9 7.8 %collective-permute-start.8 = (bf16[64,1152]{1,0:T(8,128)(2,1)S(1)}, bf16[64,1152]{1,0:T(8,128)(2,1)S(1)}, u32[]{:S(2)}, u32[]{:S(2)}) collective-permute-start(bf16[64,1152]{1,0:T(8,128)(2,1)S(1)} %get-tuple-element.45.refs_0_), channel_id=1, source_target_pairs={{0,24},{2,30},{4,28},{6,26},{8,0},{10,6},{12,4},{14,2},{16,8},{18,... | collective-permute-start | bytes 442376 | tf_op jit(solution)/shard_map/ppermute | solution.py:383
  23.2 4.6 %collective-permute-start.10 = (f32[16,128]{1,0:T(8,128)S(1)}, f32[16,128]{1,0:T(8,128)S(1)}, u32[]{:S(2)}, u32[]{:S(2)}) collective-permute-start(f32[16,128]{1,0:T(8,128)S(1)} %get-tuple-element.49.gate_ref), channel_id=1, source_target_pairs={{0,16},{2,22},{4,20},{6,18},{8,24},{10,30},{12,28},{14,26},{16,0},... | collective-permute-start | bytes 24584 | tf_op jit(solution)/shard_map/ppermute | solution.py:383
  23.2 5.4 %collective-permute-start.9 = (f32[16,128]{1,0:T(8,128)S(1)}, f32[16,128]{1,0:T(8,128)S(1)}, u32[]{:S(2)}, u32[]{:S(2)}) collective-permute-start(f32[16,128]{1,0:T(8,128)S(1)} %get-tuple-element.49.gate_ref), channel_id=1, source_target_pairs={{0,8},{2,14},{4,12},{6,10},{8,16},{10,22},{12,20},{14,18},{16,24},... | collective-permute-start | bytes 24584 | tf_op jit(solution)/shard_map/ppermute | solution.py:383
  25.8 7.4 %collective-permute-start.13 = (bf16[80,1024]{1,0:T(8,128)(2,1)S(1)}, bf16[80,1024]{1,0:T(8,128)(2,1)S(1)}, u32[]{:S(2)}, u32[]{:S(2)}) collective-permute-start(bf16[80,1024]{1,0:T(8,128)(2,1)S(1)} %get-tuple-element.57), channel_id=1, source_target_pairs={{0,1},{1,0},{2,4},{3,5},{4,2},{5,3},{6,8},{7,9},{8,6},{9,7},{10,12... | collective-permute-start | bytes 491528 | tf_op jit(solution)/shard_map/ppermute | solution.py:387
  27.4 5.8 %collective-permute-start.12 = (bf16[80,1024]{1,0:T(8,128)(2,1)S(1)}, bf16[80,1024]{1,0:T(8,128)(2,1)S(1)}, u32[]{:S(2)}, u32[]{:S(2)}) collective-permute-start(bf16[80,1024]{1,0:T(8,128)(2,1)S(1)} %get-tuple-element.57), channel_id=1, source_target_pairs={{0,2},{2,0},{4,6},{6,4},{8,10},{10,8},{12,14},{14,12},{16,18},{18,... | collective-permute-start | bytes 491528 | tf_op jit(solution)/shard_map/ppermute | solution.py:383
  28.7 1.4 %collective-permute-start.11 = (bf16[64,1152]{1,0:T(8,128)(2,1)S(1)}, bf16[64,1152]{1,0:T(8,128)(2,1)S(1)}, u32[]{:S(2)}, u32[]{:S(2)}) collective-permute-start(bf16[64,1152]{1,0:T(8,128)(2,1)S(1)} %get-tuple-element.54), channel_id=1, source_target_pairs={{0,2},{2,0},{4,6},{6,4},{8,10},{10,8},{12,14},{14,12},{16,18},{18,... | collective-permute-start | bytes 442376 | tf_op jit(solution)/shard_map/ppermute | solution.py:383
  30.2 3.7 %collective-permute-start.14 = (f32[16,128]{1,0:T(8,128)S(1)}, f32[16,128]{1,0:T(8,128)S(1)}, u32[]{:S(2)}, u32[]{:S(2)}) collective-permute-start(f32[16,128]{1,0:T(8,128)S(1)} %gate_sum.1.gate_ref), channel_id=1, source_target_pairs={{0,1},{1,0},{2,3},{3,2},{4,5},{5,4},{6,7},{7,6},{8,9},{9,8},{10,11... | collective-permute-start | bytes 24584 | tf_op jit(solution)/shard_map/ppermute | solution.py:387

commit v9 on v8

--- a/solution.py
+++ b/solution.py
@@ -146,8 +146,29 @@
     return parts[:rows] + (parts[rows : 2 * rows] + parts[2 * rows : 3 * rows])
 
 
+def scale_kernel(off_ref, owner_ref, gate_ref, grad_ref, _, out_ref, *, groups, repeat):
+    tok_rows = grad_ref.shape[0]
+    half = repeat * WINDOW
+    shard = lax.axis_index("seq")
+    is_owner, pair_owner = owner(owner_ref, 0), owner(owner_ref, 1)
+    from_chip = flag(shard % 2 == 1) * pair_owner
+    from_x = flag(shard % GAP >= 2) * (1 - (is_owner | pair_owner))
+    has_prev = from_chip | from_x | flag(shard >= GAP)
+    has_from = jnp.minimum(off_ref[0:1, 0:1], tok_rows) * (1 - has_prev)
+    row_tok = lax.broadcasted_iota(jnp.int32, (WINDOW, HEAD_DIM), 0)
+    for g in range(groups):
+        for block in range(tok_rows // WINDOW):
+            has_rows = row_tok + block * WINDOW >= has_from
+            rows = stack(grad_ref, block * WINDOW, WINDOW, g, repeat).astype(jnp.float32)
+            factors = [
+                jnp.where(has_rows, gate_ref[g * repeat + h : g * repeat + h + 1, :], 0.0) for h in range(repeat)
+            ]
+            rows = rows * jnp.concatenate(factors, axis=0)
+            out_ref[g, block * half : (block + 1) * half, :] = rows.astype(out_ref.dtype)
+
+
 def cross_kernel(
-    off_ref, owner_ref, gate_ref, self_0_ref, self_1_ref, grad_ref, own_ref, chip_ref, mine_ref, pair_ref,
+    off_ref, owner_ref, cross_rows_ref, self_0_ref, self_1_ref, grad_ref, own_ref, chip_ref, mine_ref, pair_ref,
     scores_ref, to_pair_ref, to_x_ref, in_chip_ref, own_terms_ref, mask_ref, prev, *, groups, repeat, step=2
 ):
     tok_rows, width = grad_ref.shape[0], chip_ref.shape[1]
@@ -179,7 +200,6 @@
     from_chip, from_x, from_z = (here.astype(jnp.float32) for here in (from_chip, from_x, from_z))
     use_own = lane_tok >= own_from
     has_lane = lane_tok >= has_from
-    row_tok = lax.broadcasted_iota(jnp.int32, (WINDOW, HEAD_DIM), 0)
 
     def pick(joint):
         return jnp.where(use_own, joint[img:], joint[:img])
@@ -201,16 +221,7 @@
         for g in every:
             tiles = [stack(grad_ref, block * WINDOW, WINDOW, g, repeat) for block in blocks]
             plain[g] = dot(values[g], jnp.concatenate(tiles, axis=0), NT)
-            scaled = []
-            for block in blocks:
-                has_rows = row_tok + block * WINDOW >= has_from
-                factors = [
-                    jnp.where(has_rows, gate_ref[g * repeat + h : g * repeat + h + 1, :], 0.0) for h in range(repeat)
-                ]
-                scaled.append(
-                    (tiles[block].astype(jnp.float32) * jnp.concatenate(factors, axis=0)).astype(jnp.bfloat16)
-                )
-            cross_rows[g] = jnp.concatenate(scaled, axis=0)
+            cross_rows[g] = cross_rows_ref[g]
             grad_weights[g] = dot(values[g], cross_rows[g], NT)
         weights = {g: softmax_rows(pick(scores[g]) * SCALE) for g in every}
         score_terms = {}
@@ -438,8 +449,14 @@
 
     self_forward(1, chip)
     halo = merge("halo", halos, 1, self_out[1])
+    cross_rows = call(
+        "cross_rows",
+        functools.partial(scale_kernel, groups=groups, repeat=repeat),
+        [struct((groups, repeat * tok_rows, HEAD_DIM), bf16)],
+        [VMEM] * 4 + [ANY],
+    )(off, owners, gate_rows, grad, self_out[1])[0]
     arrived = call("arrived", join_kernel, [struct((img, width + LANES + width // 2), bf16)], [VMEM] * 2 + [ANY] * 2)(
-        by_z, by_x, self_out[1], halo
+        by_z, by_x, cross_rows, halo
     )[0]
 
     by_pair = send(arrived, lambda i: i ^ 1)
@@ -459,7 +476,7 @@
             image,
         ],
         [VMEM] * 10,
-    )(off, owners, gate_rows, *self_out, grad, own, chip, arrived, by_pair)
+    )(off, owners, cross_rows, *self_out, grad, own, chip, arrived, by_pair)
     from_pair = send(to_pair, lambda i: i ^ 1)
     from_x = send(to_x, lambda i: i ^ 2)
     grad_self = call(

time: 34.9 us -> 34.6 us (level)
  waiting for transfers between devices: 8.56 us -> 7.47 us
  Pallas kernels: 8.34 us -> 8.77 us
  local copies, waits for them, and re-layouts: 2.91 us -> 3.26 us
    ppermute x12, waiting for transfers between devices: 7.96 us -> 6.96 us  [send(): return lax.ppermute(value, 'seq', [(i, where(i)) for i in range(seq)])]
    pallas_call x0 -> x1, Pallas kernels: none -> 0.41 us  [on_device(): call('cross_rows', functools.partial(scale_kernel, groups=groups, repeat=...]
  transfers between devices with their start and end apart: 15 -> 15, of which waited for: 8 -> 7; matrix products, arithmetic and copies ran while one was open for 0% -> 0% of each run, Pallas kernels for 15% -> 17%
where the time goes in v9:
time: 34.6 us; the launch traced here: 34.4 us
  starting transfers between devices  13.4 us (39%)
  Pallas kernels  8.77 us (25%)
  waiting for transfers between devices  7.47 us (22%)
  local copies, waits for them, and re-layouts  3.26 us (9%)
  between operations  1.51 us (4%)
    ppermute x12, starting transfers between devices, send(): return lax.ppermute(value, 'seq', [(i, where(i)) for i in range(seq)])  7.69 us
    ppermute x12, waiting for transfers between devices, send(): return lax.ppermute(value, 'seq', [(i, where(i)) for i in range(seq)])  6.96 us
    ppermute x3, starting transfers between devices, send_all(): lax.ppermute(value, ('seq', 'dp'), [(s * dp + d, t * dp + e) for s, d, t,...  5.71 us
    pallas_call x2, Pallas kernels, self_backward(): call(f'self_backward_{block}', functools.partial(self_back_kernel, block=...  3.09 us
    unnamed x12, local copies, waits for them, and re-layouts  2.25 us
    pallas_call x1, Pallas kernels, on_device(): call('cross', functools.partial(cross_kernel, groups=groups, repeat=repea...  1.92 us
    pallas_call x2, Pallas kernels, self_forward(): call(f'self_forward_{block}', functools.partial(self_kernel, block=block,...  1.57 us
    concatenate x1, local copies, waits for them, and re-layouts, on_device(): jnp.concatenate([own, jnp.broadcast_to(is_owner, (img, MARKS))], axis=1)  0.92 us
  transfers between devices with their start and end apart: 15, of which 7 were waited for; matrix products, arithmetic and copies ran while one was open for 0% of the time, Pallas kernels for 17%

profile of v9, /device:TPU:0, one launch (start us, length us, event | category | flops | bytes accessed | tf_op | source)
XLA Modules:
  0.0 34.4 jit_solution(10216199866400134871)
XLA Ops:
  1.3 0.9 %concatenate.3.mine_ref.own_ref = bf16[64,1408]{1,0:T(8,128)(2,1)S(1)} pad(bf16[64,1024]{1,0:T(8,128)(2,1)} %bitcast.25, bf16[]{:T(256)} %bitcast.4), padding=0_0x0_384 | pad | bytes 311298 | tf_op jit(solution)/shard_map/concatenate | solution.py:425
  2.3 0.5 %collective-permute-start = (bf16[64,1408]{1,0:T(8,128)(2,1)S(1)}, bf16[64,1408]{1,0:T(8,128)(2,1)S(1)}, u32[]{:S(2)}, u32[]{:S(2)}) collective-permute-start(bf16[64,1408]{1,0:T(8,128)(2,1)S(1)} %concatenate.3.mine_ref.own_ref), channel_id=1, source_target_pairs={{0,2},{2,0},{4,6},{6,4},{8,10},{10,8},{12,14},{14,12},{16,18},{18,... | collective-permute-start | bytes 540680 | tf_op jit(solution)/shard_map/ppermute | solution.py:394
  2.8 2.6 %collective-permute-start.2 = (bf16[80,1024]{1,0:T(8,128)(2,1)S(1)}, bf16[80,1024]{1,0:T(8,128)(2,1)S(1)}, u32[]{:S(2)}, u32[]{:S(2)}) collective-permute-start(bf16[80,1024]{1,0:T(8,128)(2,1)S(1)} %slice_bitcast_fusion.halo_ref), channel_id=1, source_target_pairs={{0,1},{1,0},{2,4},{3,5},{4,2},{5,3},{6,8},{7,9},{8,6},{9,7},{10,12... | collective-permute-start | bytes 491528 | tf_op jit(solution)/shard_map/ppermute | solution.py:398
  5.4 0.1 collective-permute-start.1
  5.5 0.0 collective-permute-done.other_ref
  5.5 0.1 chip_image.1
  5.6 0.0 copy-start.5
  5.6 1.6 %collective-permute-start.3 = (bf16[64,1152]{1,0:T(8,128)(2,1)S(1)}, bf16[64,1152]{1,0:T(8,128)(2,1)S(1)}, u32[]{:S(2)}, u32[]{:S(2)}) collective-permute-start(bf16[64,1152]{1,0:T(8,128)(2,1)S(1)} %get-tuple-element.37), channel_id=1, source_target_pairs={{0,8},{2,14},{4,12},{6,10},{8,16},{10,22},{12,20},{14,18},{16,24},... | collective-permute-start | bytes 442376 | tf_op jit(solution)/shard_map/ppermute | solution.py:394
  7.2 1.5 %collective-permute-start.4 = (bf16[64,512]{1,0:T(8,128)(2,1)S(1)}, bf16[64,512]{1,0:T(8,128)(2,1)S(1)}, u32[]{:S(2)}, u32[]{:S(2)}) collective-permute-start(bf16[64,512]{1,0:T(8,128)(2,1)S(1)} %get-tuple-element.38), channel_id=1, source_target_pairs={{0,4},{2,6},{4,0},{6,2},{8,12},{10,14},{12,8},{14,10},{16,20},{18,... | collective-permute-start | bytes 196616 | tf_op jit(solution)/shard_map/ppermute | solution.py:394
  8.8 0.7 %copy-done.4 = s32[1,128]{1,0:T(1,128)S(1)} copy-done((s32[1,128]{1,0:T(1,128)S(1)}, s32[1,128]{1,0:T(1,128)}, u32[]{:S(2)}) %copy-start.4) | copy-done | bytes 536
  9.4 1.2 %copy-done = bf16[1,128,4096]{2,1,0:T(8,128)(2,1)S(1)} copy-done((bf16[1,128,4096]{2,1,0:T(8,128)(2,1)S(1)}, bf16[1,128,4096]{2,1,0:T(8,128)(2,1)}, u32[]{:S(2)}) %copy-start) | copy-done | bytes 1048600
  10.7 0.8 %self_forward_1.1 = (bf16[4,128,512]{2,1,0:T(8,128)(2,1)S(1)}, f32[4,128,512]{2,1,0:T(8,128)S(1)}) custom-call(bf16[128,4096]{1,0:T(8,128)(2,1)S(1)} %bitcast.13, bf16[128,1024]{1,0:T(8,128)(2,1)S(1)} %bitcast.20, bf16[80,1024]{1,0:T(8,128)(2,1)S(1)} %slice_bitcast_fusion.halo_ref, s32[1,128]{1,0:T(1,128)S(1)} %copy-done.4, ...), custom_call_target="tpu_custom_call" | custom-call | flops 1000000 | bytes 100000 | tf_op jit(solution)/shard_map/self_forward_1/pallas_call | solution.py:441
  11.5 0.1 broadcast_in_dim.34.gate_ref.refs_1_
  11.5 0.3 %copy-done.2 = bf16[1,128,4096]{2,1,0:T(8,128)(2,1)S(1)} copy-done((bf16[1,128,4096]{2,1,0:T(8,128)(2,1)S(1)}, bf16[1,128,4096]{2,1,0:T(8,128)(2,1)}, u32[]{:S(2)}) %copy-start.2) | copy-done | bytes 1048600
  11.9 0.4 %cross_rows.1._.cross_rows_ref = bf16[4,1024,128]{2,1,0:T(8,128)(2,1)S(1)} custom-call(s32[8,128]{1,0:T(8,128)S(1)} %broadcast_in_dim.33.off_ref, f32[8,128]{1,0:T(8,128)S(1)} %get-tuple-element.35.owner_ref, f32[32,128]{1,0:T(8,128)S(1)} %broadcast_in_dim.34.gate_ref.refs_1_, bf16[128,4096]{1,0:T(8,128)(2,1)S(1)} %bitcast.17, ...), custom_call_target="tpu_custom_call" | custom-call | flops 1000 | bytes 1000 | tf_op jit(solution)/shard_map/cross_rows/pallas_call | solution.py:452
  12.3 0.0 copy-start.1
  12.3 0.0 collective-permute-done.2.other_ref
  12.3 0.0 collective-permute-done.1.chip_ref
  12.4 0.0 collective-permute-done.4.x_ref
  12.4 3.0 %collective-permute-done.3.z_ref = bf16[64,1152]{1,0:T(8,128)(2,1)S(1)} collective-permute-done((bf16[64,1152]{1,0:T(8,128)(2,1)S(1)}, bf16[64,1152]{1,0:T(8,128)(2,1)S(1)}, u32[]{:S(2)}, u32[]{:S(2)}) %collective-permute-start.3) | collective-permute-done | bytes 147488 | tf_op jit(solution)/shard_map/ppermute | solution.py:394
  15.4 0.1 collective-permute-start.5
  15.5 0.8 %self_forward_0.1 = (bf16[4,128,512]{2,1,0:T(8,128)(2,1)S(1)}, f32[4,128,512]{2,1,0:T(8,128)S(1)}) custom-call(bf16[128,4096]{1,0:T(8,128)(2,1)S(1)} %bitcast.14, bf16[128,1024]{1,0:T(8,128)(2,1)S(1)} %bitcast.21, bf16[64,1024]{1,0:T(8,128)(2,1)S(1)} %halo.1.__.halo_ref, s32[1,128]{1,0:T(1,128)S(1)} %copy-done.4, bf16[64,1664]{1,0:T(8,128)(2,1)S(1)} %arrived.1._.mine_ref), custom_call_target="tpu_custom_call" | custom-call | flops 1000000 | bytes 100000 | tf_op jit(solution)/shard_map/self_forward_0/pallas_call | solution.py:441
  16.3 0.6 %collective-permute-done.5.pair_ref = bf16[64,1664]{1,0:T(8,128)(2,1)S(1)} collective-permute-done((bf16[64,1664]{1,0:T(8,128)(2,1)S(1)}, bf16[64,1664]{1,0:T(8,128)(2,1)S(1)}, u32[]{:S(2)}, u32[]{:S(2)}) %collective-permute-start.5) | collective-permute-done | bytes 213024 | tf_op jit(solution)/shard_map/ppermute | solution.py:394
  16.9 1.9 %cross.1 = (bf16[4,128,1024]{2,1,0:T(8,128)(2,1)S(1)}, f32[64,1152]{1,0:T(8,128)S(1)}, bf16[64,1152]{1,0:T(8,128)(2,1)S(1)}, f32[64,1024]{1,0:T(8,128)S(1)}, f32...) custom-call(s32[8,128]{1,0:T(8,128)S(1)} %broadcast_in_dim.33.off_ref, ...), custom_call_target="tpu_custom_call" | custom-call | flops 1000 | bytes 1000 | tf_op jit(solution)/shard_map/cross/pallas_call | solution.py:466
  18.9 0.2 collective-permute-start.6
  19.1 0.0 collective-permute-start.7
  19.1 0.5 %cross_query.1._.grad_ref = bf16[4,1024,128]{2,1,0:T(8,128)(2,1)S(1)} custom-call(bf16[4,128,1024]{2,1,0:T(8,128)(2,1)S(1)} %get-tuple-element.40.scores_ref, bf16[128,4096]{1,0:T(8,128)(2,1)S(1)} %bitcast.19, bf16[64,1408]{1,0:T(8,128)(2,1)S(1)} %concatenate.3.mine_ref.own_ref, bf16[64,1024]{1,0:T(8,128)(2,1)S(1)} %get-tuple-element.41.prev, ...), custom_call_target="tpu_custom_call" | custom-call | flops 1000 | bytes 1000 | tf_op jit(solution)/shard_map/cross_query/pallas_call | solution.py:482
  19.6 0.9 %collective-permute-done.6.pair_ref = f32[64,1152]{1,0:T(8,128)S(1)} collective-permute-done((f32[64,1152]{1,0:T(8,128)S(1)}, f32[64,1152]{1,0:T(8,128)S(1)}, u32[]{:S(2)}, u32[]{:S(2)}) %collective-permute-start.6) | collective-permute-done | bytes 294944 | tf_op jit(solution)/shard_map/ppermute | solution.py:394
  20.5 0.1 outside.1
  20.6 2.3 %collective-permute-start.8 = (bf16[64,1152]{1,0:T(8,128)(2,1)S(1)}, bf16[64,1152]{1,0:T(8,128)(2,1)S(1)}, u32[]{:S(2)}, u32[]{:S(2)}) collective-permute-start(bf16[64,1152]{1,0:T(8,128)(2,1)S(1)} %get-tuple-element.45.refs_0_), channel_id=1, source_target_pairs={{0,24},{2,30},{4,28},{6,26},{8,0},{10,6},{12,4},{14,2},{16,8},{18,... | collective-permute-start | bytes 442376 | tf_op jit(solution)/shard_map/ppermute | solution.py:394
  22.9 0.0 collective-permute-start.10
  22.9 1.2 %collective-permute-start.9 = (f32[16,128]{1,0:T(8,128)S(1)}, f32[16,128]{1,0:T(8,128)S(1)}, u32[]{:S(2)}, u32[]{:S(2)}) collective-permute-start(f32[16,128]{1,0:T(8,128)S(1)} %get-tuple-element.49.gate_ref), channel_id=1, source_target_pairs={{0,8},{2,14},{4,12},{6,10},{8,16},{10,22},{12,20},{14,18},{16,24},... | collective-permute-start | bytes 24584 | tf_op jit(solution)/shard_map/ppermute | solution.py:394
  24.1 1.5 %self_backward_0.1 = (bf16[128,4096]{1,0:T(8,128)(2,1)}, bf16[80,1024]{1,0:T(8,128)(2,1)S(1)}, f32[64,1024]{1,0:T(8,128)S(1)}) custom-call(bf16[128,4096]{1,0:T(8,128)(2,1)S(1)} %bitcast.15, bf16[128,1024]{1,0:T(8,128)(2,1)S(1)} %bitcast.22, bf16[64,1024]{1,0:T(8,128)(2,1)S(1)} %halo.1.__.halo_ref, f32[4,128,512]{2,1,0:T(8,128)S(1)} %get-tuple-element.43.weights_ref, ...), custom_call_target="tpu_custom_call" | custom-call | flops 1000000 | bytes 100000 | tf_op jit(solution)/shard_map/self_backward_0/pallas_call | solution.py:490
  25.6 1.6 %collective-permute-start.13 = (bf16[80,1024]{1,0:T(8,128)(2,1)S(1)}, bf16[80,1024]{1,0:T(8,128)(2,1)S(1)}, u32[]{:S(2)}, u32[]{:S(2)}) collective-permute-start(bf16[80,1024]{1,0:T(8,128)(2,1)S(1)} %get-tuple-element.57), channel_id=1, source_target_pairs={{0,1},{1,0},{2,4},{3,5},{4,2},{5,3},{6,8},{7,9},{8,6},{9,7},{10,12... | collective-permute-start | bytes 491528 | tf_op jit(solution)/shard_map/ppermute | solution.py:398
  27.2 0.0 collective-permute-done.7.x_ref
  27.2 0.0 collective-permute-start.12
  27.2 0.3 collective-permute-done.10.refs_1_
  27.5 0.8 %collective-permute-done.9.refs_0_ = f32[16,128]{1,0:T(8,128)S(1)} collective-permute-done((f32[16,128]{1,0:T(8,128)S(1)}, f32[16,128]{1,0:T(8,128)S(1)}, u32[]{:S(2)}, u32[]{:S(2)}) %collective-permute-start.9) | collective-permute-done | bytes 8224 | tf_op jit(solution)/shard_map/ppermute | solution.py:394
  28.4 0.0 collective-permute-done.8.z_ref
  28.4 0.1 chip_sum.1
  28.4 0.2 collective-permute-start.11
  28.6 1.3 %collective-permute-done.11.pair_ref = bf16[64,1152]{1,0:T(8,128)(2,1)S(1)} collective-permute-done((bf16[64,1152]{1,0:T(8,128)(2,1)S(1)}, bf16[64,1152]{1,0:T(8,128)(2,1)S(1)}, u32[]{:S(2)}, u32[]{:S(2)}) %collective-permute-start.11) | collective-permute-done | bytes 147488 | tf_op jit(solution)/shard_map/ppermute | solution.py:394
  29.9 1.5 %collective-permute-start.14 = (f32[16,128]{1,0:T(8,128)S(1)}, f32[16,128]{1,0:T(8,128)S(1)}, u32[]{:S(2)}, u32[]{:S(2)}) collective-permute-start(f32[16,128]{1,0:T(8,128)S(1)} %gate_sum.1.gate_ref), channel_id=1, source_target_pairs={{0,1},{1,0},{2,3},{3,2},{4,5},{5,4},{6,7},{7,6},{8,9},{9,8},{10,11... | collective-permute-start | bytes 24584 | tf_op jit(solution)/shard_map/ppermute | solution.py:398
  31.4 1.5 %self_backward_1.1 = (bf16[128,4096]{1,0:T(8,128)(2,1)}, f32[64,1024]{1,0:T(8,128)S(1)}, f32[64,1024]{1,0:T(8,128)S(1)}) custom-call(bf16[128,4096]{1,0:T(8,128)(2,1)S(1)} %bitcast.16, bf16[128,1024]{1,0:T(8,128)(2,1)S(1)} %bitcast.23, bf16[80,1024]{1,0:T(8,128)(2,1)S(1)} %slice_bitcast_fusion.halo_ref, ...), custom_call_target="tpu_custom_call", output_to_operand_aliasing={{0}: (5, {})} | custom-call | flops 1000000 | bytes 100000 | tf_op jit(solution)/shard_map/self_backward_1/pallas_call | solution.py:490
  33.0 0.0 collective-permute-done.13.other_ref
  33.0 0.0 collective-permute-done.12.chip_ref
  33.0 0.5 %collective-permute-done.14.refs_0_ = f32[16,128]{1,0:T(8,128)S(1)} collective-permute-done((f32[16,128]{1,0:T(8,128)S(1)}, f32[16,128]{1,0:T(8,128)S(1)}, u32[]{:S(2)}, u32[]{:S(2)}) %collective-permute-start.14) | collective-permute-done | bytes 8224 | tf_op jit(solution)/shard_map/ppermute | solution.py:398
  33.5 0.9 %finish.1 = (bf16[64,1024]{1,0:T(8,128)(2,1)}, bf16[128,1024]{1,0:T(8,128)(2,1)}, f32[1,32]{1,0:T(1,128)}) custom-call(f32[8,128]{1,0:T(8,128)S(1)} %get-tuple-element.35.owner_ref, f32[64,1024]{1,0:T(8,128)S(1)} %get-tuple-element.53.own_ref, f32[64,1024]{1,0:T(8,128)S(1)} %get-tuple-element.51.refs_1_.mine_ref, ...), custom_call_target="tpu_custom_call" | custom-call | flops 1000 | bytes 1000 | tf_op jit(solution)/shard_map/finish/pallas_call | solution.py:533
  (14 shorter events, 0.1 us)
Async XLA Ops:
  0.6 2.2 %copy-start.3 = (bf16[1,128,1024]{2,1,0:T(8,128)(2,1)S(1)}, bf16[1,128,1024]{2,1,0:T(8,128)(2,1)}, u32[]{:S(2)}) copy-start(bf16[1,128,1024]{2,1,0:T(8,128)(2,1)} %param.8) | copy-start | bytes 786436
  2.3 3.2 %collective-permute-start = (bf16[64,1408]{1,0:T(8,128)(2,1)S(1)}, bf16[64,1408]{1,0:T(8,128)(2,1)S(1)}, u32[]{:S(2)}, u32[]{:S(2)}) collective-permute-start(bf16[64,1408]{1,0:T(8,128)(2,1)S(1)} %concatenate.3.mine_ref.own_ref), channel_id=1, source_target_pairs={{0,2},{2,0},{4,6},{6,4},{8,10},{10,8},{12,14},{14,12},{16,18},{18,... | collective-permute-start | bytes 540680 | tf_op jit(solution)/shard_map/ppermute | solution.py:394
  2.8 9.5 %collective-permute-start.2 = (bf16[80,1024]{1,0:T(8,128)(2,1)S(1)}, bf16[80,1024]{1,0:T(8,128)(2,1)S(1)}, u32[]{:S(2)}, u32[]{:S(2)}) collective-permute-start(bf16[80,1024]{1,0:T(8,128)(2,1)S(1)} %slice_bitcast_fusion.halo_ref), channel_id=1, source_target_pairs={{0,1},{1,0},{2,4},{3,5},{4,2},{5,3},{6,8},{7,9},{8,6},{9,7},{10,12... | collective-permute-start | bytes 491528 | tf_op jit(solution)/shard_map/ppermute | solution.py:398
  5.4 6.9 %collective-permute-start.1 = (bf16[80,1024]{1,0:T(8,128)(2,1)S(1)}, bf16[80,1024]{1,0:T(8,128)(2,1)S(1)}, u32[]{:S(2)}, u32[]{:S(2)}) collective-permute-start(bf16[80,1024]{1,0:T(8,128)(2,1)S(1)} %slice_bitcast_fusion.halo_ref), channel_id=1, source_target_pairs={{0,2},{2,0},{4,6},{6,4},{8,10},{10,8},{12,14},{14,12},{16,18},{18,... | collective-permute-start | bytes 491528 | tf_op jit(solution)/shard_map/ppermute | solution.py:394
  5.6 3.2 %copy-start.5 = (f32[32]{0:T(128)S(1)}, f32[32]{0:T(128)}, u32[]{:S(2)}) copy-start(f32[32]{0:T(128)} %param.12) | copy-start | bytes 388
  5.6 9.8 %collective-permute-start.3 = (bf16[64,1152]{1,0:T(8,128)(2,1)S(1)}, bf16[64,1152]{1,0:T(8,128)(2,1)S(1)}, u32[]{:S(2)}, u32[]{:S(2)}) collective-permute-start(bf16[64,1152]{1,0:T(8,128)(2,1)S(1)} %get-tuple-element.37), channel_id=1, source_target_pairs={{0,8},{2,14},{4,12},{6,10},{8,16},{10,22},{12,20},{14,18},{16,24},... | collective-permute-start | bytes 442376 | tf_op jit(solution)/shard_map/ppermute | solution.py:394
  7.2 5.2 %collective-permute-start.4 = (bf16[64,512]{1,0:T(8,128)(2,1)S(1)}, bf16[64,512]{1,0:T(8,128)(2,1)S(1)}, u32[]{:S(2)}, u32[]{:S(2)}) collective-permute-start(bf16[64,512]{1,0:T(8,128)(2,1)S(1)} %get-tuple-element.38), channel_id=1, source_target_pairs={{0,4},{2,6},{4,0},{6,2},{8,12},{10,14},{12,8},{14,10},{16,20},{18,... | collective-permute-start | bytes 196616 | tf_op jit(solution)/shard_map/ppermute | solution.py:394
  8.8 0.7 %copy-start.4 = (s32[1,128]{1,0:T(1,128)S(1)}, s32[1,128]{1,0:T(1,128)}, u32[]{:S(2)}) copy-start(s32[1,128]{1,0:T(1,128)} %segment_ref.3) | copy-start | bytes 1540
  9.4 1.2 %copy-start = (bf16[1,128,4096]{2,1,0:T(8,128)(2,1)S(1)}, bf16[1,128,4096]{2,1,0:T(8,128)(2,1)}, u32[]{:S(2)}) copy-start(bf16[1,128,4096]{2,1,0:T(8,128)(2,1)} %param.7) | copy-start | bytes 3145732
  10.7 1.2 %copy-start.2 = (bf16[1,128,4096]{2,1,0:T(8,128)(2,1)S(1)}, bf16[1,128,4096]{2,1,0:T(8,128)(2,1)}, u32[]{:S(2)}) copy-start(bf16[1,128,4096]{2,1,0:T(8,128)(2,1)} %param.13) | copy-start | bytes 3145732
  12.3 3.2 %copy-start.1 = (bf16[1,128,4096]{2,1,0:T(8,128)(2,1)S(1)}, bf16[1,128,4096]{2,1,0:T(8,128)(2,1)}, u32[]{:S(2)}) copy-start(bf16[1,128,4096]{2,1,0:T(8,128)(2,1)} %param.7) | copy-start | bytes 3145732
  15.4 1.5 %collective-permute-start.5 = (bf16[64,1664]{1,0:T(8,128)(2,1)S(1)}, bf16[64,1664]{1,0:T(8,128)(2,1)S(1)}, u32[]{:S(2)}, u32[]{:S(2)}) collective-permute-start(bf16[64,1664]{1,0:T(8,128)(2,1)S(1)} %arrived.1._.mine_ref), channel_id=1, source_target_pairs={{0,2},{2,0},{4,6},{6,4},{8,10},{10,8},{12,14},{14,12},{16,18},{18,... | collective-permute-start | bytes 638984 | tf_op jit(solution)/shard_map/ppermute | solution.py:394
  18.9 1.6 %collective-permute-start.6 = (f32[64,1152]{1,0:T(8,128)S(1)}, f32[64,1152]{1,0:T(8,128)S(1)}, u32[]{:S(2)}, u32[]{:S(2)}) collective-permute-start(f32[64,1152]{1,0:T(8,128)S(1)} %get-tuple-element.42._.mine_ref), channel_id=1, source_target_pairs={{0,2},{2,0},{4,6},{6,4},{8,10},{10,8},{12,14},{14,12},{16,18},{18,... | collective-permute-start | bytes 884744 | tf_op jit(solution)/shard_map/ppermute | solution.py:394
  19.1 8.1 %collective-permute-start.7 = (bf16[64,1152]{1,0:T(8,128)(2,1)S(1)}, bf16[64,1152]{1,0:T(8,128)(2,1)S(1)}, u32[]{:S(2)}, u32[]{:S(2)}) collective-permute-start(bf16[64,1152]{1,0:T(8,128)(2,1)S(1)} %get-tuple-element.48), channel_id=1, source_target_pairs={{0,4},{2,6},{4,0},{6,2},{8,12},{10,14},{12,8},{14,10},{16,20},{18,... | collective-permute-start | bytes 442376 | tf_op jit(solution)/shard_map/ppermute | solution.py:394
  20.6 7.7 %collective-permute-start.8 = (bf16[64,1152]{1,0:T(8,128)(2,1)S(1)}, bf16[64,1152]{1,0:T(8,128)(2,1)S(1)}, u32[]{:S(2)}, u32[]{:S(2)}) collective-permute-start(bf16[64,1152]{1,0:T(8,128)(2,1)S(1)} %get-tuple-element.45.refs_0_), channel_id=1, source_target_pairs={{0,24},{2,30},{4,28},{6,26},{8,0},{10,6},{12,4},{14,2},{16,8},{18,... | collective-permute-start | bytes 442376 | tf_op jit(solution)/shard_map/ppermute | solution.py:394
  22.9 4.6 %collective-permute-start.10 = (f32[16,128]{1,0:T(8,128)S(1)}, f32[16,128]{1,0:T(8,128)S(1)}, u32[]{:S(2)}, u32[]{:S(2)}) collective-permute-start(f32[16,128]{1,0:T(8,128)S(1)} %get-tuple-element.49.gate_ref), channel_id=1, source_target_pairs={{0,16},{2,22},{4,20},{6,18},{8,24},{10,30},{12,28},{14,26},{16,0},... | collective-permute-start | bytes 24584 | tf_op jit(solution)/shard_map/ppermute | solution.py:394
  22.9 5.4 %collective-permute-start.9 = (f32[16,128]{1,0:T(8,128)S(1)}, f32[16,128]{1,0:T(8,128)S(1)}, u32[]{:S(2)}, u32[]{:S(2)}) collective-permute-start(f32[16,128]{1,0:T(8,128)S(1)} %get-tuple-element.49.gate_ref), channel_id=1, source_target_pairs={{0,8},{2,14},{4,12},{6,10},{8,16},{10,22},{12,20},{14,18},{16,24},... | collective-permute-start | bytes 24584 | tf_op jit(solution)/shard_map/ppermute | solution.py:394
  25.6 7.3 %collective-permute-start.13 = (bf16[80,1024]{1,0:T(8,128)(2,1)S(1)}, bf16[80,1024]{1,0:T(8,128)(2,1)S(1)}, u32[]{:S(2)}, u32[]{:S(2)}) collective-permute-start(bf16[80,1024]{1,0:T(8,128)(2,1)S(1)} %get-tuple-element.57), channel_id=1, source_target_pairs={{0,1},{1,0},{2,4},{3,5},{4,2},{5,3},{6,8},{7,9},{8,6},{9,7},{10,12... | collective-permute-start | bytes 491528 | tf_op jit(solution)/shard_map/ppermute | solution.py:398
  27.2 5.8 %collective-permute-start.12 = (bf16[80,1024]{1,0:T(8,128)(2,1)S(1)}, bf16[80,1024]{1,0:T(8,128)(2,1)S(1)}, u32[]{:S(2)}, u32[]{:S(2)}) collective-permute-start(bf16[80,1024]{1,0:T(8,128)(2,1)S(1)} %get-tuple-element.57), channel_id=1, source_target_pairs={{0,2},{2,0},{4,6},{6,4},{8,10},{10,8},{12,14},{14,12},{16,18},{18,... | collective-permute-start | bytes 491528 | tf_op jit(solution)/shard_map/ppermute | solution.py:394
  28.4 1.4 %collective-permute-start.11 = (bf16[64,1152]{1,0:T(8,128)(2,1)S(1)}, bf16[64,1152]{1,0:T(8,128)(2,1)S(1)}, u32[]{:S(2)}, u32[]{:S(2)}) collective-permute-start(bf16[64,1152]{1,0:T(8,128)(2,1)S(1)} %get-tuple-element.54), channel_id=1, source_target_pairs={{0,2},{2,0},{4,6},{6,4},{8,10},{10,8},{12,14},{14,12},{16,18},{18,... | collective-permute-start | bytes 442376 | tf_op jit(solution)/shard_map/ppermute | solution.py:394
  29.9 3.7 %collective-permute-start.14 = (f32[16,128]{1,0:T(8,128)S(1)}, f32[16,128]{1,0:T(8,128)S(1)}, u32[]{:S(2)}, u32[]{:S(2)}) collective-permute-start(f32[16,128]{1,0:T(8,128)S(1)} %gate_sum.1.gate_ref), channel_id=1, source_target_pairs={{0,1},{1,0},{2,3},{3,2},{4,5},{5,4},{6,7},{7,6},{8,9},{9,8},{10,11... | collective-permute-start | bytes 24584 | tf_op jit(solution)/shard_map/ppermute | solution.py:398
